TPU v7x, 32 devices: a whole 2x2x4 slice. The times are simulated.
32 devices in a mesh: groups: 2 (over x), tensor: 16 (over z, y, core).
Axes of the slice: x: 2, y: 2, z: 4, core: 2. Of those that a mesh axis runs over, the one named last changes fastest.
Arguments:
- hidden: bfloat16 [768, 26624], P('groups', 'tensor'), parts along dimension 0, may hold values from -6 to 6
- down_matrix: bfloat16 [26624, 8192], P('tensor'), may hold values from -0.0546875 to 0.0546875
- shrink_matrices: bfloat16 [32, 26624, 64], P(None, 'tensor'), may hold values from -0.0390625 to 0.0390625
- expand_matrices: bfloat16 [32, 64, 8192], P(None, None, 'tensor'), may hold values from -0.75 to 0.75
- row_adapter_index: int32 [768], P('groups'), parts along dimension 0, may hold values from 0 to 31, as said below
- segment_first_row: int32 [64], P('groups'), parts along dimension 0, may hold values from 0 to 383, as said below
- segment_length: int32 [64], P('groups'), parts along dimension 0, may hold values from 1 to 48, as said below
Outputs:
- mixed: bfloat16 [768, 8192], P('groups', 'tensor'), parts along dimension 0
There are 2 independent parts, one for each index of `groups`. A program takes and returns all parts, laid end to end along the dimension named above; an argument that names none is the same for every part. Nothing has to cross between parts.
Inputs may be any that keep to these rules, and one draw needn't show every extreme that they name: `row_adapter_index`: row r carries the adapter a with segment_first_row[a] <= r < segment_first_row[a] + segment_length[a]. segment_first_row[0] = 0 and segment_first_row[a + 1] = segment_first_row[a] + segment_length[a]. `segment_length`: every adapter has a row; the lengths sum to 384; the longest is exactly 48.
All inputs are finite; a program needn't handle non-finite values.
Results may differ from a plain program's by a relative error of at most 0.004.
Values may be sent and summed in bfloat16 or wider, within the bound.
No kernel may reach another device: no remote copies, remote signals or barrier semaphores. Data moves between devices by JAX's collectives and lax.ppermute only.
A program may use at most 128 MiB of HBM per device.

v0:
```python
import jax
import jax.numpy as jnp
from jax import lax
from jax.sharding import PartitionSpec as P


def shrink_partial(hidden, shrink_matrices, row_adapter_index):
    adapter_total = shrink_matrices.shape[0]
    every_adapter = jnp.einsum(
        "hq,gqu->hgu", hidden, shrink_matrices, preferred_element_type=jnp.float32
    )
    picked = row_adapter_index[:, None] == jnp.arange(adapter_total, dtype=jnp.int32)[None, :]
    return jnp.sum(jnp.where(picked[:, :, None], every_adapter, 0.0), axis=1)


def expand_partial(shrunk_rows, expand_matrices, segment_first_row, segment_length):
    rows_total = shrunk_rows.shape[0]
    adapter_total = expand_matrices.shape[0]
    rows = jnp.arange(rows_total, dtype=jnp.int32)
    inside = (rows[:, None] >= segment_first_row[None, :]) & (
        rows[:, None] < (segment_first_row + segment_length)[None, :]
    )
    spread = jnp.where(inside[:, :, None], shrunk_rows[:, None, :], jnp.zeros((), jnp.bfloat16))
    spread = spread.reshape(rows_total, adapter_total * shrunk_rows.shape[1])
    adapter_table = expand_matrices.reshape(
        adapter_total * expand_matrices.shape[1], expand_matrices.shape[2]
    )
    return jnp.dot(spread, adapter_table, preferred_element_type=jnp.float32)


def on_device(
    hidden,
    down_matrix,
    shrink_matrices,
    expand_matrices,
    row_adapter_index,
    segment_first_row,
    segment_length,
):
    shrink_portion = shrink_partial(hidden, shrink_matrices, row_adapter_index)
    partial_value = jnp.dot(hidden, down_matrix, preferred_element_type=jnp.float32)
    shrunk_rows = lax.psum(shrink_portion, "tensor").astype(jnp.bfloat16)
    base_partial = lax.psum_scatter(partial_value, "tensor", scatter_dimension=1, tiled=True)
    adapter_output = expand_partial(shrunk_rows, expand_matrices, segment_first_row, segment_length)
    return (base_partial + adapter_output).astype(jnp.bfloat16)


def solution(mesh):
    in_specs = (
        P("groups", "tensor"),
        P("tensor", None),
        P(None, "tensor", None),
        P(None, None, "tensor"),
        P("groups"),
        P("groups"),
        P("groups"),
    )
    out_specs = P("groups", "tensor")
    return jax.shard_map(
        on_device, mesh=mesh, in_specs=in_specs, out_specs=out_specs, check_vma=False
    )
```

profile of v0, /device:TPU:0, one launch (start us, length us, event | category | flops | bytes accessed | tf_op | source)
XLA Modules:
  0.0 174.1 jit_solution(13163546730603418050)
XLA Ops:
  6.5 0.0 copy-start
  6.5 0.0 reduce-scatter.2.cloned.1.call-start
  6.5 19.7 %fusion.16 = f32[384,8192]{1,0:T(8,128)} fusion(bf16[384,1664]{1,0:T(8,128)(2,1)} %param.7, bf16[1664,8192]{1,0:T(8,128)(2,1)} %param.8), kind=kOutput, calls=%fused_computation.14 | convolution fusion | flops 10468982784 | bytes 41123840 | tf_op jit(solution)/shard_map/dot_general | solution.py:41
  26.2 0.0 copy-start.2
  26.2 0.0 copy-start.4
  26.2 0.0 copy-start.1
  26.2 0.0 copy-start.3
  26.3 0.0 reduce-scatter.2.cloned.1.call-update
  26.3 0.6 copy-done.2
  26.9 0.0 copy-done.4
  26.9 0.0 copy-done.1
  27.0 0.6 copy-done.3
  27.6 6.0 %fusion.17 = f32[384,2048]{0,1:S(1)} fusion(bf16[384,1664]{1,0:T(8,128)(2,1)S(1)} %copy-done.3, bf16[1664,2048]{0,1:T(8,128)(2,1)} %bitcast.16), kind=kOutput, calls=%fused_computation.15 | convolution fusion | flops 2617245696 | bytes 11239424
  33.6 0.4 select_reduce_fusion
  34.0 66.5 %psum.7 = bf16[384,64]{0,1:T(8,128)(2,1)S(1)} all-reduce(f32[384,64]{0,1:T(8,128)S(1)} %select_reduce_fusion), channel_id=1, replica_groups=mesh['groups'=2,'tensor'=16] {'tensor'}, use_global_device_ids=true, to_apply=%region_2.3 | all-reduce | flops 24576 | bytes 147456 | tf_op jit(solution)/shard_map/psum | solution.py:42
  100.4 0.1 fusion.14
  100.5 63.8 %reduce-scatter.2.cloned.1.call-done = f32[384,512]{1,0:T(8,128)} async-done(((f32[384,8192]{1,0:T(8,128)}), f32[384,512]{1,0:T(8,128)}) %reduce-scatter.2.cloned.1.call-update) | async-done | bytes 786448 | tf_op jit(solution)/shard_map/reduce_scatter | solution.py:43
  164.3 0.0 copy-done
  164.3 2.9 %fusion.9 = bf16[384,512]{1,0:T(8,128)(2,1)} fusion(f32[384,512]{1,0:T(8,128)} %reduce-scatter.2.cloned.1.call-done, bf16[32,64,512]{2,1,0:T(8,128)(2,1)S(1)} %copy-done, pred[384,32]{0,1:T(8,128)(4,1)S(1)} %fusion.14, bf16[384,64]{0,1:T(8,128)(2,1)S(1)} %psum.7), kind=kOutput, calls=%fused_computation.6 | convolution fusion | flops 806486016 | bytes 3338240 | tf_op jit(solution)/shard_map/dot_general | solution.py:28
  (2 shorter events, 0.0 us)
Async XLA Ops:
  6.5 157.8 %copy-start = (bf16[32,64,512]{2,1,0:T(8,128)(2,1)S(1)}, bf16[32,64,512]{2,1,0:T(8,128)(2,1)}, u32[]{:S(2)}) copy-start(bf16[32,64,512]{2,1,0:T(8,128)(2,1)} %param.10) | copy-start | bytes 6291460
  6.5 157.8 %reduce-scatter.2.cloned.1.call-start = ((), (), s32[]{:S(2)}) async-start(), calls=%async_computation.1 | async-start | bytes 13369344 | tf_op jit(solution)/shard_map/reduce_scatter | solution.py:43
  26.2 0.7 copy-start.2
  26.2 0.7 copy-start.4
  26.2 0.7 copy-start.1
  26.2 1.3 copy-start.3
Sparse Core Ops, SparseCore 0:
  26.4 137.8 reduce-scatter.1
where the time goes:
time: 174 us
  blocking collectives  66.5 us (38%)
  waiting for transfers between devices  63.8 us (37%)
  matrix products  28.6 us (16%)
  between operations  13.4 us (8%)
    psum x1, blocking collectives, on_device(): shrunk_rows = lax.psum(shrink_portion, 'tensor').astype(jnp.bfloat16)  66.5 us
    reduce_scatter x1, waiting for transfers between devices, on_device(): lax.psum_scatter(partial_value, 'tensor', scatter_dimension=1, tiled=True)  63.8 us
    dot_general x1, matrix products, on_device(): jnp.dot(hidden, down_matrix, preferred_element_type=jnp.float32)  19.7 us
    unnamed x1, matrix products  5.99 us
  transfers between devices with their start and end apart: 1, of which 1 were waited for; matrix products, arithmetic and copies ran while one was open for 4% of the time, Pallas kernels for 0%

commit v1 on v0

--- a/solution.py
+++ b/solution.py
@@ -1,7 +1,55 @@
+import functools
+
 import jax
 import jax.numpy as jnp
 from jax import lax
+from jax.experimental import pallas as pl
+from jax.experimental.pallas import tpu as pltpu
 from jax.sharding import PartitionSpec as P
+
+LANES = 128
+
+
+def product_body(order_ref, hidden_ref, *refs, pairs):
+    kept_weights, sent_weights = refs[:pairs], refs[pairs:2 * pairs]
+    kept_ref, sent_ref = refs[2 * pairs:]
+    width = kept_ref.shape[2]
+    weights = jnp.concatenate([ref[...] for ref in (*kept_weights, *sent_weights)], axis=1)
+    total = jnp.dot(hidden_ref[...], weights, preferred_element_type=jnp.float32)
+    for at in range(pairs):
+        kept_ref[at] = total[:, at * width:(at + 1) * width]
+        sent_ref[at] = total[:, (pairs + at) * width:(pairs + at + 1) * width].astype(jnp.bfloat16)
+
+
+def product(hidden, down_matrix, order, width, chunk, chunks, pairs=2):
+    rows, depth = hidden.shape
+    half = order.shape[0] // 2
+
+    def weight_spec(offset):
+        return pl.BlockSpec(
+            (depth, width), lambda step, order: (0, order[step * pairs + offset] * chunks + chunk)
+        )
+
+    return pl.pallas_call(
+        functools.partial(product_body, pairs=pairs),
+        grid_spec=pltpu.PrefetchScalarGridSpec(
+            num_scalar_prefetch=1,
+            grid=(half // pairs,),
+            in_specs=[pl.BlockSpec((rows, depth), lambda step, order: (0, 0))]
+            + [weight_spec(at) for at in range(pairs)]
+            + [weight_spec(half + at) for at in range(pairs)],
+            out_specs=[pl.BlockSpec((pairs, rows, width), lambda step, order: (step, 0, 0))] * 2,
+        ),
+        out_shape=[
+            jax.ShapeDtypeStruct((half, rows, width), jnp.float32),
+            jax.ShapeDtypeStruct((half, rows, width), jnp.bfloat16),
+        ],
+        compiler_params=pltpu.CompilerParams(vmem_limit_bytes=48 * 1024 * 1024),
+    )(order, hidden, *([down_matrix] * (2 * pairs)))
+
+
+def swap(value, bit, total):
+    return lax.ppermute(value, "tensor", [(place, place ^ bit) for place in range(total)])
 
 
 def shrink_partial(hidden, shrink_matrices, row_adapter_index):
@@ -28,7 +76,22 @@
     return jnp.dot(spread, adapter_table, preferred_element_type=jnp.float32)
 
 
+def chunk_bits(total, chunk, chunks):
+    bits = [1 << at for at in range(total.bit_length() - 1)]
+    if chunks > 1 and chunk == 1:
+        bits[1], bits[2] = bits[2], bits[1]
+    return bits
+
+
+def target_order(me, bits):
+    relative = [0]
+    for bit in reversed(bits):
+        relative = relative + [place | bit for place in relative]
+    return jnp.array(relative, dtype=jnp.int32) ^ me
+
+
 def on_device(
+    total,
     hidden,
     down_matrix,
     shrink_matrices,
@@ -37,12 +100,40 @@
     segment_first_row,
     segment_length,
 ):
-    shrink_portion = shrink_partial(hidden, shrink_matrices, row_adapter_index)
-    partial_value = jnp.dot(hidden, down_matrix, preferred_element_type=jnp.float32)
-    shrunk_rows = lax.psum(shrink_portion, "tensor").astype(jnp.bfloat16)
-    base_partial = lax.psum_scatter(partial_value, "tensor", scatter_dimension=1, tiled=True)
+    me = lax.axis_index("tensor").astype(jnp.int32)
+    own_width = down_matrix.shape[1] // total
+    width = min(LANES, own_width)
+    chunks = own_width // width
+    every_bits = [chunk_bits(total, chunk, chunks) for chunk in range(chunks)]
+
+    kept, sent = [], []
+    for chunk in range(chunks):
+        first, second = product(
+            hidden, down_matrix, target_order(me, every_bits[chunk]), width, chunk, chunks
+        )
+        kept.append(first)
+        sent.append(second)
+
+    shrunk = jnp.swapaxes(shrink_partial(hidden, shrink_matrices, row_adapter_index), 0, 1)
+    for bit in every_bits[0]:
+        shrunk = shrunk + swap(shrunk, bit, total)
+    shrunk_rows = jnp.swapaxes(shrunk, 0, 1).astype(jnp.bfloat16)
+
+    parts = []
+    for chunk in range(chunks):
+        bits = every_bits[chunk]
+        for level, bit in enumerate(bits):
+            arrived = swap(sent[chunk], bit, total)
+            summed = kept[chunk] + arrived.astype(jnp.float32)
+            if level + 1 < len(bits):
+                half = summed.shape[0] // 2
+                kept[chunk] = summed[:half]
+                sent[chunk] = summed[half:].astype(jnp.bfloat16)
+            else:
+                parts.append(summed[0])
+    base = jnp.concatenate(parts, axis=1)
     adapter_output = expand_partial(shrunk_rows, expand_matrices, segment_first_row, segment_length)
-    return (base_partial + adapter_output).astype(jnp.bfloat16)
+    return (base + adapter_output).astype(jnp.bfloat16)
 
 
 def solution(mesh):
@@ -57,5 +148,9 @@
     )
     out_specs = P("groups", "tensor")
     return jax.shard_map(
-        on_device, mesh=mesh, in_specs=in_specs, out_specs=out_specs, check_vma=False
+        functools.partial(on_device, mesh.shape["tensor"]),
+        mesh=mesh,
+        in_specs=in_specs,
+        out_specs=out_specs,
+        check_vma=False,
     )

time: 174 us -> 104 us (0.60)
  blocking collectives: 66.5 us -> 0 us
  Pallas kernels: 0 us -> 25.2 us
  starting transfers between devices: 0.01 us -> 20.7 us
  matrix products: 28.6 us -> 8.14 us
  waiting for transfers between devices: 63.8 us -> 45.3 us
  between operations: 13.4 us -> 0.36 us
  other arithmetic: 0.48 us -> 3.43 us
    psum x1 -> x0, blocking collectives: 66.5 us -> none  [on_device(): shrunk_rows = lax.psum(shrink_portion, 'tensor').astype(jnp.bfloat16)]
    reduce_scatter x1 -> x0, waiting for transfers between devices: 63.8 us -> none  [on_device(): lax.psum_scatter(partial_value, 'tensor', scatter_dimension=1, tiled=True)]
    ppermute x0 -> x20, waiting for transfers between devices: none -> 45.3 us  [swap(): lax.ppermute(value, 'tensor', [(place, place ^ bit) for place in range(to...]
    pallas_call x0 -> x4, Pallas kernels: none -> 25.2 us  [product(): pl.pallas_call(functools.partial(product_body, pairs=pairs), grid_spec=pl...]
    ppermute x0 -> x20, starting transfers between devices: none -> 20.7 us  [swap(): lax.ppermute(value, 'tensor', [(place, place ^ bit) for place in range(to...]
    dot_general x1 -> x0, matrix products: 19.7 us -> none  [on_device(): jnp.dot(hidden, down_matrix, preferred_element_type=jnp.float32)]
    add x0 -> x15, other arithmetic: none -> 2.02 us  [the longest x12 1.09 us: on_device(): summed = kept[chunk] + arrived.astype(jnp.float32)]
  transfers between devices with their start and end apart: 1 -> 20, of which waited for: 1 -> 10; matrix products, arithmetic and copies ran while one was open for 4% -> 2% of each run, Pallas kernels for 0% -> 24%
where the time goes in v1:
time: 104 us
  waiting for transfers between devices  45.3 us (44%)
  Pallas kernels  25.2 us (24%)
  starting transfers between devices  20.7 us (20%)
  matrix products  8.14 us (8%)
  other arithmetic  3.43 us (3%)
    ppermute x20, waiting for transfers between devices, swap(): lax.ppermute(value, 'tensor', [(place, place ^ bit) for place in range(to...  45.3 us
    pallas_call x4, Pallas kernels, product(): pl.pallas_call(functools.partial(product_body, pairs=pairs), grid_spec=pl...  25.2 us
    ppermute x20, starting transfers between devices, swap(): lax.ppermute(value, 'tensor', [(place, place ^ bit) for place in range(to...  20.7 us
    unnamed x1, matrix products  6.37 us
  transfers between devices with their start and end apart: 20, of which 10 were waited for; matrix products, arithmetic and copies ran while one was open for 2% of the time, Pallas kernels for 24%

profile of v1, /device:TPU:0, one launch (start us, length us, event | category | flops | bytes accessed | tf_op | source)
XLA Modules:
  0.0 103.9 jit_solution(10302716947506106114)
XLA Ops:
  0.8 6.4 %fusion.18 = f32[384,2048]{0,1:S(1)} fusion(bf16[384,1664]{1,0:T(8,128)(2,1)} %hidden_ref.7, bf16[1664,2048]{0,1:T(8,128)(2,1)} %bitcast.25), kind=kOutput, calls=%fused_computation.51 | convolution fusion | flops 2617245696 | bytes 11239424
  8.6 6.3 %shard_map.109 = (f32[8,384,128]{2,1,0:T(8,128)S(1)}, bf16[8,384,128]{2,1,0:T(8,128)(2,1)S(1)}) custom-call(s32[16]{0:T(128)S(1)} %get-tuple-element.22.order_ref, bf16[384,1664]{1,0:T(8,128)(2,1)S(1)} %copy-done.1, bf16[1664,8192]{1,0:T(8,128)(2,1)} %refs_3_.7, bf16[1664,8192]{1,0:T(8,128)(2,1)} %refs_3_.7, bf16[1664,8192]{1,0:T(8,128)(2,1)} %refs_3_.7, ...), custom_call_target="tpu_custom_call" | custom-call | tf_op jit(solution)/shard_map/pallas_call | solution.py:33
  16.3 2.6 %collective-permute-start.17 = (f32[64,384]{1,0:T(8,128)S(1)}, f32[64,384]{1,0:T(8,128)S(1)}, u32[]{:S(2)}, u32[]{:S(2)}) collective-permute-start(f32[64,384]{1,0:T(8,128)S(1)} %bitcast_add_fusion), channel_id=1, source_target_pairs={{0,2},{1,3},{2,0},{3,1},{4,6},{5,7},{6,4},{7,5},{8,10},{9,11},{10,... | collective-permute-start | bytes 294920 | tf_op jit(solution)/shard_map/ppermute | solution.py:52
  18.9 3.4 %collective-permute-done.17 = f32[64,384]{1,0:T(8,128)S(1)} collective-permute-done((f32[64,384]{1,0:T(8,128)S(1)}, f32[64,384]{1,0:T(8,128)S(1)}, u32[]{:S(2)}, u32[]{:S(2)}) %collective-permute-start.17) | collective-permute-done | bytes 98336 | tf_op jit(solution)/shard_map/ppermute | solution.py:52
  22.4 1.9 %collective-permute-start.18 = (f32[64,384]{1,0:T(8,128)S(1)}, f32[64,384]{1,0:T(8,128)S(1)}, u32[]{:S(2)}, u32[]{:S(2)}) collective-permute-start(f32[64,384]{1,0:T(8,128)S(1)} %add.84), channel_id=1, source_target_pairs={{0,4},{1,5},{2,6},{3,7},{4,0},{5,1},{6,2},{7,3},{8,12},{9,13},{10,... | collective-permute-start | bytes 294920 | tf_op jit(solution)/shard_map/ppermute | solution.py:52
  24.2 6.3 %shard_map.111 = (f32[8,384,128]{2,1,0:T(8,128)S(1)}, bf16[8,384,128]{2,1,0:T(8,128)(2,1)S(1)}) custom-call(s32[16]{0:T(128)S(1)} %get-tuple-element.22.order_ref, bf16[384,1664]{1,0:T(8,128)(2,1)S(1)} %copy-done.1, bf16[1664,8192]{1,0:T(8,128)(2,1)} %refs_3_.7, bf16[1664,8192]{1,0:T(8,128)(2,1)} %refs_3_.7, bf16[1664,8192]{1,0:T(8,128)(2,1)} %refs_3_.7, ...), custom_call_target="tpu_custom_call" | custom-call | tf_op jit(solution)/shard_map/pallas_call | solution.py:33
  30.6 6.3 %shard_map.112 = (f32[8,384,128]{2,1,0:T(8,128)S(1)}, bf16[8,384,128]{2,1,0:T(8,128)(2,1)S(1)}) custom-call(s32[16]{0:T(128)S(1)} %get-tuple-element.22.order_ref, bf16[384,1664]{1,0:T(8,128)(2,1)S(1)} %copy-done.1, bf16[1664,8192]{1,0:T(8,128)(2,1)} %refs_3_.7, bf16[1664,8192]{1,0:T(8,128)(2,1)} %refs_3_.7, bf16[1664,8192]{1,0:T(8,128)(2,1)} %refs_3_.7, ...), custom_call_target="tpu_custom_call" | custom-call | tf_op jit(solution)/shard_map/pallas_call | solution.py:33
  37.5 6.3 %shard_map.110 = (f32[8,384,128]{2,1,0:T(8,128)S(1)}, bf16[8,384,128]{2,1,0:T(8,128)(2,1)S(1)}) custom-call(s32[16]{0:T(128)S(1)} %get-tuple-element.21.order_ref, bf16[384,1664]{1,0:T(8,128)(2,1)S(1)} %copy-done.1, bf16[1664,8192]{1,0:T(8,128)(2,1)} %refs_3_.7, bf16[1664,8192]{1,0:T(8,128)(2,1)} %refs_3_.7, bf16[1664,8192]{1,0:T(8,128)(2,1)} %refs_3_.7, ...), custom_call_target="tpu_custom_call" | custom-call | tf_op jit(solution)/shard_map/pallas_call | solution.py:33
  44.0 2.7 %collective-permute-start.19 = (f32[64,384]{1,0:T(8,128)S(1)}, f32[64,384]{1,0:T(8,128)S(1)}, u32[]{:S(2)}, u32[]{:S(2)}) collective-permute-start(f32[64,384]{1,0:T(8,128)S(1)} %add.85), channel_id=1, source_target_pairs={{0,8},{1,9},{2,10},{3,11},{4,12},{5,13},{6,14},{7,15},{8,0},{9,1},... | collective-permute-start | bytes 294920 | tf_op jit(solution)/shard_map/ppermute | solution.py:52
  46.7 5.3 %collective-permute-done.19 = f32[64,384]{1,0:T(8,128)S(1)} collective-permute-done((f32[64,384]{1,0:T(8,128)S(1)}, f32[64,384]{1,0:T(8,128)S(1)}, u32[]{:S(2)}, u32[]{:S(2)}) %collective-permute-start.19) | collective-permute-done | bytes 98336 | tf_op jit(solution)/shard_map/ppermute | solution.py:52
  52.3 1.6 %collective-permute-start.1 = (bf16[4,384,128]{2,1,0:T(8,128)(2,1)S(1)}, bf16[4,384,128]{2,1,0:T(8,128)(2,1)S(1)}, u32[]{:S(2)}, u32[]{:S(2)}) collective-permute-start(bf16[4,384,128]{2,1,0:T(8,128)(2,1)S(1)} %slice.167), channel_id=1, source_target_pairs={{0,2},{1,3},{2,0},{3,1},{4,6},{5,7},{6,4},{7,5},{8,10},{9,11},{10,... | collective-permute-start | bytes 1179656 | tf_op jit(solution)/shard_map/ppermute | solution.py:52
  54.9 1.6 %collective-permute-start.13 = (bf16[4,384,128]{2,1,0:T(8,128)(2,1)S(1)}, bf16[4,384,128]{2,1,0:T(8,128)(2,1)S(1)}, u32[]{:S(2)}, u32[]{:S(2)}) collective-permute-start(bf16[4,384,128]{2,1,0:T(8,128)(2,1)S(1)} %slice.164), channel_id=1, source_target_pairs={{0,2},{1,3},{2,0},{3,1},{4,6},{5,7},{6,4},{7,5},{8,10},{9,11},{10,... | collective-permute-start | bytes 1179656 | tf_op jit(solution)/shard_map/ppermute | solution.py:52
  56.9 7.4 %collective-permute-done.1 = bf16[4,384,128]{2,1,0:T(8,128)(2,1)S(1)} collective-permute-done((bf16[4,384,128]{2,1,0:T(8,128)(2,1)S(1)}, bf16[4,384,128]{2,1,0:T(8,128)(2,1)S(1)}, u32[]{:S(2)}, u32[]{:S(2)}) %collective-permute-start.1) | collective-permute-done | bytes 393248 | tf_op jit(solution)/shard_map/ppermute | solution.py:52
  64.5 8.2 %collective-permute-done.9 = bf16[4,384,128]{2,1,0:T(8,128)(2,1)S(1)} collective-permute-done((bf16[4,384,128]{2,1,0:T(8,128)(2,1)S(1)}, bf16[4,384,128]{2,1,0:T(8,128)(2,1)S(1)}, u32[]{:S(2)}, u32[]{:S(2)}) %collective-permute-start.9) | collective-permute-done | bytes 393248 | tf_op jit(solution)/shard_map/ppermute | solution.py:52
  72.9 7.4 %collective-permute-done.13 = bf16[4,384,128]{2,1,0:T(8,128)(2,1)S(1)} collective-permute-done((bf16[4,384,128]{2,1,0:T(8,128)(2,1)S(1)}, bf16[4,384,128]{2,1,0:T(8,128)(2,1)S(1)}, u32[]{:S(2)}, u32[]{:S(2)}) %collective-permute-start.13) | collective-permute-done | bytes 393248 | tf_op jit(solution)/shard_map/ppermute | solution.py:52
  80.6 1.6 %collective-permute-start.6 = (bf16[2,384,128]{2,1,0:T(8,128)(2,1)S(1)}, bf16[2,384,128]{2,1,0:T(8,128)(2,1)S(1)}, u32[]{:S(2)}, u32[]{:S(2)}) collective-permute-start(bf16[2,384,128]{2,1,0:T(8,128)(2,1)S(1)} %slice.170), channel_id=1, source_target_pairs={{0,2},{1,3},{2,0},{3,1},{4,6},{5,7},{6,4},{7,5},{8,10},{9,11},{10,... | collective-permute-start | bytes 589832 | tf_op jit(solution)/shard_map/ppermute | solution.py:52
  82.3 2.8 %collective-permute-start.3 = (bf16[1,384,128]{2,1,0:T(8,128)(2,1)S(1)}, bf16[1,384,128]{2,1,0:T(8,128)(2,1)S(1)}, u32[]{:S(2)}, u32[]{:S(2)}) collective-permute-start(bf16[1,384,128]{2,1,0:T(8,128)(2,1)S(1)} %slice.175), channel_id=1, source_target_pairs={{0,8},{1,9},{2,10},{3,11},{4,12},{5,13},{6,14},{7,15},{8,0},{9,1},... | collective-permute-start | bytes 294920 | tf_op jit(solution)/shard_map/ppermute | solution.py:52
  85.4 2.5 %collective-permute-done.14 = bf16[2,384,128]{2,1,0:T(8,128)(2,1)S(1)} collective-permute-done((bf16[2,384,128]{2,1,0:T(8,128)(2,1)S(1)}, bf16[2,384,128]{2,1,0:T(8,128)(2,1)S(1)}, u32[]{:S(2)}, u32[]{:S(2)}) %collective-permute-start.14) | collective-permute-done | bytes 196640 | tf_op jit(solution)/shard_map/ppermute | solution.py:52
  88.3 2.7 %collective-permute-start.7 = (bf16[1,384,128]{2,1,0:T(8,128)(2,1)S(1)}, bf16[1,384,128]{2,1,0:T(8,128)(2,1)S(1)}, u32[]{:S(2)}, u32[]{:S(2)}) collective-permute-start(bf16[1,384,128]{2,1,0:T(8,128)(2,1)S(1)} %slice.174), channel_id=1, source_target_pairs={{0,8},{1,9},{2,10},{3,11},{4,12},{5,13},{6,14},{7,15},{8,0},{9,1},... | collective-permute-start | bytes 294920 | tf_op jit(solution)/shard_map/ppermute | solution.py:52
  91.0 5.9 %collective-permute-done.3 = bf16[1,384,128]{2,1,0:T(8,128)(2,1)S(1)} collective-permute-done((bf16[1,384,128]{2,1,0:T(8,128)(2,1)S(1)}, bf16[1,384,128]{2,1,0:T(8,128)(2,1)S(1)}, u32[]{:S(2)}, u32[]{:S(2)}) %collective-permute-start.3) | collective-permute-done | bytes 98336 | tf_op jit(solution)/shard_map/ppermute | solution.py:52
  97.0 2.1 %collective-permute-done.11 = bf16[1,384,128]{2,1,0:T(8,128)(2,1)S(1)} collective-permute-done((bf16[1,384,128]{2,1,0:T(8,128)(2,1)S(1)}, bf16[1,384,128]{2,1,0:T(8,128)(2,1)S(1)}, u32[]{:S(2)}, u32[]{:S(2)}) %collective-permute-start.11) | collective-permute-done | bytes 98336 | tf_op jit(solution)/shard_map/ppermute | solution.py:52
  99.1 2.0 %collective-permute-done.15 = bf16[1,384,128]{2,1,0:T(8,128)(2,1)S(1)} collective-permute-done((bf16[1,384,128]{2,1,0:T(8,128)(2,1)S(1)}, bf16[1,384,128]{2,1,0:T(8,128)(2,1)S(1)}, u32[]{:S(2)}, u32[]{:S(2)}) %collective-permute-start.15) | collective-permute-done | bytes 98336 | tf_op jit(solution)/shard_map/ppermute | solution.py:52
  101.1 1.0 collective-permute-done.7
  102.2 1.8 %fusion.6 = bf16[384,512]{1,0:T(8,128)(2,1)} fusion(f32[384,128]{1,0:T(8,128)S(1)} %fusion.11, f32[384,128]{1,0:T(8,128)S(1)} %fusion.12, f32[384,128]{1,0:T(8,128)S(1)} %fusion.13, f32[384,128]{1,0:T(8,128)S(1)} %fusion.14, bf16[32,64,512]{2,1,0:T(8,128)(2,1)S(1)} %copy-done, pred[384,32]{0,1:T(8,128)(4,1)S(1)} %fusion.16, bf16[384,64]{0,1:T(8,128)(2,1)S(1)} %fusion.15), kind=kOutput, calls=%fused_computation.18 | convolution fusion | flops 807075840 | bytes 3338240 | tf_op jit(solution)/shard_map/dot_general | solution.py:76
  (71 shorter events, 7.4 us)
Async XLA Ops:
  0.0 102.2 %copy-start = (bf16[32,64,512]{2,1,0:T(8,128)(2,1)S(1)}, bf16[32,64,512]{2,1,0:T(8,128)(2,1)}, u32[]{:S(2)}) copy-start(bf16[32,64,512]{2,1,0:T(8,128)(2,1)} %param.14) | copy-start | bytes 6291460
  7.3 1.3 %copy-start.1 = (bf16[384,1664]{1,0:T(8,128)(2,1)S(1)}, bf16[384,1664]{1,0:T(8,128)(2,1)}, u32[]{:S(2)}) copy-start(bf16[384,1664]{1,0:T(8,128)(2,1)} %hidden_ref.7) | copy-start | bytes 3833860
  7.7 7.7 %collective-permute-start.16 = (f32[64,384]{1,0:T(8,128)S(1)}, f32[64,384]{1,0:T(8,128)}, u32[]{:S(2)}, u32[]{:S(2)}) collective-permute-start(f32[64,384]{1,0:T(8,128)S(1)} %bitcast.24), channel_id=1, source_target_pairs={{0,1},{1,0},{2,3},{3,2},{4,5},{5,4},{6,7},{7,6},{8,9},{9,8},{10,11... | collective-permute-start | bytes 294920 | tf_op jit(solution)/shard_map/ppermute | solution.py:52
  14.9 37.2 %collective-permute-start = (bf16[8,384,128]{2,1,0:T(8,128)(2,1)S(1)}, bf16[8,384,128]{2,1,0:T(8,128)(2,1)S(1)}, u32[]{:S(2)}, u32[]{:S(2)}) collective-permute-start(bf16[8,384,128]{2,1,0:T(8,128)(2,1)S(1)} %get-tuple-element.14), channel_id=1, source_target_pairs={{0,1},{1,0},{2,3},{3,2},{4,5},{5,4},{6,7},{7,6},{8,9},{9,8},{10,11... | collective-permute-start | bytes 2359304 | tf_op jit(solution)/shard_map/ppermute | solution.py:52
  16.3 6.0 %collective-permute-start.17 = (f32[64,384]{1,0:T(8,128)S(1)}, f32[64,384]{1,0:T(8,128)S(1)}, u32[]{:S(2)}, u32[]{:S(2)}) collective-permute-start(f32[64,384]{1,0:T(8,128)S(1)} %bitcast_add_fusion), channel_id=1, source_target_pairs={{0,2},{1,3},{2,0},{3,1},{4,6},{5,7},{6,4},{7,5},{8,10},{9,11},{10,... | collective-permute-start | bytes 294920 | tf_op jit(solution)/shard_map/ppermute | solution.py:52
  22.4 21.6 %collective-permute-start.18 = (f32[64,384]{1,0:T(8,128)S(1)}, f32[64,384]{1,0:T(8,128)S(1)}, u32[]{:S(2)}, u32[]{:S(2)}) collective-permute-start(f32[64,384]{1,0:T(8,128)S(1)} %add.84), channel_id=1, source_target_pairs={{0,4},{1,5},{2,6},{3,7},{4,0},{5,1},{6,2},{7,3},{8,12},{9,13},{10,... | collective-permute-start | bytes 294920 | tf_op jit(solution)/shard_map/ppermute | solution.py:52
  30.5 23.4 %collective-permute-start.8 = (bf16[8,384,128]{2,1,0:T(8,128)(2,1)S(1)}, bf16[8,384,128]{2,1,0:T(8,128)(2,1)S(1)}, u32[]{:S(2)}, u32[]{:S(2)}) collective-permute-start(bf16[8,384,128]{2,1,0:T(8,128)(2,1)S(1)} %get-tuple-element.18), channel_id=1, source_target_pairs={{0,1},{1,0},{2,3},{3,2},{4,5},{5,4},{6,7},{7,6},{8,9},{9,8},{10,11... | collective-permute-start | bytes 2359304 | tf_op jit(solution)/shard_map/ppermute | solution.py:52
  36.9 17.7 %collective-permute-start.12 = (bf16[8,384,128]{2,1,0:T(8,128)(2,1)S(1)}, bf16[8,384,128]{2,1,0:T(8,128)(2,1)S(1)}, u32[]{:S(2)}, u32[]{:S(2)}) collective-permute-start(bf16[8,384,128]{2,1,0:T(8,128)(2,1)S(1)} %get-tuple-element.20), channel_id=1, source_target_pairs={{0,1},{1,0},{2,3},{3,2},{4,5},{5,4},{6,7},{7,6},{8,9},{9,8},{10,11... | collective-permute-start | bytes 2359304 | tf_op jit(solution)/shard_map/ppermute | solution.py:52
  37.5 6.4 %copy-start.4 = (s32[32]{0:T(128)S(1)}, s32[32]{0:T(128)}, u32[]{:S(2)}) copy-start(s32[32]{0:T(128)} %param.16) | copy-start | bytes 388
  37.5 6.4 %copy-start.5 = (s32[32]{0:T(128)S(1)}, s32[32]{0:T(128)}, u32[]{:S(2)}) copy-start(s32[32]{0:T(128)} %param.17) | copy-start | bytes 388
  43.8 12.8 %collective-permute-start.4 = (bf16[8,384,128]{2,1,0:T(8,128)(2,1)S(1)}, bf16[8,384,128]{2,1,0:T(8,128)(2,1)S(1)}, u32[]{:S(2)}, u32[]{:S(2)}) collective-permute-start(bf16[8,384,128]{2,1,0:T(8,128)(2,1)S(1)} %get-tuple-element.16), channel_id=1, source_target_pairs={{0,1},{1,0},{2,3},{3,2},{4,5},{5,4},{6,7},{7,6},{8,9},{9,8},{10,11... | collective-permute-start | bytes 2359304 | tf_op jit(solution)/shard_map/ppermute | solution.py:52
  44.0 8.1 %collective-permute-start.19 = (f32[64,384]{1,0:T(8,128)S(1)}, f32[64,384]{1,0:T(8,128)S(1)}, u32[]{:S(2)}, u32[]{:S(2)}) collective-permute-start(f32[64,384]{1,0:T(8,128)S(1)} %add.85), channel_id=1, source_target_pairs={{0,8},{1,9},{2,10},{3,11},{4,12},{5,13},{6,14},{7,15},{8,0},{9,1},... | collective-permute-start | bytes 294920 | tf_op jit(solution)/shard_map/ppermute | solution.py:52
  52.3 12.0 %collective-permute-start.1 = (bf16[4,384,128]{2,1,0:T(8,128)(2,1)S(1)}, bf16[4,384,128]{2,1,0:T(8,128)(2,1)S(1)}, u32[]{:S(2)}, u32[]{:S(2)}) collective-permute-start(bf16[4,384,128]{2,1,0:T(8,128)(2,1)S(1)} %slice.167), channel_id=1, source_target_pairs={{0,2},{1,3},{2,0},{3,1},{4,6},{5,7},{6,4},{7,5},{8,10},{9,11},{10,... | collective-permute-start | bytes 1179656 | tf_op jit(solution)/shard_map/ppermute | solution.py:52
  54.1 18.6 %collective-permute-start.9 = (bf16[4,384,128]{2,1,0:T(8,128)(2,1)S(1)}, bf16[4,384,128]{2,1,0:T(8,128)(2,1)S(1)}, u32[]{:S(2)}, u32[]{:S(2)}) collective-permute-start(bf16[4,384,128]{2,1,0:T(8,128)(2,1)S(1)} %slice.165), channel_id=1, source_target_pairs={{0,2},{1,3},{2,0},{3,1},{4,6},{5,7},{6,4},{7,5},{8,10},{9,11},{10,... | collective-permute-start | bytes 1179656 | tf_op jit(solution)/shard_map/ppermute | solution.py:52
  54.9 25.4 %collective-permute-start.13 = (bf16[4,384,128]{2,1,0:T(8,128)(2,1)S(1)}, bf16[4,384,128]{2,1,0:T(8,128)(2,1)S(1)}, u32[]{:S(2)}, u32[]{:S(2)}) collective-permute-start(bf16[4,384,128]{2,1,0:T(8,128)(2,1)S(1)} %slice.164), channel_id=1, source_target_pairs={{0,2},{1,3},{2,0},{3,1},{4,6},{5,7},{6,4},{7,5},{8,10},{9,11},{10,... | collective-permute-start | bytes 1179656 | tf_op jit(solution)/shard_map/ppermute | solution.py:52
  56.8 23.7 %collective-permute-start.5 = (bf16[4,384,128]{2,1,0:T(8,128)(2,1)S(1)}, bf16[4,384,128]{2,1,0:T(8,128)(2,1)S(1)}, u32[]{:S(2)}, u32[]{:S(2)}) collective-permute-start(bf16[4,384,128]{2,1,0:T(8,128)(2,1)S(1)} %slice.166), channel_id=1, source_target_pairs={{0,4},{1,5},{2,6},{3,7},{4,0},{5,1},{6,2},{7,3},{8,12},{9,13},{10,... | collective-permute-start | bytes 1179656 | tf_op jit(solution)/shard_map/ppermute | solution.py:52
  64.4 17.8 %collective-permute-start.2 = (bf16[2,384,128]{2,1,0:T(8,128)(2,1)S(1)}, bf16[2,384,128]{2,1,0:T(8,128)(2,1)S(1)}, u32[]{:S(2)}, u32[]{:S(2)}) collective-permute-start(bf16[2,384,128]{2,1,0:T(8,128)(2,1)S(1)} %slice.171), channel_id=1, source_target_pairs={{0,4},{1,5},{2,6},{3,7},{4,0},{5,1},{6,2},{7,3},{8,12},{9,13},{10,... | collective-permute-start | bytes 589832 | tf_op jit(solution)/shard_map/ppermute | solution.py:52
  72.8 12.3 %collective-permute-start.10 = (bf16[2,384,128]{2,1,0:T(8,128)(2,1)S(1)}, bf16[2,384,128]{2,1,0:T(8,128)(2,1)S(1)}, u32[]{:S(2)}, u32[]{:S(2)}) collective-permute-start(bf16[2,384,128]{2,1,0:T(8,128)(2,1)S(1)} %slice.169), channel_id=1, source_target_pairs={{0,4},{1,5},{2,6},{3,7},{4,0},{5,1},{6,2},{7,3},{8,12},{9,13},{10,... | collective-permute-start | bytes 589832 | tf_op jit(solution)/shard_map/ppermute | solution.py:52
  80.4 7.5 %collective-permute-start.14 = (bf16[2,384,128]{2,1,0:T(8,128)(2,1)S(1)}, bf16[2,384,128]{2,1,0:T(8,128)(2,1)S(1)}, u32[]{:S(2)}, u32[]{:S(2)}) collective-permute-start(bf16[2,384,128]{2,1,0:T(8,128)(2,1)S(1)} %slice.168), channel_id=1, source_target_pairs={{0,4},{1,5},{2,6},{3,7},{4,0},{5,1},{6,2},{7,3},{8,12},{9,13},{10,... | collective-permute-start | bytes 589832 | tf_op jit(solution)/shard_map/ppermute | solution.py:52
  80.6 7.7 %collective-permute-start.6 = (bf16[2,384,128]{2,1,0:T(8,128)(2,1)S(1)}, bf16[2,384,128]{2,1,0:T(8,128)(2,1)S(1)}, u32[]{:S(2)}, u32[]{:S(2)}) collective-permute-start(bf16[2,384,128]{2,1,0:T(8,128)(2,1)S(1)} %slice.170), channel_id=1, source_target_pairs={{0,2},{1,3},{2,0},{3,1},{4,6},{5,7},{6,4},{7,5},{8,10},{9,11},{10,... | collective-permute-start | bytes 589832 | tf_op jit(solution)/shard_map/ppermute | solution.py:52
  82.3 14.7 %collective-permute-start.3 = (bf16[1,384,128]{2,1,0:T(8,128)(2,1)S(1)}, bf16[1,384,128]{2,1,0:T(8,128)(2,1)S(1)}, u32[]{:S(2)}, u32[]{:S(2)}) collective-permute-start(bf16[1,384,128]{2,1,0:T(8,128)(2,1)S(1)} %slice.175), channel_id=1, source_target_pairs={{0,8},{1,9},{2,10},{3,11},{4,12},{5,13},{6,14},{7,15},{8,0},{9,1},... | collective-permute-start | bytes 294920 | tf_op jit(solution)/shard_map/ppermute | solution.py:52
  85.2 13.9 %collective-permute-start.11 = (bf16[1,384,128]{2,1,0:T(8,128)(2,1)S(1)}, bf16[1,384,128]{2,1,0:T(8,128)(2,1)S(1)}, u32[]{:S(2)}, u32[]{:S(2)}) collective-permute-start(bf16[1,384,128]{2,1,0:T(8,128)(2,1)S(1)} %slice.173), channel_id=1, source_target_pairs={{0,8},{1,9},{2,10},{3,11},{4,12},{5,13},{6,14},{7,15},{8,0},{9,1},... | collective-permute-start | bytes 294920 | tf_op jit(solution)/shard_map/ppermute | solution.py:52
  87.9 13.2 %collective-permute-start.15 = (bf16[1,384,128]{2,1,0:T(8,128)(2,1)S(1)}, bf16[1,384,128]{2,1,0:T(8,128)(2,1)S(1)}, u32[]{:S(2)}, u32[]{:S(2)}) collective-permute-start(bf16[1,384,128]{2,1,0:T(8,128)(2,1)S(1)} %slice.172), channel_id=1, source_target_pairs={{0,8},{1,9},{2,10},{3,11},{4,12},{5,13},{6,14},{7,15},{8,0},{9,1},... | collective-permute-start | bytes 294920 | tf_op jit(solution)/shard_map/ppermute | solution.py:52
  88.3 13.8 %collective-permute-start.7 = (bf16[1,384,128]{2,1,0:T(8,128)(2,1)S(1)}, bf16[1,384,128]{2,1,0:T(8,128)(2,1)S(1)}, u32[]{:S(2)}, u32[]{:S(2)}) collective-permute-start(bf16[1,384,128]{2,1,0:T(8,128)(2,1)S(1)} %slice.174), channel_id=1, source_target_pairs={{0,8},{1,9},{2,10},{3,11},{4,12},{5,13},{6,14},{7,15},{8,0},{9,1},... | collective-permute-start | bytes 294920 | tf_op jit(solution)/shard_map/ppermute | solution.py:52
  (2 other events, 1.9 us)

commit v2 on v0

--- a/solution.py
+++ b/solution.py
@@ -1,7 +1,60 @@
+import functools
+
 import jax
 import jax.numpy as jnp
 from jax import lax
+from jax.experimental import pallas as pl
+from jax.experimental.pallas import tpu as pltpu
 from jax.sharding import PartitionSpec as P
+
+BLOCK = 256
+
+
+def product_body(order_ref, hidden_ref, kept_weights, sent_weights, kept_ref, sent_ref):
+    hidden = hidden_ref[...]
+    sent_ref[0] = jnp.dot(
+        hidden, sent_weights[...], preferred_element_type=jnp.float32
+    ).astype(jnp.bfloat16)
+    kept_ref[0] = jnp.dot(hidden, kept_weights[...], preferred_element_type=jnp.float32)
+
+
+def product(hidden, down_matrix, order, width):
+    rows, depth = hidden.shape
+    half = order.shape[0] // 2
+    block = min(BLOCK, width)
+    blocks = width // block
+
+    def weight_spec(offset):
+        return pl.BlockSpec(
+            (depth, block), lambda at, part, order: (0, order[offset + at] * blocks + part)
+        )
+
+    return pl.pallas_call(
+        product_body,
+        grid_spec=pltpu.PrefetchScalarGridSpec(
+            num_scalar_prefetch=1,
+            grid=(half, blocks),
+            in_specs=[
+                pl.BlockSpec((rows, depth), lambda at, part, order: (0, 0)),
+                weight_spec(0),
+                weight_spec(half),
+            ],
+            out_specs=[pl.BlockSpec((1, rows, block), lambda at, part, order: (at, 0, part))] * 2,
+        ),
+        out_shape=[
+            jax.ShapeDtypeStruct((half, rows, width), jnp.float32),
+            jax.ShapeDtypeStruct((half, rows, width), jnp.bfloat16),
+        ],
+        compiler_params=pltpu.CompilerParams(vmem_limit_bytes=48 * 1024 * 1024),
+    )(order, hidden, down_matrix, down_matrix)
+
+
+def swap(value, bit, total):
+    return lax.ppermute(value, "tensor", [(place, place ^ bit) for place in range(total)])
+
+
+def after(value, earlier):
+    return lax.optimization_barrier((value, earlier))[0]
 
 
 def shrink_partial(hidden, shrink_matrices, row_adapter_index):
@@ -29,6 +82,7 @@
 
 
 def on_device(
+    total,
     hidden,
     down_matrix,
     shrink_matrices,
@@ -37,12 +91,39 @@
     segment_first_row,
     segment_length,
 ):
-    shrink_portion = shrink_partial(hidden, shrink_matrices, row_adapter_index)
-    partial_value = jnp.dot(hidden, down_matrix, preferred_element_type=jnp.float32)
-    shrunk_rows = lax.psum(shrink_portion, "tensor").astype(jnp.bfloat16)
-    base_partial = lax.psum_scatter(partial_value, "tensor", scatter_dimension=1, tiled=True)
+    me = lax.axis_index("tensor").astype(jnp.int32)
+    width = down_matrix.shape[1] // total
+    core, near = 1, 2
+    units = total // 4
+
+    kept, sent, ready = {}, {}, []
+    for unit in reversed(range(units)):
+        far = unit * 4
+        order = jnp.array([far, far | near, far | core, far | near | core], dtype=jnp.int32) ^ me
+        if len(ready) > 1:
+            order = after(order, ready[-2])
+        first, second = product(hidden, down_matrix, order, width)
+        arrived = swap(second, core, total)
+        kept[unit] = first[0] + arrived[0].astype(jnp.float32)
+        sent[unit] = (first[1] + arrived[1].astype(jnp.float32)).astype(jnp.bfloat16)
+        ready.append(sent[unit])
+
+    late_hidden = after(hidden, ready[-2])
+    shrunk = jnp.swapaxes(shrink_partial(late_hidden, shrink_matrices, row_adapter_index), 0, 1)
+    for level in range(total.bit_length() - 1):
+        shrunk = shrunk + swap(shrunk, 1 << level, total)
+    shrunk_rows = jnp.swapaxes(shrunk, 0, 1).astype(jnp.bfloat16)
     adapter_output = expand_partial(shrunk_rows, expand_matrices, segment_first_row, segment_length)
-    return (base_partial + adapter_output).astype(jnp.bfloat16)
+
+    for unit in reversed(range(units)):
+        kept[unit] = kept[unit] + swap(sent[unit], near, total).astype(jnp.float32)
+    bit = 1
+    while bit < units:
+        for unit in reversed(range(0, units, 2 * bit)):
+            moved = swap(kept[unit | bit].astype(jnp.bfloat16), 4 * bit, total)
+            kept[unit] = kept[unit] + moved.astype(jnp.float32)
+        bit *= 2
+    return (kept[0] + adapter_output).astype(jnp.bfloat16)
 
 
 def solution(mesh):
@@ -57,5 +138,9 @@
     )
     out_specs = P("groups", "tensor")
     return jax.shard_map(
-        on_device, mesh=mesh, in_specs=in_specs, out_specs=out_specs, check_vma=False
+        functools.partial(on_device, mesh.shape["tensor"]),
+        mesh=mesh,
+        in_specs=in_specs,
+        out_specs=out_specs,
+        check_vma=False,
     )

time: 174 us -> 86.1 us (0.49)
  blocking collectives: 66.5 us -> 0 us
  waiting for transfers between devices: 63.8 us -> 31.4 us
  Pallas kernels: 0 us -> 25.5 us
  matrix products: 28.6 us -> 7.86 us
  starting transfers between devices: 0.01 us -> 16.9 us
  between operations: 13.4 us -> 0.18 us
  other arithmetic: 0.48 us -> 2.41 us
    psum x1 -> x0, blocking collectives: 66.5 us -> none  [on_device(): shrunk_rows = lax.psum(shrink_portion, 'tensor').astype(jnp.bfloat16)]
    reduce_scatter x1 -> x0, waiting for transfers between devices: 63.8 us -> none  [on_device(): lax.psum_scatter(partial_value, 'tensor', scatter_dimension=1, tiled=True)]
    ppermute x0 -> x15, waiting for transfers between devices: none -> 31.4 us  [swap(): lax.ppermute(value, 'tensor', [(place, place ^ bit) for place in range(to...]
    pallas_call x0 -> x4, Pallas kernels: none -> 25.5 us  [product(): pl.pallas_call(product_body, grid_spec=pltpu.PrefetchScalarGridSpec(num_s...]
    dot_general x1 -> x0, matrix products: 19.7 us -> none  [on_device(): jnp.dot(hidden, down_matrix, preferred_element_type=jnp.float32)]
    ppermute x0 -> x15, starting transfers between devices: none -> 16.9 us  [swap(): lax.ppermute(value, 'tensor', [(place, place ^ bit) for place in range(to...]
  transfers between devices with their start and end apart: 1 -> 15, of which waited for: 1 -> 5; matrix products, arithmetic and copies ran while one was open for 4% -> 9% of each run, Pallas kernels for 0% -> 22%
where the time goes in v2:
time: 86.1 us; the launch traced here: 85.8 us
  waiting for transfers between devices  31.4 us (36%)
  Pallas kernels  25.5 us (30%)
  starting transfers between devices  16.9 us (20%)
  matrix products  7.86 us (9%)
  other arithmetic  2.41 us (3%)
  local copies, waits for them, and re-layouts  1.51 us (2%)
    ppermute x15, waiting for transfers between devices, swap(): lax.ppermute(value, 'tensor', [(place, place ^ bit) for place in range(to...  31.4 us
    pallas_call x4, Pallas kernels, product(): pl.pallas_call(product_body, grid_spec=pltpu.PrefetchScalarGridSpec(num_s...  25.5 us
    ppermute x15, starting transfers between devices, swap(): lax.ppermute(value, 'tensor', [(place, place ^ bit) for place in range(to...  16.9 us
    unnamed x1, matrix products  6 us
    dot_general x1, matrix products, expand_partial(): return jnp.dot(spread, adapter_table, preferred_element_type=jnp.float32)  1.86 us
  transfers between devices with their start and end apart: 15, of which 5 were waited for; matrix products, arithmetic and copies ran while one was open for 9% of the time, Pallas kernels for 22%

profile of v2, /device:TPU:0, one launch (start us, length us, event | category | flops | bytes accessed | tf_op | source)
XLA Modules:
  0.0 85.8 jit_solution(7211652069962736230)
XLA Ops:
  0.0 0.8 broadcast_xor_fusion
  0.8 1.3 %copy-done.1 = bf16[384,1664]{1,0:T(8,128)(2,1)S(1)} copy-done((bf16[384,1664]{1,0:T(8,128)(2,1)S(1)}, bf16[384,1664]{1,0:T(8,128)(2,1)}, u32[]{:S(2)}) %copy-start.1) | copy-done | bytes 1277976
  2.1 6.4 %shard_map.111 = (f32[2,384,512]{2,1,0:T(8,128)S(1)}, bf16[2,384,512]{2,1,0:T(8,128)(2,1)S(1)}) custom-call(s32[4]{0:T(128)S(1)} %get-tuple-element.27.order_ref, bf16[384,1664]{1,0:T(8,128)(2,1)S(1)} %copy-done.1, bf16[1664,8192]{1,0:T(8,128)(2,1)} %sent_weights.7, bf16[1664,8192]{1,0:T(8,128)(2,1)} %sent_weights.7), custom_call_target="tpu_custom_call" | custom-call | tf_op jit(solution)/shard_map/pallas_call | solution.py:32
  8.5 0.5 collective-permute-start.3
  9.0 6.4 %shard_map.109 = (f32[2,384,512]{2,1,0:T(8,128)S(1)}, bf16[2,384,512]{2,1,0:T(8,128)(2,1)S(1)}) custom-call(s32[4]{0:T(128)S(1)} %get-tuple-element.28.order_ref, bf16[384,1664]{1,0:T(8,128)(2,1)S(1)} %copy-done.2, bf16[1664,8192]{1,0:T(8,128)(2,1)} %sent_weights.7, bf16[1664,8192]{1,0:T(8,128)(2,1)} %sent_weights.7), custom_call_target="tpu_custom_call" | custom-call | tf_op jit(solution)/shard_map/pallas_call | solution.py:32
  15.7 6.4 %shard_map.112 = (f32[2,384,512]{2,1,0:T(8,128)S(1)}, bf16[2,384,512]{2,1,0:T(8,128)(2,1)S(1)}) custom-call(s32[4]{0:T(128)S(1)} %broadcast_xor_fusion.1.order_ref, bf16[384,1664]{1,0:T(8,128)(2,1)S(1)} %copy-done.2, bf16[1664,8192]{1,0:T(8,128)(2,1)} %sent_weights.7, bf16[1664,8192]{1,0:T(8,128)(2,1)} %sent_weights.7), custom_call_target="tpu_custom_call" | custom-call | tf_op jit(solution)/shard_map/pallas_call | solution.py:32
  22.1 0.5 collective-permute-start.4
  22.7 2.6 %collective-permute-start.8 = (bf16[384,512]{1,0:T(8,128)(2,1)S(1)}, bf16[384,512]{1,0:T(8,128)(2,1)S(1)}, u32[]{:S(2)}, u32[]{:S(2)}) collective-permute-start(bf16[384,512]{1,0:T(8,128)(2,1)S(1)} %fusion.20), channel_id=1, source_target_pairs={{0,2},{1,3},{2,0},{3,1},{4,6},{5,7},{6,4},{7,5},{8,10},{9,11},{10,... | collective-permute-start | bytes 1179656 | tf_op jit(solution)/shard_map/ppermute | solution.py:53
  25.5 6.4 %shard_map.110 = (f32[2,384,512]{2,1,0:T(8,128)S(1)}, bf16[2,384,512]{2,1,0:T(8,128)(2,1)S(1)}) custom-call(s32[4]{0:T(128)S(1)} %broadcast_xor_fusion.3.order_ref, bf16[384,1664]{1,0:T(8,128)(2,1)S(1)} %copy-done.2, bf16[1664,8192]{1,0:T(8,128)(2,1)} %sent_weights.7, bf16[1664,8192]{1,0:T(8,128)(2,1)} %sent_weights.7), custom_call_target="tpu_custom_call" | custom-call | tf_op jit(solution)/shard_map/pallas_call | solution.py:32
  32.2 3.1 %collective-permute-done.8 = bf16[384,512]{1,0:T(8,128)(2,1)S(1)} collective-permute-done((bf16[384,512]{1,0:T(8,128)(2,1)S(1)}, bf16[384,512]{1,0:T(8,128)(2,1)S(1)}, u32[]{:S(2)}, u32[]{:S(2)}) %collective-permute-start.8) | collective-permute-done | bytes 393248 | tf_op jit(solution)/shard_map/ppermute | solution.py:53
  35.4 2.1 %collective-permute-start.9 = (bf16[384,512]{1,0:T(8,128)(2,1)S(1)}, bf16[384,512]{1,0:T(8,128)(2,1)S(1)}, u32[]{:S(2)}, u32[]{:S(2)}) collective-permute-start(bf16[384,512]{1,0:T(8,128)(2,1)S(1)} %fusion.6), channel_id=1, source_target_pairs={{0,4},{1,5},{2,6},{3,7},{4,0},{5,1},{6,2},{7,3},{8,12},{9,13},{10,... | collective-permute-start | bytes 1179656 | tf_op jit(solution)/shard_map/ppermute | solution.py:53
  37.6 6.0 %fusion.25 = f32[384,2048]{0,1:S(1)} fusion(bf16[384,1664]{1,0:T(8,128)(2,1)S(1)} %copy-done.2, bf16[1664,2048]{0,1:T(8,128)(2,1)} %bitcast.49), kind=kOutput, calls=%fused_computation.39 | convolution fusion | flops 2617245696 | bytes 11239424
  43.7 0.4 select_reduce_fusion
  44.3 1.5 %collective-permute-start.5 = (bf16[384,512]{1,0:T(8,128)(2,1)S(1)}, bf16[384,512]{1,0:T(8,128)(2,1)S(1)}, u32[]{:S(2)}, u32[]{:S(2)}) collective-permute-start(bf16[384,512]{1,0:T(8,128)(2,1)S(1)} %fusion.21), channel_id=1, source_target_pairs={{0,2},{1,3},{2,0},{3,1},{4,6},{5,7},{6,4},{7,5},{8,10},{9,11},{10,... | collective-permute-start | bytes 1179656 | tf_op jit(solution)/shard_map/ppermute | solution.py:53
  45.8 1.2 %collective-permute-start.12 = (f32[64,384]{1,0:T(8,128)S(1)}, f32[64,384]{1,0:T(8,128)S(1)}, u32[]{:S(2)}, u32[]{:S(2)}) collective-permute-start(f32[64,384]{1,0:T(8,128)S(1)} %bitcast_add_fusion.4), channel_id=1, source_target_pairs={{0,2},{1,3},{2,0},{3,1},{4,6},{5,7},{6,4},{7,5},{8,10},{9,11},{10,... | collective-permute-start | bytes 294920 | tf_op jit(solution)/shard_map/ppermute | solution.py:53
  47.2 2.7 %collective-permute-start.10 = (bf16[384,512]{1,0:T(8,128)(2,1)S(1)}, bf16[384,512]{1,0:T(8,128)(2,1)S(1)}, u32[]{:S(2)}, u32[]{:S(2)}) collective-permute-start(bf16[384,512]{1,0:T(8,128)(2,1)S(1)} %fusion.8), channel_id=1, source_target_pairs={{0,8},{1,9},{2,10},{3,11},{4,12},{5,13},{6,14},{7,15},{8,0},{9,1},... | collective-permute-start | bytes 1179656 | tf_op jit(solution)/shard_map/ppermute | solution.py:53
  49.9 8.0 %collective-permute-done.12 = f32[64,384]{1,0:T(8,128)S(1)} collective-permute-done((f32[64,384]{1,0:T(8,128)S(1)}, f32[64,384]{1,0:T(8,128)S(1)}, u32[]{:S(2)}, u32[]{:S(2)}) %collective-permute-start.12) | collective-permute-done | bytes 98336 | tf_op jit(solution)/shard_map/ppermute | solution.py:53
  58.3 1.8 %collective-permute-start.2 = (bf16[384,512]{1,0:T(8,128)(2,1)S(1)}, bf16[384,512]{1,0:T(8,128)(2,1)S(1)}, u32[]{:S(2)}, u32[]{:S(2)}) collective-permute-start(bf16[384,512]{1,0:T(8,128)(2,1)S(1)} %fusion.19), channel_id=1, source_target_pairs={{0,2},{1,3},{2,0},{3,1},{4,6},{5,7},{6,4},{7,5},{8,10},{9,11},{10,... | collective-permute-start | bytes 1179656 | tf_op jit(solution)/shard_map/ppermute | solution.py:53
  60.1 9.4 %collective-permute-done.13 = f32[64,384]{1,0:T(8,128)S(1)} collective-permute-done((f32[64,384]{1,0:T(8,128)S(1)}, f32[64,384]{1,0:T(8,128)S(1)}, u32[]{:S(2)}, u32[]{:S(2)}) %collective-permute-start.13) | collective-permute-done | bytes 98336 | tf_op jit(solution)/shard_map/ppermute | solution.py:53
  69.5 0.7 collective-permute-start.14
  70.3 2.5 %collective-permute-start.6 = (bf16[384,512]{1,0:T(8,128)(2,1)S(1)}, bf16[384,512]{1,0:T(8,128)(2,1)S(1)}, u32[]{:S(2)}, u32[]{:S(2)}) collective-permute-start(bf16[384,512]{1,0:T(8,128)(2,1)S(1)} %fusion.9), channel_id=1, source_target_pairs={{0,4},{1,5},{2,6},{3,7},{4,0},{5,1},{6,2},{7,3},{8,12},{9,13},{10,... | collective-permute-start | bytes 1179656 | tf_op jit(solution)/shard_map/ppermute | solution.py:53
  73.0 4.2 %collective-permute-done.14 = f32[64,384]{1,0:T(8,128)S(1)} collective-permute-done((f32[64,384]{1,0:T(8,128)S(1)}, f32[64,384]{1,0:T(8,128)S(1)}, u32[]{:S(2)}, u32[]{:S(2)}) %collective-permute-start.14) | collective-permute-done | bytes 98336 | tf_op jit(solution)/shard_map/ppermute | solution.py:53
  77.2 6.7 %collective-permute-done.6 = bf16[384,512]{1,0:T(8,128)(2,1)S(1)} collective-permute-done((bf16[384,512]{1,0:T(8,128)(2,1)S(1)}, bf16[384,512]{1,0:T(8,128)(2,1)S(1)}, u32[]{:S(2)}, u32[]{:S(2)}) %collective-permute-start.6) | collective-permute-done | bytes 393248 | tf_op jit(solution)/shard_map/ppermute | solution.py:53
  83.9 1.9 %fusion.13 = bf16[384,512]{1,0:T(8,128)(2,1)} fusion(bf16[32,64,512]{2,1,0:T(8,128)(2,1)S(1)} %copy-done, pred[384,32]{0,1:T(8,128)(4,1)S(1)} %fusion.23, bf16[384,64]{0,1:T(8,128)(2,1)S(1)} %fusion.22, bf16[384,512]{1,0:T(8,128)(2,1)S(1)} %collective-permute-done.10, bf16[384,512]{1,0:T(8,128)(2,1)S(1)} %collective-permute-done.6, ...), kind=kOutput, calls=%fused_computation.16 | convolution fusion | flops 808058880 | bytes 4911104 | tf_op jit(solution)/shard_map/dot_general | solution.py:81
  (46 shorter events, 2.2 us)
Async XLA Ops:
  0.0 83.9 %copy-start = (bf16[32,64,512]{2,1,0:T(8,128)(2,1)S(1)}, bf16[32,64,512]{2,1,0:T(8,128)(2,1)}, u32[]{:S(2)}) copy-start(bf16[32,64,512]{2,1,0:T(8,128)(2,1)} %param.14) | copy-start | bytes 6291460
  0.8 1.3 %copy-start.1 = (bf16[384,1664]{1,0:T(8,128)(2,1)S(1)}, bf16[384,1664]{1,0:T(8,128)(2,1)}, u32[]{:S(2)}) copy-start(bf16[384,1664]{1,0:T(8,128)(2,1)} %hidden_ref.7) | copy-start | bytes 3833860
  2.1 6.9 %copy-start.2 = (bf16[384,1664]{1,0:T(8,128)(2,1)S(1)}, bf16[384,1664]{1,0:T(8,128)(2,1)}, u32[]{:S(2)}) copy-start(bf16[384,1664]{1,0:T(8,128)(2,1)} %hidden_ref.7) | copy-start | bytes 3833860
  8.5 7.0 %collective-permute-start.3 = (bf16[2,384,512]{2,1,0:T(8,128)(2,1)S(1)}, bf16[2,384,512]{2,1,0:T(8,128)(2,1)S(1)}, u32[]{:S(2)}, u32[]{:S(2)}) collective-permute-start(bf16[2,384,512]{2,1,0:T(8,128)(2,1)S(1)} %get-tuple-element.22), channel_id=1, source_target_pairs={{0,1},{1,0},{2,3},{3,2},{4,5},{5,4},{6,7},{7,6},{8,9},{9,8},{10,11... | collective-permute-start | bytes 2359304 | tf_op jit(solution)/shard_map/ppermute | solution.py:53
  9.0 6.5 %copy-start.7 = (s32[4]{0:T(128)S(1)}, s32[4]{0:T(128)}, u32[]{:S(2)}) copy-start(s32[4]{0:T(128)} %constant.18.clone) | copy-start | bytes 52
  15.4 9.9 %collective-permute-start = (bf16[2,384,512]{2,1,0:T(8,128)(2,1)S(1)}, bf16[2,384,512]{2,1,0:T(8,128)(2,1)S(1)}, u32[]{:S(2)}, u32[]{:S(2)}) collective-permute-start(bf16[2,384,512]{2,1,0:T(8,128)(2,1)S(1)} %get-tuple-element.17), channel_id=1, source_target_pairs={{0,1},{1,0},{2,3},{3,2},{4,5},{5,4},{6,7},{7,6},{8,9},{9,8},{10,11... | collective-permute-start | bytes 2359304 | tf_op jit(solution)/shard_map/ppermute | solution.py:53
  15.7 6.9 %copy-start.3 = (s32[384]{0:T(512)S(1)}, s32[384]{0:T(512)}, u32[]{:S(2)}) copy-start(s32[384]{0:T(512)} %param.15) | copy-start | bytes 4612
  15.7 9.6 %copy-start.6 = (s32[4]{0:T(128)S(1)}, s32[4]{0:T(128)}, u32[]{:S(2)}) copy-start(s32[4]{0:T(128)} %constant.19.clone) | copy-start | bytes 52
  22.1 15.4 %collective-permute-start.4 = (bf16[2,384,512]{2,1,0:T(8,128)(2,1)S(1)}, bf16[2,384,512]{2,1,0:T(8,128)(2,1)S(1)}, u32[]{:S(2)}, u32[]{:S(2)}) collective-permute-start(bf16[2,384,512]{2,1,0:T(8,128)(2,1)S(1)} %get-tuple-element.25), channel_id=1, source_target_pairs={{0,1},{1,0},{2,3},{3,2},{4,5},{5,4},{6,7},{7,6},{8,9},{9,8},{10,11... | collective-permute-start | bytes 2359304 | tf_op jit(solution)/shard_map/ppermute | solution.py:53
  22.7 12.6 %collective-permute-start.8 = (bf16[384,512]{1,0:T(8,128)(2,1)S(1)}, bf16[384,512]{1,0:T(8,128)(2,1)S(1)}, u32[]{:S(2)}, u32[]{:S(2)}) collective-permute-start(bf16[384,512]{1,0:T(8,128)(2,1)S(1)} %fusion.20), channel_id=1, source_target_pairs={{0,2},{1,3},{2,0},{3,1},{4,6},{5,7},{6,4},{7,5},{8,10},{9,11},{10,... | collective-permute-start | bytes 1179656 | tf_op jit(solution)/shard_map/ppermute | solution.py:53
  25.4 21.6 %collective-permute-start.7 = (bf16[384,512]{1,0:T(8,128)(2,1)S(1)}, bf16[384,512]{1,0:T(8,128)(2,1)S(1)}, u32[]{:S(2)}, u32[]{:S(2)}) collective-permute-start(bf16[384,512]{1,0:T(8,128)(2,1)S(1)} %fusion.18), channel_id=1, source_target_pairs={{0,2},{1,3},{2,0},{3,1},{4,6},{5,7},{6,4},{7,5},{8,10},{9,11},{10,... | collective-permute-start | bytes 1179656 | tf_op jit(solution)/shard_map/ppermute | solution.py:53
  31.9 26.2 %collective-permute-start.1 = (bf16[2,384,512]{2,1,0:T(8,128)(2,1)S(1)}, bf16[2,384,512]{2,1,0:T(8,128)(2,1)S(1)}, u32[]{:S(2)}, u32[]{:S(2)}) collective-permute-start(bf16[2,384,512]{2,1,0:T(8,128)(2,1)S(1)} %get-tuple-element.20), channel_id=1, source_target_pairs={{0,1},{1,0},{2,3},{3,2},{4,5},{5,4},{6,7},{7,6},{8,9},{9,8},{10,11... | collective-permute-start | bytes 2359304 | tf_op jit(solution)/shard_map/ppermute | solution.py:53
  35.4 11.6 %collective-permute-start.9 = (bf16[384,512]{1,0:T(8,128)(2,1)S(1)}, bf16[384,512]{1,0:T(8,128)(2,1)S(1)}, u32[]{:S(2)}, u32[]{:S(2)}) collective-permute-start(bf16[384,512]{1,0:T(8,128)(2,1)S(1)} %fusion.6), channel_id=1, source_target_pairs={{0,4},{1,5},{2,6},{3,7},{4,0},{5,1},{6,2},{7,3},{8,12},{9,13},{10,... | collective-permute-start | bytes 1179656 | tf_op jit(solution)/shard_map/ppermute | solution.py:53
  43.6 0.7 copy-start.4
  43.6 0.7 copy-start.5
  44.0 1.8 %collective-permute-start.11 = (f32[64,384]{1,0:T(8,128)S(1)}, f32[64,384]{1,0:T(8,128)S(1)}, u32[]{:S(2)}, u32[]{:S(2)}) collective-permute-start(f32[64,384]{1,0:T(8,128)S(1)} %bitcast.48), channel_id=1, source_target_pairs={{0,1},{1,0},{2,3},{3,2},{4,5},{5,4},{6,7},{7,6},{8,9},{9,8},{10,11... | collective-permute-start | bytes 294920 | tf_op jit(solution)/shard_map/ppermute | solution.py:53
  44.3 25.9 %collective-permute-start.5 = (bf16[384,512]{1,0:T(8,128)(2,1)S(1)}, bf16[384,512]{1,0:T(8,128)(2,1)S(1)}, u32[]{:S(2)}, u32[]{:S(2)}) collective-permute-start(bf16[384,512]{1,0:T(8,128)(2,1)S(1)} %fusion.21), channel_id=1, source_target_pairs={{0,2},{1,3},{2,0},{3,1},{4,6},{5,7},{6,4},{7,5},{8,10},{9,11},{10,... | collective-permute-start | bytes 1179656 | tf_op jit(solution)/shard_map/ppermute | solution.py:53
  45.8 12.0 %collective-permute-start.12 = (f32[64,384]{1,0:T(8,128)S(1)}, f32[64,384]{1,0:T(8,128)S(1)}, u32[]{:S(2)}, u32[]{:S(2)}) collective-permute-start(f32[64,384]{1,0:T(8,128)S(1)} %bitcast_add_fusion.4), channel_id=1, source_target_pairs={{0,2},{1,3},{2,0},{3,1},{4,6},{5,7},{6,4},{7,5},{8,10},{9,11},{10,... | collective-permute-start | bytes 294920 | tf_op jit(solution)/shard_map/ppermute | solution.py:53
  47.2 30.0 %collective-permute-start.10 = (bf16[384,512]{1,0:T(8,128)(2,1)S(1)}, bf16[384,512]{1,0:T(8,128)(2,1)S(1)}, u32[]{:S(2)}, u32[]{:S(2)}) collective-permute-start(bf16[384,512]{1,0:T(8,128)(2,1)S(1)} %fusion.8), channel_id=1, source_target_pairs={{0,8},{1,9},{2,10},{3,11},{4,12},{5,13},{6,14},{7,15},{8,0},{9,1},... | collective-permute-start | bytes 1179656 | tf_op jit(solution)/shard_map/ppermute | solution.py:53
  57.9 11.6 %collective-permute-start.13 = (f32[64,384]{1,0:T(8,128)S(1)}, f32[64,384]{1,0:T(8,128)S(1)}, u32[]{:S(2)}, u32[]{:S(2)}) collective-permute-start(f32[64,384]{1,0:T(8,128)S(1)} %add.100), channel_id=1, source_target_pairs={{0,4},{1,5},{2,6},{3,7},{4,0},{5,1},{6,2},{7,3},{8,12},{9,13},{10,... | collective-permute-start | bytes 294920 | tf_op jit(solution)/shard_map/ppermute | solution.py:53
  58.3 19.0 %collective-permute-start.2 = (bf16[384,512]{1,0:T(8,128)(2,1)S(1)}, bf16[384,512]{1,0:T(8,128)(2,1)S(1)}, u32[]{:S(2)}, u32[]{:S(2)}) collective-permute-start(bf16[384,512]{1,0:T(8,128)(2,1)S(1)} %fusion.19), channel_id=1, source_target_pairs={{0,2},{1,3},{2,0},{3,1},{4,6},{5,7},{6,4},{7,5},{8,10},{9,11},{10,... | collective-permute-start | bytes 1179656 | tf_op jit(solution)/shard_map/ppermute | solution.py:53
  69.5 7.7 %collective-permute-start.14 = (f32[64,384]{1,0:T(8,128)S(1)}, f32[64,384]{1,0:T(8,128)S(1)}, u32[]{:S(2)}, u32[]{:S(2)}) collective-permute-start(f32[64,384]{1,0:T(8,128)S(1)} %add.101), channel_id=1, source_target_pairs={{0,8},{1,9},{2,10},{3,11},{4,12},{5,13},{6,14},{7,15},{8,0},{9,1},... | collective-permute-start | bytes 294920 | tf_op jit(solution)/shard_map/ppermute | solution.py:53
  70.3 13.6 %collective-permute-start.6 = (bf16[384,512]{1,0:T(8,128)(2,1)S(1)}, bf16[384,512]{1,0:T(8,128)(2,1)S(1)}, u32[]{:S(2)}, u32[]{:S(2)}) collective-permute-start(bf16[384,512]{1,0:T(8,128)(2,1)S(1)} %fusion.9), channel_id=1, source_target_pairs={{0,4},{1,5},{2,6},{3,7},{4,0},{5,1},{6,2},{7,3},{8,12},{9,13},{10,... | collective-permute-start | bytes 1179656 | tf_op jit(solution)/shard_map/ppermute | solution.py:53

commit v3 on v2

v3 whole, which is shorter than its diff:
```python
import functools

import jax
import jax.numpy as jnp
from jax import lax
from jax.experimental import pallas as pl
from jax.experimental.pallas import tpu as pltpu
from jax.sharding import PartitionSpec as P

BLOCK = 256
DEEP = 256
WINDOW = 64
TOGETHER = 4
VMEM_LIMIT = 48 * 1024 * 1024


def deep_dot(left, right_ref, transposed=False):
    depth = left.shape[1]
    cut = depth // DEEP * DEEP
    total = None
    for first, last in ((0, cut), (cut, depth)):
        if first == last:
            continue
        right = right_ref[:, first:last] if transposed else right_ref[first:last, :]
        part = lax.dot_general(
            left[:, first:last],
            right,
            (((1,), (1 if transposed else 0,)), ((), ())),
            preferred_element_type=jnp.float32,
        )
        total = part if total is None else total + part
    return total


def product_body(order_ref, hidden_ref, weights_ref, result_ref):
    result_ref[0] = deep_dot(hidden_ref[...], weights_ref).astype(result_ref.dtype)


def product(hidden, down_matrix, order, width, dtype):
    rows, depth = hidden.shape
    targets = order.shape[0]
    block = min(BLOCK, width)
    blocks = width // block
    return pl.pallas_call(
        product_body,
        grid_spec=pltpu.PrefetchScalarGridSpec(
            num_scalar_prefetch=1,
            grid=(targets, blocks),
            in_specs=[
                pl.BlockSpec((rows, depth), lambda at, part, order: (0, 0)),
                pl.BlockSpec((depth, block), lambda at, part, order: (0, order[at] * blocks + part)),
            ],
            out_specs=pl.BlockSpec((1, rows, block), lambda at, part, order: (at, 0, part)),
        ),
        out_shape=jax.ShapeDtypeStruct((targets, rows, width), dtype),
        compiler_params=pltpu.CompilerParams(vmem_limit_bytes=VMEM_LIMIT),
        cost_estimate=pl.CostEstimate(flops=1, bytes_accessed=1, transcendentals=0),
    )(order, hidden, down_matrix)


def for_each_window(first_ref, length_ref, group, rows, body):
    window = min(WINDOW, rows)
    adapters = [group * TOGETHER + at for at in range(TOGETHER)]
    begins = [first_ref[adapter] for adapter in adapters]
    ends = [first_ref[adapter] + length_ref[adapter] for adapter in adapters]
    base = begins[0] // 16 * 16

    def step(at, carry):
        low = base + at * window
        start = pl.multiple_of(jnp.minimum(low, rows - window), 16)
        places = start + lax.broadcasted_iota(jnp.int32, (window, 1), 0)
        masks = [
            (places >= jnp.maximum(begin, low)) & (places < end) for begin, end in zip(begins, ends)
        ]
        body(pl.ds(start, window), masks)
        return carry

    lax.fori_loop(0, (ends[-1] - base + window - 1) // window, step, 0)


def shrink_body(first_ref, length_ref, hidden_ref, table_ref, packed_ref, total_ref):
    group = pl.program_id(0)
    rank = total_ref.shape[1]
    rows = total_ref.shape[0]

    @pl.when(group == 0)
    def _():
        total_ref[...] = jnp.zeros_like(total_ref)

    def body(window, masks):
        every = deep_dot(hidden_ref[window, :], table_ref, transposed=True)
        picked = total_ref[window, :]
        for at, mask in enumerate(masks):
            picked = picked + jnp.where(mask, every[:, at * rank:(at + 1) * rank], 0.0)
        total_ref[window, :] = picked

    for_each_window(first_ref, length_ref, group, rows, body)

    @pl.when(group == pl.num_programs(0) - 1)
    def _():
        packed_ref[:, :rank] = total_ref[:rows // 2, :]
        packed_ref[:, rank:] = total_ref[rows // 2:, :]


def shrink(hidden, shrink_matrices, segment_first_row, segment_length):
    rows, depth = hidden.shape
    adapters, _, rank = shrink_matrices.shape
    table = jnp.swapaxes(shrink_matrices, 1, 2).reshape(adapters * rank, depth)
    return pl.pallas_call(
        shrink_body,
        grid_spec=pltpu.PrefetchScalarGridSpec(
            num_scalar_prefetch=2,
            grid=(adapters // TOGETHER,),
            in_specs=[
                pl.BlockSpec((rows, depth), lambda group, *_: (0, 0)),
                pl.BlockSpec((TOGETHER * rank, depth), lambda group, *_: (group, 0)),
            ],
            out_specs=pl.BlockSpec((rows // 2, 2 * rank), lambda group, *_: (0, 0)),
            scratch_shapes=[pltpu.VMEM((rows, rank), jnp.float32)],
        ),
        out_shape=jax.ShapeDtypeStruct((rows // 2, 2 * rank), jnp.float32),
        compiler_params=pltpu.CompilerParams(vmem_limit_bytes=VMEM_LIMIT),
        cost_estimate=pl.CostEstimate(flops=1, bytes_accessed=1, transcendentals=0),
    )(segment_first_row, segment_length, hidden, table)


def expand_body(first_ref, length_ref, packed_ref, table_ref, result_ref, shrunk_ref):
    group = pl.program_id(0)
    rows, rank = shrunk_ref.shape

    @pl.when(group == 0)
    def _():
        shrunk_ref[:rows // 2, :] = packed_ref[:, :rank].astype(jnp.bfloat16)
        shrunk_ref[rows // 2:, :] = packed_ref[:, rank:].astype(jnp.bfloat16)
        result_ref[...] = jnp.zeros_like(result_ref)

    def body(window, masks):
        shrunk = shrunk_ref[window, :]
        spread = [jnp.where(mask, shrunk, jnp.zeros((), jnp.bfloat16)) for mask in masks]
        part = jnp.dot(
            jnp.concatenate(spread, axis=1), table_ref[...], preferred_element_type=jnp.float32
        )
        result_ref[window, :] = result_ref[window, :] + part

    for_each_window(first_ref, length_ref, group, rows, body)


def expand(packed, expand_matrices, segment_first_row, segment_length):
    rows = 2 * packed.shape[0]
    adapters, rank, width = expand_matrices.shape
    table = expand_matrices.reshape(adapters * rank, width)
    return pl.pallas_call(
        expand_body,
        grid_spec=pltpu.PrefetchScalarGridSpec(
            num_scalar_prefetch=2,
            grid=(adapters // TOGETHER,),
            in_specs=[
                pl.BlockSpec((rows // 2, 2 * rank), lambda group, *_: (0, 0)),
                pl.BlockSpec((TOGETHER * rank, width), lambda group, *_: (group, 0)),
            ],
            out_specs=pl.BlockSpec((rows, width), lambda group, *_: (0, 0)),
            scratch_shapes=[pltpu.VMEM((rows, rank), jnp.bfloat16)],
        ),
        out_shape=jax.ShapeDtypeStruct((rows, width), jnp.float32),
        compiler_params=pltpu.CompilerParams(vmem_limit_bytes=VMEM_LIMIT),
        cost_estimate=pl.CostEstimate(flops=1, bytes_accessed=1, transcendentals=0),
    )(segment_first_row, segment_length, packed, table)


def swap(value, bit, total):
    return lax.ppermute(value, "tensor", [(place, place ^ bit) for place in range(total)])


def after(value, earlier):
    return lax.optimization_barrier((value, earlier))[0]


def on_device(
    total,
    hidden,
    down_matrix,
    shrink_matrices,
    expand_matrices,
    row_adapter_index,
    segment_first_row,
    segment_length,
):
    me = lax.axis_index("tensor").astype(jnp.int32)
    width = down_matrix.shape[1] // total
    core, near = 1, 2
    units = total // 4

    kept, sent, packed, done = {}, {}, None, None
    for unit in reversed(range(units)):
        far = unit * 4
        away = jnp.array([far | core, far | near | core], dtype=jnp.int32) ^ me
        home = jnp.array([far, far | near], dtype=jnp.int32) ^ me
        if done is not None:
            away = after(away, done)
        second = product(hidden, down_matrix, away, width, jnp.bfloat16)
        first = product(hidden, down_matrix, after(home, second), width, jnp.float32)
        arrived = swap(second, core, total)
        kept[unit] = first[0] + arrived[0].astype(jnp.float32)
        sent[unit] = (first[1] + arrived[1].astype(jnp.float32)).astype(jnp.bfloat16)
        done = sent[unit]
        if packed is None:
            packed = shrink(
                hidden, shrink_matrices, after(segment_first_row, done), segment_length
            )
            done = packed

    levels = [1 << level for level in range(total.bit_length() - 1)]
    for bit in [core, *levels[2:], near]:
        packed = packed + swap(packed, bit, total)
    adapter_output = expand(packed, expand_matrices, segment_first_row, segment_length)

    for unit in reversed(range(units)):
        kept[unit] = kept[unit] + swap(sent[unit], near, total).astype(jnp.float32)
    bit = 1
    while bit < units:
        for unit in reversed(range(0, units, 2 * bit)):
            moved = swap(kept[unit | bit].astype(jnp.bfloat16), 4 * bit, total)
            kept[unit] = kept[unit] + moved.astype(jnp.float32)
        bit *= 2
    return (kept[0] + adapter_output).astype(jnp.bfloat16)


def solution(mesh):
    in_specs = (
        P("groups", "tensor"),
        P("tensor", None),
        P(None, "tensor", None),
        P(None, None, "tensor"),
        P("groups"),
        P("groups"),
        P("groups"),
    )
    out_specs = P("groups", "tensor")
    return jax.shard_map(
        functools.partial(on_device, mesh.shape["tensor"]),
        mesh=mesh,
        in_specs=in_specs,
        out_specs=out_specs,
        check_vma=False,
    )
```

time: 86.1 us -> 109 us (1.27)
  Pallas kernels: 25.5 us -> 47.3 us
  waiting for transfers between devices: 31.4 us -> 41 us
  matrix products: 7.86 us -> 0 us
  starting transfers between devices: 16.9 us -> 14.6 us
    pallas_call x0 -> x2, Pallas kernels: none -> 10.9 us  [the longest x1 8.14 us: shrink(): pl.pallas_call(shrink_body, grid_spec=pltpu.PrefetchScalarGridSpec(num_sc...]
    pallas_call x4 -> x8, Pallas kernels: 25.5 us -> 36.4 us  [product(): pl.pallas_call(product_body, grid_spec=pltpu.PrefetchScalarGridSpec(num_s...]
    ppermute x15, waiting for transfers between devices: 31.4 us -> 41 us  [swap(): lax.ppermute(value, 'tensor', [(place, place ^ bit) for place in range(to...]
    unnamed x1 -> x0, matrix products: 6 us -> none
    ppermute x15, starting transfers between devices: 16.9 us -> 14.6 us  [swap(): lax.ppermute(value, 'tensor', [(place, place ^ bit) for place in range(to...]
    dot_general x1 -> x0, matrix products: 1.86 us -> none  [expand_partial(): return jnp.dot(spread, adapter_table, preferred_element_type=jnp.float32)]
    convert_element_type x1, other arithmetic: 0.01 us -> 1.11 us  [on_device(): return (kept[0] + adapter_output).astype(jnp.bfloat16)]
    unnamed x16 -> x22, local copies, waits for them, and re-layouts: 1.51 us -> 2.48 us
  transfers between devices with their start and end apart: 15 -> 15, of which waited for: 5 -> 5; matrix products, arithmetic and copies ran while one was open for 9% -> 1% of each run, Pallas kernels for 22% -> 23%
where the time goes in v3:
time: 109 us
  Pallas kernels  47.3 us (43%)
  waiting for transfers between devices  41 us (38%)
  starting transfers between devices  14.6 us (13%)
  other arithmetic  2.97 us (3%)
  local copies, waits for them, and re-layouts  2.48 us (2%)
    ppermute x15, waiting for transfers between devices, swap(): lax.ppermute(value, 'tensor', [(place, place ^ bit) for place in range(to...  41 us
    pallas_call x8, Pallas kernels, product(): pl.pallas_call(product_body, grid_spec=pltpu.PrefetchScalarGridSpec(num_s...  36.4 us
    ppermute x15, starting transfers between devices, swap(): lax.ppermute(value, 'tensor', [(place, place ^ bit) for place in range(to...  14.6 us
    pallas_call x1, Pallas kernels, shrink(): pl.pallas_call(shrink_body, grid_spec=pltpu.PrefetchScalarGridSpec(num_sc...  8.14 us
    pallas_call x1, Pallas kernels, expand(): pl.pallas_call(expand_body, grid_spec=pltpu.PrefetchScalarGridSpec(num_sc...  2.75 us
    unnamed x22, local copies, waits for them, and re-layouts  2.48 us
  transfers between devices with their start and end apart: 15, of which 5 were waited for; matrix products, arithmetic and copies ran while one was open for 1% of the time, Pallas kernels for 23%

profile of v3, /device:TPU:0, one launch (start us, length us, event | category | flops | bytes accessed | tf_op | source)
XLA Modules:
  0.0 108.6 jit_solution(6107814898253561222)
XLA Ops:
  0.7 1.3 %copy-done = bf16[384,1664]{1,0:T(8,128)(2,1)S(1)} copy-done((bf16[384,1664]{1,0:T(8,128)(2,1)S(1)}, bf16[384,1664]{1,0:T(8,128)(2,1)}, u32[]{:S(2)}) %copy-start) | copy-done | bytes 1277976
  2.0 4.6 %shard_map.136 = bf16[2,384,512]{2,1,0:T(8,128)(2,1)S(1)} custom-call(s32[2]{0:T(128)S(1)} %broadcast_xor_fusion.order_ref, bf16[384,1664]{1,0:T(8,128)(2,1)S(1)} %copy-done, bf16[1664,8192]{1,0:T(8,128)(2,1)} %weights_ref.15), custom_call_target="tpu_custom_call" | custom-call | flops 1 | bytes 1 | tf_op jit(solution)/shard_map/pallas_call | solution.py:44
  7.1 4.6 %shard_map.137 = f32[2,384,512]{2,1,0:T(8,128)S(1)} custom-call(s32[2]{0:T(128)S(1)} %get-tuple-element.13.order_ref, bf16[384,1664]{1,0:T(8,128)(2,1)S(1)} %copy-done, bf16[1664,8192]{1,0:T(8,128)(2,1)} %weights_ref.15), custom_call_target="tpu_custom_call" | custom-call | flops 1 | bytes 1 | tf_op jit(solution)/shard_map/pallas_call | solution.py:44
  11.9 1.1 %copy-done.1 = bf16[384,1664]{1,0:T(8,128)(2,1)S(1)} copy-done((bf16[384,1664]{1,0:T(8,128)(2,1)S(1)}, bf16[384,1664]{1,0:T(8,128)(2,1)}, u32[]{:S(2)}) %copy-start.1) | copy-done | bytes 1277976
  13.0 8.1 %shard_map.138 = f32[192,128]{1,0:T(8,128)S(1)} custom-call(s32[32]{0:T(128)S(1)} %copy-done.3, s32[32]{0:T(128)S(1)} %copy-done.4, bf16[384,1664]{1,0:T(8,128)(2,1)S(1)} %copy-done.1, bf16[2048,1664]{1,0:T(8,128)(2,1)} %bitcast.45), custom_call_target="tpu_custom_call" | custom-call | flops 1 | bytes 1 | tf_op jit(solution)/shard_map/pallas_call | solution.py:109
  21.2 4.5 %shard_map.139 = bf16[2,384,512]{2,1,0:T(8,128)(2,1)S(1)} custom-call(s32[2]{0:T(128)S(1)} %get-tuple-element.15.order_ref, bf16[384,1664]{1,0:T(8,128)(2,1)S(1)} %copy-done.1, bf16[1664,8192]{1,0:T(8,128)(2,1)} %weights_ref.15), custom_call_target="tpu_custom_call" | custom-call | flops 1 | bytes 1 | tf_op jit(solution)/shard_map/pallas_call | solution.py:44
  25.8 4.5 %shard_map.140 = f32[2,384,512]{2,1,0:T(8,128)S(1)} custom-call(s32[2]{0:T(128)S(1)} %get-tuple-element.16.order_ref, bf16[384,1664]{1,0:T(8,128)(2,1)S(1)} %copy-done.1, bf16[1664,8192]{1,0:T(8,128)(2,1)} %weights_ref.15), custom_call_target="tpu_custom_call" | custom-call | flops 1 | bytes 1 | tf_op jit(solution)/shard_map/pallas_call | solution.py:44
  30.6 4.5 %shard_map.141 = bf16[2,384,512]{2,1,0:T(8,128)(2,1)S(1)} custom-call(s32[2]{0:T(128)S(1)} %broadcast_xor_fusion.4.order_ref, bf16[384,1664]{1,0:T(8,128)(2,1)S(1)} %copy-done.1, bf16[1664,8192]{1,0:T(8,128)(2,1)} %weights_ref.15), custom_call_target="tpu_custom_call" | custom-call | flops 1 | bytes 1 | tf_op jit(solution)/shard_map/pallas_call | solution.py:44
  35.6 2.6 %collective-permute-start.8 = (bf16[384,512]{1,0:T(8,128)(2,1)S(1)}, bf16[384,512]{1,0:T(8,128)(2,1)S(1)}, u32[]{:S(2)}, u32[]{:S(2)}) collective-permute-start(bf16[384,512]{1,0:T(8,128)(2,1)S(1)} %fusion.20), channel_id=1, source_target_pairs={{0,2},{1,3},{2,0},{3,1},{4,6},{5,7},{6,4},{7,5},{8,10},{9,11},{10,... | collective-permute-start | bytes 1179656 | tf_op jit(solution)/shard_map/ppermute | solution.py:171
  38.2 9.7 %collective-permute-done.8 = bf16[384,512]{1,0:T(8,128)(2,1)S(1)} collective-permute-done((bf16[384,512]{1,0:T(8,128)(2,1)S(1)}, bf16[384,512]{1,0:T(8,128)(2,1)S(1)}, u32[]{:S(2)}, u32[]{:S(2)}) %collective-permute-start.8) | collective-permute-done | bytes 393248 | tf_op jit(solution)/shard_map/ppermute | solution.py:171
  48.1 1.9 %collective-permute-start.9 = (bf16[384,512]{1,0:T(8,128)(2,1)S(1)}, bf16[384,512]{1,0:T(8,128)(2,1)S(1)}, u32[]{:S(2)}, u32[]{:S(2)}) collective-permute-start(bf16[384,512]{1,0:T(8,128)(2,1)S(1)} %fusion.2), channel_id=1, source_target_pairs={{0,4},{1,5},{2,6},{3,7},{4,0},{5,1},{6,2},{7,3},{8,12},{9,13},{10,... | collective-permute-start | bytes 1179656 | tf_op jit(solution)/shard_map/ppermute | solution.py:171
  50.0 1.5 %collective-permute-start.7 = (bf16[384,512]{1,0:T(8,128)(2,1)S(1)}, bf16[384,512]{1,0:T(8,128)(2,1)S(1)}, u32[]{:S(2)}, u32[]{:S(2)}) collective-permute-start(bf16[384,512]{1,0:T(8,128)(2,1)S(1)} %fusion.21), channel_id=1, source_target_pairs={{0,2},{1,3},{2,0},{3,1},{4,6},{5,7},{6,4},{7,5},{8,10},{9,11},{10,... | collective-permute-start | bytes 1179656 | tf_op jit(solution)/shard_map/ppermute | solution.py:171
  51.5 4.5 %shard_map.142 = f32[2,384,512]{2,1,0:T(8,128)S(1)} custom-call(s32[2]{0:T(128)S(1)} %broadcast_xor_fusion.5.order_ref, bf16[384,1664]{1,0:T(8,128)(2,1)S(1)} %copy-done.1, bf16[1664,8192]{1,0:T(8,128)(2,1)} %weights_ref.15), custom_call_target="tpu_custom_call" | custom-call | flops 1 | bytes 1 | tf_op jit(solution)/shard_map/pallas_call | solution.py:44
  56.2 4.5 %shard_map.143 = bf16[2,384,512]{2,1,0:T(8,128)(2,1)S(1)} custom-call(s32[2]{0:T(128)S(1)} %broadcast_xor_fusion.6.order_ref, bf16[384,1664]{1,0:T(8,128)(2,1)S(1)} %copy-done.1, bf16[1664,8192]{1,0:T(8,128)(2,1)} %weights_ref.15), custom_call_target="tpu_custom_call" | custom-call | flops 1 | bytes 1 | tf_op jit(solution)/shard_map/pallas_call | solution.py:44
  61.8 2.6 %collective-permute-start.10 = (bf16[384,512]{1,0:T(8,128)(2,1)S(1)}, bf16[384,512]{1,0:T(8,128)(2,1)S(1)}, u32[]{:S(2)}, u32[]{:S(2)}) collective-permute-start(bf16[384,512]{1,0:T(8,128)(2,1)S(1)} %fusion.6), channel_id=1, source_target_pairs={{0,8},{1,9},{2,10},{3,11},{4,12},{5,13},{6,14},{7,15},{8,0},{9,1},... | collective-permute-start | bytes 1179656 | tf_op jit(solution)/shard_map/ppermute | solution.py:171
  64.5 4.5 %shard_map.144 = f32[2,384,512]{2,1,0:T(8,128)S(1)} custom-call(s32[2]{0:T(128)S(1)} %get-tuple-element.20.order_ref, bf16[384,1664]{1,0:T(8,128)(2,1)S(1)} %copy-done.1, bf16[1664,8192]{1,0:T(8,128)(2,1)} %weights_ref.15), custom_call_target="tpu_custom_call" | custom-call | flops 1 | bytes 1 | tf_op jit(solution)/shard_map/pallas_call | solution.py:44
  69.0 3.3 %collective-permute-done.5 = bf16[384,512]{1,0:T(8,128)(2,1)S(1)} collective-permute-done((bf16[384,512]{1,0:T(8,128)(2,1)S(1)}, bf16[384,512]{1,0:T(8,128)(2,1)S(1)}, u32[]{:S(2)}, u32[]{:S(2)}) %collective-permute-start.5) | collective-permute-done | bytes 393248 | tf_op jit(solution)/shard_map/ppermute | solution.py:171
  73.6 1.9 %collective-permute-start.12 = (f32[192,128]{1,0:T(8,128)S(1)}, f32[192,128]{1,0:T(8,128)S(1)}, u32[]{:S(2)}, u32[]{:S(2)}) collective-permute-start(f32[192,128]{1,0:T(8,128)S(1)} %add.95), channel_id=1, source_target_pairs={{0,4},{1,5},{2,6},{3,7},{4,0},{5,1},{6,2},{7,3},{8,12},{9,13},{10,... | collective-permute-start | bytes 294920 | tf_op jit(solution)/shard_map/ppermute | solution.py:171
  75.5 17.5 %collective-permute-done.12 = f32[192,128]{1,0:T(8,128)S(1)} collective-permute-done((f32[192,128]{1,0:T(8,128)S(1)}, f32[192,128]{1,0:T(8,128)S(1)}, u32[]{:S(2)}, u32[]{:S(2)}) %collective-permute-start.12) | collective-permute-done | bytes 98336 | tf_op jit(solution)/shard_map/ppermute | solution.py:171
  93.3 6.6 %collective-permute-done.13 = f32[192,128]{1,0:T(8,128)S(1)} collective-permute-done((f32[192,128]{1,0:T(8,128)S(1)}, f32[192,128]{1,0:T(8,128)S(1)}, u32[]{:S(2)}, u32[]{:S(2)}) %collective-permute-start.13) | collective-permute-done | bytes 98336 | tf_op jit(solution)/shard_map/ppermute | solution.py:171
  99.9 0.9 collective-permute-start.14
  100.8 3.9 %collective-permute-done.14 = f32[192,128]{1,0:T(8,128)S(1)} collective-permute-done((f32[192,128]{1,0:T(8,128)S(1)}, f32[192,128]{1,0:T(8,128)S(1)}, u32[]{:S(2)}, u32[]{:S(2)}) %collective-permute-start.14) | collective-permute-done | bytes 98336 | tf_op jit(solution)/shard_map/ppermute | solution.py:171
  104.7 2.7 %shard_map.145 = f32[384,512]{1,0:T(8,128)S(1)} custom-call(s32[32]{0:T(128)S(1)} %copy-done.3, s32[32]{0:T(128)S(1)} %copy-done.4, f32[192,128]{1,0:T(8,128)S(1)} %add.98.packed_ref, bf16[2048,512]{1,0:T(8,128)(2,1)S(1)} %bitcast.44), custom_call_target="tpu_custom_call" | custom-call | flops 1 | bytes 1 | tf_op jit(solution)/shard_map/pallas_call | solution.py:152
  107.5 1.1 %fusion.16 = bf16[384,512]{1,0:T(8,128)(2,1)} fusion(f32[384,512]{1,0:T(8,128)S(1)} %shard_map.145, f32[2,384,512]{2,1,0:T(8,128)S(1)} %shard_map.144, bf16[384,512]{1,0:T(8,128)(2,1)S(1)} %collective-permute-done.10, bf16[384,512]{1,0:T(8,128)(2,1)S(1)} %collective-permute-done.6, bf16[384,512]{1,0:T(8,128)(2,1)S(1)} %collective-permute-done.4, ...), kind=kLoop, calls=%fused_computation.21 | loop fusion | flops 1966080 | bytes 3538944 | tf_op jit(solution)/shard_map/convert_element_type | solution.py:225
  (56 shorter events, 5.2 us)
Async XLA Ops:
  0.7 1.3 %copy-start = (bf16[384,1664]{1,0:T(8,128)(2,1)S(1)}, bf16[384,1664]{1,0:T(8,128)(2,1)}, u32[]{:S(2)}) copy-start(bf16[384,1664]{1,0:T(8,128)(2,1)} %hidden_ref.17) | copy-start | bytes 3833860
  2.0 5.1 %copy-start.7 = (s32[2]{0:T(128)S(1)}, s32[2]{0:T(128)}, u32[]{:S(2)}) copy-start(s32[2]{0:T(128)} %constant.22.clone) | copy-start | bytes 28
  6.5 5.2 %collective-permute-start = (bf16[2,384,512]{2,1,0:T(8,128)(2,1)S(1)}, bf16[2,384,512]{2,1,0:T(8,128)(2,1)S(1)}, u32[]{:S(2)}, u32[]{:S(2)}) collective-permute-start(bf16[2,384,512]{2,1,0:T(8,128)(2,1)S(1)} %shard_map.136), channel_id=1, source_target_pairs={{0,1},{1,0},{2,3},{3,2},{4,5},{5,4},{6,7},{7,6},{8,9},{9,8},{10,11... | collective-permute-start | bytes 2359304 | tf_op jit(solution)/shard_map/ppermute | solution.py:171
  7.1 4.6 %copy-start.5 = (s32[2]{0:T(128)S(1)}, s32[2]{0:T(128)}, u32[]{:S(2)}) copy-start(s32[2]{0:T(128)} %constant.24.clone) | copy-start | bytes 28
  7.1 4.6 %copy-start.6 = (s32[2]{0:T(128)S(1)}, s32[2]{0:T(128)}, u32[]{:S(2)}) copy-start(s32[2]{0:T(128)} %constant.23.clone) | copy-start | bytes 28
  11.7 1.3 %copy-start.1 = (bf16[384,1664]{1,0:T(8,128)(2,1)S(1)}, bf16[384,1664]{1,0:T(8,128)(2,1)}, u32[]{:S(2)}) copy-start(bf16[384,1664]{1,0:T(8,128)(2,1)} %hidden_ref.17) | copy-start | bytes 3833860
  21.2 4.7 %copy-start.10 = (s32[2]{0:T(128)S(1)}, s32[2]{0:T(128)}, u32[]{:S(2)}) copy-start(s32[2]{0:T(128)} %constant.25.clone) | copy-start | bytes 28
  25.7 4.7 %collective-permute-start.1 = (bf16[2,384,512]{2,1,0:T(8,128)(2,1)S(1)}, bf16[2,384,512]{2,1,0:T(8,128)(2,1)S(1)}, u32[]{:S(2)}, u32[]{:S(2)}) collective-permute-start(bf16[2,384,512]{2,1,0:T(8,128)(2,1)S(1)} %shard_map.139), channel_id=1, source_target_pairs={{0,1},{1,0},{2,3},{3,2},{4,5},{5,4},{6,7},{7,6},{8,9},{9,8},{10,11... | collective-permute-start | bytes 2359304 | tf_op jit(solution)/shard_map/ppermute | solution.py:171
  30.5 7.7 %copy-start.9 = (s32[2]{0:T(128)S(1)}, s32[2]{0:T(128)}, u32[]{:S(2)}) copy-start(s32[2]{0:T(128)} %constant.26.clone) | copy-start | bytes 28
  30.6 7.7 %copy-start.8 = (s32[2]{0:T(128)S(1)}, s32[2]{0:T(128)}, u32[]{:S(2)}) copy-start(s32[2]{0:T(128)} %constant.27.clone) | copy-start | bytes 28
  35.1 20.9 %collective-permute-start.2 = (bf16[2,384,512]{2,1,0:T(8,128)(2,1)S(1)}, bf16[2,384,512]{2,1,0:T(8,128)(2,1)S(1)}, u32[]{:S(2)}, u32[]{:S(2)}) collective-permute-start(bf16[2,384,512]{2,1,0:T(8,128)(2,1)S(1)} %shard_map.141), channel_id=1, source_target_pairs={{0,1},{1,0},{2,3},{3,2},{4,5},{5,4},{6,7},{7,6},{8,9},{9,8},{10,11... | collective-permute-start | bytes 2359304 | tf_op jit(solution)/shard_map/ppermute | solution.py:171
  35.6 12.3 %collective-permute-start.8 = (bf16[384,512]{1,0:T(8,128)(2,1)S(1)}, bf16[384,512]{1,0:T(8,128)(2,1)S(1)}, u32[]{:S(2)}, u32[]{:S(2)}) collective-permute-start(bf16[384,512]{1,0:T(8,128)(2,1)S(1)} %fusion.20), channel_id=1, source_target_pairs={{0,2},{1,3},{2,0},{3,1},{4,6},{5,7},{6,4},{7,5},{8,10},{9,11},{10,... | collective-permute-start | bytes 1179656 | tf_op jit(solution)/shard_map/ppermute | solution.py:171
  48.1 13.5 %collective-permute-start.9 = (bf16[384,512]{1,0:T(8,128)(2,1)S(1)}, bf16[384,512]{1,0:T(8,128)(2,1)S(1)}, u32[]{:S(2)}, u32[]{:S(2)}) collective-permute-start(bf16[384,512]{1,0:T(8,128)(2,1)S(1)} %fusion.2), channel_id=1, source_target_pairs={{0,4},{1,5},{2,6},{3,7},{4,0},{5,1},{6,2},{7,3},{8,12},{9,13},{10,... | collective-permute-start | bytes 1179656 | tf_op jit(solution)/shard_map/ppermute | solution.py:171
  50.0 11.6 %collective-permute-start.7 = (bf16[384,512]{1,0:T(8,128)(2,1)S(1)}, bf16[384,512]{1,0:T(8,128)(2,1)S(1)}, u32[]{:S(2)}, u32[]{:S(2)}) collective-permute-start(bf16[384,512]{1,0:T(8,128)(2,1)S(1)} %fusion.21), channel_id=1, source_target_pairs={{0,2},{1,3},{2,0},{3,1},{4,6},{5,7},{6,4},{7,5},{8,10},{9,11},{10,... | collective-permute-start | bytes 1179656 | tf_op jit(solution)/shard_map/ppermute | solution.py:171
  60.7 12.3 %collective-permute-start.3 = (bf16[2,384,512]{2,1,0:T(8,128)(2,1)S(1)}, bf16[2,384,512]{2,1,0:T(8,128)(2,1)S(1)}, u32[]{:S(2)}, u32[]{:S(2)}) collective-permute-start(bf16[2,384,512]{2,1,0:T(8,128)(2,1)S(1)} %shard_map.143), channel_id=1, source_target_pairs={{0,1},{1,0},{2,3},{3,2},{4,5},{5,4},{6,7},{7,6},{8,9},{9,8},{10,11... | collective-permute-start | bytes 2359304 | tf_op jit(solution)/shard_map/ppermute | solution.py:171
  60.8 11.5 %collective-permute-start.5 = (bf16[384,512]{1,0:T(8,128)(2,1)S(1)}, bf16[384,512]{1,0:T(8,128)(2,1)S(1)}, u32[]{:S(2)}, u32[]{:S(2)}) collective-permute-start(bf16[384,512]{1,0:T(8,128)(2,1)S(1)} %fusion.22), channel_id=1, source_target_pairs={{0,2},{1,3},{2,0},{3,1},{4,6},{5,7},{6,4},{7,5},{8,10},{9,11},{10,... | collective-permute-start | bytes 1179656 | tf_op jit(solution)/shard_map/ppermute | solution.py:171
  61.4 12.2 %collective-permute-start.11 = (f32[192,128]{1,0:T(8,128)S(1)}, f32[192,128]{1,0:T(8,128)S(1)}, u32[]{:S(2)}, u32[]{:S(2)}) collective-permute-start(f32[192,128]{1,0:T(8,128)S(1)} %shard_map.138), channel_id=1, source_target_pairs={{0,1},{1,0},{2,3},{3,2},{4,5},{5,4},{6,7},{7,6},{8,9},{9,8},{10,11... | collective-permute-start | bytes 294920 | tf_op jit(solution)/shard_map/ppermute | solution.py:171
  61.8 45.7 %collective-permute-start.10 = (bf16[384,512]{1,0:T(8,128)(2,1)S(1)}, bf16[384,512]{1,0:T(8,128)(2,1)S(1)}, u32[]{:S(2)}, u32[]{:S(2)}) collective-permute-start(bf16[384,512]{1,0:T(8,128)(2,1)S(1)} %fusion.6), channel_id=1, source_target_pairs={{0,8},{1,9},{2,10},{3,11},{4,12},{5,13},{6,14},{7,15},{8,0},{9,1},... | collective-permute-start | bytes 1179656 | tf_op jit(solution)/shard_map/ppermute | solution.py:171
  72.5 32.2 %copy-start.2 = (bf16[32,64,512]{2,1,0:T(8,128)(2,1)S(1)}, bf16[32,64,512]{2,1,0:T(8,128)(2,1)}, u32[]{:S(2)}) copy-start(bf16[32,64,512]{2,1,0:T(8,128)(2,1)} %param.18) | copy-start | bytes 6291460
  72.5 34.9 %collective-permute-start.6 = (bf16[384,512]{1,0:T(8,128)(2,1)S(1)}, bf16[384,512]{1,0:T(8,128)(2,1)S(1)}, u32[]{:S(2)}, u32[]{:S(2)}) collective-permute-start(bf16[384,512]{1,0:T(8,128)(2,1)S(1)} %fusion.9), channel_id=1, source_target_pairs={{0,4},{1,5},{2,6},{3,7},{4,0},{5,1},{6,2},{7,3},{8,12},{9,13},{10,... | collective-permute-start | bytes 1179656 | tf_op jit(solution)/shard_map/ppermute | solution.py:171
  73.2 34.3 %collective-permute-start.4 = (bf16[384,512]{1,0:T(8,128)(2,1)S(1)}, bf16[384,512]{1,0:T(8,128)(2,1)S(1)}, u32[]{:S(2)}, u32[]{:S(2)}) collective-permute-start(bf16[384,512]{1,0:T(8,128)(2,1)S(1)} %fusion.23), channel_id=1, source_target_pairs={{0,2},{1,3},{2,0},{3,1},{4,6},{5,7},{6,4},{7,5},{8,10},{9,11},{10,... | collective-permute-start | bytes 1179656 | tf_op jit(solution)/shard_map/ppermute | solution.py:171
  73.6 19.4 %collective-permute-start.12 = (f32[192,128]{1,0:T(8,128)S(1)}, f32[192,128]{1,0:T(8,128)S(1)}, u32[]{:S(2)}, u32[]{:S(2)}) collective-permute-start(f32[192,128]{1,0:T(8,128)S(1)} %add.95), channel_id=1, source_target_pairs={{0,4},{1,5},{2,6},{3,7},{4,0},{5,1},{6,2},{7,3},{8,12},{9,13},{10,... | collective-permute-start | bytes 294920 | tf_op jit(solution)/shard_map/ppermute | solution.py:171
  93.0 6.9 %collective-permute-start.13 = (f32[192,128]{1,0:T(8,128)S(1)}, f32[192,128]{1,0:T(8,128)S(1)}, u32[]{:S(2)}, u32[]{:S(2)}) collective-permute-start(f32[192,128]{1,0:T(8,128)S(1)} %add.96), channel_id=1, source_target_pairs={{0,8},{1,9},{2,10},{3,11},{4,12},{5,13},{6,14},{7,15},{8,0},{9,1},... | collective-permute-start | bytes 294920 | tf_op jit(solution)/shard_map/ppermute | solution.py:171
  99.9 4.8 %collective-permute-start.14 = (f32[192,128]{1,0:T(8,128)S(1)}, f32[192,128]{1,0:T(8,128)S(1)}, u32[]{:S(2)}, u32[]{:S(2)}) collective-permute-start(f32[192,128]{1,0:T(8,128)S(1)} %add.97), channel_id=1, source_target_pairs={{0,2},{1,3},{2,0},{3,1},{4,6},{5,7},{6,4},{7,5},{8,10},{9,11},{10,... | collective-permute-start | bytes 294920 | tf_op jit(solution)/shard_map/ppermute | solution.py:171
  (2 other events, 2.6 us)

commit v4 on v3

v4 whole, which is shorter than its diff:
```python
import functools

import jax
import jax.numpy as jnp
from jax import lax
from jax.experimental import pallas as pl
from jax.experimental.pallas import tpu as pltpu
from jax.sharding import PartitionSpec as P

BLOCK = 256
VMEM_LIMIT = 48 * 1024 * 1024
WINDOW = 128
TOGETHER = 4
FLOPS = 1_000_000


def product_body(targets_ref, hidden_ref, down_ref, *refs, sent, earlier):
    *result_refs, buffer, arrived = refs[earlier:]
    width = result_refs[0].shape[-1]
    block = buffer.shape[2]
    blocks = width // block
    targets = buffer.shape[0] // blocks
    copies = []
    for at in range(targets):
        for part in range(blocks):
            slot = at * blocks + part
            column = pl.multiple_of(targets_ref[at] * width + part * block, block)
            copies.append(
                pltpu.make_async_copy(
                    down_ref.at[:, pl.ds(column, block)], buffer.at[slot], arrived.at[slot]
                )
            )
            copies[-1].start()
    for at in range(targets):
        for part in range(blocks):
            slot = at * blocks + part
            copies[slot].wait()
            total = jnp.dot(hidden_ref[...], buffer[slot], preferred_element_type=jnp.float32)
            columns = slice(part * block, (part + 1) * block)
            if at < sent:
                result_refs[0][at, :, columns] = total.astype(jnp.bfloat16)
            else:
                result_refs[(1 if sent else 0) + at - sent][:, columns] = total


def product(hidden, down_matrix, sent, kept, width, earlier):
    rows, depth = hidden.shape
    block = min(BLOCK, width)
    slots = (len(sent) + len(kept)) * (width // block)
    vmem = pl.BlockSpec(memory_space=pltpu.VMEM)
    out_shape = [jax.ShapeDtypeStruct((rows, width), jnp.float32)] * len(kept)
    if sent:
        out_shape = [jax.ShapeDtypeStruct((len(sent), rows, width), jnp.bfloat16)] + out_shape
    results = pl.pallas_call(
        functools.partial(product_body, sent=len(sent), earlier=len(earlier)),
        in_specs=[pl.BlockSpec(memory_space=pltpu.SMEM), vmem]
        + [pl.BlockSpec(memory_space=pl.ANY)] * (1 + len(earlier)),
        out_specs=[vmem] * len(out_shape),
        out_shape=out_shape,
        scratch_shapes=[
            pltpu.VMEM((slots, depth, block), jnp.bfloat16),
            pltpu.SemaphoreType.DMA((slots,)),
        ],
        compiler_params=pltpu.CompilerParams(vmem_limit_bytes=VMEM_LIMIT),
        cost_estimate=pl.CostEstimate(flops=FLOPS, bytes_accessed=1024, transcendentals=0),
    )(jnp.stack(sent + kept), hidden, down_matrix, *earlier)
    return (results[0], list(results[1:])) if sent else (None, list(results))


def swap(value, bit, total):
    return lax.ppermute(value, "tensor", [(place, place ^ bit) for place in range(total)])


def for_each_window(first_ref, length_ref, group, rows, body):
    window = min(WINDOW, rows)
    adapters = [group * TOGETHER + at for at in range(TOGETHER)]
    begins = [first_ref[adapter] for adapter in adapters]
    ends = [first_ref[adapter] + length_ref[adapter] for adapter in adapters]
    base = begins[0] // 16 * 16

    def step(at, carry):
        low = base + at * window
        start = pl.multiple_of(jnp.minimum(low, rows - window), 16)
        places = start + lax.broadcasted_iota(jnp.int32, (window, 1), 0)
        masks = [
            (places >= jnp.maximum(begin, low)) & (places < end) for begin, end in zip(begins, ends)
        ]
        body(pl.ds(start, window), masks)
        return carry

    lax.fori_loop(0, (ends[-1] - base + window - 1) // window, step, 0)


def shrink_body(first_ref, length_ref, hidden_ref, table_ref, earlier_ref, packed_ref, total_ref):
    group = pl.program_id(0)
    rank = total_ref.shape[1]
    rows = total_ref.shape[0]

    @pl.when(group == 0)
    def _():
        total_ref[...] = jnp.zeros_like(total_ref)

    def body(window, masks):
        every = lax.dot_general(
            hidden_ref[window, :],
            table_ref[...],
            (((1,), (1,)), ((), ())),
            preferred_element_type=jnp.float32,
        )
        picked = total_ref[window, :]
        for at, mask in enumerate(masks):
            picked = picked + jnp.where(mask, every[:, at * rank:(at + 1) * rank], 0.0)
        total_ref[window, :] = picked

    for_each_window(first_ref, length_ref, group, rows, body)

    @pl.when(group == pl.num_programs(0) - 1)
    def _():
        packed_ref[:, :rank] = total_ref[:rows // 2, :]
        packed_ref[:, rank:] = total_ref[rows // 2:, :]


def shrink(hidden, shrink_matrices, segment_first_row, segment_length, earlier):
    rows, depth = hidden.shape
    adapters, _, rank = shrink_matrices.shape
    table = jnp.swapaxes(shrink_matrices, 1, 2).reshape(adapters * rank, depth)
    return pl.pallas_call(
        shrink_body,
        grid_spec=pltpu.PrefetchScalarGridSpec(
            num_scalar_prefetch=2,
            grid=(adapters // TOGETHER,),
            in_specs=[
                pl.BlockSpec((rows, depth), lambda group, *_: (0, 0)),
                pl.BlockSpec((TOGETHER * rank, depth), lambda group, *_: (group, 0)),
                pl.BlockSpec(memory_space=pl.ANY),
            ],
            out_specs=pl.BlockSpec((rows // 2, 2 * rank), lambda group, *_: (0, 0)),
            scratch_shapes=[pltpu.VMEM((rows, rank), jnp.float32)],
        ),
        out_shape=jax.ShapeDtypeStruct((rows // 2, 2 * rank), jnp.float32),
        compiler_params=pltpu.CompilerParams(vmem_limit_bytes=VMEM_LIMIT),
        cost_estimate=pl.CostEstimate(flops=FLOPS, bytes_accessed=1, transcendentals=0),
    )(segment_first_row, segment_length, hidden, table, earlier)


def expand_body(first_ref, length_ref, packed_ref, table_ref, result_ref, shrunk_ref):
    group = pl.program_id(0)
    rows, rank = shrunk_ref.shape

    @pl.when(group == 0)
    def _():
        shrunk_ref[:rows // 2, :] = packed_ref[:, :rank].astype(jnp.bfloat16)
        shrunk_ref[rows // 2:, :] = packed_ref[:, rank:].astype(jnp.bfloat16)
        result_ref[...] = jnp.zeros_like(result_ref)

    def body(window, masks):
        shrunk = shrunk_ref[window, :]
        spread = [jnp.where(mask, shrunk, jnp.zeros((), jnp.bfloat16)) for mask in masks]
        part = jnp.dot(
            jnp.concatenate(spread, axis=1), table_ref[...], preferred_element_type=jnp.float32
        )
        result_ref[window, :] = result_ref[window, :] + part

    for_each_window(first_ref, length_ref, group, rows, body)


def expand(packed, expand_matrices, segment_first_row, segment_length):
    rows = 2 * packed.shape[0]
    adapters, rank, width = expand_matrices.shape
    table = expand_matrices.reshape(adapters * rank, width)
    return pl.pallas_call(
        expand_body,
        grid_spec=pltpu.PrefetchScalarGridSpec(
            num_scalar_prefetch=2,
            grid=(adapters // TOGETHER,),
            in_specs=[
                pl.BlockSpec((rows // 2, 2 * rank), lambda group, *_: (0, 0)),
                pl.BlockSpec((TOGETHER * rank, width), lambda group, *_: (group, 0)),
            ],
            out_specs=pl.BlockSpec((rows, width), lambda group, *_: (0, 0)),
            scratch_shapes=[pltpu.VMEM((rows, rank), jnp.bfloat16)],
        ),
        out_shape=jax.ShapeDtypeStruct((rows, width), jnp.float32),
        compiler_params=pltpu.CompilerParams(vmem_limit_bytes=VMEM_LIMIT),
        cost_estimate=pl.CostEstimate(flops=FLOPS, bytes_accessed=1, transcendentals=0),
    )(segment_first_row, segment_length, packed, table)


def on_device(
    total,
    hidden,
    down_matrix,
    shrink_matrices,
    expand_matrices,
    row_adapter_index,
    segment_first_row,
    segment_length,
):
    me = lax.axis_index("tensor").astype(jnp.int32)
    width = down_matrix.shape[1] // total
    core, near = 1, 2
    units = total // 4

    def out_of(unit):
        return me ^ (unit * 4 | near)

    def home_of(unit):
        return me ^ (unit * 4)

    kept_out, kept_home, crossed, incoming = {}, {}, {}, {}

    def settle(unit, arrived):
        value = kept_home[unit] + arrived.astype(jnp.float32) + crossed[unit].astype(jnp.float32)
        for moved in incoming.pop(unit, []):
            value = value + moved.astype(jnp.float32)
        if not unit:
            return value
        bit = unit & -unit
        moving = value.astype(jnp.bfloat16)
        incoming.setdefault(unit ^ bit, []).append(swap(moving, 4 * bit, total))
        return moving

    top = units - 1
    values, _ = product(hidden, down_matrix, [out_of(top) ^ core], [], width, [])
    packed, ready = None, [values]
    steps = [near, *(4 << at for at in range(top.bit_length())), core]
    for unit in reversed(range(units)):
        arrived = swap(values, core, total)
        sent, kept = [], [out_of(unit)]
        if unit:
            sent.append(out_of(unit - 1) ^ core)
        sent.append(home_of(unit) ^ core)
        if unit < top:
            kept.append(home_of(unit + 1))
        if not unit:
            kept.append(home_of(0))
        values, results = product(hidden, down_matrix, sent, kept, width, ready)
        kept_out[unit] = results[0]
        if unit < top:
            kept_home[unit + 1] = results[1]
        if not unit:
            kept_home[0] = results[-1]
        if packed is not None and steps:
            moved, kept_out[unit] = lax.optimization_barrier(
                (swap(packed, steps.pop(0), total), kept_out[unit])
            )
            packed = packed + moved
        leaving = (kept_out[unit] + arrived[0].astype(jnp.float32)).astype(jnp.bfloat16)
        ready = [leaving]
        if unit < top:
            ready.append(settle(unit + 1, arrived[1]))
        crossed[unit] = swap(leaving, near, total)
        if packed is None:
            packed = shrink(
                hidden, shrink_matrices, segment_first_row, segment_length, leaving
            )
        ready.append(packed)
    kept = [settle(0, swap(values, core, total)[0])]

    for bit in steps:
        packed = packed + swap(packed, bit, total)
    adapter_output = expand(packed, expand_matrices, segment_first_row, segment_length)
    return (kept[0] + adapter_output).astype(jnp.bfloat16)


def solution(mesh):
    in_specs = (
        P("groups", "tensor"),
        P("tensor", None),
        P(None, "tensor", None),
        P(None, None, "tensor"),
        P("groups"),
        P("groups"),
        P("groups"),
    )
    out_specs = P("groups", "tensor")
    return jax.shard_map(
        functools.partial(on_device, mesh.shape["tensor"]),
        mesh=mesh,
        in_specs=in_specs,
        out_specs=out_specs,
        check_vma=False,
    )
```

time: 109 us -> 85.7 us (0.79)
  waiting for transfers between devices: 41 us -> 15.7 us
  other arithmetic: 2.97 us -> 6.12 us
  local copies, waits for them, and re-layouts: 2.48 us -> 1.32 us
    ppermute x15 -> x16, waiting for transfers between devices: 41 us -> 15.7 us  [swap(): lax.ppermute(value, 'tensor', [(place, place ^ bit) for place in range(to...]
    convert_element_type x7 -> x4, other arithmetic: 1.13 us -> 4.66 us  [the longest x2 3.1 us: settle(): moving = value.astype(jnp.bfloat16)]
    unnamed x22 -> x10, local copies, waits for them, and re-layouts: 2.48 us -> 1.32 us
    pallas_call x8 -> x5, Pallas kernels: 36.4 us -> 37.1 us  [product(): pl.pallas_call(functools.partial(product_body, sent=len(sent), earlier=le...]
    ppermute x15 -> x16, starting transfers between devices: 14.6 us -> 14 us  [swap(): lax.ppermute(value, 'tensor', [(place, place ^ bit) for place in range(to...]
  transfers between devices with their start and end apart: 15 -> 16, of which waited for: 5 -> 6; matrix products, arithmetic and copies ran while one was open for 1% -> 6% of each run, Pallas kernels for 23% -> 53%
where the time goes in v4:
time: 85.7 us; the launch traced here: 85.4 us
  Pallas kernels  48.1 us (56%)
  waiting for transfers between devices  15.7 us (18%)
  starting transfers between devices  14 us (16%)
  other arithmetic  6.12 us (7%)
  local copies, waits for them, and re-layouts  1.32 us (2%)
    pallas_call x5, Pallas kernels, product(): pl.pallas_call(functools.partial(product_body, sent=len(sent), earlier=le...  37.1 us
    ppermute x16, waiting for transfers between devices, swap(): lax.ppermute(value, 'tensor', [(place, place ^ bit) for place in range(to...  15.7 us
    ppermute x16, starting transfers between devices, swap(): lax.ppermute(value, 'tensor', [(place, place ^ bit) for place in range(to...  14 us
    pallas_call x1, Pallas kernels, shrink(): pl.pallas_call(shrink_body, grid_spec=pltpu.PrefetchScalarGridSpec(num_sc...  8.25 us
    convert_element_type x2, other arithmetic, settle(): moving = value.astype(jnp.bfloat16)  3.1 us
    pallas_call x1, Pallas kernels, expand(): pl.pallas_call(expand_body, grid_spec=pltpu.PrefetchScalarGridSpec(num_sc...  2.76 us
  transfers between devices with their start and end apart: 16, of which 6 were waited for; matrix products, arithmetic and copies ran while one was open for 6% of the time, Pallas kernels for 53%

profile of v4, /device:TPU:0, one launch (start us, length us, event | category | flops | bytes accessed | tf_op | source)
XLA Modules:
  0.0 85.4 jit_solution(7413660006786043007)
XLA Ops:
  0.0 1.3 %copy-done = bf16[384,1664]{1,0:T(8,128)(2,1)S(1)} copy-done((bf16[384,1664]{1,0:T(8,128)(2,1)S(1)}, bf16[384,1664]{1,0:T(8,128)(2,1)}, u32[]{:S(2)}) %copy-start) | copy-done | bytes 1277976
  1.3 3.0 %shard_map.64.refs_0_ = bf16[1,384,512]{2,1,0:T(8,128)(2,1)S(1)} custom-call(s32[1]{0:T(128)} %bitcast.9.targets_ref, bf16[384,1664]{1,0:T(8,128)(2,1)S(1)} %copy-done, bf16[1664,8192]{1,0:T(8,128)(2,1)} %down_ref.9), custom_call_target="tpu_custom_call" | custom-call | flops 1000000 | bytes 1024 | tf_op jit(solution)/shard_map/pallas_call | solution.py:54
  4.3 0.5 collective-permute-start
  4.9 7.5 %shard_map.65 = (bf16[2,384,512]{2,1,0:T(8,128)(2,1)}, f32[384,512]{1,0:T(8,128)S(1)}) custom-call(s32[3]{0:T(128)S(1)} %pad_add_fusion.1.targets_ref, bf16[384,1664]{1,0:T(8,128)(2,1)S(1)} %copy-done.1, bf16[1664,8192]{1,0:T(8,128)(2,1)} %down_ref.9, bf16[1,384,512]{2,1,0:T(8,128)(2,1)S(1)} %shard_map.64.refs_0_), custom_call_target="tpu_custom_call" | custom-call | flops 1000000 | bytes 1024 | tf_op jit(solution)/shard_map/pallas_call | solution.py:54
  12.7 3.0 %collective-permute-start.4 = (bf16[384,512]{1,0:T(8,128)(2,1)S(1)}, bf16[384,512]{1,0:T(8,128)(2,1)S(1)}, u32[]{:S(2)}, u32[]{:S(2)}) collective-permute-start(bf16[384,512]{1,0:T(8,128)(2,1)S(1)} %fusion.15.earlier_ref.refs_0_), channel_id=1, source_target_pairs={{0,2},{1,3},{2,0},{3,1},{4,6},{5,7},{6,4},{7,5},{8,10},{9,11},{10,... | collective-permute-start | bytes 1179656 | tf_op jit(solution)/shard_map/ppermute | solution.py:71
  15.7 8.3 %shard_map.66.refs_1_ = f32[192,128]{1,0:T(8,128)S(1)} custom-call(s32[32]{0:T(128)S(1)} %copy-done.3, s32[32]{0:T(128)S(1)} %copy-done.4, bf16[384,1664]{1,0:T(8,128)(2,1)S(1)} %copy-done.1, bf16[2048,1664]{1,0:T(8,128)(2,1)} %bitcast.57, bf16[384,512]{1,0:T(8,128)(2,1)S(1)} %fusion.15.earlier_ref.refs_0_), custom_call_target="tpu_custom_call" | custom-call | flops 1000000 | bytes 1 | tf_op jit(solution)/shard_map/pallas_call | solution.py:127
  24.2 8.6 %shard_map.67 = (bf16[2,384,512]{2,1,0:T(8,128)(2,1)S(1)}, f32[384,512]{1,0:T(8,128)S(1)}, f32[384,512]{1,0:T(8,128)S(1)}) custom-call(s32[4]{0:T(128)S(1)} %pad_add_fusion.2.targets_ref, bf16[384,1664]{1,0:T(8,128)(2,1)S(1)} %copy-done.1, bf16[1664,8192]{1,0:T(8,128)(2,1)} %down_ref.9, bf16[384,512]{1,0:T(8,128)(2,1)S(1)} %fusion.15.earlier_ref.refs_0_, ...), custom_call_target="tpu_custom_call" | custom-call | flops 1000000 | bytes 1024 | tf_op jit(solution)/shard_map/pallas_call | solution.py:54
  32.9 1.4 %fusion.13 = (bf16[384,512]{1,0:T(8,128)(2,1)S(1)}, bf16[384,512]{1,0:T(8,128)(2,1)S(1)}) fusion(f32[384,512]{1,0:T(8,128)S(1)} %get-tuple-element.28, bf16[384,512]{1,0:T(8,128)(2,1)S(1)} %collective-permute-done.4, bf16[2,384,512]{2,1,0:T(8,128)(2,1)} %collective-permute-done.3, f32[384,512]{1,0:T(8,128)S(1)} %get-tuple-element.26), kind=kLoop, calls=%fused_computation.19 | loop fusion | flops 1572864 | bytes 3538944 | tf_op jit(solution)/shard_map/convert_element_type | solution.py:219
  34.4 2.1 %collective-permute-start.7 = (bf16[384,512]{1,0:T(8,128)(2,1)S(1)}, bf16[384,512]{1,0:T(8,128)(2,1)S(1)}, u32[]{:S(2)}, u32[]{:S(2)}) collective-permute-start(bf16[384,512]{1,0:T(8,128)(2,1)S(1)} %get-tuple-element.45.refs_1_), channel_id=1, source_target_pairs={{0,4},{1,5},{2,6},{3,7},{4,0},{5,1},{6,2},{7,3},{8,12},{9,13},{10,... | collective-permute-start | bytes 1179656 | tf_op jit(solution)/shard_map/ppermute | solution.py:71
  36.5 1.5 %collective-permute-start.6 = (bf16[384,512]{1,0:T(8,128)(2,1)S(1)}, bf16[384,512]{1,0:T(8,128)(2,1)}, u32[]{:S(2)}, u32[]{:S(2)}) collective-permute-start(bf16[384,512]{1,0:T(8,128)(2,1)S(1)} %get-tuple-element.46.refs_0_), channel_id=1, source_target_pairs={{0,2},{1,3},{2,0},{3,1},{4,6},{5,7},{6,4},{7,5},{8,10},{9,11},{10,... | collective-permute-start | bytes 1179656 | tf_op jit(solution)/shard_map/ppermute | solution.py:71
  38.6 9.3 %shard_map.68 = (bf16[2,384,512]{2,1,0:T(8,128)(2,1)}, f32[384,512]{1,0:T(8,128)S(1)}, f32[384,512]{1,0:T(8,128)S(1)}) custom-call(s32[4]{0:T(128)S(1)} %pad_add_fusion.3.targets_ref, bf16[384,1664]{1,0:T(8,128)(2,1)S(1)} %copy-done.1, bf16[1664,8192]{1,0:T(8,128)(2,1)} %down_ref.9, bf16[384,512]{1,0:T(8,128)(2,1)S(1)} %get-tuple-element.46.refs_0_, ...), custom_call_target="tpu_custom_call" | custom-call | flops 1000000 | bytes 1024 | tf_op jit(solution)/shard_map/pallas_call | solution.py:54
  48.4 1.7 %fusion.10 = (bf16[384,512]{1,0:T(8,128)(2,1)S(1)}, bf16[384,512]{1,0:T(8,128)(2,1)S(1)}) fusion(f32[384,512]{1,0:T(8,128)S(1)} %get-tuple-element.32, bf16[384,512]{1,0:T(8,128)(2,1)S(1)} %collective-permute-done.7, bf16[384,512]{1,0:T(8,128)(2,1)} %collective-permute-done.6, bf16[2,384,512]{2,1,0:T(8,128)(2,1)} %collective-permute-done.5, ...), kind=kLoop, calls=%fused_computation.14 | loop fusion | flops 1966080 | bytes 3932160 | tf_op jit(solution)/shard_map/convert_element_type | solution.py:219
  50.0 1.7 %collective-permute-start.13 = (bf16[384,512]{1,0:T(8,128)(2,1)S(1)}, bf16[384,512]{1,0:T(8,128)(2,1)S(1)}, u32[]{:S(2)}, u32[]{:S(2)}) collective-permute-start(bf16[384,512]{1,0:T(8,128)(2,1)S(1)} %get-tuple-element.44.refs_0_), channel_id=1, source_target_pairs={{0,2},{1,3},{2,0},{3,1},{4,6},{5,7},{6,4},{7,5},{8,10},{9,11},{10,... | collective-permute-start | bytes 1179656 | tf_op jit(solution)/shard_map/ppermute | solution.py:71
  51.8 2.7 %collective-permute-start.9 = (f32[192,128]{1,0:T(8,128)S(1)}, f32[192,128]{1,0:T(8,128)S(1)}, u32[]{:S(2)}, u32[]{:S(2)}) collective-permute-start(f32[192,128]{1,0:T(8,128)S(1)} %add.69.refs_2_), channel_id=1, source_target_pairs={{0,8},{1,9},{2,10},{3,11},{4,12},{5,13},{6,14},{7,15},{8,0},{9,1},... | collective-permute-start | bytes 294920 | tf_op jit(solution)/shard_map/ppermute | solution.py:71
  54.9 8.6 %shard_map.69 = (bf16[1,384,512]{2,1,0:T(8,128)(2,1)S(1)}, f32[384,512]{1,0:T(8,128)S(1)}, f32[384,512]{1,0:T(8,128)S(1)}, f32[384,512]{1,0:T(8,128)S(1)}) custom-call(s32[4]{0:T(128)S(1)} %pad_add_fusion.targets_ref, bf16[384,1664]{1,0:T(8,128)(2,1)S(1)} %copy-done.1, bf16[1664,8192]{1,0:T(8,128)(2,1)} %down_ref.9, ...), custom_call_target="tpu_custom_call" | custom-call | flops 1000000 | bytes 1024 | tf_op jit(solution)/shard_map/pallas_call | solution.py:54
  63.5 4.7 %collective-permute-done.9 = f32[192,128]{1,0:T(8,128)S(1)} collective-permute-done((f32[192,128]{1,0:T(8,128)S(1)}, f32[192,128]{1,0:T(8,128)S(1)}, u32[]{:S(2)}, u32[]{:S(2)}) %collective-permute-start.9) | collective-permute-done | bytes 98336 | tf_op jit(solution)/shard_map/ppermute | solution.py:71
  68.2 1.4 %fusion.2 = (bf16[384,512]{1,0:T(8,128)(2,1)S(1)}, bf16[384,512]{1,0:T(8,128)(2,1)S(1)}) fusion(f32[384,512]{1,0:T(8,128)S(1)} %get-tuple-element.37, bf16[2,384,512]{2,1,0:T(8,128)(2,1)} %collective-permute-done.10, bf16[384,512]{1,0:T(8,128)(2,1)S(1)} %collective-permute-done.13, f32[384,512]{1,0:T(8,128)S(1)} %get-tuple-element.39), kind=kLoop, calls=%fused_computation.4 | loop fusion | flops 1572864 | bytes 3538944 | tf_op jit(solution)/shard_map/convert_element_type | solution.py:248
  69.6 0.9 %collective-permute-start.11 = (bf16[384,512]{1,0:T(8,128)(2,1)S(1)}, bf16[384,512]{1,0:T(8,128)(2,1)S(1)}, u32[]{:S(2)}, u32[]{:S(2)}) collective-permute-start(bf16[384,512]{1,0:T(8,128)(2,1)S(1)} %get-tuple-element.41), channel_id=1, source_target_pairs={{0,2},{1,3},{2,0},{3,1},{4,6},{5,7},{6,4},{7,5},{8,10},{9,11},{10,... | collective-permute-start | bytes 1179656 | tf_op jit(solution)/shard_map/ppermute | solution.py:71
  70.8 1.1 %collective-permute-done.15 = f32[192,128]{1,0:T(8,128)S(1)} collective-permute-done((f32[192,128]{1,0:T(8,128)S(1)}, f32[192,128]{1,0:T(8,128)S(1)}, u32[]{:S(2)}, u32[]{:S(2)}) %collective-permute-start.15) | collective-permute-done | bytes 98336 | tf_op jit(solution)/shard_map/ppermute | solution.py:71
  72.0 2.8 %shard_map.70 = f32[384,512]{1,0:T(8,128)S(1)} custom-call(s32[32]{0:T(128)S(1)} %copy-done.3, s32[32]{0:T(128)S(1)} %copy-done.4, f32[192,128]{1,0:T(8,128)S(1)} %add.78.packed_ref, bf16[2048,512]{1,0:T(8,128)(2,1)S(1)} %bitcast.56), custom_call_target="tpu_custom_call" | custom-call | flops 1000000 | bytes 1 | tf_op jit(solution)/shard_map/pallas_call | solution.py:171
  74.7 1.2 %collective-permute-done.12 = bf16[384,512]{1,0:T(8,128)(2,1)S(1)} collective-permute-done((bf16[384,512]{1,0:T(8,128)(2,1)S(1)}, bf16[384,512]{1,0:T(8,128)(2,1)S(1)}, u32[]{:S(2)}, u32[]{:S(2)}) %collective-permute-start.12) | collective-permute-done | bytes 393248 | tf_op jit(solution)/shard_map/ppermute | solution.py:71
  75.9 5.3 %collective-permute-done.11 = bf16[384,512]{1,0:T(8,128)(2,1)S(1)} collective-permute-done((bf16[384,512]{1,0:T(8,128)(2,1)S(1)}, bf16[384,512]{1,0:T(8,128)(2,1)S(1)}, u32[]{:S(2)}, u32[]{:S(2)}) %collective-permute-start.11) | collective-permute-done | bytes 393248 | tf_op jit(solution)/shard_map/ppermute | solution.py:71
  81.2 3.0 %collective-permute-done.14 = bf16[384,512]{1,0:T(8,128)(2,1)S(1)} collective-permute-done((bf16[384,512]{1,0:T(8,128)(2,1)S(1)}, bf16[384,512]{1,0:T(8,128)(2,1)S(1)}, u32[]{:S(2)}, u32[]{:S(2)}) %collective-permute-start.14) | collective-permute-done | bytes 393248 | tf_op jit(solution)/shard_map/ppermute | solution.py:71
  84.2 1.1 %fusion.7 = bf16[384,512]{1,0:T(8,128)(2,1)} fusion(f32[384,512]{1,0:T(8,128)S(1)} %shard_map.70, f32[384,512]{1,0:T(8,128)S(1)} %get-tuple-element.34, bf16[384,512]{1,0:T(8,128)(2,1)S(1)} %collective-permute-done.14, bf16[384,512]{1,0:T(8,128)(2,1)S(1)} %collective-permute-done.12, bf16[384,512]{1,0:T(8,128)(2,1)S(1)} %collective-permute-done.11, ...), kind=kLoop, calls=%fused_computation.10 | loop fusion | flops 1966080 | bytes 3538944 | tf_op jit(solution)/shard_map/convert_element_type | solution.py:263
  (38 shorter events, 2.4 us)
Async XLA Ops:
  0.0 1.3 %copy-start = (bf16[384,1664]{1,0:T(8,128)(2,1)S(1)}, bf16[384,1664]{1,0:T(8,128)(2,1)}, u32[]{:S(2)}) copy-start(bf16[384,1664]{1,0:T(8,128)(2,1)} %hidden_ref.11) | copy-start | bytes 3833860
  1.3 3.6 %copy-start.1 = (bf16[384,1664]{1,0:T(8,128)(2,1)S(1)}, bf16[384,1664]{1,0:T(8,128)(2,1)}, u32[]{:S(2)}) copy-start(bf16[384,1664]{1,0:T(8,128)(2,1)} %hidden_ref.11) | copy-start | bytes 3833860
  4.3 8.3 %collective-permute-start = (bf16[1,384,512]{2,1,0:T(8,128)(2,1)S(1)}, bf16[1,384,512]{2,1,0:T(8,128)(2,1)S(1)}, u32[]{:S(2)}, u32[]{:S(2)}) collective-permute-start(bf16[1,384,512]{2,1,0:T(8,128)(2,1)S(1)} %shard_map.64.refs_0_), channel_id=1, source_target_pairs={{0,1},{1,0},{2,3},{3,2},{4,5},{5,4},{6,7},{7,6},{8,9},{9,8},{10,11... | collective-permute-start | bytes 1179656 | tf_op jit(solution)/shard_map/ppermute | solution.py:71
  4.9 10.8 %copy-start.3 = (s32[32]{0:T(128)S(1)}, s32[32]{0:T(128)}, u32[]{:S(2)}) copy-start(s32[32]{0:T(128)} %first_ref.3) | copy-start | bytes 388
  4.9 10.8 %copy-start.4 = (s32[32]{0:T(128)S(1)}, s32[32]{0:T(128)}, u32[]{:S(2)}) copy-start(s32[32]{0:T(128)} %length_ref.3) | copy-start | bytes 388
  12.5 20.5 %collective-permute-start.3 = (bf16[2,384,512]{2,1,0:T(8,128)(2,1)}, bf16[2,384,512]{2,1,0:T(8,128)(2,1)}, u32[]{:S(2)}, u32[]{:S(2)}) collective-permute-start(bf16[2,384,512]{2,1,0:T(8,128)(2,1)} %get-tuple-element.27), channel_id=1, source_target_pairs={{0,1},{1,0},{2,3},{3,2},{4,5},{5,4},{6,7},{7,6},{8,9},{9,8},{10,11... | collective-permute-start | bytes 2359304 | tf_op jit(solution)/shard_map/ppermute | solution.py:71
  12.7 20.2 %collective-permute-start.4 = (bf16[384,512]{1,0:T(8,128)(2,1)S(1)}, bf16[384,512]{1,0:T(8,128)(2,1)S(1)}, u32[]{:S(2)}, u32[]{:S(2)}) collective-permute-start(bf16[384,512]{1,0:T(8,128)(2,1)S(1)} %fusion.15.earlier_ref.refs_0_), channel_id=1, source_target_pairs={{0,2},{1,3},{2,0},{3,1},{4,6},{5,7},{6,4},{7,5},{8,10},{9,11},{10,... | collective-permute-start | bytes 1179656 | tf_op jit(solution)/shard_map/ppermute | solution.py:71
  24.0 8.9 %collective-permute-start.1 = (f32[192,128]{1,0:T(8,128)S(1)}, f32[192,128]{1,0:T(8,128)S(1)}, u32[]{:S(2)}, u32[]{:S(2)}) collective-permute-start(f32[192,128]{1,0:T(8,128)S(1)} %shard_map.66.refs_1_), channel_id=1, source_target_pairs={{0,2},{1,3},{2,0},{3,1},{4,6},{5,7},{6,4},{7,5},{8,10},{9,11},{10,... | collective-permute-start | bytes 294920 | tf_op jit(solution)/shard_map/ppermute | solution.py:71
  32.8 15.5 %collective-permute-start.5 = (bf16[2,384,512]{2,1,0:T(8,128)(2,1)S(1)}, bf16[2,384,512]{2,1,0:T(8,128)(2,1)}, u32[]{:S(2)}, u32[]{:S(2)}) collective-permute-start(bf16[2,384,512]{2,1,0:T(8,128)(2,1)S(1)} %get-tuple-element.31), channel_id=1, source_target_pairs={{0,1},{1,0},{2,3},{3,2},{4,5},{5,4},{6,7},{7,6},{8,9},{9,8},{10,11... | collective-permute-start | bytes 2359304 | tf_op jit(solution)/shard_map/ppermute | solution.py:71
  34.4 14.0 %collective-permute-start.7 = (bf16[384,512]{1,0:T(8,128)(2,1)S(1)}, bf16[384,512]{1,0:T(8,128)(2,1)S(1)}, u32[]{:S(2)}, u32[]{:S(2)}) collective-permute-start(bf16[384,512]{1,0:T(8,128)(2,1)S(1)} %get-tuple-element.45.refs_1_), channel_id=1, source_target_pairs={{0,4},{1,5},{2,6},{3,7},{4,0},{5,1},{6,2},{7,3},{8,12},{9,13},{10,... | collective-permute-start | bytes 1179656 | tf_op jit(solution)/shard_map/ppermute | solution.py:71
  36.5 11.9 %collective-permute-start.6 = (bf16[384,512]{1,0:T(8,128)(2,1)S(1)}, bf16[384,512]{1,0:T(8,128)(2,1)}, u32[]{:S(2)}, u32[]{:S(2)}) collective-permute-start(bf16[384,512]{1,0:T(8,128)(2,1)S(1)} %get-tuple-element.46.refs_0_), channel_id=1, source_target_pairs={{0,2},{1,3},{2,0},{3,1},{4,6},{5,7},{6,4},{7,5},{8,10},{9,11},{10,... | collective-permute-start | bytes 1179656 | tf_op jit(solution)/shard_map/ppermute | solution.py:71
  38.0 10.3 %collective-permute-start.2 = (f32[192,128]{1,0:T(8,128)S(1)}, f32[192,128]{1,0:T(8,128)S(1)}, u32[]{:S(2)}, u32[]{:S(2)}) collective-permute-start(f32[192,128]{1,0:T(8,128)S(1)} %add.61.refs_2_), channel_id=1, source_target_pairs={{0,4},{1,5},{2,6},{3,7},{4,0},{5,1},{6,2},{7,3},{8,12},{9,13},{10,... | collective-permute-start | bytes 294920 | tf_op jit(solution)/shard_map/ppermute | solution.py:71
  47.9 20.3 %collective-permute-start.10 = (bf16[2,384,512]{2,1,0:T(8,128)(2,1)}, bf16[2,384,512]{2,1,0:T(8,128)(2,1)}, u32[]{:S(2)}, u32[]{:S(2)}) collective-permute-start(bf16[2,384,512]{2,1,0:T(8,128)(2,1)} %get-tuple-element.38), channel_id=1, source_target_pairs={{0,1},{1,0},{2,3},{3,2},{4,5},{5,4},{6,7},{7,6},{8,9},{9,8},{10,11... | collective-permute-start | bytes 2359304 | tf_op jit(solution)/shard_map/ppermute | solution.py:71
  50.0 18.1 %collective-permute-start.13 = (bf16[384,512]{1,0:T(8,128)(2,1)S(1)}, bf16[384,512]{1,0:T(8,128)(2,1)S(1)}, u32[]{:S(2)}, u32[]{:S(2)}) collective-permute-start(bf16[384,512]{1,0:T(8,128)(2,1)S(1)} %get-tuple-element.44.refs_0_), channel_id=1, source_target_pairs={{0,2},{1,3},{2,0},{3,1},{4,6},{5,7},{6,4},{7,5},{8,10},{9,11},{10,... | collective-permute-start | bytes 1179656 | tf_op jit(solution)/shard_map/ppermute | solution.py:71
  51.8 16.4 %collective-permute-start.9 = (f32[192,128]{1,0:T(8,128)S(1)}, f32[192,128]{1,0:T(8,128)S(1)}, u32[]{:S(2)}, u32[]{:S(2)}) collective-permute-start(f32[192,128]{1,0:T(8,128)S(1)} %add.69.refs_2_), channel_id=1, source_target_pairs={{0,8},{1,9},{2,10},{3,11},{4,12},{5,13},{6,14},{7,15},{8,0},{9,1},... | collective-permute-start | bytes 294920 | tf_op jit(solution)/shard_map/ppermute | solution.py:71
  54.5 17.4 %copy-start.2 = (bf16[32,64,512]{2,1,0:T(8,128)(2,1)S(1)}, bf16[32,64,512]{2,1,0:T(8,128)(2,1)}, u32[]{:S(2)}) copy-start(bf16[32,64,512]{2,1,0:T(8,128)(2,1)} %param.10) | copy-start | bytes 6291460
  54.5 21.4 %collective-permute-start.12 = (bf16[384,512]{1,0:T(8,128)(2,1)S(1)}, bf16[384,512]{1,0:T(8,128)(2,1)S(1)}, u32[]{:S(2)}, u32[]{:S(2)}) collective-permute-start(bf16[384,512]{1,0:T(8,128)(2,1)S(1)} %get-tuple-element.43.refs_1_), channel_id=1, source_target_pairs={{0,8},{1,9},{2,10},{3,11},{4,12},{5,13},{6,14},{7,15},{8,0},{9,1},... | collective-permute-start | bytes 1179656 | tf_op jit(solution)/shard_map/ppermute | solution.py:71
  68.2 7.8 %collective-permute-start.8 = (bf16[1,384,512]{2,1,0:T(8,128)(2,1)S(1)}, bf16[1,384,512]{2,1,0:T(8,128)(2,1)S(1)}, u32[]{:S(2)}, u32[]{:S(2)}) collective-permute-start(bf16[1,384,512]{2,1,0:T(8,128)(2,1)S(1)} %get-tuple-element.35), channel_id=1, source_target_pairs={{0,1},{1,0},{2,3},{3,2},{4,5},{5,4},{6,7},{7,6},{8,9},{9,8},{10,11... | collective-permute-start | bytes 1179656 | tf_op jit(solution)/shard_map/ppermute | solution.py:71
  69.6 11.6 %collective-permute-start.11 = (bf16[384,512]{1,0:T(8,128)(2,1)S(1)}, bf16[384,512]{1,0:T(8,128)(2,1)S(1)}, u32[]{:S(2)}, u32[]{:S(2)}) collective-permute-start(bf16[384,512]{1,0:T(8,128)(2,1)S(1)} %get-tuple-element.41), channel_id=1, source_target_pairs={{0,2},{1,3},{2,0},{3,1},{4,6},{5,7},{6,4},{7,5},{8,10},{9,11},{10,... | collective-permute-start | bytes 1179656 | tf_op jit(solution)/shard_map/ppermute | solution.py:71
  70.5 13.7 %collective-permute-start.14 = (bf16[384,512]{1,0:T(8,128)(2,1)S(1)}, bf16[384,512]{1,0:T(8,128)(2,1)S(1)}, u32[]{:S(2)}, u32[]{:S(2)}) collective-permute-start(bf16[384,512]{1,0:T(8,128)(2,1)S(1)} %get-tuple-element.42), channel_id=1, source_target_pairs={{0,4},{1,5},{2,6},{3,7},{4,0},{5,1},{6,2},{7,3},{8,12},{9,13},{10,... | collective-permute-start | bytes 1179656 | tf_op jit(solution)/shard_map/ppermute | solution.py:71
  70.6 1.4 %collective-permute-start.15 = (f32[192,128]{1,0:T(8,128)S(1)}, f32[192,128]{1,0:T(8,128)S(1)}, u32[]{:S(2)}, u32[]{:S(2)}) collective-permute-start(f32[192,128]{1,0:T(8,128)S(1)} %add.77), channel_id=1, source_target_pairs={{0,1},{1,0},{2,3},{3,2},{4,5},{5,4},{6,7},{7,6},{8,9},{9,8},{10,11... | collective-permute-start | bytes 294920 | tf_op jit(solution)/shard_map/ppermute | solution.py:71

commit v5 on v4

--- a/solution.py
+++ b/solution.py
@@ -8,7 +8,9 @@
 from jax.sharding import PartitionSpec as P
 
 BLOCK = 256
-VMEM_LIMIT = 48 * 1024 * 1024
+SLOTS = 3
+PIECES = 2
+VMEM_LIMIT = 40 * 1024 * 1024
 WINDOW = 128
 TOGETHER = 4
 FLOPS = 1_000_000
@@ -19,47 +21,59 @@
     width = result_refs[0].shape[-1]
     block = buffer.shape[2]
     blocks = width // block
-    targets = buffer.shape[0] // blocks
-    copies = []
-    for at in range(targets):
-        for part in range(blocks):
-            slot = at * blocks + part
-            column = pl.multiple_of(targets_ref[at] * width + part * block, block)
-            copies.append(
-                pltpu.make_async_copy(
-                    down_ref.at[:, pl.ds(column, block)], buffer.at[slot], arrived.at[slot]
-                )
+    steps = [(at, part) for at in range(targets_ref.shape[0]) for part in range(blocks)]
+    slots, pieces = arrived.shape
+    deep = buffer.shape[1] // pieces
+
+    def copies(step):
+        at, part = steps[step]
+        column = pl.multiple_of(targets_ref[at] * width + part * block, block)
+        for piece in range(pieces):
+            rows = pl.ds(piece * deep, deep)
+            yield pltpu.make_async_copy(
+                down_ref.at[rows, pl.ds(column, block)],
+                buffer.at[step % slots, rows],
+                arrived.at[step % slots, piece],
             )
-            copies[-1].start()
-    for at in range(targets):
-        for part in range(blocks):
-            slot = at * blocks + part
-            copies[slot].wait()
-            total = jnp.dot(hidden_ref[...], buffer[slot], preferred_element_type=jnp.float32)
-            columns = slice(part * block, (part + 1) * block)
-            if at < sent:
-                result_refs[0][at, :, columns] = total.astype(jnp.bfloat16)
-            else:
-                result_refs[(1 if sent else 0) + at - sent][:, columns] = total
+
+    for step in range(min(slots - 1, len(steps))):
+        for copy in copies(step):
+            copy.start()
+    for step, (at, part) in enumerate(steps):
+        if step + slots - 1 < len(steps):
+            for copy in copies(step + slots - 1):
+                copy.start()
+        for copy in copies(step):
+            copy.wait()
+        total = jnp.dot(
+            hidden_ref[...], buffer[step % slots], preferred_element_type=jnp.float32
+        )
+        columns = slice(part * block, (part + 1) * block)
+        if at < sent:
+            result_refs[0][at, :, columns] = total.astype(jnp.bfloat16)
+        else:
+            result_refs[(1 if sent else 0) + at - sent][:, columns] = total
 
 
 def product(hidden, down_matrix, sent, kept, width, earlier):
     rows, depth = hidden.shape
     block = min(BLOCK, width)
-    slots = (len(sent) + len(kept)) * (width // block)
+    pieces = PIECES if depth % (16 * PIECES) == 0 else 1
     vmem = pl.BlockSpec(memory_space=pltpu.VMEM)
     out_shape = [jax.ShapeDtypeStruct((rows, width), jnp.float32)] * len(kept)
     if sent:
         out_shape = [jax.ShapeDtypeStruct((len(sent), rows, width), jnp.bfloat16)] + out_shape
     results = pl.pallas_call(
         functools.partial(product_body, sent=len(sent), earlier=len(earlier)),
-        in_specs=[pl.BlockSpec(memory_space=pltpu.SMEM), vmem]
-        + [pl.BlockSpec(memory_space=pl.ANY)] * (1 + len(earlier)),
+        in_specs=[
+            pl.BlockSpec(memory_space=pltpu.SMEM), vmem, pl.BlockSpec(memory_space=pltpu.HBM)
+        ]
+        + [pl.BlockSpec(memory_space=pl.ANY)] * len(earlier),
         out_specs=[vmem] * len(out_shape),
         out_shape=out_shape,
         scratch_shapes=[
-            pltpu.VMEM((slots, depth, block), jnp.bfloat16),
-            pltpu.SemaphoreType.DMA((slots,)),
+            pltpu.VMEM((SLOTS, depth, block), jnp.bfloat16),
+            pltpu.SemaphoreType.DMA((SLOTS, pieces)),
         ],
         compiler_params=pltpu.CompilerParams(vmem_limit_bytes=VMEM_LIMIT),
         cost_estimate=pl.CostEstimate(flops=FLOPS, bytes_accessed=1024, transcendentals=0),
@@ -91,56 +105,15 @@
     lax.fori_loop(0, (ends[-1] - base + window - 1) // window, step, 0)
 
 
-def shrink_body(first_ref, length_ref, hidden_ref, table_ref, earlier_ref, packed_ref, total_ref):
-    group = pl.program_id(0)
-    rank = total_ref.shape[1]
-    rows = total_ref.shape[0]
-
-    @pl.when(group == 0)
-    def _():
-        total_ref[...] = jnp.zeros_like(total_ref)
-
-    def body(window, masks):
-        every = lax.dot_general(
-            hidden_ref[window, :],
-            table_ref[...],
-            (((1,), (1,)), ((), ())),
-            preferred_element_type=jnp.float32,
-        )
-        picked = total_ref[window, :]
-        for at, mask in enumerate(masks):
-            picked = picked + jnp.where(mask, every[:, at * rank:(at + 1) * rank], 0.0)
-        total_ref[window, :] = picked
-
-    for_each_window(first_ref, length_ref, group, rows, body)
-
-    @pl.when(group == pl.num_programs(0) - 1)
-    def _():
-        packed_ref[:, :rank] = total_ref[:rows // 2, :]
-        packed_ref[:, rank:] = total_ref[rows // 2:, :]
-
-
-def shrink(hidden, shrink_matrices, segment_first_row, segment_length, earlier):
-    rows, depth = hidden.shape
-    adapters, _, rank = shrink_matrices.shape
-    table = jnp.swapaxes(shrink_matrices, 1, 2).reshape(adapters * rank, depth)
-    return pl.pallas_call(
-        shrink_body,
-        grid_spec=pltpu.PrefetchScalarGridSpec(
-            num_scalar_prefetch=2,
-            grid=(adapters // TOGETHER,),
-            in_specs=[
-                pl.BlockSpec((rows, depth), lambda group, *_: (0, 0)),
-                pl.BlockSpec((TOGETHER * rank, depth), lambda group, *_: (group, 0)),
-                pl.BlockSpec(memory_space=pl.ANY),
-            ],
-            out_specs=pl.BlockSpec((rows // 2, 2 * rank), lambda group, *_: (0, 0)),
-            scratch_shapes=[pltpu.VMEM((rows, rank), jnp.float32)],
-        ),
-        out_shape=jax.ShapeDtypeStruct((rows // 2, 2 * rank), jnp.float32),
-        compiler_params=pltpu.CompilerParams(vmem_limit_bytes=VMEM_LIMIT),
-        cost_estimate=pl.CostEstimate(flops=FLOPS, bytes_accessed=1, transcendentals=0),
-    )(segment_first_row, segment_length, hidden, table, earlier)
+def shrink(hidden, shrink_matrices, row_adapter_index):
+    adapters = shrink_matrices.shape[0]
+    every_adapter = jnp.einsum(
+        "hq,gqu->hgu", hidden, shrink_matrices, preferred_element_type=jnp.float32
+    )
+    picked = row_adapter_index[:, None] == jnp.arange(adapters, dtype=jnp.int32)[None, :]
+    partial = jnp.sum(jnp.where(picked[:, :, None], every_adapter, 0.0), axis=1)
+    half = hidden.shape[0] // 2
+    return jnp.concatenate([partial[:half], partial[half:]], axis=1)
 
 
 def expand_body(first_ref, length_ref, packed_ref, table_ref, result_ref, shrunk_ref):
@@ -223,7 +196,7 @@
     top = units - 1
     values, _ = product(hidden, down_matrix, [out_of(top) ^ core], [], width, [])
     packed, ready = None, [values]
-    steps = [near, *(4 << at for at in range(top.bit_length())), core]
+    steps = [*(4 << at for at in reversed(range(top.bit_length()))), near, core]
     for unit in reversed(range(units)):
         arrived = swap(values, core, total)
         sent, kept = [], [out_of(unit)]
@@ -244,16 +217,15 @@
             moved, kept_out[unit] = lax.optimization_barrier(
                 (swap(packed, steps.pop(0), total), kept_out[unit])
             )
-            packed = packed + moved
+            packed = packed + moved.astype(jnp.float32)
         leaving = (kept_out[unit] + arrived[0].astype(jnp.float32)).astype(jnp.bfloat16)
         ready = [leaving]
         if unit < top:
             ready.append(settle(unit + 1, arrived[1]))
+        if packed is None:
+            late, leaving = lax.optimization_barrier((hidden, leaving))
+            packed = shrink(late, shrink_matrices, row_adapter_index)
         crossed[unit] = swap(leaving, near, total)
-        if packed is None:
-            packed = shrink(
-                hidden, shrink_matrices, segment_first_row, segment_length, leaving
-            )
         ready.append(packed)
     kept = [settle(0, swap(values, core, total)[0])]
 

time: 85.7 us -> 83.1 us (0.970)
  Pallas kernels: 48.1 us -> 39.7 us
  matrix products: 0 us -> 6.17 us
  waiting for transfers between devices: 15.7 us -> 13 us
  other arithmetic: 6.12 us -> 7.55 us
    pallas_call x1 -> x0, Pallas kernels: 8.25 us -> none  [shrink(): pl.pallas_call(shrink_body, grid_spec=pltpu.PrefetchScalarGridSpec(num_sc...]
    unnamed x0 -> x1, matrix products: none -> 6.17 us
    ppermute x16, waiting for transfers between devices: 15.7 us -> 13 us  [swap(): lax.ppermute(value, 'tensor', [(place, place ^ bit) for place in range(to...]
    add x3, other arithmetic: 0.04 us -> 1.01 us  [on_device(): packed = packed + moved.astype(jnp.float32)]
  transfers between devices with their start and end apart: 16 -> 16, of which waited for: 6 -> 6; matrix products, arithmetic and copies ran while one was open for 6% -> 16% of each run, Pallas kernels for 53% -> 44%
where the time goes in v5:
time: 83.1 us; the launch traced here: 82.7 us
  Pallas kernels  39.7 us (48%)
  starting transfers between devices  14.5 us (17%)
  waiting for transfers between devices  13 us (16%)
  other arithmetic  7.55 us (9%)
  matrix products  6.17 us (7%)
  local copies, waits for them, and re-layouts  1.6 us (2%)
    pallas_call x5, Pallas kernels, product(): pl.pallas_call(functools.partial(product_body, sent=len(sent), earlier=le...  36.9 us
    ppermute x16, starting transfers between devices, swap(): lax.ppermute(value, 'tensor', [(place, place ^ bit) for place in range(to...  14.5 us
    ppermute x16, waiting for transfers between devices, swap(): lax.ppermute(value, 'tensor', [(place, place ^ bit) for place in range(to...  13 us
    unnamed x1, matrix products  6.17 us
    convert_element_type x2, other arithmetic, settle(): moving = value.astype(jnp.bfloat16)  3.01 us
    pallas_call x1, Pallas kernels, expand(): pl.pallas_call(expand_body, grid_spec=pltpu.PrefetchScalarGridSpec(num_sc...  2.76 us
  transfers between devices with their start and end apart: 16, of which 6 were waited for; matrix products, arithmetic and copies ran while one was open for 16% of the time, Pallas kernels for 44%

profile of v5, /device:TPU:0, one launch (start us, length us, event | category | flops | bytes accessed | tf_op | source)
XLA Modules:
  0.0 82.7 jit_solution(16054663309788167175)
XLA Ops:
  0.0 1.3 %copy-done = bf16[384,1664]{1,0:T(8,128)(2,1)S(1)} copy-done((bf16[384,1664]{1,0:T(8,128)(2,1)S(1)}, bf16[384,1664]{1,0:T(8,128)(2,1)}, u32[]{:S(2)}) %copy-start) | copy-done | bytes 1277976
  1.3 3.0 %shard_map.73.refs_0_ = bf16[1,384,512]{2,1,0:T(8,128)(2,1)S(1)} custom-call(s32[1]{0:T(128)} %bitcast.7.targets_ref, bf16[384,1664]{1,0:T(8,128)(2,1)S(1)} %copy-done, bf16[1664,8192]{1,0:T(8,128)(2,1)} %down_ref.9), custom_call_target="tpu_custom_call" | custom-call | flops 1000000 | bytes 1024 | tf_op jit(solution)/shard_map/pallas_call | solution.py:66
  4.9 7.5 %shard_map.74 = (bf16[2,384,512]{2,1,0:T(8,128)(2,1)}, f32[384,512]{1,0:T(8,128)S(1)}) custom-call(s32[3]{0:T(128)S(1)} %pad_add_fusion.1.targets_ref, bf16[384,1664]{1,0:T(8,128)(2,1)S(1)} %copy-done.1, bf16[1664,8192]{1,0:T(8,128)(2,1)} %down_ref.9, bf16[1,384,512]{2,1,0:T(8,128)(2,1)S(1)} %shard_map.73.refs_0_), custom_call_target="tpu_custom_call" | custom-call | flops 1000000 | bytes 1024 | tf_op jit(solution)/shard_map/pallas_call | solution.py:66
  12.7 3.0 %collective-permute-start.4 = (bf16[384,512]{1,0:T(8,128)(2,1)S(1)}, bf16[384,512]{1,0:T(8,128)(2,1)}, u32[]{:S(2)}, u32[]{:S(2)}) collective-permute-start(bf16[384,512]{1,0:T(8,128)(2,1)S(1)} %fusion.15.refs_0_), channel_id=1, source_target_pairs={{0,2},{1,3},{2,0},{3,1},{4,6},{5,7},{6,4},{7,5},{8,10},{9,11},{10,... | collective-permute-start | bytes 1179656 | tf_op jit(solution)/shard_map/ppermute | solution.py:85
  15.7 6.2 %fusion.17 = f32[384,2048]{0,1:S(1)} fusion(bf16[384,1664]{1,0:T(8,128)(2,1)S(1)} %copy-done.1, bf16[1664,2048]{0,1:T(8,128)(2,1)} %bitcast.61), kind=kOutput, calls=%fused_computation.38 | convolution fusion | flops 2617245696 | bytes 11239424
  22.7 2.6 %collective-permute-start.1 = (f32[192,128]{1,0:T(8,128)S(1)}, f32[192,128]{1,0:T(8,128)}, u32[]{:S(2)}, u32[]{:S(2)}) collective-permute-start(f32[192,128]{1,0:T(8,128)S(1)} %pad_maximum_fusion.refs_1_), channel_id=1, source_target_pairs={{0,8},{1,9},{2,10},{3,11},{4,12},{5,13},{6,14},{7,15},{8,0},{9,1},... | collective-permute-start | bytes 294920 | tf_op jit(solution)/shard_map/ppermute | solution.py:85
  25.4 9.2 %shard_map.75 = (bf16[2,384,512]{2,1,0:T(8,128)(2,1)}, f32[384,512]{1,0:T(8,128)S(1)}, f32[384,512]{1,0:T(8,128)S(1)}) custom-call(s32[4]{0:T(128)S(1)} %pad_add_fusion.2.targets_ref, bf16[384,1664]{1,0:T(8,128)(2,1)S(1)} %copy-done.1, bf16[1664,8192]{1,0:T(8,128)(2,1)} %down_ref.9, bf16[384,512]{1,0:T(8,128)(2,1)S(1)} %fusion.15.refs_0_, ...), custom_call_target="tpu_custom_call" | custom-call | flops 1000000 | bytes 1024 | tf_op jit(solution)/shard_map/pallas_call | solution.py:66
  34.8 1.5 %fusion.13 = (bf16[384,512]{1,0:T(8,128)(2,1)S(1)}, bf16[384,512]{1,0:T(8,128)(2,1)S(1)}) fusion(f32[384,512]{1,0:T(8,128)S(1)} %get-tuple-element.31, bf16[384,512]{1,0:T(8,128)(2,1)} %collective-permute-done.4, bf16[2,384,512]{2,1,0:T(8,128)(2,1)} %collective-permute-done.3, f32[384,512]{1,0:T(8,128)S(1)} %get-tuple-element.29), kind=kLoop, calls=%fused_computation.20 | loop fusion | flops 1572864 | bytes 3538944 | tf_op jit(solution)/shard_map/convert_element_type | solution.py:192
  36.3 1.6 %collective-permute-start.7 = (bf16[384,512]{1,0:T(8,128)(2,1)S(1)}, bf16[384,512]{1,0:T(8,128)(2,1)S(1)}, u32[]{:S(2)}, u32[]{:S(2)}) collective-permute-start(bf16[384,512]{1,0:T(8,128)(2,1)S(1)} %get-tuple-element.49.refs_1_), channel_id=1, source_target_pairs={{0,4},{1,5},{2,6},{3,7},{4,0},{5,1},{6,2},{7,3},{8,12},{9,13},{10,... | collective-permute-start | bytes 1179656 | tf_op jit(solution)/shard_map/ppermute | solution.py:85
  38.4 1.0 %fusion.20.refs_2_ = f32[192,128]{1,0:T(8,128)S(1)} fusion(f32[192,128]{1,0:T(8,128)} %collective-permute-done.1, f32[192,64]{1,0:T(8,128)S(1)} %copy.11, f32[192,64]{1,0:T(8,128)S(1)} %copy.10), kind=kLoop, calls=%fused_computation.39 | loop fusion | flops 49152 | bytes 294912 | tf_op jit(solution)/shard_map/add | solution.py:220
  40.0 8.6 %shard_map.76 = (bf16[2,384,512]{2,1,0:T(8,128)(2,1)S(1)}, f32[384,512]{1,0:T(8,128)S(1)}, f32[384,512]{1,0:T(8,128)S(1)}) custom-call(s32[4]{0:T(128)S(1)} %pad_add_fusion.3.targets_ref, bf16[384,1664]{1,0:T(8,128)(2,1)S(1)} %copy-done.1, bf16[1664,8192]{1,0:T(8,128)(2,1)} %down_ref.9, bf16[384,512]{1,0:T(8,128)(2,1)S(1)} %get-tuple-element.50.refs_0_, ...), custom_call_target="tpu_custom_call" | custom-call | flops 1000000 | bytes 1024 | tf_op jit(solution)/shard_map/pallas_call | solution.py:66
  48.7 1.2 %collective-permute-done.2 = f32[192,128]{1,0:T(8,128)S(1)} collective-permute-done((f32[192,128]{1,0:T(8,128)S(1)}, f32[192,128]{1,0:T(8,128)S(1)}, u32[]{:S(2)}, u32[]{:S(2)}) %collective-permute-start.2) | collective-permute-done | bytes 98336 | tf_op jit(solution)/shard_map/ppermute | solution.py:85
  50.0 1.5 %fusion.10 = (bf16[384,512]{1,0:T(8,128)(2,1)S(1)}, bf16[384,512]{1,0:T(8,128)(2,1)S(1)}) fusion(f32[384,512]{1,0:T(8,128)S(1)} %get-tuple-element.36, bf16[384,512]{1,0:T(8,128)(2,1)S(1)} %collective-permute-done.7, bf16[384,512]{1,0:T(8,128)(2,1)S(1)} %collective-permute-done.6, bf16[2,384,512]{2,1,0:T(8,128)(2,1)} %collective-permute-done.5, ...), kind=kLoop, calls=%fused_computation.15 | loop fusion | flops 1966080 | bytes 3932160 | tf_op jit(solution)/shard_map/convert_element_type | solution.py:192
  52.0 1.6 %collective-permute-start.9 = (f32[192,128]{1,0:T(8,128)S(1)}, f32[192,128]{1,0:T(8,128)S(1)}, u32[]{:S(2)}, u32[]{:S(2)}) collective-permute-start(f32[192,128]{1,0:T(8,128)S(1)} %add.69.refs_2_), channel_id=1, source_target_pairs={{0,2},{1,3},{2,0},{3,1},{4,6},{5,7},{6,4},{7,5},{8,10},{9,11},{10,... | collective-permute-start | bytes 294920 | tf_op jit(solution)/shard_map/ppermute | solution.py:85
  54.0 8.6 %shard_map.77 = (bf16[1,384,512]{2,1,0:T(8,128)(2,1)S(1)}, f32[384,512]{1,0:T(8,128)S(1)}, f32[384,512]{1,0:T(8,128)S(1)}, f32[384,512]{1,0:T(8,128)S(1)}) custom-call(s32[4]{0:T(128)S(1)} %pad_add_fusion.targets_ref, bf16[384,1664]{1,0:T(8,128)(2,1)S(1)} %copy-done.1, bf16[1664,8192]{1,0:T(8,128)(2,1)} %down_ref.9, ...), custom_call_target="tpu_custom_call" | custom-call | flops 1000000 | bytes 1024 | tf_op jit(solution)/shard_map/pallas_call | solution.py:66
  62.7 1.6 %collective-permute-done.9 = f32[192,128]{1,0:T(8,128)S(1)} collective-permute-done((f32[192,128]{1,0:T(8,128)S(1)}, f32[192,128]{1,0:T(8,128)S(1)}, u32[]{:S(2)}, u32[]{:S(2)}) %collective-permute-start.9) | collective-permute-done | bytes 98336 | tf_op jit(solution)/shard_map/ppermute | solution.py:85
  64.3 1.5 %fusion.2 = (bf16[384,512]{1,0:T(8,128)(2,1)S(1)}, bf16[384,512]{1,0:T(8,128)(2,1)S(1)}) fusion(f32[384,512]{1,0:T(8,128)S(1)} %get-tuple-element.41, bf16[2,384,512]{2,1,0:T(8,128)(2,1)} %collective-permute-done.10, bf16[384,512]{1,0:T(8,128)(2,1)S(1)} %collective-permute-done.13, f32[384,512]{1,0:T(8,128)S(1)} %get-tuple-element.43), kind=kLoop, calls=%fused_computation.5 | loop fusion | flops 1572864 | bytes 3538944 | tf_op jit(solution)/shard_map/convert_element_type | solution.py:221
  65.8 1.2 %collective-permute-start.11 = (bf16[384,512]{1,0:T(8,128)(2,1)S(1)}, bf16[384,512]{1,0:T(8,128)(2,1)S(1)}, u32[]{:S(2)}, u32[]{:S(2)}) collective-permute-start(bf16[384,512]{1,0:T(8,128)(2,1)S(1)} %get-tuple-element.45), channel_id=1, source_target_pairs={{0,2},{1,3},{2,0},{3,1},{4,6},{5,7},{6,4},{7,5},{8,10},{9,11},{10,... | collective-permute-start | bytes 1179656 | tf_op jit(solution)/shard_map/ppermute | solution.py:85
  67.0 1.6 %collective-permute-start.14 = (bf16[384,512]{1,0:T(8,128)(2,1)S(1)}, bf16[384,512]{1,0:T(8,128)(2,1)S(1)}, u32[]{:S(2)}, u32[]{:S(2)}) collective-permute-start(bf16[384,512]{1,0:T(8,128)(2,1)S(1)} %get-tuple-element.46), channel_id=1, source_target_pairs={{0,4},{1,5},{2,6},{3,7},{4,0},{5,1},{6,2},{7,3},{8,12},{9,13},{10,... | collective-permute-start | bytes 1179656 | tf_op jit(solution)/shard_map/ppermute | solution.py:85
  68.7 1.3 %collective-permute-done.15 = f32[192,128]{1,0:T(8,128)S(1)} collective-permute-done((f32[192,128]{1,0:T(8,128)S(1)}, f32[192,128]{1,0:T(8,128)S(1)}, u32[]{:S(2)}, u32[]{:S(2)}) %collective-permute-start.15) | collective-permute-done | bytes 98336 | tf_op jit(solution)/shard_map/ppermute | solution.py:85
  70.0 2.8 %shard_map.78 = f32[384,512]{1,0:T(8,128)S(1)} custom-call(s32[32]{0:T(128)S(1)} %copy-done.3, s32[32]{0:T(128)S(1)} %copy-done.4, f32[192,128]{1,0:T(8,128)S(1)} %add.78.packed_ref, bf16[2048,512]{1,0:T(8,128)(2,1)S(1)} %bitcast.59), custom_call_target="tpu_custom_call" | custom-call | flops 1000000 | bytes 1 | tf_op jit(solution)/shard_map/pallas_call | solution.py:144
  73.3 4.1 %collective-permute-done.11 = bf16[384,512]{1,0:T(8,128)(2,1)S(1)} collective-permute-done((bf16[384,512]{1,0:T(8,128)(2,1)S(1)}, bf16[384,512]{1,0:T(8,128)(2,1)S(1)}, u32[]{:S(2)}, u32[]{:S(2)}) %collective-permute-start.11) | collective-permute-done | bytes 393248 | tf_op jit(solution)/shard_map/ppermute | solution.py:85
  77.4 4.2 %collective-permute-done.14 = bf16[384,512]{1,0:T(8,128)(2,1)S(1)} collective-permute-done((bf16[384,512]{1,0:T(8,128)(2,1)S(1)}, bf16[384,512]{1,0:T(8,128)(2,1)S(1)}, u32[]{:S(2)}, u32[]{:S(2)}) %collective-permute-start.14) | collective-permute-done | bytes 393248 | tf_op jit(solution)/shard_map/ppermute | solution.py:85
  81.6 1.1 %fusion.7 = bf16[384,512]{1,0:T(8,128)(2,1)} fusion(f32[384,512]{1,0:T(8,128)S(1)} %shard_map.78, f32[384,512]{1,0:T(8,128)S(1)} %get-tuple-element.38, bf16[384,512]{1,0:T(8,128)(2,1)S(1)} %collective-permute-done.14, bf16[384,512]{1,0:T(8,128)(2,1)S(1)} %collective-permute-done.12, bf16[384,512]{1,0:T(8,128)(2,1)S(1)} %collective-permute-done.11, ...), kind=kLoop, calls=%fused_computation.11 | loop fusion | flops 1966080 | bytes 3538944 | tf_op jit(solution)/shard_map/convert_element_type | solution.py:235
  (46 shorter events, 4.6 us)
Async XLA Ops:
  0.0 1.3 %copy-start = (bf16[384,1664]{1,0:T(8,128)(2,1)S(1)}, bf16[384,1664]{1,0:T(8,128)(2,1)}, u32[]{:S(2)}) copy-start(bf16[384,1664]{1,0:T(8,128)(2,1)} %hidden_ref.9) | copy-start | bytes 3833860
  1.3 3.6 %copy-start.1 = (bf16[384,1664]{1,0:T(8,128)(2,1)S(1)}, bf16[384,1664]{1,0:T(8,128)(2,1)}, u32[]{:S(2)}) copy-start(bf16[384,1664]{1,0:T(8,128)(2,1)} %hidden_ref.9) | copy-start | bytes 3833860
  4.3 8.2 %collective-permute-start = (bf16[1,384,512]{2,1,0:T(8,128)(2,1)S(1)}, bf16[1,384,512]{2,1,0:T(8,128)(2,1)S(1)}, u32[]{:S(2)}, u32[]{:S(2)}) collective-permute-start(bf16[1,384,512]{2,1,0:T(8,128)(2,1)S(1)} %shard_map.73.refs_0_), channel_id=1, source_target_pairs={{0,1},{1,0},{2,3},{3,2},{4,5},{5,4},{6,7},{7,6},{8,9},{9,8},{10,11... | collective-permute-start | bytes 1179656 | tf_op jit(solution)/shard_map/ppermute | solution.py:85
  4.9 7.6 %copy-start.5 = (s32[384]{0:T(512)S(1)}, s32[384]{0:T(512)}, u32[]{:S(2)}) copy-start(s32[384]{0:T(512)} %param.11) | copy-start | bytes 4612
  12.4 22.3 %collective-permute-start.3 = (bf16[2,384,512]{2,1,0:T(8,128)(2,1)}, bf16[2,384,512]{2,1,0:T(8,128)(2,1)}, u32[]{:S(2)}, u32[]{:S(2)}) collective-permute-start(bf16[2,384,512]{2,1,0:T(8,128)(2,1)} %get-tuple-element.30), channel_id=1, source_target_pairs={{0,1},{1,0},{2,3},{3,2},{4,5},{5,4},{6,7},{7,6},{8,9},{9,8},{10,11... | collective-permute-start | bytes 2359304 | tf_op jit(solution)/shard_map/ppermute | solution.py:85
  12.7 22.0 %collective-permute-start.4 = (bf16[384,512]{1,0:T(8,128)(2,1)S(1)}, bf16[384,512]{1,0:T(8,128)(2,1)}, u32[]{:S(2)}, u32[]{:S(2)}) collective-permute-start(bf16[384,512]{1,0:T(8,128)(2,1)S(1)} %fusion.15.refs_0_), channel_id=1, source_target_pairs={{0,2},{1,3},{2,0},{3,1},{4,6},{5,7},{6,4},{7,5},{8,10},{9,11},{10,... | collective-permute-start | bytes 1179656 | tf_op jit(solution)/shard_map/ppermute | solution.py:85
  22.7 12.0 %collective-permute-start.1 = (f32[192,128]{1,0:T(8,128)S(1)}, f32[192,128]{1,0:T(8,128)}, u32[]{:S(2)}, u32[]{:S(2)}) collective-permute-start(f32[192,128]{1,0:T(8,128)S(1)} %pad_maximum_fusion.refs_1_), channel_id=1, source_target_pairs={{0,8},{1,9},{2,10},{3,11},{4,12},{5,13},{6,14},{7,15},{8,0},{9,1},... | collective-permute-start | bytes 294920 | tf_op jit(solution)/shard_map/ppermute | solution.py:85
  34.6 15.3 %collective-permute-start.5 = (bf16[2,384,512]{2,1,0:T(8,128)(2,1)}, bf16[2,384,512]{2,1,0:T(8,128)(2,1)}, u32[]{:S(2)}, u32[]{:S(2)}) collective-permute-start(bf16[2,384,512]{2,1,0:T(8,128)(2,1)} %get-tuple-element.35), channel_id=1, source_target_pairs={{0,1},{1,0},{2,3},{3,2},{4,5},{5,4},{6,7},{7,6},{8,9},{9,8},{10,11... | collective-permute-start | bytes 2359304 | tf_op jit(solution)/shard_map/ppermute | solution.py:85
  36.3 13.7 %collective-permute-start.7 = (bf16[384,512]{1,0:T(8,128)(2,1)S(1)}, bf16[384,512]{1,0:T(8,128)(2,1)S(1)}, u32[]{:S(2)}, u32[]{:S(2)}) collective-permute-start(bf16[384,512]{1,0:T(8,128)(2,1)S(1)} %get-tuple-element.49.refs_1_), channel_id=1, source_target_pairs={{0,4},{1,5},{2,6},{3,7},{4,0},{5,1},{6,2},{7,3},{8,12},{9,13},{10,... | collective-permute-start | bytes 1179656 | tf_op jit(solution)/shard_map/ppermute | solution.py:85
  37.9 12.0 %collective-permute-start.6 = (bf16[384,512]{1,0:T(8,128)(2,1)S(1)}, bf16[384,512]{1,0:T(8,128)(2,1)S(1)}, u32[]{:S(2)}, u32[]{:S(2)}) collective-permute-start(bf16[384,512]{1,0:T(8,128)(2,1)S(1)} %get-tuple-element.50.refs_0_), channel_id=1, source_target_pairs={{0,2},{1,3},{2,0},{3,1},{4,6},{5,7},{6,4},{7,5},{8,10},{9,11},{10,... | collective-permute-start | bytes 1179656 | tf_op jit(solution)/shard_map/ppermute | solution.py:85
  39.4 10.5 %collective-permute-start.2 = (f32[192,128]{1,0:T(8,128)S(1)}, f32[192,128]{1,0:T(8,128)S(1)}, u32[]{:S(2)}, u32[]{:S(2)}) collective-permute-start(f32[192,128]{1,0:T(8,128)S(1)} %fusion.20.refs_2_), channel_id=1, source_target_pairs={{0,4},{1,5},{2,6},{3,7},{4,0},{5,1},{6,2},{7,3},{8,12},{9,13},{10,... | collective-permute-start | bytes 294920 | tf_op jit(solution)/shard_map/ppermute | solution.py:85
  48.6 15.7 %collective-permute-start.10 = (bf16[2,384,512]{2,1,0:T(8,128)(2,1)S(1)}, bf16[2,384,512]{2,1,0:T(8,128)(2,1)}, u32[]{:S(2)}, u32[]{:S(2)}) collective-permute-start(bf16[2,384,512]{2,1,0:T(8,128)(2,1)S(1)} %get-tuple-element.42), channel_id=1, source_target_pairs={{0,1},{1,0},{2,3},{3,2},{4,5},{5,4},{6,7},{7,6},{8,9},{9,8},{10,11... | collective-permute-start | bytes 2359304 | tf_op jit(solution)/shard_map/ppermute | solution.py:85
  51.5 12.9 %collective-permute-start.13 = (bf16[384,512]{1,0:T(8,128)(2,1)S(1)}, bf16[384,512]{1,0:T(8,128)(2,1)S(1)}, u32[]{:S(2)}, u32[]{:S(2)}) collective-permute-start(bf16[384,512]{1,0:T(8,128)(2,1)S(1)} %get-tuple-element.48.refs_0_), channel_id=1, source_target_pairs={{0,2},{1,3},{2,0},{3,1},{4,6},{5,7},{6,4},{7,5},{8,10},{9,11},{10,... | collective-permute-start | bytes 1179656 | tf_op jit(solution)/shard_map/ppermute | solution.py:85
  52.0 12.3 %collective-permute-start.9 = (f32[192,128]{1,0:T(8,128)S(1)}, f32[192,128]{1,0:T(8,128)S(1)}, u32[]{:S(2)}, u32[]{:S(2)}) collective-permute-start(f32[192,128]{1,0:T(8,128)S(1)} %add.69.refs_2_), channel_id=1, source_target_pairs={{0,2},{1,3},{2,0},{3,1},{4,6},{5,7},{6,4},{7,5},{8,10},{9,11},{10,... | collective-permute-start | bytes 294920 | tf_op jit(solution)/shard_map/ppermute | solution.py:85
  53.7 19.6 %collective-permute-start.12 = (bf16[384,512]{1,0:T(8,128)(2,1)S(1)}, bf16[384,512]{1,0:T(8,128)(2,1)S(1)}, u32[]{:S(2)}, u32[]{:S(2)}) collective-permute-start(bf16[384,512]{1,0:T(8,128)(2,1)S(1)} %get-tuple-element.47.refs_1_), channel_id=1, source_target_pairs={{0,8},{1,9},{2,10},{3,11},{4,12},{5,13},{6,14},{7,15},{8,0},{9,1},... | collective-permute-start | bytes 1179656 | tf_op jit(solution)/shard_map/ppermute | solution.py:85
  62.7 7.3 %copy-start.2 = (bf16[32,64,512]{2,1,0:T(8,128)(2,1)S(1)}, bf16[32,64,512]{2,1,0:T(8,128)(2,1)}, u32[]{:S(2)}) copy-start(bf16[32,64,512]{2,1,0:T(8,128)(2,1)} %param.10) | copy-start | bytes 6291460
  62.7 7.3 %copy-start.3 = (s32[32]{0:T(128)S(1)}, s32[32]{0:T(128)}, u32[]{:S(2)}) copy-start(s32[32]{0:T(128)} %first_ref.1) | copy-start | bytes 388
  62.7 7.3 %copy-start.4 = (s32[32]{0:T(128)S(1)}, s32[32]{0:T(128)}, u32[]{:S(2)}) copy-start(s32[32]{0:T(128)} %length_ref.1) | copy-start | bytes 388
  64.3 8.9 %collective-permute-start.8 = (bf16[1,384,512]{2,1,0:T(8,128)(2,1)S(1)}, bf16[1,384,512]{2,1,0:T(8,128)(2,1)S(1)}, u32[]{:S(2)}, u32[]{:S(2)}) collective-permute-start(bf16[1,384,512]{2,1,0:T(8,128)(2,1)S(1)} %get-tuple-element.39), channel_id=1, source_target_pairs={{0,1},{1,0},{2,3},{3,2},{4,5},{5,4},{6,7},{7,6},{8,9},{9,8},{10,11... | collective-permute-start | bytes 1179656 | tf_op jit(solution)/shard_map/ppermute | solution.py:85
  65.8 11.6 %collective-permute-start.11 = (bf16[384,512]{1,0:T(8,128)(2,1)S(1)}, bf16[384,512]{1,0:T(8,128)(2,1)S(1)}, u32[]{:S(2)}, u32[]{:S(2)}) collective-permute-start(bf16[384,512]{1,0:T(8,128)(2,1)S(1)} %get-tuple-element.45), channel_id=1, source_target_pairs={{0,2},{1,3},{2,0},{3,1},{4,6},{5,7},{6,4},{7,5},{8,10},{9,11},{10,... | collective-permute-start | bytes 1179656 | tf_op jit(solution)/shard_map/ppermute | solution.py:85
  67.0 14.6 %collective-permute-start.14 = (bf16[384,512]{1,0:T(8,128)(2,1)S(1)}, bf16[384,512]{1,0:T(8,128)(2,1)S(1)}, u32[]{:S(2)}, u32[]{:S(2)}) collective-permute-start(bf16[384,512]{1,0:T(8,128)(2,1)S(1)} %get-tuple-element.46), channel_id=1, source_target_pairs={{0,4},{1,5},{2,6},{3,7},{4,0},{5,1},{6,2},{7,3},{8,12},{9,13},{10,... | collective-permute-start | bytes 1179656 | tf_op jit(solution)/shard_map/ppermute | solution.py:85
  68.6 1.4 %collective-permute-start.15 = (f32[192,128]{1,0:T(8,128)S(1)}, f32[192,128]{1,0:T(8,128)S(1)}, u32[]{:S(2)}, u32[]{:S(2)}) collective-permute-start(f32[192,128]{1,0:T(8,128)S(1)} %add.77), channel_id=1, source_target_pairs={{0,1},{1,0},{2,3},{3,2},{4,5},{5,4},{6,7},{7,6},{8,9},{9,8},{10,11... | collective-permute-start | bytes 294920 | tf_op jit(solution)/shard_map/ppermute | solution.py:85

commit v6 on v5

--- a/solution.py
+++ b/solution.py
@@ -7,64 +7,60 @@
 from jax.experimental.pallas import tpu as pltpu
 from jax.sharding import PartitionSpec as P
 
-BLOCK = 256
-SLOTS = 3
-PIECES = 2
-VMEM_LIMIT = 40 * 1024 * 1024
+VMEM_LIMIT = 39 * 1024 * 1024
 WINDOW = 128
 TOGETHER = 4
 FLOPS = 1_000_000
 
 
-def product_body(targets_ref, hidden_ref, down_ref, *refs, sent, earlier):
+def product_body(targets_ref, hidden_ref, down_ref, *refs, sent, kept, earlier):
     *result_refs, buffer, arrived = refs[earlier:]
-    width = result_refs[0].shape[-1]
-    block = buffer.shape[2]
-    blocks = width // block
-    steps = [(at, part) for at in range(targets_ref.shape[0]) for part in range(blocks)]
-    slots, pieces = arrived.shape
-    deep = buffer.shape[1] // pieces
-
-    def copies(step):
-        at, part = steps[step]
-        column = pl.multiple_of(targets_ref[at] * width + part * block, block)
-        for piece in range(pieces):
-            rows = pl.ds(piece * deep, deep)
-            yield pltpu.make_async_copy(
-                down_ref.at[rows, pl.ds(column, block)],
-                buffer.at[step % slots, rows],
-                arrived.at[step % slots, piece],
-            )
-
-    for step in range(min(slots - 1, len(steps))):
-        for copy in copies(step):
-            copy.start()
-    for step, (at, part) in enumerate(steps):
-        if step + slots - 1 < len(steps):
-            for copy in copies(step + slots - 1):
-                copy.start()
-        for copy in copies(step):
-            copy.wait()
-        total = jnp.dot(
-            hidden_ref[...], buffer[step % slots], preferred_element_type=jnp.float32
+    width = buffer.shape[2]
+
+    def copy(at):
+        column = pl.multiple_of(targets_ref[at] * width, width)
+        return pltpu.make_async_copy(
+            down_ref.at[:, pl.ds(column, width)], buffer.at[at % 2], arrived.at[at % 2]
         )
-        columns = slice(part * block, (part + 1) * block)
-        if at < sent:
-            result_refs[0][at, :, columns] = total.astype(jnp.bfloat16)
-        else:
-            result_refs[(1 if sent else 0) + at - sent][:, columns] = total
+
+    copy(0).start()
+
+    def step(at, carry):
+        @pl.when(at + 1 < sent + kept)
+        def _():
+            copy(at + 1).start()
+
+        copy(at).wait()
+        total = jnp.dot(hidden_ref[...], buffer[at % 2], preferred_element_type=jnp.float32)
+        if sent:
+
+            @pl.when(at < sent)
+            def _():
+                result_refs[0][jnp.minimum(at, sent - 1)] = total.astype(jnp.bfloat16)
+
+        if kept:
+
+            @pl.when(at >= sent)
+            def _():
+                result_refs[-1][jnp.maximum(at - sent, 0)] = total
+
+        return carry
+
+    lax.fori_loop(0, sent + kept, step, 0)
 
 
 def product(hidden, down_matrix, sent, kept, width, earlier):
     rows, depth = hidden.shape
-    block = min(BLOCK, width)
-    pieces = PIECES if depth % (16 * PIECES) == 0 else 1
     vmem = pl.BlockSpec(memory_space=pltpu.VMEM)
-    out_shape = [jax.ShapeDtypeStruct((rows, width), jnp.float32)] * len(kept)
+    out_shape = []
     if sent:
-        out_shape = [jax.ShapeDtypeStruct((len(sent), rows, width), jnp.bfloat16)] + out_shape
+        out_shape.append(jax.ShapeDtypeStruct((len(sent), rows, width), jnp.bfloat16))
+    if kept:
+        out_shape.append(jax.ShapeDtypeStruct((len(kept), rows, width), jnp.float32))
     results = pl.pallas_call(
-        functools.partial(product_body, sent=len(sent), earlier=len(earlier)),
+        functools.partial(
+            product_body, sent=len(sent), kept=len(kept), earlier=len(earlier)
+        ),
         in_specs=[
             pl.BlockSpec(memory_space=pltpu.SMEM), vmem, pl.BlockSpec(memory_space=pltpu.HBM)
         ]
@@ -72,13 +68,13 @@
         out_specs=[vmem] * len(out_shape),
         out_shape=out_shape,
         scratch_shapes=[
-            pltpu.VMEM((SLOTS, depth, block), jnp.bfloat16),
-            pltpu.SemaphoreType.DMA((SLOTS, pieces)),
+            pltpu.VMEM((2, depth, width), jnp.bfloat16),
+            pltpu.SemaphoreType.DMA((2,)),
         ],
         compiler_params=pltpu.CompilerParams(vmem_limit_bytes=VMEM_LIMIT),
         cost_estimate=pl.CostEstimate(flops=FLOPS, bytes_accessed=1024, transcendentals=0),
     )(jnp.stack(sent + kept), hidden, down_matrix, *earlier)
-    return (results[0], list(results[1:])) if sent else (None, list(results))
+    return (results[0] if sent else None), (results[-1] if kept else None)
 
 
 def swap(value, bit, total):

time: 83.1 us -> 77.3 us (0.930)
  Pallas kernels: 39.7 us -> 29.7 us
  waiting for transfers between devices: 13 us -> 18.8 us
  other arithmetic: 7.55 us -> 6.54 us
    pallas_call x5, Pallas kernels: 36.9 us -> 26.9 us  [product(): pl.pallas_call(functools.partial(product_body, sent=len(sent), kept=len(k...]
    ppermute x16, waiting for transfers between devices: 13 us -> 18.8 us  [swap(): lax.ppermute(value, 'tensor', [(place, place ^ bit) for place in range(to...]
    convert_element_type x2, other arithmetic: 3.01 us -> 1.85 us  [settle(): moving = value.astype(jnp.bfloat16)]
    convert_element_type x2, other arithmetic: 1.6 us -> 2.69 us  [on_device(): (kept_out[unit] + arrived[0].astype(jnp.float32)).astype(jnp.bfloat16)]
    add x3, other arithmetic: 1.01 us -> 0.11 us  [on_device(): packed = packed + moved.astype(jnp.float32)]
  transfers between devices with their start and end apart: 16 -> 16, of which waited for: 6 -> 6; matrix products, arithmetic and copies ran while one was open for 16% -> 15% of each run, Pallas kernels for 44% -> 35%
where the time goes in v6:
time: 77.3 us; the launch traced here: 76.9 us
  Pallas kernels  29.7 us (38%)
  waiting for transfers between devices  18.8 us (24%)
  starting transfers between devices  13.9 us (18%)
  other arithmetic  6.54 us (8%)
  matrix products  5.99 us (8%)
  local copies, waits for them, and re-layouts  1.76 us (2%)
    pallas_call x5, Pallas kernels, product(): pl.pallas_call(functools.partial(product_body, sent=len(sent), kept=len(k...  26.9 us
    ppermute x16, waiting for transfers between devices, swap(): lax.ppermute(value, 'tensor', [(place, place ^ bit) for place in range(to...  18.8 us
    ppermute x16, starting transfers between devices, swap(): lax.ppermute(value, 'tensor', [(place, place ^ bit) for place in range(to...  13.9 us
    unnamed x1, matrix products  5.99 us
    pallas_call x1, Pallas kernels, expand(): pl.pallas_call(expand_body, grid_spec=pltpu.PrefetchScalarGridSpec(num_sc...  2.76 us
    convert_element_type x2, other arithmetic, on_device(): (kept_out[unit] + arrived[0].astype(jnp.float32)).astype(jnp.bfloat16)  2.69 us
    convert_element_type x2, other arithmetic, settle(): moving = value.astype(jnp.bfloat16)  1.85 us
  transfers between devices with their start and end apart: 16, of which 6 were waited for; matrix products, arithmetic and copies ran while one was open for 15% of the time, Pallas kernels for 35%

profile of v6, /device:TPU:0, one launch (start us, length us, event | category | flops | bytes accessed | tf_op | source)
XLA Modules:
  0.0 76.9 jit_solution(7804501659123272829)
XLA Ops:
  0.0 1.3 %copy-done = bf16[384,1664]{1,0:T(8,128)(2,1)S(1)} copy-done((bf16[384,1664]{1,0:T(8,128)(2,1)S(1)}, bf16[384,1664]{1,0:T(8,128)(2,1)}, u32[]{:S(2)}) %copy-start) | copy-done | bytes 1277976
  1.3 2.4 %shard_map.73.refs_0_ = bf16[1,384,512]{2,1,0:T(8,128)(2,1)S(1)} custom-call(s32[1]{0:T(128)} %bitcast.7.targets_ref, bf16[384,1664]{1,0:T(8,128)(2,1)S(1)} %copy-done, bf16[1664,8192]{1,0:T(8,128)(2,1)} %down_ref.9), custom_call_target="tpu_custom_call" | custom-call | flops 1000000 | bytes 1024 | tf_op jit(solution)/shard_map/pallas_call | solution.py:60
  4.4 5.3 %shard_map.74 = (bf16[2,384,512]{2,1,0:T(8,128)(2,1)S(1)}, f32[1,384,512]{2,1,0:T(8,128)S(1)}) custom-call(s32[3]{0:T(128)S(1)} %pad_add_fusion.1.targets_ref, bf16[384,1664]{1,0:T(8,128)(2,1)S(1)} %copy-done.1, bf16[1664,8192]{1,0:T(8,128)(2,1)} %down_ref.9, bf16[1,384,512]{2,1,0:T(8,128)(2,1)S(1)} %shard_map.73.refs_0_), custom_call_target="tpu_custom_call" | custom-call | flops 1000000 | bytes 1024 | tf_op jit(solution)/shard_map/pallas_call | solution.py:60
  10.0 1.1 %fusion.11.refs_0_ = bf16[384,512]{1,0:T(8,128)(2,1)S(1)} fusion(f32[1,384,512]{2,1,0:T(8,128)S(1)} %get-tuple-element.21, bf16[1,384,512]{2,1,0:T(8,128)(2,1)} %collective-permute-done), kind=kLoop, calls=%fused_computation.23 | loop fusion | flops 589824 | bytes 1572864 | tf_op jit(solution)/shard_map/convert_element_type | solution.py:217
  11.1 3.0 %collective-permute-start.4 = (bf16[384,512]{1,0:T(8,128)(2,1)S(1)}, bf16[384,512]{1,0:T(8,128)(2,1)}, u32[]{:S(2)}, u32[]{:S(2)}) collective-permute-start(bf16[384,512]{1,0:T(8,128)(2,1)S(1)} %fusion.11.refs_0_), channel_id=1, source_target_pairs={{0,2},{1,3},{2,0},{3,1},{4,6},{5,7},{6,4},{7,5},{8,10},{9,11},{10,... | collective-permute-start | bytes 1179656 | tf_op jit(solution)/shard_map/ppermute | solution.py:81
  14.2 6.0 %fusion.13 = f32[384,2048]{0,1:S(1)} fusion(bf16[384,1664]{1,0:T(8,128)(2,1)S(1)} %copy-done.1, bf16[1664,2048]{0,1:T(8,128)(2,1)} %bitcast.72), kind=kOutput, calls=%fused_computation.34 | convolution fusion | flops 2617245696 | bytes 11239424
  20.9 2.7 %collective-permute-start.1 = (f32[192,128]{1,0:T(8,128)S(1)}, f32[192,128]{1,0:T(8,128)S(1)}, u32[]{:S(2)}, u32[]{:S(2)}) collective-permute-start(f32[192,128]{1,0:T(8,128)S(1)} %pad_maximum_fusion.refs_1_), channel_id=1, source_target_pairs={{0,8},{1,9},{2,10},{3,11},{4,12},{5,13},{6,14},{7,15},{8,0},{9,1},... | collective-permute-start | bytes 294920 | tf_op jit(solution)/shard_map/ppermute | solution.py:81
  23.6 6.4 %shard_map.75 = (bf16[2,384,512]{2,1,0:T(8,128)(2,1)S(1)}, f32[2,384,512]{2,1,0:T(8,128)S(1)}) custom-call(s32[4]{0:T(128)S(1)} %pad_add_fusion.2.targets_ref, bf16[384,1664]{1,0:T(8,128)(2,1)S(1)} %copy-done.1, bf16[1664,8192]{1,0:T(8,128)(2,1)} %down_ref.9, bf16[384,512]{1,0:T(8,128)(2,1)S(1)} %fusion.11.refs_0_, f32[192,128]{1,0:T(8,128)S(1)} %pad_maximum_fusion.refs_1_), custom_call_target="tpu_custom_call" | custom-call | flops 1000000 | bytes 1024 | tf_op jit(solution)/shard_map/pallas_call | solution.py:60
  30.1 1.5 %fusion.10 = (bf16[384,512]{1,0:T(8,128)(2,1)S(1)}, bf16[384,512]{1,0:T(8,128)(2,1)S(1)}) fusion(bf16[384,512]{1,0:T(8,128)(2,1)} %collective-permute-done.4, f32[2,384,512]{2,1,0:T(8,128)S(1)} %get-tuple-element.23, bf16[2,384,512]{2,1,0:T(8,128)(2,1)} %collective-permute-done.3, f32[384,512]{1,0:T(8,128)S(1)} %slice_bitcast_fusion.2), kind=kLoop, calls=%fused_computation.18 | loop fusion | flops 1572864 | bytes 3538944 | tf_op jit(solution)/shard_map/convert_element_type | solution.py:188
  31.6 1.6 %collective-permute-start.7 = (bf16[384,512]{1,0:T(8,128)(2,1)S(1)}, bf16[384,512]{1,0:T(8,128)(2,1)S(1)}, u32[]{:S(2)}, u32[]{:S(2)}) collective-permute-start(bf16[384,512]{1,0:T(8,128)(2,1)S(1)} %get-tuple-element.41.refs_1_), channel_id=1, source_target_pairs={{0,4},{1,5},{2,6},{3,7},{4,0},{5,1},{6,2},{7,3},{8,12},{9,13},{10,... | collective-permute-start | bytes 1179656 | tf_op jit(solution)/shard_map/ppermute | solution.py:81
  34.4 6.4 %shard_map.76 = (bf16[2,384,512]{2,1,0:T(8,128)(2,1)S(1)}, f32[2,384,512]{2,1,0:T(8,128)S(1)}) custom-call(s32[4]{0:T(128)S(1)} %pad_add_fusion.3.targets_ref, bf16[384,1664]{1,0:T(8,128)(2,1)S(1)} %copy-done.1, bf16[1664,8192]{1,0:T(8,128)(2,1)} %down_ref.9, bf16[384,512]{1,0:T(8,128)(2,1)S(1)} %get-tuple-element.42.refs_0_, ...), custom_call_target="tpu_custom_call" | custom-call | flops 1000000 | bytes 1024 | tf_op jit(solution)/shard_map/pallas_call | solution.py:60
  40.9 4.4 %collective-permute-done.2 = f32[192,128]{1,0:T(8,128)S(1)} collective-permute-done((f32[192,128]{1,0:T(8,128)S(1)}, f32[192,128]{1,0:T(8,128)S(1)}, u32[]{:S(2)}, u32[]{:S(2)}) %collective-permute-start.2) | collective-permute-done | bytes 98336 | tf_op jit(solution)/shard_map/ppermute | solution.py:81
  45.7 0.6 collective-permute-start.13
  46.3 1.6 %collective-permute-start.9 = (f32[192,128]{1,0:T(8,128)S(1)}, f32[192,128]{1,0:T(8,128)S(1)}, u32[]{:S(2)}, u32[]{:S(2)}) collective-permute-start(f32[192,128]{1,0:T(8,128)S(1)} %add.84.refs_2_), channel_id=1, source_target_pairs={{0,2},{1,3},{2,0},{3,1},{4,6},{5,7},{6,4},{7,5},{8,10},{9,11},{10,... | collective-permute-start | bytes 294920 | tf_op jit(solution)/shard_map/ppermute | solution.py:81
  48.2 6.4 %shard_map.77 = (bf16[1,384,512]{2,1,0:T(8,128)(2,1)S(1)}, f32[3,384,512]{2,1,0:T(8,128)S(1)}) custom-call(s32[4]{0:T(128)S(1)} %pad_add_fusion.targets_ref, bf16[384,1664]{1,0:T(8,128)(2,1)S(1)} %copy-done.1, bf16[1664,8192]{1,0:T(8,128)(2,1)} %down_ref.9, bf16[384,512]{1,0:T(8,128)(2,1)S(1)} %get-tuple-element.40.refs_0_, ...), custom_call_target="tpu_custom_call" | custom-call | flops 1000000 | bytes 1024 | tf_op jit(solution)/shard_map/pallas_call | solution.py:60
  54.8 3.7 %collective-permute-done.9 = f32[192,128]{1,0:T(8,128)S(1)} collective-permute-done((f32[192,128]{1,0:T(8,128)S(1)}, f32[192,128]{1,0:T(8,128)S(1)}, u32[]{:S(2)}, u32[]{:S(2)}) %collective-permute-start.9) | collective-permute-done | bytes 98336 | tf_op jit(solution)/shard_map/ppermute | solution.py:81
  58.6 1.6 %fusion = (bf16[384,512]{1,0:T(8,128)(2,1)S(1)}, bf16[384,512]{1,0:T(8,128)(2,1)S(1)}) fusion(f32[384,512]{1,0:T(8,128)S(1)} %slice_bitcast_fusion, bf16[2,384,512]{2,1,0:T(8,128)(2,1)} %collective-permute-done.10, bf16[384,512]{1,0:T(8,128)(2,1)} %collective-permute-done.13, f32[3,384,512]{2,1,0:T(8,128)S(1)} %get-tuple-element.32), kind=kLoop, calls=%fused_computation.2 | loop fusion | flops 1572864 | bytes 3538944 | tf_op jit(solution)/shard_map/convert_element_type | solution.py:217
  60.7 1.6 %collective-permute-start.14 = (bf16[384,512]{1,0:T(8,128)(2,1)S(1)}, bf16[384,512]{1,0:T(8,128)(2,1)S(1)}, u32[]{:S(2)}, u32[]{:S(2)}) collective-permute-start(bf16[384,512]{1,0:T(8,128)(2,1)S(1)} %get-tuple-element.38), channel_id=1, source_target_pairs={{0,4},{1,5},{2,6},{3,7},{4,0},{5,1},{6,2},{7,3},{8,12},{9,13},{10,... | collective-permute-start | bytes 1179656 | tf_op jit(solution)/shard_map/ppermute | solution.py:81
  62.3 1.3 %collective-permute-done.15 = f32[192,128]{1,0:T(8,128)S(1)} collective-permute-done((f32[192,128]{1,0:T(8,128)S(1)}, f32[192,128]{1,0:T(8,128)S(1)}, u32[]{:S(2)}, u32[]{:S(2)}) %collective-permute-start.15) | collective-permute-done | bytes 98336 | tf_op jit(solution)/shard_map/ppermute | solution.py:81
  63.7 2.8 %shard_map.78 = f32[384,512]{1,0:T(8,128)S(1)} custom-call(s32[32]{0:T(128)S(1)} %copy-done.3, s32[32]{0:T(128)S(1)} %copy-done.4, f32[192,128]{1,0:T(8,128)S(1)} %add.95.packed_ref, bf16[2048,512]{1,0:T(8,128)(2,1)S(1)} %bitcast.70), custom_call_target="tpu_custom_call" | custom-call | flops 1000000 | bytes 1 | tf_op jit(solution)/shard_map/pallas_call | solution.py:140
  66.5 1.0 %collective-permute-done.12 = bf16[384,512]{1,0:T(8,128)(2,1)S(1)} collective-permute-done((bf16[384,512]{1,0:T(8,128)(2,1)S(1)}, bf16[384,512]{1,0:T(8,128)(2,1)S(1)}, u32[]{:S(2)}, u32[]{:S(2)}) %collective-permute-start.12) | collective-permute-done | bytes 393248 | tf_op jit(solution)/shard_map/ppermute | solution.py:81
  67.5 2.6 %collective-permute-done.11 = bf16[384,512]{1,0:T(8,128)(2,1)S(1)} collective-permute-done((bf16[384,512]{1,0:T(8,128)(2,1)S(1)}, bf16[384,512]{1,0:T(8,128)(2,1)S(1)}, u32[]{:S(2)}, u32[]{:S(2)}) %collective-permute-start.11) | collective-permute-done | bytes 393248 | tf_op jit(solution)/shard_map/ppermute | solution.py:81
  70.1 5.7 %collective-permute-done.14 = bf16[384,512]{1,0:T(8,128)(2,1)S(1)} collective-permute-done((bf16[384,512]{1,0:T(8,128)(2,1)S(1)}, bf16[384,512]{1,0:T(8,128)(2,1)S(1)}, u32[]{:S(2)}, u32[]{:S(2)}) %collective-permute-start.14) | collective-permute-done | bytes 393248 | tf_op jit(solution)/shard_map/ppermute | solution.py:81
  75.8 1.1 %fusion.7 = bf16[384,512]{1,0:T(8,128)(2,1)} fusion(f32[384,512]{1,0:T(8,128)S(1)} %shard_map.78, bf16[384,512]{1,0:T(8,128)(2,1)S(1)} %collective-permute-done.14, bf16[384,512]{1,0:T(8,128)(2,1)S(1)} %collective-permute-done.12, bf16[384,512]{1,0:T(8,128)(2,1)S(1)} %collective-permute-done.11, bf16[1,384,512]{2,1,0:T(8,128)(2,1)S(1)} %collective-permute-done.8, ...), kind=kLoop, calls=%fused_computation.13 | loop fusion | flops 1966080 | bytes 3538944 | tf_op jit(solution)/shard_map/convert_element_type | solution.py:231
  (49 shorter events, 4.6 us)
Async XLA Ops:
  0.0 1.3 %copy-start = (bf16[384,1664]{1,0:T(8,128)(2,1)S(1)}, bf16[384,1664]{1,0:T(8,128)(2,1)}, u32[]{:S(2)}) copy-start(bf16[384,1664]{1,0:T(8,128)(2,1)} %hidden_ref.9) | copy-start | bytes 3833860
  1.3 3.1 %copy-start.1 = (bf16[384,1664]{1,0:T(8,128)(2,1)S(1)}, bf16[384,1664]{1,0:T(8,128)(2,1)}, u32[]{:S(2)}) copy-start(bf16[384,1664]{1,0:T(8,128)(2,1)} %hidden_ref.9) | copy-start | bytes 3833860
  3.8 6.2 %collective-permute-start = (bf16[1,384,512]{2,1,0:T(8,128)(2,1)S(1)}, bf16[1,384,512]{2,1,0:T(8,128)(2,1)}, u32[]{:S(2)}, u32[]{:S(2)}) collective-permute-start(bf16[1,384,512]{2,1,0:T(8,128)(2,1)S(1)} %shard_map.73.refs_0_), channel_id=1, source_target_pairs={{0,1},{1,0},{2,3},{3,2},{4,5},{5,4},{6,7},{7,6},{8,9},{9,8},{10,11... | collective-permute-start | bytes 1179656 | tf_op jit(solution)/shard_map/ppermute | solution.py:81
  4.4 5.6 %copy-start.5 = (s32[384]{0:T(512)S(1)}, s32[384]{0:T(512)}, u32[]{:S(2)}) copy-start(s32[384]{0:T(512)} %param.11) | copy-start | bytes 4612
  9.7 20.4 %collective-permute-start.3 = (bf16[2,384,512]{2,1,0:T(8,128)(2,1)S(1)}, bf16[2,384,512]{2,1,0:T(8,128)(2,1)}, u32[]{:S(2)}, u32[]{:S(2)}) collective-permute-start(bf16[2,384,512]{2,1,0:T(8,128)(2,1)S(1)} %get-tuple-element.26), channel_id=1, source_target_pairs={{0,1},{1,0},{2,3},{3,2},{4,5},{5,4},{6,7},{7,6},{8,9},{9,8},{10,11... | collective-permute-start | bytes 2359304 | tf_op jit(solution)/shard_map/ppermute | solution.py:81
  11.1 19.0 %collective-permute-start.4 = (bf16[384,512]{1,0:T(8,128)(2,1)S(1)}, bf16[384,512]{1,0:T(8,128)(2,1)}, u32[]{:S(2)}, u32[]{:S(2)}) collective-permute-start(bf16[384,512]{1,0:T(8,128)(2,1)S(1)} %fusion.11.refs_0_), channel_id=1, source_target_pairs={{0,2},{1,3},{2,0},{3,1},{4,6},{5,7},{6,4},{7,5},{8,10},{9,11},{10,... | collective-permute-start | bytes 1179656 | tf_op jit(solution)/shard_map/ppermute | solution.py:81
  20.9 9.2 %collective-permute-start.1 = (f32[192,128]{1,0:T(8,128)S(1)}, f32[192,128]{1,0:T(8,128)S(1)}, u32[]{:S(2)}, u32[]{:S(2)}) collective-permute-start(f32[192,128]{1,0:T(8,128)S(1)} %pad_maximum_fusion.refs_1_), channel_id=1, source_target_pairs={{0,8},{1,9},{2,10},{3,11},{4,12},{5,13},{6,14},{7,15},{8,0},{9,1},... | collective-permute-start | bytes 294920 | tf_op jit(solution)/shard_map/ppermute | solution.py:81
  30.0 15.3 %collective-permute-start.5 = (bf16[2,384,512]{2,1,0:T(8,128)(2,1)S(1)}, bf16[2,384,512]{2,1,0:T(8,128)(2,1)S(1)}, u32[]{:S(2)}, u32[]{:S(2)}) collective-permute-start(bf16[2,384,512]{2,1,0:T(8,128)(2,1)S(1)} %get-tuple-element.30), channel_id=1, source_target_pairs={{0,1},{1,0},{2,3},{3,2},{4,5},{5,4},{6,7},{7,6},{8,9},{9,8},{10,11... | collective-permute-start | bytes 2359304 | tf_op jit(solution)/shard_map/ppermute | solution.py:81
  31.6 13.7 %collective-permute-start.7 = (bf16[384,512]{1,0:T(8,128)(2,1)S(1)}, bf16[384,512]{1,0:T(8,128)(2,1)S(1)}, u32[]{:S(2)}, u32[]{:S(2)}) collective-permute-start(bf16[384,512]{1,0:T(8,128)(2,1)S(1)} %get-tuple-element.41.refs_1_), channel_id=1, source_target_pairs={{0,4},{1,5},{2,6},{3,7},{4,0},{5,1},{6,2},{7,3},{8,12},{9,13},{10,... | collective-permute-start | bytes 1179656 | tf_op jit(solution)/shard_map/ppermute | solution.py:81
  33.3 12.0 %collective-permute-start.6 = (bf16[384,512]{1,0:T(8,128)(2,1)S(1)}, bf16[384,512]{1,0:T(8,128)(2,1)S(1)}, u32[]{:S(2)}, u32[]{:S(2)}) collective-permute-start(bf16[384,512]{1,0:T(8,128)(2,1)S(1)} %get-tuple-element.42.refs_0_), channel_id=1, source_target_pairs={{0,2},{1,3},{2,0},{3,1},{4,6},{5,7},{6,4},{7,5},{8,10},{9,11},{10,... | collective-permute-start | bytes 1179656 | tf_op jit(solution)/shard_map/ppermute | solution.py:81
  33.9 11.4 %collective-permute-start.2 = (f32[192,128]{1,0:T(8,128)S(1)}, f32[192,128]{1,0:T(8,128)S(1)}, u32[]{:S(2)}, u32[]{:S(2)}) collective-permute-start(f32[192,128]{1,0:T(8,128)S(1)} %fusion.16.refs_2_), channel_id=1, source_target_pairs={{0,4},{1,5},{2,6},{3,7},{4,0},{5,1},{6,2},{7,3},{8,12},{9,13},{10,... | collective-permute-start | bytes 294920 | tf_op jit(solution)/shard_map/ppermute | solution.py:81
  40.8 17.8 %collective-permute-start.10 = (bf16[2,384,512]{2,1,0:T(8,128)(2,1)S(1)}, bf16[2,384,512]{2,1,0:T(8,128)(2,1)}, u32[]{:S(2)}, u32[]{:S(2)}) collective-permute-start(bf16[2,384,512]{2,1,0:T(8,128)(2,1)S(1)} %get-tuple-element.35), channel_id=1, source_target_pairs={{0,1},{1,0},{2,3},{3,2},{4,5},{5,4},{6,7},{7,6},{8,9},{9,8},{10,11... | collective-permute-start | bytes 2359304 | tf_op jit(solution)/shard_map/ppermute | solution.py:81
  45.7 12.9 %collective-permute-start.13 = (bf16[384,512]{1,0:T(8,128)(2,1)S(1)}, bf16[384,512]{1,0:T(8,128)(2,1)}, u32[]{:S(2)}, u32[]{:S(2)}) collective-permute-start(bf16[384,512]{1,0:T(8,128)(2,1)S(1)} %get-tuple-element.40.refs_0_), channel_id=1, source_target_pairs={{0,2},{1,3},{2,0},{3,1},{4,6},{5,7},{6,4},{7,5},{8,10},{9,11},{10,... | collective-permute-start | bytes 1179656 | tf_op jit(solution)/shard_map/ppermute | solution.py:81
  46.3 12.2 %collective-permute-start.9 = (f32[192,128]{1,0:T(8,128)S(1)}, f32[192,128]{1,0:T(8,128)S(1)}, u32[]{:S(2)}, u32[]{:S(2)}) collective-permute-start(f32[192,128]{1,0:T(8,128)S(1)} %add.84.refs_2_), channel_id=1, source_target_pairs={{0,2},{1,3},{2,0},{3,1},{4,6},{5,7},{6,4},{7,5},{8,10},{9,11},{10,... | collective-permute-start | bytes 294920 | tf_op jit(solution)/shard_map/ppermute | solution.py:81
  47.9 19.6 %collective-permute-start.12 = (bf16[384,512]{1,0:T(8,128)(2,1)S(1)}, bf16[384,512]{1,0:T(8,128)(2,1)S(1)}, u32[]{:S(2)}, u32[]{:S(2)}) collective-permute-start(bf16[384,512]{1,0:T(8,128)(2,1)S(1)} %get-tuple-element.39.refs_1_), channel_id=1, source_target_pairs={{0,8},{1,9},{2,10},{3,11},{4,12},{5,13},{6,14},{7,15},{8,0},{9,1},... | collective-permute-start | bytes 1179656 | tf_op jit(solution)/shard_map/ppermute | solution.py:81
  54.6 12.9 %collective-permute-start.8 = (bf16[1,384,512]{2,1,0:T(8,128)(2,1)S(1)}, bf16[1,384,512]{2,1,0:T(8,128)(2,1)S(1)}, u32[]{:S(2)}, u32[]{:S(2)}) collective-permute-start(bf16[1,384,512]{2,1,0:T(8,128)(2,1)S(1)} %get-tuple-element.33), channel_id=1, source_target_pairs={{0,1},{1,0},{2,3},{3,2},{4,5},{5,4},{6,7},{7,6},{8,9},{9,8},{10,11... | collective-permute-start | bytes 1179656 | tf_op jit(solution)/shard_map/ppermute | solution.py:81
  54.8 8.9 %copy-start.2 = (bf16[32,64,512]{2,1,0:T(8,128)(2,1)S(1)}, bf16[32,64,512]{2,1,0:T(8,128)(2,1)}, u32[]{:S(2)}) copy-start(bf16[32,64,512]{2,1,0:T(8,128)(2,1)} %param.10) | copy-start | bytes 6291460
  54.8 8.9 %copy-start.3 = (s32[32]{0:T(128)S(1)}, s32[32]{0:T(128)}, u32[]{:S(2)}) copy-start(s32[32]{0:T(128)} %first_ref.1) | copy-start | bytes 388
  54.8 8.9 %copy-start.4 = (s32[32]{0:T(128)S(1)}, s32[32]{0:T(128)}, u32[]{:S(2)}) copy-start(s32[32]{0:T(128)} %length_ref.1) | copy-start | bytes 388
  60.1 10.0 %collective-permute-start.11 = (bf16[384,512]{1,0:T(8,128)(2,1)S(1)}, bf16[384,512]{1,0:T(8,128)(2,1)S(1)}, u32[]{:S(2)}, u32[]{:S(2)}) collective-permute-start(bf16[384,512]{1,0:T(8,128)(2,1)S(1)} %get-tuple-element.37), channel_id=1, source_target_pairs={{0,2},{1,3},{2,0},{3,1},{4,6},{5,7},{6,4},{7,5},{8,10},{9,11},{10,... | collective-permute-start | bytes 1179656 | tf_op jit(solution)/shard_map/ppermute | solution.py:81
  60.7 15.1 %collective-permute-start.14 = (bf16[384,512]{1,0:T(8,128)(2,1)S(1)}, bf16[384,512]{1,0:T(8,128)(2,1)S(1)}, u32[]{:S(2)}, u32[]{:S(2)}) collective-permute-start(bf16[384,512]{1,0:T(8,128)(2,1)S(1)} %get-tuple-element.38), channel_id=1, source_target_pairs={{0,4},{1,5},{2,6},{3,7},{4,0},{5,1},{6,2},{7,3},{8,12},{9,13},{10,... | collective-permute-start | bytes 1179656 | tf_op jit(solution)/shard_map/ppermute | solution.py:81
  62.3 1.4 %collective-permute-start.15 = (f32[192,128]{1,0:T(8,128)S(1)}, f32[192,128]{1,0:T(8,128)S(1)}, u32[]{:S(2)}, u32[]{:S(2)}) collective-permute-start(f32[192,128]{1,0:T(8,128)S(1)} %add.94), channel_id=1, source_target_pairs={{0,1},{1,0},{2,3},{3,2},{4,5},{5,4},{6,7},{7,6},{8,9},{9,8},{10,11... | collective-permute-start | bytes 294920 | tf_op jit(solution)/shard_map/ppermute | solution.py:81

commit v7 on v6

--- a/solution.py
+++ b/solution.py
@@ -7,30 +7,41 @@
 from jax.experimental.pallas import tpu as pltpu
 from jax.sharding import PartitionSpec as P
 
+PIECES = 4
 VMEM_LIMIT = 39 * 1024 * 1024
 WINDOW = 128
 TOGETHER = 4
-FLOPS = 1_000_000
+FLOPS = 10_000_000_000
 
 
 def product_body(targets_ref, hidden_ref, down_ref, *refs, sent, kept, earlier):
     *result_refs, buffer, arrived = refs[earlier:]
     width = buffer.shape[2]
 
-    def copy(at):
+    pieces = arrived.shape[1]
+    deep = buffer.shape[1] // pieces
+
+    def copies(at):
         column = pl.multiple_of(targets_ref[at] * width, width)
-        return pltpu.make_async_copy(
-            down_ref.at[:, pl.ds(column, width)], buffer.at[at % 2], arrived.at[at % 2]
-        )
-
-    copy(0).start()
+        for piece in range(pieces):
+            rows = pl.ds(piece * deep, deep)
+            yield pltpu.make_async_copy(
+                down_ref.at[rows, pl.ds(column, width)],
+                buffer.at[at % 2, rows],
+                arrived.at[at % 2, piece],
+            )
+
+    for copy in copies(0):
+        copy.start()
 
     def step(at, carry):
         @pl.when(at + 1 < sent + kept)
         def _():
-            copy(at + 1).start()
-
-        copy(at).wait()
+            for copy in copies(at + 1):
+                copy.start()
+
+        for copy in copies(at):
+            copy.wait()
         total = jnp.dot(hidden_ref[...], buffer[at % 2], preferred_element_type=jnp.float32)
         if sent:
 
@@ -51,6 +62,7 @@
 
 def product(hidden, down_matrix, sent, kept, width, earlier):
     rows, depth = hidden.shape
+    pieces = PIECES if depth % (16 * PIECES) == 0 else 1
     vmem = pl.BlockSpec(memory_space=pltpu.VMEM)
     out_shape = []
     if sent:
@@ -69,7 +81,7 @@
         out_shape=out_shape,
         scratch_shapes=[
             pltpu.VMEM((2, depth, width), jnp.bfloat16),
-            pltpu.SemaphoreType.DMA((2,)),
+            pltpu.SemaphoreType.DMA((2, pieces)),
         ],
         compiler_params=pltpu.CompilerParams(vmem_limit_bytes=VMEM_LIMIT),
         cost_estimate=pl.CostEstimate(flops=FLOPS, bytes_accessed=1024, transcendentals=0),
@@ -176,23 +188,33 @@
     def home_of(unit):
         return me ^ (unit * 4)
 
-    kept_out, kept_home, crossed, incoming = {}, {}, {}, {}
+    kept_home, crossed, incoming = {}, {}, {}
 
     def settle(unit, arrived):
         value = kept_home[unit] + arrived.astype(jnp.float32) + crossed[unit].astype(jnp.float32)
         for moved in incoming.pop(unit, []):
             value = value + moved.astype(jnp.float32)
-        if not unit:
-            return value
+        return value.astype(jnp.bfloat16) if unit else value
+
+    def send_on(unit, moving):
         bit = unit & -unit
-        moving = value.astype(jnp.bfloat16)
         incoming.setdefault(unit ^ bit, []).append(swap(moving, 4 * bit, total))
         return moving
 
     top = units - 1
-    values, _ = product(hidden, down_matrix, [out_of(top) ^ core], [], width, [])
-    packed, ready = None, [values]
-    steps = [*(4 << at for at in reversed(range(top.bit_length()))), near, core]
+    packed = shrink(hidden, shrink_matrices, row_adapter_index)
+    steps = [near, *(4 << at for at in reversed(range(top.bit_length()))), core]
+
+    def gather(value):
+        nonlocal packed
+        if steps:
+            moved, value = lax.optimization_barrier((swap(packed, steps.pop(0), total), value))
+            packed = packed + moved
+        return value
+
+    values, _ = product(hidden, down_matrix, [out_of(top) ^ core], [], width, [packed])
+    values = gather(values)
+    ready = [values]
     for unit in reversed(range(units)):
         arrived = swap(values, core, total)
         sent, kept = [], [out_of(unit)]
@@ -203,26 +225,19 @@
             kept.append(home_of(unit + 1))
         if not unit:
             kept.append(home_of(0))
-        values, results = product(hidden, down_matrix, sent, kept, width, ready)
-        kept_out[unit] = results[0]
+        values, results = product(hidden, down_matrix, sent, kept, width, ready + [packed])
+        results = gather(results)
         if unit < top:
             kept_home[unit + 1] = results[1]
         if not unit:
             kept_home[0] = results[-1]
-        if packed is not None and steps:
-            moved, kept_out[unit] = lax.optimization_barrier(
-                (swap(packed, steps.pop(0), total), kept_out[unit])
-            )
-            packed = packed + moved.astype(jnp.float32)
-        leaving = (kept_out[unit] + arrived[0].astype(jnp.float32)).astype(jnp.bfloat16)
-        ready = [leaving]
+        ready = []
         if unit < top:
-            ready.append(settle(unit + 1, arrived[1]))
-        if packed is None:
-            late, leaving = lax.optimization_barrier((hidden, leaving))
-            packed = shrink(late, shrink_matrices, row_adapter_index)
+            moving, arrived = lax.optimization_barrier((settle(unit + 1, arrived[1]), arrived))
+            ready.append(send_on(unit + 1, moving))
+        leaving = (results[0] + arrived[0].astype(jnp.float32)).astype(jnp.bfloat16)
+        ready.append(leaving)
         crossed[unit] = swap(leaving, near, total)
-        ready.append(packed)
     kept = [settle(0, swap(values, core, total)[0])]
 
     for bit in steps:

time: 77.3 us -> 75.4 us (0.975)
  other arithmetic: 6.54 us -> 3.81 us
  local copies, waits for them, and re-layouts: 1.76 us -> 0.29 us
  starting transfers between devices: 13.9 us -> 15.3 us
  waiting for transfers between devices: 18.8 us -> 19.7 us
    convert_element_type x4 -> x7, other arithmetic: 4.54 us -> 1.12 us  [the longest x3 0.58 us: settle(): return value.astype(jnp.bfloat16) if unit else value]
    ppermute x16, starting transfers between devices: 13.9 us -> 15.3 us  [swap(): lax.ppermute(value, 'tensor', [(place, place ^ bit) for place in range(to...]
    unnamed x14 -> x10, local copies, waits for them, and re-layouts: 1.52 us -> 0.21 us
    ppermute x16, waiting for transfers between devices: 18.8 us -> 19.7 us  [swap(): lax.ppermute(value, 'tensor', [(place, place ^ bit) for place in range(to...]
  transfers between devices with their start and end apart: 16 -> 16, of which waited for: 6 -> 8; matrix products, arithmetic and copies ran while one was open for 15% -> 2% of each run, Pallas kernels for 35% -> 39%
where the time goes in v7:
time: 75.4 us; the launch traced here: 75 us
  Pallas kernels  29.3 us (39%)
  waiting for transfers between devices  19.7 us (26%)
  starting transfers between devices  15.3 us (20%)
  matrix products  6.37 us (8%)
  other arithmetic  3.81 us (5%)
    pallas_call x5, Pallas kernels, product(): pl.pallas_call(functools.partial(product_body, sent=len(sent), kept=len(k...  26.6 us
    ppermute x16, waiting for transfers between devices, swap(): lax.ppermute(value, 'tensor', [(place, place ^ bit) for place in range(to...  19.7 us
    ppermute x16, starting transfers between devices, swap(): lax.ppermute(value, 'tensor', [(place, place ^ bit) for place in range(to...  15.3 us
    unnamed x1, matrix products  6.37 us
    pallas_call x1, Pallas kernels, expand(): pl.pallas_call(expand_body, grid_spec=pltpu.PrefetchScalarGridSpec(num_sc...  2.76 us
  transfers between devices with their start and end apart: 16, of which 8 were waited for; matrix products, arithmetic and copies ran while one was open for 2% of the time, Pallas kernels for 39%

profile of v7, /device:TPU:0, one launch (start us, length us, event | category | flops | bytes accessed | tf_op | source)
XLA Modules:
  0.0 75.0 jit_solution(1048601706026585211)
XLA Ops:
  0.0 0.7 iota_compare_fusion
  0.7 6.4 %fusion.13 = f32[384,2048]{0,1:S(1)} fusion(bf16[384,1664]{1,0:T(8,128)(2,1)} %hidden_ref.9, bf16[1664,2048]{0,1:T(8,128)(2,1)} %bitcast.57), kind=kOutput, calls=%fused_computation.28 | convolution fusion | flops 2617245696 | bytes 11239424
  7.9 3.0 %collective-permute-start = (f32[192,128]{1,0:T(8,128)S(1)}, f32[192,128]{1,0:T(8,128)S(1)}, u32[]{:S(2)}, u32[]{:S(2)}) collective-permute-start(f32[192,128]{1,0:T(8,128)S(1)} %pad_maximum_fusion.refs_0_), channel_id=1, source_target_pairs={{0,2},{1,3},{2,0},{3,1},{4,6},{5,7},{6,4},{7,5},{8,10},{9,11},{10,... | collective-permute-start | bytes 294920 | tf_op jit(solution)/shard_map/ppermute | solution.py:93
  10.9 2.3 %shard_map.73.refs_0_ = bf16[1,384,512]{2,1,0:T(8,128)(2,1)S(1)} custom-call(s32[1]{0:T(128)} %bitcast.7.targets_ref, bf16[384,1664]{1,0:T(8,128)(2,1)S(1)} %copy-done.1, bf16[1664,8192]{1,0:T(8,128)(2,1)} %down_ref.9, f32[192,128]{1,0:T(8,128)S(1)} %pad_maximum_fusion.refs_0_), custom_call_target="tpu_custom_call" | custom-call | flops 10000000000 | bytes 1024 | tf_op jit(solution)/shard_map/pallas_call | solution.py:72
  13.8 3.0 %collective-permute-start.1 = (f32[192,128]{1,0:T(8,128)S(1)}, f32[192,128]{1,0:T(8,128)S(1)}, u32[]{:S(2)}, u32[]{:S(2)}) collective-permute-start(f32[192,128]{1,0:T(8,128)S(1)} %fusion.16.refs_1_), channel_id=1, source_target_pairs={{0,8},{1,9},{2,10},{3,11},{4,12},{5,13},{6,14},{7,15},{8,0},{9,1},... | collective-permute-start | bytes 294920 | tf_op jit(solution)/shard_map/ppermute | solution.py:93
  16.8 5.3 %shard_map.74 = (bf16[2,384,512]{2,1,0:T(8,128)(2,1)S(1)}, f32[1,384,512]{2,1,0:T(8,128)S(1)}) custom-call(s32[3]{0:T(128)S(1)} %pad_add_fusion.1.targets_ref, bf16[384,1664]{1,0:T(8,128)(2,1)S(1)} %copy-done.1, bf16[1664,8192]{1,0:T(8,128)(2,1)} %down_ref.9, bf16[1,384,512]{2,1,0:T(8,128)(2,1)S(1)} %shard_map.73.refs_0_, f32[192,128]{1,0:T(8,128)S(1)} %fusion.16.refs_1_), custom_call_target="tpu_custom_call" | custom-call | flops 10000000000 | bytes 1024 | tf_op jit(solution)/shard_map/pallas_call | solution.py:72
  22.0 0.6 collective-permute-start.5
  22.6 1.6 %collective-permute-start.2 = (f32[192,128]{1,0:T(8,128)S(1)}, f32[192,128]{1,0:T(8,128)S(1)}, u32[]{:S(2)}, u32[]{:S(2)}) collective-permute-start(f32[192,128]{1,0:T(8,128)S(1)} %add.77.refs_1_), channel_id=1, source_target_pairs={{0,4},{1,5},{2,6},{3,7},{4,0},{5,1},{6,2},{7,3},{8,12},{9,13},{10,... | collective-permute-start | bytes 294920 | tf_op jit(solution)/shard_map/ppermute | solution.py:93
  24.4 1.6 %collective-permute-start.6 = (bf16[384,512]{1,0:T(8,128)(2,1)S(1)}, bf16[384,512]{1,0:T(8,128)(2,1)S(1)}, u32[]{:S(2)}, u32[]{:S(2)}) collective-permute-start(bf16[384,512]{1,0:T(8,128)(2,1)S(1)} %fusion.8.refs_0_), channel_id=1, source_target_pairs={{0,2},{1,3},{2,0},{3,1},{4,6},{5,7},{6,4},{7,5},{8,10},{9,11},{10,... | collective-permute-start | bytes 1179656 | tf_op jit(solution)/shard_map/ppermute | solution.py:93
  26.0 6.3 %shard_map.75 = (bf16[2,384,512]{2,1,0:T(8,128)(2,1)S(1)}, f32[2,384,512]{2,1,0:T(8,128)S(1)}) custom-call(s32[4]{0:T(128)S(1)} %pad_add_fusion.2.targets_ref, bf16[384,1664]{1,0:T(8,128)(2,1)S(1)} %copy-done.1, bf16[1664,8192]{1,0:T(8,128)(2,1)} %down_ref.9, bf16[384,512]{1,0:T(8,128)(2,1)S(1)} %fusion.8.refs_0_, f32[192,128]{1,0:T(8,128)S(1)} %add.77.refs_1_), custom_call_target="tpu_custom_call" | custom-call | flops 10000000000 | bytes 1024 | tf_op jit(solution)/shard_map/pallas_call | solution.py:72
  32.9 2.3 %collective-permute-done.6 = bf16[384,512]{1,0:T(8,128)(2,1)S(1)} collective-permute-done((bf16[384,512]{1,0:T(8,128)(2,1)S(1)}, bf16[384,512]{1,0:T(8,128)(2,1)S(1)}, u32[]{:S(2)}, u32[]{:S(2)}) %collective-permute-start.6) | collective-permute-done | bytes 393248 | tf_op jit(solution)/shard_map/ppermute | solution.py:93
  35.6 1.6 %collective-permute-start.8 = (bf16[384,512]{1,0:T(8,128)(2,1)S(1)}, bf16[384,512]{1,0:T(8,128)(2,1)S(1)}, u32[]{:S(2)}, u32[]{:S(2)}) collective-permute-start(bf16[384,512]{1,0:T(8,128)(2,1)S(1)} %fusion.9.refs_1_), channel_id=1, source_target_pairs={{0,2},{1,3},{2,0},{3,1},{4,6},{5,7},{6,4},{7,5},{8,10},{9,11},{10,... | collective-permute-start | bytes 1179656 | tf_op jit(solution)/shard_map/ppermute | solution.py:93
  37.6 6.3 %shard_map.76 = (bf16[2,384,512]{2,1,0:T(8,128)(2,1)S(1)}, f32[2,384,512]{2,1,0:T(8,128)S(1)}) custom-call(s32[4]{0:T(128)S(1)} %pad_add_fusion.3.targets_ref, bf16[384,1664]{1,0:T(8,128)(2,1)S(1)} %copy-done.1, bf16[1664,8192]{1,0:T(8,128)(2,1)} %down_ref.9, bf16[384,512]{1,0:T(8,128)(2,1)S(1)} %fusion.7.refs_0_, bf16[384,512]{1,0:T(8,128)(2,1)S(1)} %fusion.9.refs_1_, ...), custom_call_target="tpu_custom_call" | custom-call | flops 10000000000 | bytes 1024 | tf_op jit(solution)/shard_map/pallas_call | solution.py:72
  44.0 1.5 %collective-permute-done.8 = bf16[384,512]{1,0:T(8,128)(2,1)S(1)} collective-permute-done((bf16[384,512]{1,0:T(8,128)(2,1)S(1)}, bf16[384,512]{1,0:T(8,128)(2,1)S(1)}, u32[]{:S(2)}, u32[]{:S(2)}) %collective-permute-start.8) | collective-permute-done | bytes 393248 | tf_op jit(solution)/shard_map/ppermute | solution.py:93
  45.5 1.2 %collective-permute-done.9 = bf16[384,512]{1,0:T(8,128)(2,1)S(1)} collective-permute-done((bf16[384,512]{1,0:T(8,128)(2,1)S(1)}, bf16[384,512]{1,0:T(8,128)(2,1)S(1)}, u32[]{:S(2)}, u32[]{:S(2)}) %collective-permute-start.9) | collective-permute-done | bytes 393248 | tf_op jit(solution)/shard_map/ppermute | solution.py:93
  47.1 0.6 collective-permute-start.12
  47.7 6.3 %shard_map.77 = (bf16[1,384,512]{2,1,0:T(8,128)(2,1)S(1)}, f32[3,384,512]{2,1,0:T(8,128)S(1)}) custom-call(s32[4]{0:T(128)S(1)} %pad_add_fusion.targets_ref, bf16[384,1664]{1,0:T(8,128)(2,1)S(1)} %copy-done.1, bf16[1664,8192]{1,0:T(8,128)(2,1)} %down_ref.9, bf16[384,512]{1,0:T(8,128)(2,1)S(1)} %fusion.6.refs_0_, bf16[384,512]{1,0:T(8,128)(2,1)S(1)} %fusion.10.refs_1_, ...), custom_call_target="tpu_custom_call" | custom-call | flops 10000000000 | bytes 1024 | tf_op jit(solution)/shard_map/pallas_call | solution.py:72
  54.1 1.9 %collective-permute-done.12 = bf16[384,512]{1,0:T(8,128)(2,1)S(1)} collective-permute-done((bf16[384,512]{1,0:T(8,128)(2,1)S(1)}, bf16[384,512]{1,0:T(8,128)(2,1)S(1)}, u32[]{:S(2)}, u32[]{:S(2)}) %collective-permute-start.12) | collective-permute-done | bytes 393248 | tf_op jit(solution)/shard_map/ppermute | solution.py:93
  56.3 0.6 collective-permute-start.13
  56.9 1.6 %collective-permute-start.15 = (bf16[384,512]{1,0:T(8,128)(2,1)S(1)}, bf16[384,512]{1,0:T(8,128)(2,1)S(1)}, u32[]{:S(2)}, u32[]{:S(2)}) collective-permute-start(bf16[384,512]{1,0:T(8,128)(2,1)S(1)} %fusion), channel_id=1, source_target_pairs={{0,4},{1,5},{2,6},{3,7},{4,0},{5,1},{6,2},{7,3},{8,12},{9,13},{10,... | collective-permute-start | bytes 1179656 | tf_op jit(solution)/shard_map/ppermute | solution.py:93
  58.5 2.8 %shard_map.78 = f32[384,512]{1,0:T(8,128)S(1)} custom-call(s32[32]{0:T(128)S(1)} %copy-done.2, s32[32]{0:T(128)S(1)} %copy-done.3, f32[192,128]{1,0:T(8,128)S(1)} %add.89.refs_2_.packed_ref, bf16[2048,512]{1,0:T(8,128)(2,1)S(1)} %bitcast.55), custom_call_target="tpu_custom_call" | custom-call | flops 10000000000 | bytes 1 | tf_op jit(solution)/shard_map/pallas_call | solution.py:152
  61.3 4.4 %collective-permute-done.14 = bf16[384,512]{1,0:T(8,128)(2,1)S(1)} collective-permute-done((bf16[384,512]{1,0:T(8,128)(2,1)S(1)}, bf16[384,512]{1,0:T(8,128)(2,1)S(1)}, u32[]{:S(2)}, u32[]{:S(2)}) %collective-permute-start.14) | collective-permute-done | bytes 393248 | tf_op jit(solution)/shard_map/ppermute | solution.py:93
  66.1 7.9 %collective-permute-done.15 = bf16[384,512]{1,0:T(8,128)(2,1)S(1)} collective-permute-done((bf16[384,512]{1,0:T(8,128)(2,1)S(1)}, bf16[384,512]{1,0:T(8,128)(2,1)S(1)}, u32[]{:S(2)}, u32[]{:S(2)}) %collective-permute-start.15) | collective-permute-done | bytes 393248 | tf_op jit(solution)/shard_map/ppermute | solution.py:93
  74.0 1.1 %fusion.4 = bf16[384,512]{1,0:T(8,128)(2,1)} fusion(f32[384,512]{1,0:T(8,128)S(1)} %shard_map.78, bf16[384,512]{1,0:T(8,128)(2,1)S(1)} %collective-permute-done.15, bf16[384,512]{1,0:T(8,128)(2,1)S(1)} %collective-permute-done.14, bf16[384,512]{1,0:T(8,128)(2,1)S(1)} %collective-permute-done.13, bf16[1,384,512]{2,1,0:T(8,128)(2,1)S(1)} %collective-permute-done.10, ...), kind=kLoop, calls=%fused_computation.7 | loop fusion | flops 1966080 | bytes 3538944 | tf_op jit(solution)/shard_map/convert_element_type | solution.py:246
  (45 shorter events, 4.1 us)
Async XLA Ops:
  7.1 3.8 %copy-start.1 = (bf16[384,1664]{1,0:T(8,128)(2,1)S(1)}, bf16[384,1664]{1,0:T(8,128)(2,1)}, u32[]{:S(2)}) copy-start(bf16[384,1664]{1,0:T(8,128)(2,1)} %hidden_ref.9) | copy-start | bytes 3833860
  7.9 5.8 %collective-permute-start = (f32[192,128]{1,0:T(8,128)S(1)}, f32[192,128]{1,0:T(8,128)S(1)}, u32[]{:S(2)}, u32[]{:S(2)}) collective-permute-start(f32[192,128]{1,0:T(8,128)S(1)} %pad_maximum_fusion.refs_0_), channel_id=1, source_target_pairs={{0,2},{1,3},{2,0},{3,1},{4,6},{5,7},{6,4},{7,5},{8,10},{9,11},{10,... | collective-permute-start | bytes 294920 | tf_op jit(solution)/shard_map/ppermute | solution.py:93
  13.8 8.8 %collective-permute-start.1 = (f32[192,128]{1,0:T(8,128)S(1)}, f32[192,128]{1,0:T(8,128)S(1)}, u32[]{:S(2)}, u32[]{:S(2)}) collective-permute-start(f32[192,128]{1,0:T(8,128)S(1)} %fusion.16.refs_1_), channel_id=1, source_target_pairs={{0,8},{1,9},{2,10},{3,11},{4,12},{5,13},{6,14},{7,15},{8,0},{9,1},... | collective-permute-start | bytes 294920 | tf_op jit(solution)/shard_map/ppermute | solution.py:93
  16.8 7.5 %collective-permute-start.3 = (bf16[1,384,512]{2,1,0:T(8,128)(2,1)S(1)}, bf16[1,384,512]{2,1,0:T(8,128)(2,1)S(1)}, u32[]{:S(2)}, u32[]{:S(2)}) collective-permute-start(bf16[1,384,512]{2,1,0:T(8,128)(2,1)S(1)} %shard_map.73.refs_0_), channel_id=1, source_target_pairs={{0,1},{1,0},{2,3},{3,2},{4,5},{5,4},{6,7},{7,6},{8,9},{9,8},{10,11... | collective-permute-start | bytes 1179656 | tf_op jit(solution)/shard_map/ppermute | solution.py:93
  22.0 13.2 %collective-permute-start.5 = (bf16[2,384,512]{2,1,0:T(8,128)(2,1)S(1)}, bf16[2,384,512]{2,1,0:T(8,128)(2,1)S(1)}, u32[]{:S(2)}, u32[]{:S(2)}) collective-permute-start(bf16[2,384,512]{2,1,0:T(8,128)(2,1)S(1)} %get-tuple-element.35), channel_id=1, source_target_pairs={{0,1},{1,0},{2,3},{3,2},{4,5},{5,4},{6,7},{7,6},{8,9},{9,8},{10,11... | collective-permute-start | bytes 2359304 | tf_op jit(solution)/shard_map/ppermute | solution.py:93
  22.6 9.7 %collective-permute-start.2 = (f32[192,128]{1,0:T(8,128)S(1)}, f32[192,128]{1,0:T(8,128)S(1)}, u32[]{:S(2)}, u32[]{:S(2)}) collective-permute-start(f32[192,128]{1,0:T(8,128)S(1)} %add.77.refs_1_), channel_id=1, source_target_pairs={{0,4},{1,5},{2,6},{3,7},{4,0},{5,1},{6,2},{7,3},{8,12},{9,13},{10,... | collective-permute-start | bytes 294920 | tf_op jit(solution)/shard_map/ppermute | solution.py:93
  24.4 10.8 %collective-permute-start.6 = (bf16[384,512]{1,0:T(8,128)(2,1)S(1)}, bf16[384,512]{1,0:T(8,128)(2,1)S(1)}, u32[]{:S(2)}, u32[]{:S(2)}) collective-permute-start(bf16[384,512]{1,0:T(8,128)(2,1)S(1)} %fusion.8.refs_0_), channel_id=1, source_target_pairs={{0,2},{1,3},{2,0},{3,1},{4,6},{5,7},{6,4},{7,5},{8,10},{9,11},{10,... | collective-permute-start | bytes 1179656 | tf_op jit(solution)/shard_map/ppermute | solution.py:93
  32.3 11.6 %collective-permute-start.4 = (f32[192,128]{1,0:T(8,128)S(1)}, f32[192,128]{1,0:T(8,128)S(1)}, u32[]{:S(2)}, u32[]{:S(2)}) collective-permute-start(f32[192,128]{1,0:T(8,128)S(1)} %add.79.refs_2_), channel_id=1, source_target_pairs={{0,1},{1,0},{2,3},{3,2},{4,5},{5,4},{6,7},{7,6},{8,9},{9,8},{10,11... | collective-permute-start | bytes 294920 | tf_op jit(solution)/shard_map/ppermute | solution.py:93
  32.4 14.3 %collective-permute-start.7 = (bf16[2,384,512]{2,1,0:T(8,128)(2,1)S(1)}, bf16[2,384,512]{2,1,0:T(8,128)(2,1)S(1)}, u32[]{:S(2)}, u32[]{:S(2)}) collective-permute-start(bf16[2,384,512]{2,1,0:T(8,128)(2,1)S(1)} %get-tuple-element.40), channel_id=1, source_target_pairs={{0,1},{1,0},{2,3},{3,2},{4,5},{5,4},{6,7},{7,6},{8,9},{9,8},{10,11... | collective-permute-start | bytes 2359304 | tf_op jit(solution)/shard_map/ppermute | solution.py:93
  35.6 9.9 %collective-permute-start.8 = (bf16[384,512]{1,0:T(8,128)(2,1)S(1)}, bf16[384,512]{1,0:T(8,128)(2,1)S(1)}, u32[]{:S(2)}, u32[]{:S(2)}) collective-permute-start(bf16[384,512]{1,0:T(8,128)(2,1)S(1)} %fusion.9.refs_1_), channel_id=1, source_target_pairs={{0,2},{1,3},{2,0},{3,1},{4,6},{5,7},{6,4},{7,5},{8,10},{9,11},{10,... | collective-permute-start | bytes 1179656 | tf_op jit(solution)/shard_map/ppermute | solution.py:93
  37.2 9.6 %collective-permute-start.9 = (bf16[384,512]{1,0:T(8,128)(2,1)S(1)}, bf16[384,512]{1,0:T(8,128)(2,1)S(1)}, u32[]{:S(2)}, u32[]{:S(2)}) collective-permute-start(bf16[384,512]{1,0:T(8,128)(2,1)S(1)} %fusion.7.refs_0_), channel_id=1, source_target_pairs={{0,4},{1,5},{2,6},{3,7},{4,0},{5,1},{6,2},{7,3},{8,12},{9,13},{10,... | collective-permute-start | bytes 1179656 | tf_op jit(solution)/shard_map/ppermute | solution.py:93
  44.0 12.0 %collective-permute-start.11 = (bf16[2,384,512]{2,1,0:T(8,128)(2,1)S(1)}, bf16[2,384,512]{2,1,0:T(8,128)(2,1)S(1)}, u32[]{:S(2)}, u32[]{:S(2)}) collective-permute-start(bf16[2,384,512]{2,1,0:T(8,128)(2,1)S(1)} %get-tuple-element.46), channel_id=1, source_target_pairs={{0,1},{1,0},{2,3},{3,2},{4,5},{5,4},{6,7},{7,6},{8,9},{9,8},{10,11... | collective-permute-start | bytes 2359304 | tf_op jit(solution)/shard_map/ppermute | solution.py:93
  47.1 8.9 %collective-permute-start.12 = (bf16[384,512]{1,0:T(8,128)(2,1)S(1)}, bf16[384,512]{1,0:T(8,128)(2,1)S(1)}, u32[]{:S(2)}, u32[]{:S(2)}) collective-permute-start(bf16[384,512]{1,0:T(8,128)(2,1)S(1)} %fusion.10.refs_1_), channel_id=1, source_target_pairs={{0,2},{1,3},{2,0},{3,1},{4,6},{5,7},{6,4},{7,5},{8,10},{9,11},{10,... | collective-permute-start | bytes 1179656 | tf_op jit(solution)/shard_map/ppermute | solution.py:93
  47.7 18.0 %collective-permute-start.14 = (bf16[384,512]{1,0:T(8,128)(2,1)S(1)}, bf16[384,512]{1,0:T(8,128)(2,1)S(1)}, u32[]{:S(2)}, u32[]{:S(2)}) collective-permute-start(bf16[384,512]{1,0:T(8,128)(2,1)S(1)} %fusion.6.refs_0_), channel_id=1, source_target_pairs={{0,8},{1,9},{2,10},{3,11},{4,12},{5,13},{6,14},{7,15},{8,0},{9,1},... | collective-permute-start | bytes 1179656 | tf_op jit(solution)/shard_map/ppermute | solution.py:93
  54.0 4.4 %copy-start = (bf16[32,64,512]{2,1,0:T(8,128)(2,1)S(1)}, bf16[32,64,512]{2,1,0:T(8,128)(2,1)}, u32[]{:S(2)}) copy-start(bf16[32,64,512]{2,1,0:T(8,128)(2,1)} %param.10) | copy-start | bytes 6291460
  54.0 4.4 %copy-start.2 = (s32[32]{0:T(128)S(1)}, s32[32]{0:T(128)}, u32[]{:S(2)}) copy-start(s32[32]{0:T(128)} %first_ref.1) | copy-start | bytes 388
  54.1 4.4 %copy-start.3 = (s32[32]{0:T(128)S(1)}, s32[32]{0:T(128)}, u32[]{:S(2)}) copy-start(s32[32]{0:T(128)} %length_ref.1) | copy-start | bytes 388
  54.1 7.2 %collective-permute-start.10 = (bf16[1,384,512]{2,1,0:T(8,128)(2,1)S(1)}, bf16[1,384,512]{2,1,0:T(8,128)(2,1)S(1)}, u32[]{:S(2)}, u32[]{:S(2)}) collective-permute-start(bf16[1,384,512]{2,1,0:T(8,128)(2,1)S(1)} %get-tuple-element.45), channel_id=1, source_target_pairs={{0,1},{1,0},{2,3},{3,2},{4,5},{5,4},{6,7},{7,6},{8,9},{9,8},{10,11... | collective-permute-start | bytes 1179656 | tf_op jit(solution)/shard_map/ppermute | solution.py:93
  56.3 9.7 %collective-permute-start.13 = (bf16[384,512]{1,0:T(8,128)(2,1)S(1)}, bf16[384,512]{1,0:T(8,128)(2,1)S(1)}, u32[]{:S(2)}, u32[]{:S(2)}) collective-permute-start(bf16[384,512]{1,0:T(8,128)(2,1)S(1)} %fusion.11), channel_id=1, source_target_pairs={{0,2},{1,3},{2,0},{3,1},{4,6},{5,7},{6,4},{7,5},{8,10},{9,11},{10,... | collective-permute-start | bytes 1179656 | tf_op jit(solution)/shard_map/ppermute | solution.py:93
  56.9 17.1 %collective-permute-start.15 = (bf16[384,512]{1,0:T(8,128)(2,1)S(1)}, bf16[384,512]{1,0:T(8,128)(2,1)S(1)}, u32[]{:S(2)}, u32[]{:S(2)}) collective-permute-start(bf16[384,512]{1,0:T(8,128)(2,1)S(1)} %fusion), channel_id=1, source_target_pairs={{0,4},{1,5},{2,6},{3,7},{4,0},{5,1},{6,2},{7,3},{8,12},{9,13},{10,... | collective-permute-start | bytes 1179656 | tf_op jit(solution)/shard_map/ppermute | solution.py:93

commit v8 on v7

--- a/solution.py
+++ b/solution.py
@@ -12,6 +12,7 @@
 WINDOW = 128
 TOGETHER = 4
 FLOPS = 10_000_000_000
+EXPAND_FLOPS = 1_000_000
 
 
 def product_body(targets_ref, hidden_ref, down_ref, *refs, sent, kept, earlier):
@@ -93,6 +94,23 @@
     return lax.ppermute(value, "tensor", [(place, place ^ bit) for place in range(total)])
 
 
+def attach(value, packed):
+    high = packed.astype(jnp.bfloat16)
+    low = (packed - high.astype(jnp.float32)).astype(jnp.bfloat16)
+    both = jnp.concatenate([high, low])
+    pieces = value.shape[1] // both.shape[1]
+    return jnp.concatenate([value, jnp.concatenate(jnp.split(both, pieces), axis=1)])
+
+
+def detach(value, packed):
+    rows, columns = packed.shape
+    pieces = value.shape[1] // columns
+    below = 2 * rows // pieces
+    above = value.shape[0] - below
+    both = jnp.concatenate(jnp.split(value[above:], pieces, axis=1)).astype(jnp.float32)
+    return value[:above], both[:rows] + both[rows:]
+
+
 def for_each_window(first_ref, length_ref, group, rows, body):
     window = min(WINDOW, rows)
     adapters = [group * TOGETHER + at for at in range(TOGETHER)]
@@ -163,7 +181,7 @@
         ),
         out_shape=jax.ShapeDtypeStruct((rows, width), jnp.float32),
         compiler_params=pltpu.CompilerParams(vmem_limit_bytes=VMEM_LIMIT),
-        cost_estimate=pl.CostEstimate(flops=FLOPS, bytes_accessed=1, transcendentals=0),
+        cost_estimate=pl.CostEstimate(flops=EXPAND_FLOPS, bytes_accessed=1, transcendentals=0),
     )(segment_first_row, segment_length, packed, table)
 
 
@@ -190,30 +208,32 @@
 
     kept_home, crossed, incoming = {}, {}, {}
 
+    packed, steps = None, [*(4 << at for at in reversed(range((units - 1).bit_length()))), near, core]
+
+    def send(value, bit, carry):
+        nonlocal packed
+        if not carry or packed is None or steps[:1] != [bit]:
+            return swap(value, bit, total), None
+        steps.pop(0)
+        own, packed = packed, None
+        arrived, shrinks = detach(swap(attach(value, own), bit, total), own)
+        return arrived, own + shrinks
+
     def settle(unit, arrived):
+        nonlocal packed
         value = kept_home[unit] + arrived.astype(jnp.float32) + crossed[unit].astype(jnp.float32)
-        for moved in incoming.pop(unit, []):
+        for moved, shrinks in incoming.pop(unit, []):
             value = value + moved.astype(jnp.float32)
-        return value.astype(jnp.bfloat16) if unit else value
-
-    def send_on(unit, moving):
+            packed = packed if shrinks is None else shrinks
+        if not unit:
+            return value
         bit = unit & -unit
-        incoming.setdefault(unit ^ bit, []).append(swap(moving, 4 * bit, total))
+        moving = value.astype(jnp.bfloat16)
+        incoming.setdefault(unit ^ bit, []).append(send(moving, 4 * bit, unit == top))
         return moving
 
     top = units - 1
-    packed = shrink(hidden, shrink_matrices, row_adapter_index)
-    steps = [near, *(4 << at for at in reversed(range(top.bit_length()))), core]
-
-    def gather(value):
-        nonlocal packed
-        if steps:
-            moved, value = lax.optimization_barrier((swap(packed, steps.pop(0), total), value))
-            packed = packed + moved
-        return value
-
-    values, _ = product(hidden, down_matrix, [out_of(top) ^ core], [], width, [packed])
-    values = gather(values)
+    values, _ = product(hidden, down_matrix, [out_of(top) ^ core], [], width, [])
     ready = [values]
     for unit in reversed(range(units)):
         arrived = swap(values, core, total)
@@ -225,18 +245,24 @@
             kept.append(home_of(unit + 1))
         if not unit:
             kept.append(home_of(0))
-        values, results = product(hidden, down_matrix, sent, kept, width, ready + [packed])
-        results = gather(results)
+        values, results = product(hidden, down_matrix, sent, kept, width, ready)
+        if packed is not None and steps and steps[0] != core:
+            moved, results = lax.optimization_barrier((swap(packed, steps.pop(0), total), results))
+            packed = packed + moved
         if unit < top:
             kept_home[unit + 1] = results[1]
         if not unit:
             kept_home[0] = results[-1]
-        ready = []
+        leaving = (results[0] + arrived[0].astype(jnp.float32)).astype(jnp.bfloat16)
+        ready = [leaving]
         if unit < top:
-            moving, arrived = lax.optimization_barrier((settle(unit + 1, arrived[1]), arrived))
-            ready.append(send_on(unit + 1, moving))
-        leaving = (results[0] + arrived[0].astype(jnp.float32)).astype(jnp.bfloat16)
-        ready.append(leaving)
+            leaving, arrived = lax.optimization_barrier((leaving, arrived))
+            ready.append(settle(unit + 1, arrived[1]))
+        if unit == top:
+            late, ready[-1] = lax.optimization_barrier((hidden, ready[-1]))
+            packed = shrink(late, shrink_matrices, row_adapter_index)
+        if packed is not None:
+            ready.append(packed)
         crossed[unit] = swap(leaving, near, total)
     kept = [settle(0, swap(values, core, total)[0])]
 

time: 75.4 us -> 76 us (level)
  waiting for transfers between devices: 19.7 us -> 17.4 us
  other arithmetic: 3.81 us -> 6.08 us
  local copies, waits for them, and re-layouts: 0.29 us -> 1.62 us
    ppermute x16 -> x15, waiting for transfers between devices: 19.7 us -> 17.4 us  [swap(): lax.ppermute(value, 'tensor', [(place, place ^ bit) for place in range(to...]
    convert_element_type x4, other arithmetic: 0.54 us -> 2.5 us  [on_device(): leaving = (results[0] + arrived[0].astype(jnp.float32)).astype(jnp.bfloat16)]
    unnamed x10 -> x14, local copies, waits for them, and re-layouts: 0.21 us -> 1.52 us
    convert_element_type x3 -> x5, other arithmetic: 0.58 us -> 1.66 us  [the longest x3 1.55 us: settle(): moving = value.astype(jnp.bfloat16)]
    ppermute x16 -> x15, starting transfers between devices: 15.3 us -> 14.6 us  [swap(): lax.ppermute(value, 'tensor', [(place, place ^ bit) for place in range(to...]
  transfers between devices with their start and end apart: 16 -> 15, of which waited for: 8 -> 4; matrix products, arithmetic and copies ran while one was open for 2% -> 15% of each run, Pallas kernels for 39% -> 36%
where the time goes in v8:
time: 76 us; the launch traced here: 75.5 us
  Pallas kernels  29.4 us (39%)
  waiting for transfers between devices  17.4 us (23%)
  starting transfers between devices  14.6 us (19%)
  other arithmetic  6.08 us (8%)
  matrix products  5.99 us (8%)
  local copies, waits for them, and re-layouts  1.62 us (2%)
    pallas_call x5, Pallas kernels, product(): pl.pallas_call(functools.partial(product_body, sent=len(sent), kept=len(k...  26.7 us
    ppermute x15, waiting for transfers between devices, swap(): lax.ppermute(value, 'tensor', [(place, place ^ bit) for place in range(to...  17.4 us
    ppermute x15, starting transfers between devices, swap(): lax.ppermute(value, 'tensor', [(place, place ^ bit) for place in range(to...  14.6 us
    unnamed x1, matrix products  5.99 us
    pallas_call x1, Pallas kernels, expand(): pl.pallas_call(expand_body, grid_spec=pltpu.PrefetchScalarGridSpec(num_sc...  2.76 us
    convert_element_type x4, other arithmetic, on_device(): leaving = (results[0] + arrived[0].astype(jnp.float32)).astype(jnp.bfloat16)  2.5 us
    convert_element_type x3, other arithmetic, settle(): moving = value.astype(jnp.bfloat16)  1.55 us
  transfers between devices with their start and end apart: 15, of which 4 were waited for; matrix products, arithmetic and copies ran while one was open for 15% of the time, Pallas kernels for 36%

profile of v8, /device:TPU:0, one launch (start us, length us, event | category | flops | bytes accessed | tf_op | source)
XLA Modules:
  0.0 75.5 jit_solution(7940861212722839962)
XLA Ops:
  0.0 1.3 %copy-done.3 = bf16[384,1664]{1,0:T(8,128)(2,1)S(1)} copy-done((bf16[384,1664]{1,0:T(8,128)(2,1)S(1)}, bf16[384,1664]{1,0:T(8,128)(2,1)}, u32[]{:S(2)}) %copy-start.3) | copy-done | bytes 1277976
  1.3 2.4 %shard_map.73.refs_0_ = bf16[1,384,512]{2,1,0:T(8,128)(2,1)S(1)} custom-call(s32[1]{0:T(128)} %bitcast.3.targets_ref, bf16[384,1664]{1,0:T(8,128)(2,1)S(1)} %copy-done.3, bf16[1664,8192]{1,0:T(8,128)(2,1)} %down_ref.9), custom_call_target="tpu_custom_call" | custom-call | flops 10000000000 | bytes 1024 | tf_op jit(solution)/shard_map/pallas_call | solution.py:73
  3.8 0.5 collective-permute-start
  4.4 5.3 %shard_map.74 = (bf16[2,384,512]{2,1,0:T(8,128)(2,1)S(1)}, f32[1,384,512]{2,1,0:T(8,128)S(1)}) custom-call(s32[3]{0:T(128)S(1)} %pad_add_fusion.targets_ref, bf16[384,1664]{1,0:T(8,128)(2,1)S(1)} %copy-done.4, bf16[1664,8192]{1,0:T(8,128)(2,1)} %down_ref.9, bf16[1,384,512]{2,1,0:T(8,128)(2,1)S(1)} %shard_map.73.refs_0_), custom_call_target="tpu_custom_call" | custom-call | flops 10000000000 | bytes 1024 | tf_op jit(solution)/shard_map/pallas_call | solution.py:73
  10.0 1.1 %fusion.8.refs_0_ = bf16[384,512]{1,0:T(8,128)(2,1)S(1)} fusion(f32[1,384,512]{2,1,0:T(8,128)S(1)} %get-tuple-element.25, bf16[1,384,512]{2,1,0:T(8,128)(2,1)} %collective-permute-done), kind=kLoop, calls=%fused_computation.18 | loop fusion | flops 589824 | bytes 1572864 | tf_op jit(solution)/shard_map/convert_element_type | solution.py:256
  11.2 3.0 %collective-permute-start.3 = (bf16[384,512]{1,0:T(8,128)(2,1)S(1)}, bf16[384,512]{1,0:T(8,128)(2,1)S(1)}, u32[]{:S(2)}, u32[]{:S(2)}) collective-permute-start(bf16[384,512]{1,0:T(8,128)(2,1)S(1)} %fusion.8.refs_0_), channel_id=1, source_target_pairs={{0,2},{1,3},{2,0},{3,1},{4,6},{5,7},{6,4},{7,5},{8,10},{9,11},{10,... | collective-permute-start | bytes 1179656 | tf_op jit(solution)/shard_map/ppermute | solution.py:94
  14.2 6.0 %fusion.17 = f32[384,2048]{0,1:S(1)} fusion(bf16[384,1664]{1,0:T(8,128)(2,1)S(1)} %copy-done.4, bf16[1664,2048]{0,1:T(8,128)(2,1)} %bitcast.57), kind=kOutput, calls=%fused_computation.36 | convolution fusion | flops 2617245696 | bytes 11239424
  21.0 2.7 %collective-permute-start.1 = (f32[192,128]{1,0:T(8,128)S(1)}, f32[192,128]{1,0:T(8,128)S(1)}, u32[]{:S(2)}, u32[]{:S(2)}) collective-permute-start(f32[192,128]{1,0:T(8,128)S(1)} %pad_maximum_fusion.refs_1_), channel_id=1, source_target_pairs={{0,8},{1,9},{2,10},{3,11},{4,12},{5,13},{6,14},{7,15},{8,0},{9,1},... | collective-permute-start | bytes 294920 | tf_op jit(solution)/shard_map/ppermute | solution.py:94
  23.6 6.3 %shard_map.75 = (bf16[2,384,512]{2,1,0:T(8,128)(2,1)S(1)}, f32[2,384,512]{2,1,0:T(8,128)S(1)}) custom-call(s32[4]{0:T(128)S(1)} %pad_add_fusion.1.targets_ref, bf16[384,1664]{1,0:T(8,128)(2,1)S(1)} %copy-done.4, bf16[1664,8192]{1,0:T(8,128)(2,1)} %down_ref.9, bf16[384,512]{1,0:T(8,128)(2,1)S(1)} %fusion.8.refs_0_, f32[192,128]{1,0:T(8,128)S(1)} %pad_maximum_fusion.refs_1_), custom_call_target="tpu_custom_call" | custom-call | flops 10000000000 | bytes 1024 | tf_op jit(solution)/shard_map/pallas_call | solution.py:73
  30.2 1.1 %fusion.9.refs_0_ = bf16[384,512]{1,0:T(8,128)(2,1)S(1)} fusion(f32[2,384,512]{2,1,0:T(8,128)S(1)} %get-tuple-element.30, bf16[2,384,512]{2,1,0:T(8,128)(2,1)} %collective-permute-done.2), kind=kLoop, calls=%fused_computation.19 | loop fusion | flops 589824 | bytes 1572864 | tf_op jit(solution)/shard_map/convert_element_type | solution.py:256
  31.3 0.6 collective-permute-start.7
  31.8 1.2 %fusion.7.refs_1_ = bf16[384,512]{1,0:T(8,128)(2,1)S(1)} fusion(bf16[384,512]{1,0:T(8,128)(2,1)S(1)} %collective-permute-done.3, f32[2,384,512]{2,1,0:T(8,128)S(1)} %get-tuple-element.30, bf16[2,384,512]{2,1,0:T(8,128)(2,1)} %collective-permute-done.2), kind=kLoop, calls=%fused_computation.12 | loop fusion | flops 983040 | bytes 1966080 | tf_op jit(solution)/shard_map/convert_element_type | solution.py:231
  33.0 1.6 %collective-permute-start.4 = (bf16[480,512]{1,0:T(8,128)(2,1)S(1)}, bf16[480,512]{1,0:T(8,128)(2,1)S(1)}, u32[]{:S(2)}, u32[]{:S(2)}) collective-permute-start(bf16[480,512]{1,0:T(8,128)(2,1)S(1)} %maximum_maximum_fusion), channel_id=1, source_target_pairs={{0,4},{1,5},{2,6},{3,7},{4,0},{5,1},{6,2},{7,3},{8,12},{9,13},{10,... | collective-permute-start | bytes 1474568 | tf_op jit(solution)/shard_map/ppermute | solution.py:94
  34.7 6.3 %shard_map.76 = (bf16[2,384,512]{2,1,0:T(8,128)(2,1)S(1)}, f32[2,384,512]{2,1,0:T(8,128)S(1)}) custom-call(s32[4]{0:T(128)S(1)} %pad_add_fusion.3.targets_ref, bf16[384,1664]{1,0:T(8,128)(2,1)S(1)} %copy-done.4, bf16[1664,8192]{1,0:T(8,128)(2,1)} %down_ref.9, bf16[384,512]{1,0:T(8,128)(2,1)S(1)} %fusion.9.refs_0_, bf16[384,512]{1,0:T(8,128)(2,1)S(1)} %fusion.7.refs_1_), custom_call_target="tpu_custom_call" | custom-call | flops 10000000000 | bytes 1024 | tf_op jit(solution)/shard_map/pallas_call | solution.py:73
  41.2 1.6 %collective-permute-start.12 = (bf16[384,512]{1,0:T(8,128)(2,1)S(1)}, bf16[384,512]{1,0:T(8,128)(2,1)S(1)}, u32[]{:S(2)}, u32[]{:S(2)}) collective-permute-start(bf16[384,512]{1,0:T(8,128)(2,1)S(1)} %fusion.10.refs_0_), channel_id=1, source_target_pairs={{0,2},{1,3},{2,0},{3,1},{4,6},{5,7},{6,4},{7,5},{8,10},{9,11},{10,... | collective-permute-start | bytes 1179656 | tf_op jit(solution)/shard_map/ppermute | solution.py:94
  42.8 3.6 %collective-permute-done.4 = bf16[480,512]{1,0:T(8,128)(2,1)S(1)} collective-permute-done((bf16[480,512]{1,0:T(8,128)(2,1)S(1)}, bf16[480,512]{1,0:T(8,128)(2,1)S(1)}, u32[]{:S(2)}, u32[]{:S(2)}) %collective-permute-start.4) | collective-permute-done | bytes 491552 | tf_op jit(solution)/shard_map/ppermute | solution.py:94
  46.5 1.6 %collective-permute-start.5 = (f32[192,128]{1,0:T(8,128)S(1)}, f32[192,128]{1,0:T(8,128)S(1)}, u32[]{:S(2)}, u32[]{:S(2)}) collective-permute-start(f32[192,128]{1,0:T(8,128)S(1)} %fusion.12.refs_2_), channel_id=1, source_target_pairs={{0,2},{1,3},{2,0},{3,1},{4,6},{5,7},{6,4},{7,5},{8,10},{9,11},{10,... | collective-permute-start | bytes 294920 | tf_op jit(solution)/shard_map/ppermute | solution.py:94
  48.8 6.3 %shard_map.77 = (bf16[1,384,512]{2,1,0:T(8,128)(2,1)S(1)}, f32[3,384,512]{2,1,0:T(8,128)S(1)}) custom-call(s32[4]{0:T(128)S(1)} %pad_add_fusion.2.targets_ref, bf16[384,1664]{1,0:T(8,128)(2,1)S(1)} %copy-done.4, bf16[1664,8192]{1,0:T(8,128)(2,1)} %down_ref.9, bf16[384,512]{1,0:T(8,128)(2,1)S(1)} %fusion.10.refs_0_, bf16[384,512]{1,0:T(8,128)(2,1)S(1)} %fusion.6.refs_1_, ...), custom_call_target="tpu_custom_call" | custom-call | flops 10000000000 | bytes 1024 | tf_op jit(solution)/shard_map/pallas_call | solution.py:73
  55.5 1.7 %collective-permute-start.13 = (bf16[384,512]{1,0:T(8,128)(2,1)S(1)}, bf16[384,512]{1,0:T(8,128)(2,1)S(1)}, u32[]{:S(2)}, u32[]{:S(2)}) collective-permute-start(bf16[384,512]{1,0:T(8,128)(2,1)S(1)} %fusion), channel_id=1, source_target_pairs={{0,4},{1,5},{2,6},{3,7},{4,0},{5,1},{6,2},{7,3},{8,12},{9,13},{10,... | collective-permute-start | bytes 1179656 | tf_op jit(solution)/shard_map/ppermute | solution.py:94
  57.8 1.3 %collective-permute-done.14 = f32[192,128]{1,0:T(8,128)S(1)} collective-permute-done((f32[192,128]{1,0:T(8,128)S(1)}, f32[192,128]{1,0:T(8,128)S(1)}, u32[]{:S(2)}, u32[]{:S(2)}) %collective-permute-start.14) | collective-permute-done | bytes 98336 | tf_op jit(solution)/shard_map/ppermute | solution.py:94
  59.2 2.8 %shard_map.78 = f32[384,512]{1,0:T(8,128)S(1)} custom-call(s32[32]{0:T(128)S(1)} %copy-done.1, s32[32]{0:T(128)S(1)} %copy-done.2, f32[192,128]{1,0:T(8,128)S(1)} %add.102.packed_ref, bf16[2048,512]{1,0:T(8,128)(2,1)S(1)} %bitcast.55), custom_call_target="tpu_custom_call" | custom-call | flops 1000000 | bytes 1 | tf_op jit(solution)/shard_map/pallas_call | solution.py:170
  61.9 6.0 %collective-permute-done.11 = bf16[384,512]{1,0:T(8,128)(2,1)S(1)} collective-permute-done((bf16[384,512]{1,0:T(8,128)(2,1)S(1)}, bf16[384,512]{1,0:T(8,128)(2,1)S(1)}, u32[]{:S(2)}, u32[]{:S(2)}) %collective-permute-start.11) | collective-permute-done | bytes 393248 | tf_op jit(solution)/shard_map/ppermute | solution.py:94
  68.0 6.4 %collective-permute-done.13 = bf16[384,512]{1,0:T(8,128)(2,1)S(1)} collective-permute-done((bf16[384,512]{1,0:T(8,128)(2,1)S(1)}, bf16[384,512]{1,0:T(8,128)(2,1)S(1)}, u32[]{:S(2)}, u32[]{:S(2)}) %collective-permute-start.13) | collective-permute-done | bytes 393248 | tf_op jit(solution)/shard_map/ppermute | solution.py:94
  74.4 1.1 %fusion.4 = bf16[384,512]{1,0:T(8,128)(2,1)} fusion(f32[384,512]{1,0:T(8,128)S(1)} %shard_map.78, bf16[384,512]{1,0:T(8,128)(2,1)S(1)} %collective-permute-done.13, bf16[384,512]{1,0:T(8,128)(2,1)S(1)} %collective-permute-done.11, bf16[384,512]{1,0:T(8,128)(2,1)S(1)} %collective-permute-done.10, bf16[1,384,512]{2,1,0:T(8,128)(2,1)S(1)} %collective-permute-done.8, ...), kind=kLoop, calls=%fused_computation.7 | loop fusion | flops 1966080 | bytes 3538944 | tf_op jit(solution)/shard_map/convert_element_type | solution.py:272
  (51 shorter events, 3.3 us)
Async XLA Ops:
  0.0 1.3 %copy-start.3 = (bf16[384,1664]{1,0:T(8,128)(2,1)S(1)}, bf16[384,1664]{1,0:T(8,128)(2,1)}, u32[]{:S(2)}) copy-start(bf16[384,1664]{1,0:T(8,128)(2,1)} %hidden_ref.9) | copy-start | bytes 3833860
  1.3 3.1 %copy-start.4 = (bf16[384,1664]{1,0:T(8,128)(2,1)S(1)}, bf16[384,1664]{1,0:T(8,128)(2,1)}, u32[]{:S(2)}) copy-start(bf16[384,1664]{1,0:T(8,128)(2,1)} %hidden_ref.9) | copy-start | bytes 3833860
  3.8 6.3 %collective-permute-start = (bf16[1,384,512]{2,1,0:T(8,128)(2,1)S(1)}, bf16[1,384,512]{2,1,0:T(8,128)(2,1)}, u32[]{:S(2)}, u32[]{:S(2)}) collective-permute-start(bf16[1,384,512]{2,1,0:T(8,128)(2,1)S(1)} %shard_map.73.refs_0_), channel_id=1, source_target_pairs={{0,1},{1,0},{2,3},{3,2},{4,5},{5,4},{6,7},{7,6},{8,9},{9,8},{10,11... | collective-permute-start | bytes 1179656 | tf_op jit(solution)/shard_map/ppermute | solution.py:94
  4.4 5.6 %copy-start.5 = (s32[384]{0:T(512)S(1)}, s32[384]{0:T(512)}, u32[]{:S(2)}) copy-start(s32[384]{0:T(512)} %param.11) | copy-start | bytes 4612
  9.6 20.5 %collective-permute-start.2 = (bf16[2,384,512]{2,1,0:T(8,128)(2,1)S(1)}, bf16[2,384,512]{2,1,0:T(8,128)(2,1)}, u32[]{:S(2)}, u32[]{:S(2)}) collective-permute-start(bf16[2,384,512]{2,1,0:T(8,128)(2,1)S(1)} %get-tuple-element.31), channel_id=1, source_target_pairs={{0,1},{1,0},{2,3},{3,2},{4,5},{5,4},{6,7},{7,6},{8,9},{9,8},{10,11... | collective-permute-start | bytes 2359304 | tf_op jit(solution)/shard_map/ppermute | solution.py:94
  11.2 20.7 %collective-permute-start.3 = (bf16[384,512]{1,0:T(8,128)(2,1)S(1)}, bf16[384,512]{1,0:T(8,128)(2,1)S(1)}, u32[]{:S(2)}, u32[]{:S(2)}) collective-permute-start(bf16[384,512]{1,0:T(8,128)(2,1)S(1)} %fusion.8.refs_0_), channel_id=1, source_target_pairs={{0,2},{1,3},{2,0},{3,1},{4,6},{5,7},{6,4},{7,5},{8,10},{9,11},{10,... | collective-permute-start | bytes 1179656 | tf_op jit(solution)/shard_map/ppermute | solution.py:94
  21.0 9.1 %collective-permute-start.1 = (f32[192,128]{1,0:T(8,128)S(1)}, f32[192,128]{1,0:T(8,128)S(1)}, u32[]{:S(2)}, u32[]{:S(2)}) collective-permute-start(f32[192,128]{1,0:T(8,128)S(1)} %pad_maximum_fusion.refs_1_), channel_id=1, source_target_pairs={{0,8},{1,9},{2,10},{3,11},{4,12},{5,13},{6,14},{7,15},{8,0},{9,1},... | collective-permute-start | bytes 294920 | tf_op jit(solution)/shard_map/ppermute | solution.py:94
  29.9 11.2 %collective-permute-start.6 = (bf16[2,384,512]{2,1,0:T(8,128)(2,1)S(1)}, bf16[2,384,512]{2,1,0:T(8,128)(2,1)S(1)}, u32[]{:S(2)}, u32[]{:S(2)}) collective-permute-start(bf16[2,384,512]{2,1,0:T(8,128)(2,1)S(1)} %get-tuple-element.34), channel_id=1, source_target_pairs={{0,1},{1,0},{2,3},{3,2},{4,5},{5,4},{6,7},{7,6},{8,9},{9,8},{10,11... | collective-permute-start | bytes 2359304 | tf_op jit(solution)/shard_map/ppermute | solution.py:94
  31.3 16.8 %collective-permute-start.7 = (bf16[384,512]{1,0:T(8,128)(2,1)S(1)}, bf16[384,512]{1,0:T(8,128)(2,1)S(1)}, u32[]{:S(2)}, u32[]{:S(2)}) collective-permute-start(bf16[384,512]{1,0:T(8,128)(2,1)S(1)} %fusion.9.refs_0_), channel_id=1, source_target_pairs={{0,2},{1,3},{2,0},{3,1},{4,6},{5,7},{6,4},{7,5},{8,10},{9,11},{10,... | collective-permute-start | bytes 1179656 | tf_op jit(solution)/shard_map/ppermute | solution.py:94
  33.0 13.4 %collective-permute-start.4 = (bf16[480,512]{1,0:T(8,128)(2,1)S(1)}, bf16[480,512]{1,0:T(8,128)(2,1)S(1)}, u32[]{:S(2)}, u32[]{:S(2)}) collective-permute-start(bf16[480,512]{1,0:T(8,128)(2,1)S(1)} %maximum_maximum_fusion), channel_id=1, source_target_pairs={{0,4},{1,5},{2,6},{3,7},{4,0},{5,1},{6,2},{7,3},{8,12},{9,13},{10,... | collective-permute-start | bytes 1474568 | tf_op jit(solution)/shard_map/ppermute | solution.py:94
  41.0 14.2 %collective-permute-start.9 = (bf16[2,384,512]{2,1,0:T(8,128)(2,1)S(1)}, bf16[2,384,512]{2,1,0:T(8,128)(2,1)S(1)}, u32[]{:S(2)}, u32[]{:S(2)}) collective-permute-start(bf16[2,384,512]{2,1,0:T(8,128)(2,1)S(1)} %get-tuple-element.40), channel_id=1, source_target_pairs={{0,1},{1,0},{2,3},{3,2},{4,5},{5,4},{6,7},{7,6},{8,9},{9,8},{10,11... | collective-permute-start | bytes 2359304 | tf_op jit(solution)/shard_map/ppermute | solution.py:94
  41.2 14.1 %collective-permute-start.12 = (bf16[384,512]{1,0:T(8,128)(2,1)S(1)}, bf16[384,512]{1,0:T(8,128)(2,1)S(1)}, u32[]{:S(2)}, u32[]{:S(2)}) collective-permute-start(bf16[384,512]{1,0:T(8,128)(2,1)S(1)} %fusion.10.refs_0_), channel_id=1, source_target_pairs={{0,2},{1,3},{2,0},{3,1},{4,6},{5,7},{6,4},{7,5},{8,10},{9,11},{10,... | collective-permute-start | bytes 1179656 | tf_op jit(solution)/shard_map/ppermute | solution.py:94
  46.5 8.7 %collective-permute-start.5 = (f32[192,128]{1,0:T(8,128)S(1)}, f32[192,128]{1,0:T(8,128)S(1)}, u32[]{:S(2)}, u32[]{:S(2)}) collective-permute-start(f32[192,128]{1,0:T(8,128)S(1)} %fusion.12.refs_2_), channel_id=1, source_target_pairs={{0,2},{1,3},{2,0},{3,1},{4,6},{5,7},{6,4},{7,5},{8,10},{9,11},{10,... | collective-permute-start | bytes 294920 | tf_op jit(solution)/shard_map/ppermute | solution.py:94
  48.4 19.6 %collective-permute-start.11 = (bf16[384,512]{1,0:T(8,128)(2,1)S(1)}, bf16[384,512]{1,0:T(8,128)(2,1)S(1)}, u32[]{:S(2)}, u32[]{:S(2)}) collective-permute-start(bf16[384,512]{1,0:T(8,128)(2,1)S(1)} %fusion.6.refs_1_), channel_id=1, source_target_pairs={{0,8},{1,9},{2,10},{3,11},{4,12},{5,13},{6,14},{7,15},{8,0},{9,1},... | collective-permute-start | bytes 1179656 | tf_op jit(solution)/shard_map/ppermute | solution.py:94
  55.1 4.0 %copy-start = (bf16[32,64,512]{2,1,0:T(8,128)(2,1)S(1)}, bf16[32,64,512]{2,1,0:T(8,128)(2,1)}, u32[]{:S(2)}) copy-start(bf16[32,64,512]{2,1,0:T(8,128)(2,1)} %param.10) | copy-start | bytes 6291460
  55.1 4.0 %copy-start.1 = (s32[32]{0:T(128)S(1)}, s32[32]{0:T(128)}, u32[]{:S(2)}) copy-start(s32[32]{0:T(128)} %first_ref.1) | copy-start | bytes 388
  55.1 4.0 %copy-start.2 = (s32[32]{0:T(128)S(1)}, s32[32]{0:T(128)}, u32[]{:S(2)}) copy-start(s32[32]{0:T(128)} %length_ref.1) | copy-start | bytes 388
  55.1 12.9 %collective-permute-start.8 = (bf16[1,384,512]{2,1,0:T(8,128)(2,1)S(1)}, bf16[1,384,512]{2,1,0:T(8,128)(2,1)S(1)}, u32[]{:S(2)}, u32[]{:S(2)}) collective-permute-start(bf16[1,384,512]{2,1,0:T(8,128)(2,1)S(1)} %get-tuple-element.39), channel_id=1, source_target_pairs={{0,1},{1,0},{2,3},{3,2},{4,5},{5,4},{6,7},{7,6},{8,9},{9,8},{10,11... | collective-permute-start | bytes 1179656 | tf_op jit(solution)/shard_map/ppermute | solution.py:94
  55.5 18.9 %collective-permute-start.13 = (bf16[384,512]{1,0:T(8,128)(2,1)S(1)}, bf16[384,512]{1,0:T(8,128)(2,1)S(1)}, u32[]{:S(2)}, u32[]{:S(2)}) collective-permute-start(bf16[384,512]{1,0:T(8,128)(2,1)S(1)} %fusion), channel_id=1, source_target_pairs={{0,4},{1,5},{2,6},{3,7},{4,0},{5,1},{6,2},{7,3},{8,12},{9,13},{10,... | collective-permute-start | bytes 1179656 | tf_op jit(solution)/shard_map/ppermute | solution.py:94
  57.2 17.2 %collective-permute-start.10 = (bf16[384,512]{1,0:T(8,128)(2,1)S(1)}, bf16[384,512]{1,0:T(8,128)(2,1)S(1)}, u32[]{:S(2)}, u32[]{:S(2)}) collective-permute-start(bf16[384,512]{1,0:T(8,128)(2,1)S(1)} %fusion.11), channel_id=1, source_target_pairs={{0,2},{1,3},{2,0},{3,1},{4,6},{5,7},{6,4},{7,5},{8,10},{9,11},{10,... | collective-permute-start | bytes 1179656 | tf_op jit(solution)/shard_map/ppermute | solution.py:94
  57.7 1.4 %collective-permute-start.14 = (f32[192,128]{1,0:T(8,128)S(1)}, f32[192,128]{1,0:T(8,128)S(1)}, u32[]{:S(2)}, u32[]{:S(2)}) collective-permute-start(f32[192,128]{1,0:T(8,128)S(1)} %add.101), channel_id=1, source_target_pairs={{0,1},{1,0},{2,3},{3,2},{4,5},{5,4},{6,7},{7,6},{8,9},{9,8},{10,11... | collective-permute-start | bytes 294920 | tf_op jit(solution)/shard_map/ppermute | solution.py:94

commit v9 on v8

v9 whole, which is shorter than its diff:
```python
import functools

import jax
import jax.numpy as jnp
from jax import lax
from jax.experimental import pallas as pl
from jax.experimental.pallas import tpu as pltpu
from jax.sharding import PartitionSpec as P

VMEM_LIMIT = 39 * 1024 * 1024
WINDOW = 128
TOGETHER = 4
FLOPS = 2_500_000_000
EXPAND_FLOPS = 1_000_000


def product_body(table_ref, hidden_ref, down_ref, *refs, base, sent, kept, first, last, earlier):
    sent_ref = kept_ref = None
    refs = list(refs[earlier + (0 if first else 1):])
    if sent:
        sent_ref = refs.pop(0)
    if kept:
        kept_ref = refs.pop(0)
    buffer = refs.pop(0)
    arrived = refs.pop()
    width = buffer.shape[2]
    targets = sent + kept

    def copy(at):
        column = pl.multiple_of(table_ref[base + at] * width, width)
        slot = (base + at) % 2
        return pltpu.make_async_copy(
            down_ref.at[:, pl.ds(column, width)], buffer.at[slot], arrived.at[slot]
        )

    if first:
        copy(0).start()

    def step(at, carry):
        @pl.when(at + 1 < targets + (0 if last else 1))
        def _():
            copy(at + 1).start()

        @pl.when(at >= (0 if first else 1))
        def _():
            copy(at).wait()

        total = jnp.dot(
            hidden_ref[...], buffer[(base + at) % 2], preferred_element_type=jnp.float32
        )
        if sent:

            @pl.when(at < sent)
            def _():
                sent_ref[jnp.minimum(at, sent - 1)] = total.astype(jnp.bfloat16)

        if kept:

            @pl.when(at >= sent)
            def _():
                kept_ref[jnp.maximum(at - sent, 0)] = total

        return carry

    lax.fori_loop(0, targets, step, 0)
    if not last:
        copy(targets).wait()


def product(table, hidden, down_matrix, buffer, base, sent, kept, width, last, earlier):
    rows, depth = hidden.shape
    first = buffer is None
    vmem = pl.BlockSpec(memory_space=pltpu.VMEM)
    anywhere = pl.BlockSpec(memory_space=pl.ANY)
    out_shape = []
    if sent:
        out_shape.append(jax.ShapeDtypeStruct((sent, rows, width), jnp.bfloat16))
    if kept:
        out_shape.append(jax.ShapeDtypeStruct((kept, rows, width), jnp.float32))
    place = len(out_shape)
    out_shape.append(jax.ShapeDtypeStruct((2, depth, width), jnp.bfloat16))
    results = pl.pallas_call(
        functools.partial(
            product_body, base=base, sent=sent, kept=kept, first=first, last=last,
            earlier=len(earlier),
        ),
        in_specs=[
            pl.BlockSpec(memory_space=pltpu.SMEM),
            vmem,
            pl.BlockSpec(memory_space=pltpu.HBM),
        ]
        + ([] if first else [vmem])
        + [anywhere] * len(earlier),
        out_specs=[vmem] * len(out_shape),
        out_shape=out_shape,
        scratch_shapes=[pltpu.SemaphoreType.DMA((2,))],
        input_output_aliases={} if first else {3: place},
        compiler_params=pltpu.CompilerParams(vmem_limit_bytes=VMEM_LIMIT),
        cost_estimate=pl.CostEstimate(flops=FLOPS, bytes_accessed=1024, transcendentals=0),
    )(table, hidden, down_matrix, *([] if first else [buffer]), *earlier)
    return results[0] if sent else None, results[place - 1] if kept else None, results[place]


def swap(value, bit, total):
    return lax.ppermute(value, "tensor", [(place, place ^ bit) for place in range(total)])


def attach(value, packed):
    below = jnp.pad(packed.astype(jnp.bfloat16), ((0, 0), (0, value.shape[1] - packed.shape[1])))
    return jnp.concatenate([value, below])


def detach(value, packed):
    height, columns = packed.shape
    above = value.shape[0] - height
    return value[:above], value[above:, :columns].astype(jnp.float32)


def for_each_window(first_ref, length_ref, group, rows, body):
    window = min(WINDOW, rows)
    adapters = [group * TOGETHER + at for at in range(TOGETHER)]
    begins = [first_ref[adapter] for adapter in adapters]
    ends = [first_ref[adapter] + length_ref[adapter] for adapter in adapters]
    base = begins[0] // 16 * 16

    def step(at, carry):
        low = base + at * window
        start = pl.multiple_of(jnp.minimum(low, rows - window), 16)
        places = start + lax.broadcasted_iota(jnp.int32, (window, 1), 0)
        masks = [
            (places >= jnp.maximum(begin, low)) & (places < end) for begin, end in zip(begins, ends)
        ]
        body(pl.ds(start, window), masks)
        return carry

    lax.fori_loop(0, (ends[-1] - base + window - 1) // window, step, 0)


def shrink(hidden, shrink_matrices, row_adapter_index):
    adapters = shrink_matrices.shape[0]
    every_adapter = jnp.einsum(
        "hq,gqu->hgu", hidden, shrink_matrices, preferred_element_type=jnp.float32
    )
    picked = row_adapter_index[:, None] == jnp.arange(adapters, dtype=jnp.int32)[None, :]
    partial = jnp.sum(jnp.where(picked[:, :, None], every_adapter, 0.0), axis=1)
    return jnp.swapaxes(partial, 0, 1)


def expand_body(first_ref, length_ref, packed_ref, table_ref, result_ref, shrunk_ref):
    group = pl.program_id(0)

    @pl.when(group == 0)
    def _():
        shrunk_ref[...] = packed_ref[...].T.astype(jnp.bfloat16)
        result_ref[...] = jnp.zeros_like(result_ref)

    def body(window, masks):
        shrunk = shrunk_ref[window, :]
        spread = [jnp.where(mask, shrunk, jnp.zeros((), jnp.bfloat16)) for mask in masks]
        part = jnp.dot(
            jnp.concatenate(spread, axis=1), table_ref[...], preferred_element_type=jnp.float32
        )
        result_ref[window, :] = result_ref[window, :] + part

    for_each_window(first_ref, length_ref, group, shrunk_ref.shape[0], body)


def expand(packed, expand_matrices, segment_first_row, segment_length):
    rows = packed.shape[1]
    adapters, rank, width = expand_matrices.shape
    table = expand_matrices.reshape(adapters * rank, width)
    return pl.pallas_call(
        expand_body,
        grid_spec=pltpu.PrefetchScalarGridSpec(
            num_scalar_prefetch=2,
            grid=(adapters // TOGETHER,),
            in_specs=[
                pl.BlockSpec((rank, rows), lambda group, *_: (0, 0)),
                pl.BlockSpec((TOGETHER * rank, width), lambda group, *_: (group, 0)),
            ],
            out_specs=pl.BlockSpec((rows, width), lambda group, *_: (0, 0)),
            scratch_shapes=[pltpu.VMEM((rows, rank), jnp.bfloat16)],
        ),
        out_shape=jax.ShapeDtypeStruct((rows, width), jnp.float32),
        compiler_params=pltpu.CompilerParams(vmem_limit_bytes=VMEM_LIMIT),
        cost_estimate=pl.CostEstimate(flops=EXPAND_FLOPS, bytes_accessed=1, transcendentals=0),
    )(segment_first_row, segment_length, packed, table)


def on_device(
    total,
    hidden,
    down_matrix,
    shrink_matrices,
    expand_matrices,
    row_adapter_index,
    segment_first_row,
    segment_length,
):
    me = lax.axis_index("tensor").astype(jnp.int32)
    width = down_matrix.shape[1] // total
    core, near = 1, 2
    units = total // 4

    kept_home, crossed, incoming = {}, {}, {}

    packed, steps = None, [*(4 << at for at in reversed(range((units - 1).bit_length()))), near, core]

    def send(value, bit, carry):
        nonlocal packed
        if not carry or packed is None or steps[:1] != [bit]:
            return swap(value, bit, total), None
        steps.pop(0)
        own, packed = packed, None
        arrived, shrinks = detach(swap(attach(value, own), bit, total), own)
        return arrived, own + shrinks

    def settle(unit, arrived):
        nonlocal packed
        value = kept_home[unit] + arrived.astype(jnp.float32) + crossed[unit].astype(jnp.float32)
        for moved, shrinks in incoming.pop(unit, []):
            value = value + moved.astype(jnp.float32)
            packed = packed if shrinks is None else shrinks
        if not unit:
            return value
        bit = unit & -unit
        moving = value.astype(jnp.bfloat16)
        incoming.setdefault(unit ^ bit, []).append(send(moving, 4 * bit, unit == top))
        return moving

    top = units - 1
    order = [top * 4 | near | core]
    for unit in reversed(range(units)):
        order += [(unit - 1) * 4 | near | core] * (unit > 0) + [unit * 4 | core, unit * 4 | near]
        order += [(unit + 1) * 4] * (unit < top) + [0] * (not unit)
    table = jnp.array(order, dtype=jnp.int32) ^ me

    values, _, buffer = product(table, hidden, down_matrix, None, 0, 1, 0, width, False, [])
    base, ready = 1, []
    for unit in reversed(range(units)):
        arrived = swap(values, core, total)
        sent, kept = 1 + (unit > 0), 1 + (unit < top) + (not unit)
        values, results, buffer = product(
            table, hidden, down_matrix, buffer, base, sent, kept, width, not unit, ready
        )
        base += sent + kept
        if packed is not None and steps and steps[0] != core:
            moved, results = lax.optimization_barrier((swap(packed, steps.pop(0), total), results))
            packed = packed + moved
        if unit < top:
            kept_home[unit + 1] = results[1]
        if not unit:
            kept_home[0] = results[-1]
        leaving = (results[0] + arrived[0].astype(jnp.float32)).astype(jnp.bfloat16)
        if unit == top:
            late, leaving = lax.optimization_barrier((hidden, leaving))
        ready = [leaving]
        if unit < top:
            leaving, arrived = lax.optimization_barrier((leaving, arrived))
            ready.append(settle(unit + 1, arrived[1]))
        if unit == top:
            packed = shrink(late, shrink_matrices, row_adapter_index)
        if packed is not None:
            ready.append(packed)
        crossed[unit] = swap(leaving, near, total)
    kept = [settle(0, swap(values, core, total)[0])]

    for bit in steps:
        packed = packed + swap(packed, bit, total)
    adapter_output = expand(packed, expand_matrices, segment_first_row, segment_length)
    return (kept[0] + adapter_output).astype(jnp.bfloat16)


def solution(mesh):
    in_specs = (
        P("groups", "tensor"),
        P("tensor", None),
        P(None, "tensor", None),
        P(None, None, "tensor"),
        P("groups"),
        P("groups"),
        P("groups"),
    )
    out_specs = P("groups", "tensor")
    return jax.shard_map(
        functools.partial(on_device, mesh.shape["tensor"]),
        mesh=mesh,
        in_specs=in_specs,
        out_specs=out_specs,
        check_vma=False,
    )
```

time: 76 us -> 71.8 us (0.945)
  waiting for transfers between devices: 17.4 us -> 21.8 us
  other arithmetic: 6.08 us -> 3.3 us
  Pallas kernels: 29.4 us -> 27.1 us
  matrix products: 5.99 us -> 4.03 us
  starting transfers between devices: 14.6 us -> 13.5 us
    ppermute x15, waiting for transfers between devices: 17.4 us -> 21.8 us  [swap(): lax.ppermute(value, 'tensor', [(place, place ^ bit) for place in range(to...]
    pallas_call x5, Pallas kernels: 26.7 us -> 24.3 us  [product(): pl.pallas_call(functools.partial(product_body, base=base, sent=sent, kept...]
    convert_element_type x4, other arithmetic: 2.5 us -> 0.52 us  [on_device(): leaving = (results[0] + arrived[0].astype(jnp.float32)).astype(jnp.bfloat16)]
    unnamed x1, matrix products: 5.99 us -> 4.03 us
    ppermute x15, starting transfers between devices: 14.6 us -> 13.5 us  [swap(): lax.ppermute(value, 'tensor', [(place, place ^ bit) for place in range(to...]
    convert_element_type x3, other arithmetic: 1.55 us -> 0.53 us  [settle(): moving = value.astype(jnp.bfloat16)]
  transfers between devices with their start and end apart: 15 -> 15, of which waited for: 4 -> 6; matrix products, arithmetic and copies ran while one was open for 15% -> 8% of each run, Pallas kernels for 36% -> 34%
where the time goes in v9:
time: 71.8 us; the launch traced here: 71.4 us
  Pallas kernels  27.1 us (38%)
  waiting for transfers between devices  21.8 us (30%)
  starting transfers between devices  13.5 us (19%)
  matrix products  4.03 us (6%)
  other arithmetic  3.3 us (5%)
  local copies, waits for them, and re-layouts  1.33 us (2%)
    pallas_call x5, Pallas kernels, product(): pl.pallas_call(functools.partial(product_body, base=base, sent=sent, kept...  24.3 us
    ppermute x15, waiting for transfers between devices, swap(): lax.ppermute(value, 'tensor', [(place, place ^ bit) for place in range(to...  21.8 us
    ppermute x15, starting transfers between devices, swap(): lax.ppermute(value, 'tensor', [(place, place ^ bit) for place in range(to...  13.5 us
    unnamed x1, matrix products  4.03 us
    pallas_call x1, Pallas kernels, expand(): pl.pallas_call(expand_body, grid_spec=pltpu.PrefetchScalarGridSpec(num_sc...  2.78 us
  transfers between devices with their start and end apart: 15, of which 6 were waited for; matrix products, arithmetic and copies ran while one was open for 8% of the time, Pallas kernels for 34%

profile of v9, /device:TPU:0, one launch (start us, length us, event | category | flops | bytes accessed | tf_op | source)
XLA Modules:
  0.0 71.4 jit_solution(3705051880802878503)
XLA Ops:
  0.0 0.7 broadcast_xor_fusion.table_ref
  0.7 1.3 %copy-done = bf16[384,1664]{1,0:T(8,128)(2,1)S(1)} copy-done((bf16[384,1664]{1,0:T(8,128)(2,1)S(1)}, bf16[384,1664]{1,0:T(8,128)(2,1)}, u32[]{:S(2)}) %copy-start) | copy-done | bytes 1277976
  2.0 3.2 %shard_map.82 = (bf16[1,384,512]{2,1,0:T(8,128)(2,1)S(1)}, bf16[2,1664,512]{2,1,0:T(8,128)(2,1)S(1)}) custom-call(s32[16]{0:T(128)S(1)} %broadcast_xor_fusion.table_ref, bf16[384,1664]{1,0:T(8,128)(2,1)S(1)} %copy-done, bf16[1664,8192]{1,0:T(8,128)(2,1)} %down_ref.9), custom_call_target="tpu_custom_call" | custom-call | flops 2500000000 | bytes 1024 | tf_op jit(solution)/shard_map/pallas_call | solution.py:82
  5.1 0.5 collective-permute-start
  5.7 4.6 %shard_map.83 = (bf16[2,384,512]{2,1,0:T(8,128)(2,1)S(1)}, f32[1,384,512]{2,1,0:T(8,128)S(1)}, bf16[2,1664,512]{2,1,0:T(8,128)(2,1)S(1)}) custom-call(s32[16]{0:T(128)S(1)} %broadcast_xor_fusion.table_ref, bf16[384,1664]{1,0:T(8,128)(2,1)S(1)} %copy-done, bf16[1664,8192]{1,0:T(8,128)(2,1)} %down_ref.9, ...), custom_call_target="tpu_custom_call", output_to_operand_aliasing={{2}: (3, {})} | custom-call | flops 2500000000 | bytes 1024 | tf_op jit(solution)/shard_map/pallas_call | solution.py:82
  10.6 4.0 %fusion.15 = f32[384,2048]{0,1:S(1)} fusion(bf16[384,1664]{1,0:T(8,128)(2,1)S(1)} %copy-done, bf16[1664,2048]{0,1:T(8,128)(2,1)S(1)} %bitcast.51), kind=kOutput, calls=%fused_computation.29 | convolution fusion | flops 2617245696 | bytes 11239424
  15.0 4.1 %collective-permute-start.1 = (f32[64,384]{1,0:T(8,128)S(1)}, f32[64,384]{1,0:T(8,128)S(1)}, u32[]{:S(2)}, u32[]{:S(2)}) collective-permute-start(f32[64,384]{1,0:T(8,128)S(1)} %bitcast.46), channel_id=1, source_target_pairs={{0,8},{1,9},{2,10},{3,11},{4,12},{5,13},{6,14},{7,15},{8,0},{9,1},... | collective-permute-start | bytes 294920 | tf_op jit(solution)/shard_map/ppermute | solution.py:105
  19.2 1.5 %collective-permute-start.3 = (bf16[384,512]{1,0:T(8,128)(2,1)S(1)}, bf16[384,512]{1,0:T(8,128)(2,1)S(1)}, u32[]{:S(2)}, u32[]{:S(2)}) collective-permute-start(bf16[384,512]{1,0:T(8,128)(2,1)S(1)} %fusion.10.refs_1_), channel_id=1, source_target_pairs={{0,2},{1,3},{2,0},{3,1},{4,6},{5,7},{6,4},{7,5},{8,10},{9,11},{10,... | collective-permute-start | bytes 1179656 | tf_op jit(solution)/shard_map/ppermute | solution.py:105
  20.7 5.6 %shard_map.84 = (bf16[2,384,512]{2,1,0:T(8,128)(2,1)S(1)}, f32[2,384,512]{2,1,0:T(8,128)S(1)}, bf16[2,1664,512]{2,1,0:T(8,128)(2,1)S(1)}) custom-call(s32[16]{0:T(128)S(1)} %broadcast_xor_fusion.table_ref, bf16[384,1664]{1,0:T(8,128)(2,1)S(1)} %copy-done, bf16[1664,8192]{1,0:T(8,128)(2,1)} %down_ref.9, ...), custom_call_target="tpu_custom_call", output_to_operand_aliasing={{2}: (3, {})} | custom-call | flops 2500000000 | bytes 1024 | tf_op jit(solution)/shard_map/pallas_call | solution.py:82
  26.5 3.4 %collective-permute-done.3 = bf16[384,512]{1,0:T(8,128)(2,1)S(1)} collective-permute-done((bf16[384,512]{1,0:T(8,128)(2,1)S(1)}, bf16[384,512]{1,0:T(8,128)(2,1)S(1)}, u32[]{:S(2)}, u32[]{:S(2)}) %collective-permute-start.3) | collective-permute-done | bytes 393248 | tf_op jit(solution)/shard_map/ppermute | solution.py:105
  30.1 1.6 %collective-permute-start.4 = (bf16[448,512]{1,0:T(8,128)(2,1)S(1)}, bf16[448,512]{1,0:T(8,128)(2,1)S(1)}, u32[]{:S(2)}, u32[]{:S(2)}) collective-permute-start(bf16[448,512]{1,0:T(8,128)(2,1)S(1)} %fusion.9), channel_id=1, source_target_pairs={{0,4},{1,5},{2,6},{3,7},{4,0},{5,1},{6,2},{7,3},{8,12},{9,13},{10,... | collective-permute-start | bytes 1376264 | tf_op jit(solution)/shard_map/ppermute | solution.py:105
  31.8 1.5 %collective-permute-start.7 = (bf16[384,512]{1,0:T(8,128)(2,1)S(1)}, bf16[384,512]{1,0:T(8,128)(2,1)S(1)}, u32[]{:S(2)}, u32[]{:S(2)}) collective-permute-start(bf16[384,512]{1,0:T(8,128)(2,1)S(1)} %fusion.11.refs_1_), channel_id=1, source_target_pairs={{0,2},{1,3},{2,0},{3,1},{4,6},{5,7},{6,4},{7,5},{8,10},{9,11},{10,... | collective-permute-start | bytes 1179656 | tf_op jit(solution)/shard_map/ppermute | solution.py:105
  33.3 5.6 %shard_map.85 = (bf16[2,384,512]{2,1,0:T(8,128)(2,1)S(1)}, f32[2,384,512]{2,1,0:T(8,128)S(1)}, bf16[2,1664,512]{2,1,0:T(8,128)(2,1)S(1)}) custom-call(s32[16]{0:T(128)S(1)} %broadcast_xor_fusion.table_ref, bf16[384,1664]{1,0:T(8,128)(2,1)S(1)} %copy-done, bf16[1664,8192]{1,0:T(8,128)(2,1)} %down_ref.9, ...), custom_call_target="tpu_custom_call", output_to_operand_aliasing={{2}: (3, {})} | custom-call | flops 2500000000 | bytes 1024 | tf_op jit(solution)/shard_map/pallas_call | solution.py:82
  39.1 0.6 collective-permute-start.12
  39.7 1.8 %collective-permute-done.4 = bf16[448,512]{1,0:T(8,128)(2,1)S(1)} collective-permute-done((bf16[448,512]{1,0:T(8,128)(2,1)S(1)}, bf16[448,512]{1,0:T(8,128)(2,1)S(1)}, u32[]{:S(2)}, u32[]{:S(2)}) %collective-permute-start.4) | collective-permute-done | bytes 458784 | tf_op jit(solution)/shard_map/ppermute | solution.py:105
  41.5 1.6 %collective-permute-start.5 = (f32[64,384]{1,0:T(8,128)S(1)}, f32[64,384]{1,0:T(8,128)S(1)}, u32[]{:S(2)}, u32[]{:S(2)}) collective-permute-start(f32[64,384]{1,0:T(8,128)S(1)} %convert_add_fusion.refs_3_), channel_id=1, source_target_pairs={{0,2},{1,3},{2,0},{3,1},{4,6},{5,7},{6,4},{7,5},{8,10},{9,11},{10,... | collective-permute-start | bytes 294920 | tf_op jit(solution)/shard_map/ppermute | solution.py:105
  43.7 5.4 %shard_map.86 = (bf16[1,384,512]{2,1,0:T(8,128)(2,1)S(1)}, f32[3,384,512]{2,1,0:T(8,128)S(1)}, bf16[2,1664,512]{2,1,0:T(8,128)(2,1)S(1)}) custom-call(s32[16]{0:T(128)S(1)} %broadcast_xor_fusion.table_ref, bf16[384,1664]{1,0:T(8,128)(2,1)S(1)} %copy-done, bf16[1664,8192]{1,0:T(8,128)(2,1)} %down_ref.9, ...), custom_call_target="tpu_custom_call", output_to_operand_aliasing={{2}: (3, {})} | custom-call | flops 2500000000 | bytes 1024 | tf_op jit(solution)/shard_map/pallas_call | solution.py:82
  49.2 3.5 %collective-permute-done.5 = f32[64,384]{1,0:T(8,128)S(1)} collective-permute-done((f32[64,384]{1,0:T(8,128)S(1)}, f32[64,384]{1,0:T(8,128)S(1)}, u32[]{:S(2)}, u32[]{:S(2)}) %collective-permute-start.5) | collective-permute-done | bytes 98336 | tf_op jit(solution)/shard_map/ppermute | solution.py:105
  53.6 0.6 collective-permute-start.10
  54.3 1.3 %collective-permute-done.14 = f32[64,384]{1,0:T(8,128)S(1)} collective-permute-done((f32[64,384]{1,0:T(8,128)S(1)}, f32[64,384]{1,0:T(8,128)S(1)}, u32[]{:S(2)}, u32[]{:S(2)}) %collective-permute-start.14) | collective-permute-done | bytes 98336 | tf_op jit(solution)/shard_map/ppermute | solution.py:105
  55.7 2.8 %shard_map.87 = f32[384,512]{1,0:T(8,128)S(1)} custom-call(s32[32]{0:T(128)S(1)} %copy-done.2, s32[32]{0:T(128)S(1)} %copy-done.3, f32[64,384]{1,0:T(8,128)S(1)} %add.100.packed_ref, bf16[2048,512]{1,0:T(8,128)(2,1)S(1)} %bitcast.45), custom_call_target="tpu_custom_call" | custom-call | flops 1000000 | bytes 1 | tf_op jit(solution)/shard_map/pallas_call | solution.py:172
  58.5 3.5 %collective-permute-done.11 = bf16[384,512]{1,0:T(8,128)(2,1)S(1)} collective-permute-done((bf16[384,512]{1,0:T(8,128)(2,1)S(1)}, bf16[384,512]{1,0:T(8,128)(2,1)S(1)}, u32[]{:S(2)}, u32[]{:S(2)}) %collective-permute-start.11) | collective-permute-done | bytes 393248 | tf_op jit(solution)/shard_map/ppermute | solution.py:105
  61.9 8.3 %collective-permute-done.13 = bf16[384,512]{1,0:T(8,128)(2,1)S(1)} collective-permute-done((bf16[384,512]{1,0:T(8,128)(2,1)S(1)}, bf16[384,512]{1,0:T(8,128)(2,1)S(1)}, u32[]{:S(2)}, u32[]{:S(2)}) %collective-permute-start.13) | collective-permute-done | bytes 393248 | tf_op jit(solution)/shard_map/ppermute | solution.py:105
  70.2 1.1 %fusion.5 = bf16[384,512]{1,0:T(8,128)(2,1)} fusion(f32[384,512]{1,0:T(8,128)S(1)} %shard_map.87, bf16[384,512]{1,0:T(8,128)(2,1)S(1)} %collective-permute-done.13, bf16[384,512]{1,0:T(8,128)(2,1)S(1)} %collective-permute-done.11, bf16[384,512]{1,0:T(8,128)(2,1)S(1)} %collective-permute-done.10, bf16[1,384,512]{2,1,0:T(8,128)(2,1)S(1)} %collective-permute-done.8, ...), kind=kLoop, calls=%fused_computation.9 | loop fusion | flops 1966080 | bytes 3538944 | tf_op jit(solution)/shard_map/convert_element_type | solution.py:271
  (44 shorter events, 3.0 us)
Async XLA Ops:
  0.7 1.3 %copy-start = (bf16[384,1664]{1,0:T(8,128)(2,1)S(1)}, bf16[384,1664]{1,0:T(8,128)(2,1)}, u32[]{:S(2)}) copy-start(bf16[384,1664]{1,0:T(8,128)(2,1)} %hidden_ref.9) | copy-start | bytes 3833860
  2.0 8.6 %slice-start = ((s8[6815744]{0:T(1024)(128)(4,1)}), s8[4194304]{0:T(1024)(128)(4,1)S(1)}, s32[]{:S(2)}) async-start(s8[6815744]{0:T(1024)(128)(4,1)} %bitcast.49), calls=%async_computation | async-start | bytes 8388608
  5.1 5.3 %collective-permute-start = (bf16[1,384,512]{2,1,0:T(8,128)(2,1)S(1)}, bf16[1,384,512]{2,1,0:T(8,128)(2,1)S(1)}, u32[]{:S(2)}, u32[]{:S(2)}) collective-permute-start(bf16[1,384,512]{2,1,0:T(8,128)(2,1)S(1)} %get-tuple-element.32), channel_id=1, source_target_pairs={{0,1},{1,0},{2,3},{3,2},{4,5},{5,4},{6,7},{7,6},{8,9},{9,8},{10,11... | collective-permute-start | bytes 1179656 | tf_op jit(solution)/shard_map/ppermute | solution.py:105
  5.7 4.8 %copy-start.4 = (s32[384]{0:T(512)S(1)}, s32[384]{0:T(512)}, u32[]{:S(2)}) copy-start(s32[384]{0:T(512)} %param.12) | copy-start | bytes 4612
  5.7 5.0 %slice-start.1 = ((s8[6815744]{0:T(1024)(128)(4,1)}), s8[2621440]{0:T(1024)(128)(4,1)S(1)}, s32[]{:S(2)}) async-start(s8[6815744]{0:T(1024)(128)(4,1)} %bitcast.49), calls=%async_computation.1 | async-start | bytes 5242880
  10.3 16.1 %collective-permute-start.2 = (bf16[2,384,512]{2,1,0:T(8,128)(2,1)S(1)}, bf16[2,384,512]{2,1,0:T(8,128)(2,1)S(1)}, u32[]{:S(2)}, u32[]{:S(2)}) collective-permute-start(bf16[2,384,512]{2,1,0:T(8,128)(2,1)S(1)} %get-tuple-element.39), channel_id=1, source_target_pairs={{0,1},{1,0},{2,3},{3,2},{4,5},{5,4},{6,7},{7,6},{8,9},{9,8},{10,11... | collective-permute-start | bytes 2359304 | tf_op jit(solution)/shard_map/ppermute | solution.py:105
  15.0 11.3 %collective-permute-start.1 = (f32[64,384]{1,0:T(8,128)S(1)}, f32[64,384]{1,0:T(8,128)S(1)}, u32[]{:S(2)}, u32[]{:S(2)}) collective-permute-start(f32[64,384]{1,0:T(8,128)S(1)} %bitcast.46), channel_id=1, source_target_pairs={{0,8},{1,9},{2,10},{3,11},{4,12},{5,13},{6,14},{7,15},{8,0},{9,1},... | collective-permute-start | bytes 294920 | tf_op jit(solution)/shard_map/ppermute | solution.py:105
  19.2 10.8 %collective-permute-start.3 = (bf16[384,512]{1,0:T(8,128)(2,1)S(1)}, bf16[384,512]{1,0:T(8,128)(2,1)S(1)}, u32[]{:S(2)}, u32[]{:S(2)}) collective-permute-start(bf16[384,512]{1,0:T(8,128)(2,1)S(1)} %fusion.10.refs_1_), channel_id=1, source_target_pairs={{0,2},{1,3},{2,0},{3,1},{4,6},{5,7},{6,4},{7,5},{8,10},{9,11},{10,... | collective-permute-start | bytes 1179656 | tf_op jit(solution)/shard_map/ppermute | solution.py:105
  26.2 12.7 %collective-permute-start.6 = (bf16[2,384,512]{2,1,0:T(8,128)(2,1)S(1)}, bf16[2,384,512]{2,1,0:T(8,128)(2,1)S(1)}, u32[]{:S(2)}, u32[]{:S(2)}) collective-permute-start(bf16[2,384,512]{2,1,0:T(8,128)(2,1)S(1)} %get-tuple-element.44), channel_id=1, source_target_pairs={{0,1},{1,0},{2,3},{3,2},{4,5},{5,4},{6,7},{7,6},{8,9},{9,8},{10,11... | collective-permute-start | bytes 2359304 | tf_op jit(solution)/shard_map/ppermute | solution.py:105
  30.1 11.3 %collective-permute-start.4 = (bf16[448,512]{1,0:T(8,128)(2,1)S(1)}, bf16[448,512]{1,0:T(8,128)(2,1)S(1)}, u32[]{:S(2)}, u32[]{:S(2)}) collective-permute-start(bf16[448,512]{1,0:T(8,128)(2,1)S(1)} %fusion.9), channel_id=1, source_target_pairs={{0,4},{1,5},{2,6},{3,7},{4,0},{5,1},{6,2},{7,3},{8,12},{9,13},{10,... | collective-permute-start | bytes 1376264 | tf_op jit(solution)/shard_map/ppermute | solution.py:105
  31.8 11.3 %collective-permute-start.7 = (bf16[384,512]{1,0:T(8,128)(2,1)S(1)}, bf16[384,512]{1,0:T(8,128)(2,1)S(1)}, u32[]{:S(2)}, u32[]{:S(2)}) collective-permute-start(bf16[384,512]{1,0:T(8,128)(2,1)S(1)} %fusion.11.refs_1_), channel_id=1, source_target_pairs={{0,2},{1,3},{2,0},{3,1},{4,6},{5,7},{6,4},{7,5},{8,10},{9,11},{10,... | collective-permute-start | bytes 1179656 | tf_op jit(solution)/shard_map/ppermute | solution.py:105
  38.9 13.9 %collective-permute-start.9 = (bf16[2,384,512]{2,1,0:T(8,128)(2,1)S(1)}, bf16[2,384,512]{2,1,0:T(8,128)(2,1)S(1)}, u32[]{:S(2)}, u32[]{:S(2)}) collective-permute-start(bf16[2,384,512]{2,1,0:T(8,128)(2,1)S(1)} %get-tuple-element.50), channel_id=1, source_target_pairs={{0,1},{1,0},{2,3},{3,2},{4,5},{5,4},{6,7},{7,6},{8,9},{9,8},{10,11... | collective-permute-start | bytes 2359304 | tf_op jit(solution)/shard_map/ppermute | solution.py:105
  39.1 13.8 %collective-permute-start.12 = (bf16[384,512]{1,0:T(8,128)(2,1)S(1)}, bf16[384,512]{1,0:T(8,128)(2,1)S(1)}, u32[]{:S(2)}, u32[]{:S(2)}) collective-permute-start(bf16[384,512]{1,0:T(8,128)(2,1)S(1)} %fusion.12.refs_1_), channel_id=1, source_target_pairs={{0,2},{1,3},{2,0},{3,1},{4,6},{5,7},{6,4},{7,5},{8,10},{9,11},{10,... | collective-permute-start | bytes 1179656 | tf_op jit(solution)/shard_map/ppermute | solution.py:105
  41.5 11.3 %collective-permute-start.5 = (f32[64,384]{1,0:T(8,128)S(1)}, f32[64,384]{1,0:T(8,128)S(1)}, u32[]{:S(2)}, u32[]{:S(2)}) collective-permute-start(f32[64,384]{1,0:T(8,128)S(1)} %convert_add_fusion.refs_3_), channel_id=1, source_target_pairs={{0,2},{1,3},{2,0},{3,1},{4,6},{5,7},{6,4},{7,5},{8,10},{9,11},{10,... | collective-permute-start | bytes 294920 | tf_op jit(solution)/shard_map/ppermute | solution.py:105
  43.3 18.6 %collective-permute-start.11 = (bf16[384,512]{1,0:T(8,128)(2,1)S(1)}, bf16[384,512]{1,0:T(8,128)(2,1)S(1)}, u32[]{:S(2)}, u32[]{:S(2)}) collective-permute-start(bf16[384,512]{1,0:T(8,128)(2,1)S(1)} %fusion.7.refs_2_), channel_id=1, source_target_pairs={{0,8},{1,9},{2,10},{3,11},{4,12},{5,13},{6,14},{7,15},{8,0},{9,1},... | collective-permute-start | bytes 1179656 | tf_op jit(solution)/shard_map/ppermute | solution.py:105
  49.1 6.5 %copy-start.1 = (bf16[32,64,512]{2,1,0:T(8,128)(2,1)S(1)}, bf16[32,64,512]{2,1,0:T(8,128)(2,1)}, u32[]{:S(2)}) copy-start(bf16[32,64,512]{2,1,0:T(8,128)(2,1)} %param.11) | copy-start | bytes 6291460
  49.1 6.5 %copy-start.2 = (s32[32]{0:T(128)S(1)}, s32[32]{0:T(128)}, u32[]{:S(2)}) copy-start(s32[32]{0:T(128)} %first_ref.1) | copy-start | bytes 388
  49.1 6.5 %copy-start.3 = (s32[32]{0:T(128)S(1)}, s32[32]{0:T(128)}, u32[]{:S(2)}) copy-start(s32[32]{0:T(128)} %length_ref.1) | copy-start | bytes 388
  49.2 9.3 %collective-permute-start.8 = (bf16[1,384,512]{2,1,0:T(8,128)(2,1)S(1)}, bf16[1,384,512]{2,1,0:T(8,128)(2,1)S(1)}, u32[]{:S(2)}, u32[]{:S(2)}) collective-permute-start(bf16[1,384,512]{2,1,0:T(8,128)(2,1)S(1)} %get-tuple-element.49), channel_id=1, source_target_pairs={{0,1},{1,0},{2,3},{3,2},{4,5},{5,4},{6,7},{7,6},{8,9},{9,8},{10,11... | collective-permute-start | bytes 1179656 | tf_op jit(solution)/shard_map/ppermute | solution.py:105
  53.1 17.2 %collective-permute-start.13 = (bf16[384,512]{1,0:T(8,128)(2,1)S(1)}, bf16[384,512]{1,0:T(8,128)(2,1)S(1)}, u32[]{:S(2)}, u32[]{:S(2)}) collective-permute-start(bf16[384,512]{1,0:T(8,128)(2,1)S(1)} %fusion.1), channel_id=1, source_target_pairs={{0,4},{1,5},{2,6},{3,7},{4,0},{5,1},{6,2},{7,3},{8,12},{9,13},{10,... | collective-permute-start | bytes 1179656 | tf_op jit(solution)/shard_map/ppermute | solution.py:105
  53.6 16.7 %collective-permute-start.10 = (bf16[384,512]{1,0:T(8,128)(2,1)S(1)}, bf16[384,512]{1,0:T(8,128)(2,1)S(1)}, u32[]{:S(2)}, u32[]{:S(2)}) collective-permute-start(bf16[384,512]{1,0:T(8,128)(2,1)S(1)} %fusion.13), channel_id=1, source_target_pairs={{0,2},{1,3},{2,0},{3,1},{4,6},{5,7},{6,4},{7,5},{8,10},{9,11},{10,... | collective-permute-start | bytes 1179656 | tf_op jit(solution)/shard_map/ppermute | solution.py:105
  54.3 1.4 %collective-permute-start.14 = (f32[64,384]{1,0:T(8,128)S(1)}, f32[64,384]{1,0:T(8,128)S(1)}, u32[]{:S(2)}, u32[]{:S(2)}) collective-permute-start(f32[64,384]{1,0:T(8,128)S(1)} %add.99), channel_id=1, source_target_pairs={{0,1},{1,0},{2,3},{3,2},{4,5},{5,4},{6,7},{7,6},{8,9},{9,8},{10,11... | collective-permute-start | bytes 294920 | tf_op jit(solution)/shard_map/ppermute | solution.py:105

commit v10 on v9

--- a/solution.py
+++ b/solution.py
@@ -11,6 +11,7 @@
 WINDOW = 128
 TOGETHER = 4
 FLOPS = 2_500_000_000
+FIRST_FLOPS = 10_000_000_000
 EXPAND_FLOPS = 1_000_000
 
 
@@ -67,7 +68,7 @@
         copy(targets).wait()
 
 
-def product(table, hidden, down_matrix, buffer, base, sent, kept, width, last, earlier):
+def product(table, hidden, down_matrix, buffer, base, sent, kept, width, last, flops, earlier):
     rows, depth = hidden.shape
     first = buffer is None
     vmem = pl.BlockSpec(memory_space=pltpu.VMEM)
@@ -96,7 +97,7 @@
         scratch_shapes=[pltpu.SemaphoreType.DMA((2,))],
         input_output_aliases={} if first else {3: place},
         compiler_params=pltpu.CompilerParams(vmem_limit_bytes=VMEM_LIMIT),
-        cost_estimate=pl.CostEstimate(flops=FLOPS, bytes_accessed=1024, transcendentals=0),
+        cost_estimate=pl.CostEstimate(flops=flops, bytes_accessed=1024, transcendentals=0),
     )(table, hidden, down_matrix, *([] if first else [buffer]), *earlier)
     return results[0] if sent else None, results[place - 1] if kept else None, results[place]
 
@@ -204,11 +205,12 @@
 
     kept_home, crossed, incoming = {}, {}, {}
 
-    packed, steps = None, [*(4 << at for at in reversed(range((units - 1).bit_length()))), near, core]
+    packed, steps = None, [near, *(4 << at for at in range((units - 1).bit_length())), core]
 
     def send(value, bit, carry):
         nonlocal packed
-        if not carry or packed is None or steps[:1] != [bit]:
+        fits = packed is not None and packed.shape[1] <= value.shape[1]
+        if not carry or not fits or steps[:1] != [bit]:
             return swap(value, bit, total), None
         steps.pop(0)
         own, packed = packed, None
@@ -235,13 +237,14 @@
         order += [(unit + 1) * 4] * (unit < top) + [0] * (not unit)
     table = jnp.array(order, dtype=jnp.int32) ^ me
 
-    values, _, buffer = product(table, hidden, down_matrix, None, 0, 1, 0, width, False, [])
+    values, _, buffer = product(table, hidden, down_matrix, None, 0, 1, 0, width, False, FLOPS, [])
     base, ready = 1, []
     for unit in reversed(range(units)):
         arrived = swap(values, core, total)
         sent, kept = 1 + (unit > 0), 1 + (unit < top) + (not unit)
         values, results, buffer = product(
-            table, hidden, down_matrix, buffer, base, sent, kept, width, not unit, ready
+            table, hidden, down_matrix, buffer, base, sent, kept, width, not unit,
+            FIRST_FLOPS if unit == top - 1 else FLOPS, ready,
         )
         base += sent + kept
         if packed is not None and steps and steps[0] != core:

time: 71.8 us -> 75 us (1.045)
  waiting for transfers between devices: 21.8 us -> 26 us
  starting transfers between devices: 13.5 us -> 12.6 us
    ppermute x15, waiting for transfers between devices: 21.8 us -> 26 us  [swap(): lax.ppermute(value, 'tensor', [(place, place ^ bit) for place in range(to...]
    ppermute x15, starting transfers between devices: 13.5 us -> 12.6 us  [swap(): lax.ppermute(value, 'tensor', [(place, place ^ bit) for place in range(to...]
  transfers between devices with their start and end apart: 15 -> 15, of which waited for: 6 -> 6; matrix products, arithmetic and copies ran while one was open for 8% -> 7% of each run, Pallas kernels for 34% -> 32%
where the time goes in v10:
time: 75 us; the launch traced here: 74.6 us
  Pallas kernels  27.1 us (36%)
  waiting for transfers between devices  26 us (35%)
  starting transfers between devices  12.6 us (17%)
  matrix products  4.03 us (5%)
  other arithmetic  3.3 us (4%)
  local copies, waits for them, and re-layouts  1.33 us (2%)
    ppermute x15, waiting for transfers between devices, swap(): lax.ppermute(value, 'tensor', [(place, place ^ bit) for place in range(to...  26 us
    pallas_call x5, Pallas kernels, product(): pl.pallas_call(functools.partial(product_body, base=base, sent=sent, kept...  24.3 us
    ppermute x15, starting transfers between devices, swap(): lax.ppermute(value, 'tensor', [(place, place ^ bit) for place in range(to...  12.6 us
    unnamed x1, matrix products  4.03 us
    pallas_call x1, Pallas kernels, expand(): pl.pallas_call(expand_body, grid_spec=pltpu.PrefetchScalarGridSpec(num_sc...  2.78 us
  transfers between devices with their start and end apart: 15, of which 6 were waited for; matrix products, arithmetic and copies ran while one was open for 7% of the time, Pallas kernels for 32%

profile of v10, /device:TPU:0, one launch (start us, length us, event | category | flops | bytes accessed | tf_op | source)
XLA Modules:
  0.0 74.6 jit_solution(13470285257302347959)
XLA Ops:
  0.0 0.7 broadcast_xor_fusion.table_ref
  0.7 1.3 %copy-done = bf16[384,1664]{1,0:T(8,128)(2,1)S(1)} copy-done((bf16[384,1664]{1,0:T(8,128)(2,1)S(1)}, bf16[384,1664]{1,0:T(8,128)(2,1)}, u32[]{:S(2)}) %copy-start) | copy-done | bytes 1277976
  2.0 3.2 %shard_map.82 = (bf16[1,384,512]{2,1,0:T(8,128)(2,1)S(1)}, bf16[2,1664,512]{2,1,0:T(8,128)(2,1)S(1)}) custom-call(s32[16]{0:T(128)S(1)} %broadcast_xor_fusion.table_ref, bf16[384,1664]{1,0:T(8,128)(2,1)S(1)} %copy-done, bf16[1664,8192]{1,0:T(8,128)(2,1)} %down_ref.9), custom_call_target="tpu_custom_call" | custom-call | flops 2500000000 | bytes 1024 | tf_op jit(solution)/shard_map/pallas_call | solution.py:83
  5.1 0.5 collective-permute-start
  5.7 4.6 %shard_map.83 = (bf16[2,384,512]{2,1,0:T(8,128)(2,1)S(1)}, f32[1,384,512]{2,1,0:T(8,128)S(1)}, bf16[2,1664,512]{2,1,0:T(8,128)(2,1)S(1)}) custom-call(s32[16]{0:T(128)S(1)} %broadcast_xor_fusion.table_ref, bf16[384,1664]{1,0:T(8,128)(2,1)S(1)} %copy-done, bf16[1664,8192]{1,0:T(8,128)(2,1)} %down_ref.9, ...), custom_call_target="tpu_custom_call", output_to_operand_aliasing={{2}: (3, {})} | custom-call | flops 2500000000 | bytes 1024 | tf_op jit(solution)/shard_map/pallas_call | solution.py:83
  10.6 4.0 %fusion.15 = f32[384,2048]{0,1:S(1)} fusion(bf16[384,1664]{1,0:T(8,128)(2,1)S(1)} %copy-done, bf16[1664,2048]{0,1:T(8,128)(2,1)S(1)} %bitcast.51), kind=kOutput, calls=%fused_computation.29 | convolution fusion | flops 2617245696 | bytes 11239424
  15.0 3.0 %collective-permute-start.1 = (f32[64,384]{1,0:T(8,128)S(1)}, f32[64,384]{1,0:T(8,128)S(1)}, u32[]{:S(2)}, u32[]{:S(2)}) collective-permute-start(f32[64,384]{1,0:T(8,128)S(1)} %bitcast.46), channel_id=1, source_target_pairs={{0,2},{1,3},{2,0},{3,1},{4,6},{5,7},{6,4},{7,5},{8,10},{9,11},{10,... | collective-permute-start | bytes 294920 | tf_op jit(solution)/shard_map/ppermute | solution.py:106
  18.2 5.6 %shard_map.84 = (bf16[2,384,512]{2,1,0:T(8,128)(2,1)S(1)}, f32[2,384,512]{2,1,0:T(8,128)S(1)}, bf16[2,1664,512]{2,1,0:T(8,128)(2,1)S(1)}) custom-call(s32[16]{0:T(128)S(1)} %broadcast_xor_fusion.table_ref, bf16[384,1664]{1,0:T(8,128)(2,1)S(1)} %copy-done, bf16[1664,8192]{1,0:T(8,128)(2,1)} %down_ref.9, ...), custom_call_target="tpu_custom_call", output_to_operand_aliasing={{2}: (3, {})} | custom-call | flops 10000000000 | bytes 1024 | tf_op jit(solution)/shard_map/pallas_call | solution.py:83
  24.0 5.5 %collective-permute-done.3 = bf16[384,512]{1,0:T(8,128)(2,1)S(1)} collective-permute-done((bf16[384,512]{1,0:T(8,128)(2,1)S(1)}, bf16[384,512]{1,0:T(8,128)(2,1)S(1)}, u32[]{:S(2)}, u32[]{:S(2)}) %collective-permute-start.3) | collective-permute-done | bytes 393248 | tf_op jit(solution)/shard_map/ppermute | solution.py:106
  29.7 1.9 %collective-permute-start.4 = (bf16[448,512]{1,0:T(8,128)(2,1)S(1)}, bf16[448,512]{1,0:T(8,128)(2,1)S(1)}, u32[]{:S(2)}, u32[]{:S(2)}) collective-permute-start(bf16[448,512]{1,0:T(8,128)(2,1)S(1)} %fusion.9), channel_id=1, source_target_pairs={{0,4},{1,5},{2,6},{3,7},{4,0},{5,1},{6,2},{7,3},{8,12},{9,13},{10,... | collective-permute-start | bytes 1376264 | tf_op jit(solution)/shard_map/ppermute | solution.py:106
  31.6 1.5 %collective-permute-start.7 = (bf16[384,512]{1,0:T(8,128)(2,1)S(1)}, bf16[384,512]{1,0:T(8,128)(2,1)S(1)}, u32[]{:S(2)}, u32[]{:S(2)}) collective-permute-start(bf16[384,512]{1,0:T(8,128)(2,1)S(1)} %fusion.11.refs_1_), channel_id=1, source_target_pairs={{0,2},{1,3},{2,0},{3,1},{4,6},{5,7},{6,4},{7,5},{8,10},{9,11},{10,... | collective-permute-start | bytes 1179656 | tf_op jit(solution)/shard_map/ppermute | solution.py:106
  33.1 5.6 %shard_map.85 = (bf16[2,384,512]{2,1,0:T(8,128)(2,1)S(1)}, f32[2,384,512]{2,1,0:T(8,128)S(1)}, bf16[2,1664,512]{2,1,0:T(8,128)(2,1)S(1)}) custom-call(s32[16]{0:T(128)S(1)} %broadcast_xor_fusion.table_ref, bf16[384,1664]{1,0:T(8,128)(2,1)S(1)} %copy-done, bf16[1664,8192]{1,0:T(8,128)(2,1)} %down_ref.9, ...), custom_call_target="tpu_custom_call", output_to_operand_aliasing={{2}: (3, {})} | custom-call | flops 2500000000 | bytes 1024 | tf_op jit(solution)/shard_map/pallas_call | solution.py:83
  38.9 0.6 collective-permute-start.12
  39.4 2.2 %collective-permute-done.4 = bf16[448,512]{1,0:T(8,128)(2,1)S(1)} collective-permute-done((bf16[448,512]{1,0:T(8,128)(2,1)S(1)}, bf16[448,512]{1,0:T(8,128)(2,1)S(1)}, u32[]{:S(2)}, u32[]{:S(2)}) %collective-permute-start.4) | collective-permute-done | bytes 458784 | tf_op jit(solution)/shard_map/ppermute | solution.py:106
  41.7 2.6 %collective-permute-start.5 = (f32[64,384]{1,0:T(8,128)S(1)}, f32[64,384]{1,0:T(8,128)S(1)}, u32[]{:S(2)}, u32[]{:S(2)}) collective-permute-start(f32[64,384]{1,0:T(8,128)S(1)} %convert_add_fusion.refs_3_), channel_id=1, source_target_pairs={{0,8},{1,9},{2,10},{3,11},{4,12},{5,13},{6,14},{7,15},{8,0},{9,1},... | collective-permute-start | bytes 294920 | tf_op jit(solution)/shard_map/ppermute | solution.py:106
  44.5 0.4 collective-permute-start.11
  45.0 5.4 %shard_map.86 = (bf16[1,384,512]{2,1,0:T(8,128)(2,1)S(1)}, f32[3,384,512]{2,1,0:T(8,128)S(1)}, bf16[2,1664,512]{2,1,0:T(8,128)(2,1)S(1)}) custom-call(s32[16]{0:T(128)S(1)} %broadcast_xor_fusion.table_ref, bf16[384,1664]{1,0:T(8,128)(2,1)S(1)} %copy-done, bf16[1664,8192]{1,0:T(8,128)(2,1)} %down_ref.9, ...), custom_call_target="tpu_custom_call", output_to_operand_aliasing={{2}: (3, {})} | custom-call | flops 2500000000 | bytes 1024 | tf_op jit(solution)/shard_map/pallas_call | solution.py:83
  50.5 7.3 %collective-permute-done.5 = f32[64,384]{1,0:T(8,128)S(1)} collective-permute-done((f32[64,384]{1,0:T(8,128)S(1)}, f32[64,384]{1,0:T(8,128)S(1)}, u32[]{:S(2)}, u32[]{:S(2)}) %collective-permute-start.5) | collective-permute-done | bytes 98336 | tf_op jit(solution)/shard_map/ppermute | solution.py:106
  58.2 1.5 %collective-permute-start.10 = (bf16[384,512]{1,0:T(8,128)(2,1)S(1)}, bf16[384,512]{1,0:T(8,128)(2,1)S(1)}, u32[]{:S(2)}, u32[]{:S(2)}) collective-permute-start(bf16[384,512]{1,0:T(8,128)(2,1)S(1)} %fusion.13), channel_id=1, source_target_pairs={{0,2},{1,3},{2,0},{3,1},{4,6},{5,7},{6,4},{7,5},{8,10},{9,11},{10,... | collective-permute-start | bytes 1179656 | tf_op jit(solution)/shard_map/ppermute | solution.py:106
  59.8 1.3 %collective-permute-done.14 = f32[64,384]{1,0:T(8,128)S(1)} collective-permute-done((f32[64,384]{1,0:T(8,128)S(1)}, f32[64,384]{1,0:T(8,128)S(1)}, u32[]{:S(2)}, u32[]{:S(2)}) %collective-permute-start.14) | collective-permute-done | bytes 98336 | tf_op jit(solution)/shard_map/ppermute | solution.py:106
  61.1 2.8 %shard_map.87 = f32[384,512]{1,0:T(8,128)S(1)} custom-call(s32[32]{0:T(128)S(1)} %copy-done.2, s32[32]{0:T(128)S(1)} %copy-done.3, f32[64,384]{1,0:T(8,128)S(1)} %add.100.packed_ref, bf16[2048,512]{1,0:T(8,128)(2,1)S(1)} %bitcast.45), custom_call_target="tpu_custom_call" | custom-call | flops 1000000 | bytes 1 | tf_op jit(solution)/shard_map/pallas_call | solution.py:173
  63.9 1.3 %collective-permute-done.11 = bf16[384,512]{1,0:T(8,128)(2,1)S(1)} collective-permute-done((bf16[384,512]{1,0:T(8,128)(2,1)S(1)}, bf16[384,512]{1,0:T(8,128)(2,1)S(1)}, u32[]{:S(2)}, u32[]{:S(2)}) %collective-permute-start.11) | collective-permute-done | bytes 393248 | tf_op jit(solution)/shard_map/ppermute | solution.py:106
  65.2 8.3 %collective-permute-done.13 = bf16[384,512]{1,0:T(8,128)(2,1)S(1)} collective-permute-done((bf16[384,512]{1,0:T(8,128)(2,1)S(1)}, bf16[384,512]{1,0:T(8,128)(2,1)S(1)}, u32[]{:S(2)}, u32[]{:S(2)}) %collective-permute-start.13) | collective-permute-done | bytes 393248 | tf_op jit(solution)/shard_map/ppermute | solution.py:106
  73.5 1.1 %fusion.5 = bf16[384,512]{1,0:T(8,128)(2,1)} fusion(f32[384,512]{1,0:T(8,128)S(1)} %shard_map.87, bf16[384,512]{1,0:T(8,128)(2,1)S(1)} %collective-permute-done.13, bf16[384,512]{1,0:T(8,128)(2,1)S(1)} %collective-permute-done.11, bf16[384,512]{1,0:T(8,128)(2,1)S(1)} %collective-permute-done.10, bf16[1,384,512]{2,1,0:T(8,128)(2,1)S(1)} %collective-permute-done.8, ...), kind=kLoop, calls=%fused_computation.9 | loop fusion | flops 1966080 | bytes 3538944 | tf_op jit(solution)/shard_map/convert_element_type | solution.py:274
  (44 shorter events, 2.1 us)
Async XLA Ops:
  0.7 1.3 %copy-start = (bf16[384,1664]{1,0:T(8,128)(2,1)S(1)}, bf16[384,1664]{1,0:T(8,128)(2,1)}, u32[]{:S(2)}) copy-start(bf16[384,1664]{1,0:T(8,128)(2,1)} %hidden_ref.9) | copy-start | bytes 3833860
  2.0 8.6 %slice-start = ((s8[6815744]{0:T(1024)(128)(4,1)}), s8[4194304]{0:T(1024)(128)(4,1)S(1)}, s32[]{:S(2)}) async-start(s8[6815744]{0:T(1024)(128)(4,1)} %bitcast.49), calls=%async_computation | async-start | bytes 8388608
  5.1 5.3 %collective-permute-start = (bf16[1,384,512]{2,1,0:T(8,128)(2,1)S(1)}, bf16[1,384,512]{2,1,0:T(8,128)(2,1)S(1)}, u32[]{:S(2)}, u32[]{:S(2)}) collective-permute-start(bf16[1,384,512]{2,1,0:T(8,128)(2,1)S(1)} %get-tuple-element.32), channel_id=1, source_target_pairs={{0,1},{1,0},{2,3},{3,2},{4,5},{5,4},{6,7},{7,6},{8,9},{9,8},{10,11... | collective-permute-start | bytes 1179656 | tf_op jit(solution)/shard_map/ppermute | solution.py:106
  5.7 4.8 %copy-start.4 = (s32[384]{0:T(512)S(1)}, s32[384]{0:T(512)}, u32[]{:S(2)}) copy-start(s32[384]{0:T(512)} %param.12) | copy-start | bytes 4612
  5.7 5.0 %slice-start.1 = ((s8[6815744]{0:T(1024)(128)(4,1)}), s8[2621440]{0:T(1024)(128)(4,1)S(1)}, s32[]{:S(2)}) async-start(s8[6815744]{0:T(1024)(128)(4,1)} %bitcast.49), calls=%async_computation.1 | async-start | bytes 5242880
  10.3 13.5 %collective-permute-start.2 = (bf16[2,384,512]{2,1,0:T(8,128)(2,1)S(1)}, bf16[2,384,512]{2,1,0:T(8,128)(2,1)S(1)}, u32[]{:S(2)}, u32[]{:S(2)}) collective-permute-start(bf16[2,384,512]{2,1,0:T(8,128)(2,1)S(1)} %get-tuple-element.39), channel_id=1, source_target_pairs={{0,1},{1,0},{2,3},{3,2},{4,5},{5,4},{6,7},{7,6},{8,9},{9,8},{10,11... | collective-permute-start | bytes 2359304 | tf_op jit(solution)/shard_map/ppermute | solution.py:106
  15.0 8.8 %collective-permute-start.1 = (f32[64,384]{1,0:T(8,128)S(1)}, f32[64,384]{1,0:T(8,128)S(1)}, u32[]{:S(2)}, u32[]{:S(2)}) collective-permute-start(f32[64,384]{1,0:T(8,128)S(1)} %bitcast.46), channel_id=1, source_target_pairs={{0,2},{1,3},{2,0},{3,1},{4,6},{5,7},{6,4},{7,5},{8,10},{9,11},{10,... | collective-permute-start | bytes 294920 | tf_op jit(solution)/shard_map/ppermute | solution.py:106
  18.1 11.4 %collective-permute-start.3 = (bf16[384,512]{1,0:T(8,128)(2,1)S(1)}, bf16[384,512]{1,0:T(8,128)(2,1)S(1)}, u32[]{:S(2)}, u32[]{:S(2)}) collective-permute-start(bf16[384,512]{1,0:T(8,128)(2,1)S(1)} %fusion.10.refs_1_), channel_id=1, source_target_pairs={{0,2},{1,3},{2,0},{3,1},{4,6},{5,7},{6,4},{7,5},{8,10},{9,11},{10,... | collective-permute-start | bytes 1179656 | tf_op jit(solution)/shard_map/ppermute | solution.py:106
  23.7 15.0 %collective-permute-start.6 = (bf16[2,384,512]{2,1,0:T(8,128)(2,1)S(1)}, bf16[2,384,512]{2,1,0:T(8,128)(2,1)S(1)}, u32[]{:S(2)}, u32[]{:S(2)}) collective-permute-start(bf16[2,384,512]{2,1,0:T(8,128)(2,1)S(1)} %get-tuple-element.44), channel_id=1, source_target_pairs={{0,1},{1,0},{2,3},{3,2},{4,5},{5,4},{6,7},{7,6},{8,9},{9,8},{10,11... | collective-permute-start | bytes 2359304 | tf_op jit(solution)/shard_map/ppermute | solution.py:106
  29.7 12.0 %collective-permute-start.4 = (bf16[448,512]{1,0:T(8,128)(2,1)S(1)}, bf16[448,512]{1,0:T(8,128)(2,1)S(1)}, u32[]{:S(2)}, u32[]{:S(2)}) collective-permute-start(bf16[448,512]{1,0:T(8,128)(2,1)S(1)} %fusion.9), channel_id=1, source_target_pairs={{0,4},{1,5},{2,6},{3,7},{4,0},{5,1},{6,2},{7,3},{8,12},{9,13},{10,... | collective-permute-start | bytes 1376264 | tf_op jit(solution)/shard_map/ppermute | solution.py:106
  31.6 12.8 %collective-permute-start.7 = (bf16[384,512]{1,0:T(8,128)(2,1)S(1)}, bf16[384,512]{1,0:T(8,128)(2,1)S(1)}, u32[]{:S(2)}, u32[]{:S(2)}) collective-permute-start(bf16[384,512]{1,0:T(8,128)(2,1)S(1)} %fusion.11.refs_1_), channel_id=1, source_target_pairs={{0,2},{1,3},{2,0},{3,1},{4,6},{5,7},{6,4},{7,5},{8,10},{9,11},{10,... | collective-permute-start | bytes 1179656 | tf_op jit(solution)/shard_map/ppermute | solution.py:106
  38.7 19.2 %collective-permute-start.9 = (bf16[2,384,512]{2,1,0:T(8,128)(2,1)S(1)}, bf16[2,384,512]{2,1,0:T(8,128)(2,1)S(1)}, u32[]{:S(2)}, u32[]{:S(2)}) collective-permute-start(bf16[2,384,512]{2,1,0:T(8,128)(2,1)S(1)} %get-tuple-element.50), channel_id=1, source_target_pairs={{0,1},{1,0},{2,3},{3,2},{4,5},{5,4},{6,7},{7,6},{8,9},{9,8},{10,11... | collective-permute-start | bytes 2359304 | tf_op jit(solution)/shard_map/ppermute | solution.py:106
  38.9 19.1 %collective-permute-start.12 = (bf16[384,512]{1,0:T(8,128)(2,1)S(1)}, bf16[384,512]{1,0:T(8,128)(2,1)S(1)}, u32[]{:S(2)}, u32[]{:S(2)}) collective-permute-start(bf16[384,512]{1,0:T(8,128)(2,1)S(1)} %fusion.12.refs_1_), channel_id=1, source_target_pairs={{0,2},{1,3},{2,0},{3,1},{4,6},{5,7},{6,4},{7,5},{8,10},{9,11},{10,... | collective-permute-start | bytes 1179656 | tf_op jit(solution)/shard_map/ppermute | solution.py:106
  41.7 16.1 %collective-permute-start.5 = (f32[64,384]{1,0:T(8,128)S(1)}, f32[64,384]{1,0:T(8,128)S(1)}, u32[]{:S(2)}, u32[]{:S(2)}) collective-permute-start(f32[64,384]{1,0:T(8,128)S(1)} %convert_add_fusion.refs_3_), channel_id=1, source_target_pairs={{0,8},{1,9},{2,10},{3,11},{4,12},{5,13},{6,14},{7,15},{8,0},{9,1},... | collective-permute-start | bytes 294920 | tf_op jit(solution)/shard_map/ppermute | solution.py:106
  44.5 20.7 %collective-permute-start.11 = (bf16[384,512]{1,0:T(8,128)(2,1)S(1)}, bf16[384,512]{1,0:T(8,128)(2,1)S(1)}, u32[]{:S(2)}, u32[]{:S(2)}) collective-permute-start(bf16[384,512]{1,0:T(8,128)(2,1)S(1)} %fusion.7.refs_2_), channel_id=1, source_target_pairs={{0,8},{1,9},{2,10},{3,11},{4,12},{5,13},{6,14},{7,15},{8,0},{9,1},... | collective-permute-start | bytes 1179656 | tf_op jit(solution)/shard_map/ppermute | solution.py:106
  50.4 10.7 %copy-start.1 = (bf16[32,64,512]{2,1,0:T(8,128)(2,1)S(1)}, bf16[32,64,512]{2,1,0:T(8,128)(2,1)}, u32[]{:S(2)}) copy-start(bf16[32,64,512]{2,1,0:T(8,128)(2,1)} %param.11) | copy-start | bytes 6291460
  50.4 10.7 %copy-start.2 = (s32[32]{0:T(128)S(1)}, s32[32]{0:T(128)}, u32[]{:S(2)}) copy-start(s32[32]{0:T(128)} %first_ref.1) | copy-start | bytes 388
  50.4 10.7 %copy-start.3 = (s32[32]{0:T(128)S(1)}, s32[32]{0:T(128)}, u32[]{:S(2)}) copy-start(s32[32]{0:T(128)} %length_ref.1) | copy-start | bytes 388
  50.4 13.5 %collective-permute-start.8 = (bf16[1,384,512]{2,1,0:T(8,128)(2,1)S(1)}, bf16[1,384,512]{2,1,0:T(8,128)(2,1)S(1)}, u32[]{:S(2)}, u32[]{:S(2)}) collective-permute-start(bf16[1,384,512]{2,1,0:T(8,128)(2,1)S(1)} %get-tuple-element.49), channel_id=1, source_target_pairs={{0,1},{1,0},{2,3},{3,2},{4,5},{5,4},{6,7},{7,6},{8,9},{9,8},{10,11... | collective-permute-start | bytes 1179656 | tf_op jit(solution)/shard_map/ppermute | solution.py:106
  58.1 15.4 %collective-permute-start.13 = (bf16[384,512]{1,0:T(8,128)(2,1)S(1)}, bf16[384,512]{1,0:T(8,128)(2,1)S(1)}, u32[]{:S(2)}, u32[]{:S(2)}) collective-permute-start(bf16[384,512]{1,0:T(8,128)(2,1)S(1)} %fusion.1), channel_id=1, source_target_pairs={{0,4},{1,5},{2,6},{3,7},{4,0},{5,1},{6,2},{7,3},{8,12},{9,13},{10,... | collective-permute-start | bytes 1179656 | tf_op jit(solution)/shard_map/ppermute | solution.py:106
  58.2 15.3 %collective-permute-start.10 = (bf16[384,512]{1,0:T(8,128)(2,1)S(1)}, bf16[384,512]{1,0:T(8,128)(2,1)S(1)}, u32[]{:S(2)}, u32[]{:S(2)}) collective-permute-start(bf16[384,512]{1,0:T(8,128)(2,1)S(1)} %fusion.13), channel_id=1, source_target_pairs={{0,2},{1,3},{2,0},{3,1},{4,6},{5,7},{6,4},{7,5},{8,10},{9,11},{10,... | collective-permute-start | bytes 1179656 | tf_op jit(solution)/shard_map/ppermute | solution.py:106
  59.7 1.4 %collective-permute-start.14 = (f32[64,384]{1,0:T(8,128)S(1)}, f32[64,384]{1,0:T(8,128)S(1)}, u32[]{:S(2)}, u32[]{:S(2)}) collective-permute-start(f32[64,384]{1,0:T(8,128)S(1)} %add.99), channel_id=1, source_target_pairs={{0,1},{1,0},{2,3},{3,2},{4,5},{5,4},{6,7},{7,6},{8,9},{9,8},{10,11... | collective-permute-start | bytes 294920 | tf_op jit(solution)/shard_map/ppermute | solution.py:106

commit v11 on v10

--- a/solution.py
+++ b/solution.py
@@ -106,17 +106,6 @@
     return lax.ppermute(value, "tensor", [(place, place ^ bit) for place in range(total)])
 
 
-def attach(value, packed):
-    below = jnp.pad(packed.astype(jnp.bfloat16), ((0, 0), (0, value.shape[1] - packed.shape[1])))
-    return jnp.concatenate([value, below])
-
-
-def detach(value, packed):
-    height, columns = packed.shape
-    above = value.shape[0] - height
-    return value[:above], value[above:, :columns].astype(jnp.float32)
-
-
 def for_each_window(first_ref, length_ref, group, rows, body):
     window = min(WINDOW, rows)
     adapters = [group * TOGETHER + at for at in range(TOGETHER)]
@@ -207,27 +196,15 @@
 
     packed, steps = None, [near, *(4 << at for at in range((units - 1).bit_length())), core]
 
-    def send(value, bit, carry):
-        nonlocal packed
-        fits = packed is not None and packed.shape[1] <= value.shape[1]
-        if not carry or not fits or steps[:1] != [bit]:
-            return swap(value, bit, total), None
-        steps.pop(0)
-        own, packed = packed, None
-        arrived, shrinks = detach(swap(attach(value, own), bit, total), own)
-        return arrived, own + shrinks
-
     def settle(unit, arrived):
-        nonlocal packed
         value = kept_home[unit] + arrived.astype(jnp.float32) + crossed[unit].astype(jnp.float32)
-        for moved, shrinks in incoming.pop(unit, []):
+        for moved in incoming.pop(unit, []):
             value = value + moved.astype(jnp.float32)
-            packed = packed if shrinks is None else shrinks
         if not unit:
             return value
         bit = unit & -unit
         moving = value.astype(jnp.bfloat16)
-        incoming.setdefault(unit ^ bit, []).append(send(moving, 4 * bit, unit == top))
+        incoming.setdefault(unit ^ bit, []).append(swap(moving, 4 * bit, total))
         return moving
 
     top = units - 1
@@ -255,13 +232,13 @@
         if not unit:
             kept_home[0] = results[-1]
         leaving = (results[0] + arrived[0].astype(jnp.float32)).astype(jnp.bfloat16)
-        if unit == top:
+        if unit == max(top - 1, 0):
             late, leaving = lax.optimization_barrier((hidden, leaving))
         ready = [leaving]
         if unit < top:
             leaving, arrived = lax.optimization_barrier((leaving, arrived))
             ready.append(settle(unit + 1, arrived[1]))
-        if unit == top:
+        if unit == max(top - 1, 0):
             packed = shrink(late, shrink_matrices, row_adapter_index)
         if packed is not None:
             ready.append(packed)
@@ -269,7 +246,8 @@
     kept = [settle(0, swap(values, core, total)[0])]
 
     for bit in steps:
-        packed = packed + swap(packed, bit, total)
+        kind = jnp.bfloat16 if bit > near else jnp.float32
+        packed = packed + swap(packed.astype(kind), bit, total).astype(jnp.float32)
     adapter_output = expand(packed, expand_matrices, segment_first_row, segment_length)
     return (kept[0] + adapter_output).astype(jnp.bfloat16)
 

time: 75 us -> 73.3 us (0.977)
  waiting for transfers between devices: 26 us -> 22.8 us
  starting transfers between devices: 12.6 us -> 14.5 us
    ppermute x15 -> x16, waiting for transfers between devices: 26 us -> 22.8 us  [swap(): lax.ppermute(value, 'tensor', [(place, place ^ bit) for place in range(to...]
    ppermute x15 -> x16, starting transfers between devices: 12.6 us -> 14.5 us  [swap(): lax.ppermute(value, 'tensor', [(place, place ^ bit) for place in range(to...]
  transfers between devices with their start and end apart: 15 -> 16, of which waited for: 6 -> 5; matrix products, arithmetic and copies ran while one was open for 7% -> 8% of each run, Pallas kernels for 32% -> 33%
where the time goes in v11:
time: 73.3 us; the launch traced here: 72.9 us
  Pallas kernels  26.7 us (36%)
  waiting for transfers between devices  22.8 us (31%)
  starting transfers between devices  14.5 us (20%)
  matrix products  3.92 us (5%)
  other arithmetic  3.39 us (5%)
  local copies, waits for them, and re-layouts  1.34 us (2%)
    pallas_call x5, Pallas kernels, product(): pl.pallas_call(functools.partial(product_body, base=base, sent=sent, kept...  24 us
    ppermute x16, waiting for transfers between devices, swap(): lax.ppermute(value, 'tensor', [(place, place ^ bit) for place in range(to...  22.8 us
    ppermute x16, starting transfers between devices, swap(): lax.ppermute(value, 'tensor', [(place, place ^ bit) for place in range(to...  14.5 us
    unnamed x1, matrix products  3.92 us
    pallas_call x1, Pallas kernels, expand(): pl.pallas_call(expand_body, grid_spec=pltpu.PrefetchScalarGridSpec(num_sc...  2.78 us
  transfers between devices with their start and end apart: 16, of which 5 were waited for; matrix products, arithmetic and copies ran while one was open for 8% of the time, Pallas kernels for 33%

profile of v11, /device:TPU:0, one launch (start us, length us, event | category | flops | bytes accessed | tf_op | source)
XLA Modules:
  0.0 72.9 jit_solution(17199178866369029901)
XLA Ops:
  0.0 0.7 broadcast_xor_fusion.table_ref
  0.7 1.3 %copy-done = bf16[384,1664]{1,0:T(8,128)(2,1)S(1)} copy-done((bf16[384,1664]{1,0:T(8,128)(2,1)S(1)}, bf16[384,1664]{1,0:T(8,128)(2,1)}, u32[]{:S(2)}) %copy-start) | copy-done | bytes 1277976
  2.0 2.9 %shard_map.82 = (bf16[1,384,512]{2,1,0:T(8,128)(2,1)S(1)}, bf16[2,1664,512]{2,1,0:T(8,128)(2,1)S(1)}) custom-call(s32[16]{0:T(128)S(1)} %broadcast_xor_fusion.table_ref, bf16[384,1664]{1,0:T(8,128)(2,1)S(1)} %copy-done, bf16[1664,8192]{1,0:T(8,128)(2,1)} %down_ref.9), custom_call_target="tpu_custom_call" | custom-call | flops 2500000000 | bytes 1024 | tf_op jit(solution)/shard_map/pallas_call | solution.py:83
  5.4 4.4 %shard_map.83 = (bf16[2,384,512]{2,1,0:T(8,128)(2,1)S(1)}, f32[1,384,512]{2,1,0:T(8,128)S(1)}, bf16[2,1664,512]{2,1,0:T(8,128)(2,1)S(1)}) custom-call(s32[16]{0:T(128)S(1)} %broadcast_xor_fusion.table_ref, bf16[384,1664]{1,0:T(8,128)(2,1)S(1)} %copy-done, bf16[1664,8192]{1,0:T(8,128)(2,1)} %down_ref.9, ...), custom_call_target="tpu_custom_call", output_to_operand_aliasing={{2}: (3, {})} | custom-call | flops 2500000000 | bytes 1024 | tf_op jit(solution)/shard_map/pallas_call | solution.py:83
  10.1 3.0 %collective-permute-start.3 = (bf16[384,512]{1,0:T(8,128)(2,1)S(1)}, bf16[384,512]{1,0:T(8,128)(2,1)S(1)}, u32[]{:S(2)}, u32[]{:S(2)}) collective-permute-start(bf16[384,512]{1,0:T(8,128)(2,1)S(1)} %fusion.8.refs_1_), channel_id=1, source_target_pairs={{0,2},{1,3},{2,0},{3,1},{4,6},{5,7},{6,4},{7,5},{8,10},{9,11},{10,... | collective-permute-start | bytes 1179656 | tf_op jit(solution)/shard_map/ppermute | solution.py:106
  13.1 5.7 %shard_map.84 = (bf16[2,384,512]{2,1,0:T(8,128)(2,1)S(1)}, f32[2,384,512]{2,1,0:T(8,128)S(1)}, bf16[2,1664,512]{2,1,0:T(8,128)(2,1)S(1)}) custom-call(s32[16]{0:T(128)S(1)} %broadcast_xor_fusion.table_ref, bf16[384,1664]{1,0:T(8,128)(2,1)S(1)} %copy-done, bf16[1664,8192]{1,0:T(8,128)(2,1)} %down_ref.9, ...), custom_call_target="tpu_custom_call", output_to_operand_aliasing={{2}: (3, {})} | custom-call | flops 10000000000 | bytes 1024 | tf_op jit(solution)/shard_map/pallas_call | solution.py:83
  19.1 3.9 %fusion.13 = f32[384,2048]{0,1:S(1)} fusion(bf16[384,1664]{1,0:T(8,128)(2,1)S(1)} %copy-done, bf16[1664,2048]{0,1:T(8,128)(2,1)S(1)} %bitcast.47), kind=kOutput, calls=%fused_computation.26 | convolution fusion | flops 2617245696 | bytes 11239424
  23.4 0.7 collective-permute-start.2
  24.3 2.1 %collective-permute-start.7 = (bf16[384,512]{1,0:T(8,128)(2,1)S(1)}, bf16[384,512]{1,0:T(8,128)(2,1)S(1)}, u32[]{:S(2)}, u32[]{:S(2)}) collective-permute-start(bf16[384,512]{1,0:T(8,128)(2,1)S(1)} %fusion.7.refs_2_), channel_id=1, source_target_pairs={{0,4},{1,5},{2,6},{3,7},{4,0},{5,1},{6,2},{7,3},{8,12},{9,13},{10,... | collective-permute-start | bytes 1179656 | tf_op jit(solution)/shard_map/ppermute | solution.py:106
  26.4 5.6 %shard_map.85 = (bf16[2,384,512]{2,1,0:T(8,128)(2,1)S(1)}, f32[2,384,512]{2,1,0:T(8,128)S(1)}, bf16[2,1664,512]{2,1,0:T(8,128)(2,1)S(1)}) custom-call(s32[16]{0:T(128)S(1)} %broadcast_xor_fusion.table_ref, bf16[384,1664]{1,0:T(8,128)(2,1)S(1)} %copy-done, bf16[1664,8192]{1,0:T(8,128)(2,1)} %down_ref.9, ...), custom_call_target="tpu_custom_call", output_to_operand_aliasing={{2}: (3, {})} | custom-call | flops 2500000000 | bytes 1024 | tf_op jit(solution)/shard_map/pallas_call | solution.py:83
  32.0 1.0 %collective-permute-start.6 = (bf16[384,512]{1,0:T(8,128)(2,1)S(1)}, bf16[384,512]{1,0:T(8,128)(2,1)S(1)}, u32[]{:S(2)}, u32[]{:S(2)}) collective-permute-start(bf16[384,512]{1,0:T(8,128)(2,1)S(1)} %fusion.9.refs_1_), channel_id=1, source_target_pairs={{0,2},{1,3},{2,0},{3,1},{4,6},{5,7},{6,4},{7,5},{8,10},{9,11},{10,... | collective-permute-start | bytes 1179656 | tf_op jit(solution)/shard_map/ppermute | solution.py:106
  33.0 0.6 collective-permute-start.4
  33.7 0.7 collective-permute-start.12
  34.4 1.3 %collective-permute-done.7 = bf16[384,512]{1,0:T(8,128)(2,1)S(1)} collective-permute-done((bf16[384,512]{1,0:T(8,128)(2,1)S(1)}, bf16[384,512]{1,0:T(8,128)(2,1)S(1)}, u32[]{:S(2)}, u32[]{:S(2)}) %collective-permute-start.7) | collective-permute-done | bytes 393248 | tf_op jit(solution)/shard_map/ppermute | solution.py:106
  35.7 8.3 %collective-permute-done.6 = bf16[384,512]{1,0:T(8,128)(2,1)S(1)} collective-permute-done((bf16[384,512]{1,0:T(8,128)(2,1)S(1)}, bf16[384,512]{1,0:T(8,128)(2,1)S(1)}, u32[]{:S(2)}, u32[]{:S(2)}) %collective-permute-start.6) | collective-permute-done | bytes 393248 | tf_op jit(solution)/shard_map/ppermute | solution.py:106
  44.3 2.7 %collective-permute-start.11 = (bf16[384,512]{1,0:T(8,128)(2,1)S(1)}, bf16[384,512]{1,0:T(8,128)(2,1)S(1)}, u32[]{:S(2)}, u32[]{:S(2)}) collective-permute-start(bf16[384,512]{1,0:T(8,128)(2,1)S(1)} %fusion.6.refs_2_), channel_id=1, source_target_pairs={{0,8},{1,9},{2,10},{3,11},{4,12},{5,13},{6,14},{7,15},{8,0},{9,1},... | collective-permute-start | bytes 1179656 | tf_op jit(solution)/shard_map/ppermute | solution.py:106
  46.9 5.4 %shard_map.86 = (bf16[1,384,512]{2,1,0:T(8,128)(2,1)S(1)}, f32[3,384,512]{2,1,0:T(8,128)S(1)}, bf16[2,1664,512]{2,1,0:T(8,128)(2,1)S(1)}) custom-call(s32[16]{0:T(128)S(1)} %broadcast_xor_fusion.table_ref, bf16[384,1664]{1,0:T(8,128)(2,1)S(1)} %copy-done, bf16[1664,8192]{1,0:T(8,128)(2,1)} %down_ref.9, ...), custom_call_target="tpu_custom_call", output_to_operand_aliasing={{2}: (3, {})} | custom-call | flops 2500000000 | bytes 1024 | tf_op jit(solution)/shard_map/pallas_call | solution.py:83
  53.3 0.9 %collective-permute-start.10 = (bf16[384,512]{1,0:T(8,128)(2,1)S(1)}, bf16[384,512]{1,0:T(8,128)(2,1)S(1)}, u32[]{:S(2)}, u32[]{:S(2)}) collective-permute-start(bf16[384,512]{1,0:T(8,128)(2,1)S(1)} %fusion.11), channel_id=1, source_target_pairs={{0,2},{1,3},{2,0},{3,1},{4,6},{5,7},{6,4},{7,5},{8,10},{9,11},{10,... | collective-permute-start | bytes 1179656 | tf_op jit(solution)/shard_map/ppermute | solution.py:106
  54.3 1.5 %collective-permute-start.14 = (bf16[64,384]{1,0:T(8,128)(2,1)S(1)}, bf16[64,384]{1,0:T(8,128)(2,1)S(1)}, u32[]{:S(2)}, u32[]{:S(2)}) collective-permute-start(bf16[64,384]{1,0:T(8,128)(2,1)S(1)} %get-tuple-element.55), channel_id=1, source_target_pairs={{0,8},{1,9},{2,10},{3,11},{4,12},{5,13},{6,14},{7,15},{8,0},{9,1},... | collective-permute-start | bytes 147464 | tf_op jit(solution)/shard_map/ppermute | solution.py:106
  55.7 8.2 %collective-permute-done.14 = bf16[64,384]{1,0:T(8,128)(2,1)S(1)} collective-permute-done((bf16[64,384]{1,0:T(8,128)(2,1)S(1)}, bf16[64,384]{1,0:T(8,128)(2,1)S(1)}, u32[]{:S(2)}, u32[]{:S(2)}) %collective-permute-start.14) | collective-permute-done | bytes 49184 | tf_op jit(solution)/shard_map/ppermute | solution.py:106
  64.1 1.3 %collective-permute-done.15 = f32[64,384]{1,0:T(8,128)S(1)} collective-permute-done((f32[64,384]{1,0:T(8,128)S(1)}, f32[64,384]{1,0:T(8,128)S(1)}, u32[]{:S(2)}, u32[]{:S(2)}) %collective-permute-start.15) | collective-permute-done | bytes 98336 | tf_op jit(solution)/shard_map/ppermute | solution.py:106
  65.4 2.8 %shard_map.87 = f32[384,512]{1,0:T(8,128)S(1)} custom-call(s32[32]{0:T(128)S(1)} %copy-done.2, s32[32]{0:T(128)S(1)} %copy-done.3, f32[64,384]{1,0:T(8,128)S(1)} %add.98.packed_ref, bf16[2048,512]{1,0:T(8,128)(2,1)S(1)} %bitcast.41), custom_call_target="tpu_custom_call" | custom-call | flops 1000000 | bytes 1 | tf_op jit(solution)/shard_map/pallas_call | solution.py:162
  68.2 3.6 %collective-permute-done.13 = bf16[384,512]{1,0:T(8,128)(2,1)S(1)} collective-permute-done((bf16[384,512]{1,0:T(8,128)(2,1)S(1)}, bf16[384,512]{1,0:T(8,128)(2,1)S(1)}, u32[]{:S(2)}, u32[]{:S(2)}) %collective-permute-start.13) | collective-permute-done | bytes 393248 | tf_op jit(solution)/shard_map/ppermute | solution.py:106
  71.8 1.1 %fusion.4 = bf16[384,512]{1,0:T(8,128)(2,1)} fusion(f32[384,512]{1,0:T(8,128)S(1)} %shard_map.87, bf16[384,512]{1,0:T(8,128)(2,1)S(1)} %collective-permute-done.13, bf16[384,512]{1,0:T(8,128)(2,1)S(1)} %collective-permute-done.11, bf16[384,512]{1,0:T(8,128)(2,1)S(1)} %collective-permute-done.10, bf16[1,384,512]{2,1,0:T(8,128)(2,1)S(1)} %collective-permute-done.8, ...), kind=kLoop, calls=%fused_computation.7 | loop fusion | flops 1966080 | bytes 3538944 | tf_op jit(solution)/shard_map/convert_element_type | solution.py:252
  (45 shorter events, 3.1 us)
Async XLA Ops:
  0.7 1.3 %copy-start = (bf16[384,1664]{1,0:T(8,128)(2,1)S(1)}, bf16[384,1664]{1,0:T(8,128)(2,1)}, u32[]{:S(2)}) copy-start(bf16[384,1664]{1,0:T(8,128)(2,1)} %hidden_ref.9) | copy-start | bytes 3833860
  4.9 5.1 %collective-permute-start = (bf16[1,384,512]{2,1,0:T(8,128)(2,1)S(1)}, bf16[1,384,512]{2,1,0:T(8,128)(2,1)S(1)}, u32[]{:S(2)}, u32[]{:S(2)}) collective-permute-start(bf16[1,384,512]{2,1,0:T(8,128)(2,1)S(1)} %get-tuple-element.33), channel_id=1, source_target_pairs={{0,1},{1,0},{2,3},{3,2},{4,5},{5,4},{6,7},{7,6},{8,9},{9,8},{10,11... | collective-permute-start | bytes 1179656 | tf_op jit(solution)/shard_map/ppermute | solution.py:106
  5.4 4.6 %copy-start.4 = (s32[384]{0:T(512)S(1)}, s32[384]{0:T(512)}, u32[]{:S(2)}) copy-start(s32[384]{0:T(512)} %param.12) | copy-start | bytes 4612
  9.8 9.1 %collective-permute-start.1 = (bf16[2,384,512]{2,1,0:T(8,128)(2,1)S(1)}, bf16[2,384,512]{2,1,0:T(8,128)(2,1)S(1)}, u32[]{:S(2)}, u32[]{:S(2)}) collective-permute-start(bf16[2,384,512]{2,1,0:T(8,128)(2,1)S(1)} %get-tuple-element.35), channel_id=1, source_target_pairs={{0,1},{1,0},{2,3},{3,2},{4,5},{5,4},{6,7},{7,6},{8,9},{9,8},{10,11... | collective-permute-start | bytes 2359304 | tf_op jit(solution)/shard_map/ppermute | solution.py:106
  10.0 9.1 %slice-start = ((s8[6815744]{0:T(1024)(128)(4,1)}), s8[4194304]{0:T(1024)(128)(4,1)S(1)}, s32[]{:S(2)}) async-start(s8[6815744]{0:T(1024)(128)(4,1)} %bitcast.45), calls=%async_computation | async-start | bytes 8388608
  10.1 14.0 %collective-permute-start.3 = (bf16[384,512]{1,0:T(8,128)(2,1)S(1)}, bf16[384,512]{1,0:T(8,128)(2,1)S(1)}, u32[]{:S(2)}, u32[]{:S(2)}) collective-permute-start(bf16[384,512]{1,0:T(8,128)(2,1)S(1)} %fusion.8.refs_1_), channel_id=1, source_target_pairs={{0,2},{1,3},{2,0},{3,1},{4,6},{5,7},{6,4},{7,5},{8,10},{9,11},{10,... | collective-permute-start | bytes 1179656 | tf_op jit(solution)/shard_map/ppermute | solution.py:106
  13.1 6.0 %slice-start.1 = ((s8[6815744]{0:T(1024)(128)(4,1)}), s8[2621440]{0:T(1024)(128)(4,1)S(1)}, s32[]{:S(2)}) async-start(s8[6815744]{0:T(1024)(128)(4,1)} %bitcast.45), calls=%async_computation.1 | async-start | bytes 5242880
  18.9 14.7 %collective-permute-start.5 = (bf16[2,384,512]{2,1,0:T(8,128)(2,1)S(1)}, bf16[2,384,512]{2,1,0:T(8,128)(2,1)S(1)}, u32[]{:S(2)}, u32[]{:S(2)}) collective-permute-start(bf16[2,384,512]{2,1,0:T(8,128)(2,1)S(1)} %get-tuple-element.44), channel_id=1, source_target_pairs={{0,1},{1,0},{2,3},{3,2},{4,5},{5,4},{6,7},{7,6},{8,9},{9,8},{10,11... | collective-permute-start | bytes 2359304 | tf_op jit(solution)/shard_map/ppermute | solution.py:106
  23.4 9.6 %collective-permute-start.2 = (f32[64,384]{1,0:T(8,128)S(1)}, f32[64,384]{1,0:T(8,128)S(1)}, u32[]{:S(2)}, u32[]{:S(2)}) collective-permute-start(f32[64,384]{1,0:T(8,128)S(1)} %bitcast.42), channel_id=1, source_target_pairs={{0,2},{1,3},{2,0},{3,1},{4,6},{5,7},{6,4},{7,5},{8,10},{9,11},{10,... | collective-permute-start | bytes 294920 | tf_op jit(solution)/shard_map/ppermute | solution.py:106
  24.3 11.4 %collective-permute-start.7 = (bf16[384,512]{1,0:T(8,128)(2,1)S(1)}, bf16[384,512]{1,0:T(8,128)(2,1)S(1)}, u32[]{:S(2)}, u32[]{:S(2)}) collective-permute-start(bf16[384,512]{1,0:T(8,128)(2,1)S(1)} %fusion.7.refs_2_), channel_id=1, source_target_pairs={{0,4},{1,5},{2,6},{3,7},{4,0},{5,1},{6,2},{7,3},{8,12},{9,13},{10,... | collective-permute-start | bytes 1179656 | tf_op jit(solution)/shard_map/ppermute | solution.py:106
  32.0 12.1 %collective-permute-start.6 = (bf16[384,512]{1,0:T(8,128)(2,1)S(1)}, bf16[384,512]{1,0:T(8,128)(2,1)S(1)}, u32[]{:S(2)}, u32[]{:S(2)}) collective-permute-start(bf16[384,512]{1,0:T(8,128)(2,1)S(1)} %fusion.9.refs_1_), channel_id=1, source_target_pairs={{0,2},{1,3},{2,0},{3,1},{4,6},{5,7},{6,4},{7,5},{8,10},{9,11},{10,... | collective-permute-start | bytes 1179656 | tf_op jit(solution)/shard_map/ppermute | solution.py:106
  33.0 19.5 %collective-permute-start.9 = (bf16[2,384,512]{2,1,0:T(8,128)(2,1)S(1)}, bf16[2,384,512]{2,1,0:T(8,128)(2,1)S(1)}, u32[]{:S(2)}, u32[]{:S(2)}) collective-permute-start(bf16[2,384,512]{2,1,0:T(8,128)(2,1)S(1)} %get-tuple-element.50), channel_id=1, source_target_pairs={{0,1},{1,0},{2,3},{3,2},{4,5},{5,4},{6,7},{7,6},{8,9},{9,8},{10,11... | collective-permute-start | bytes 2359304 | tf_op jit(solution)/shard_map/ppermute | solution.py:106
  33.0 19.3 %collective-permute-start.4 = (f32[64,384]{1,0:T(8,128)S(1)}, f32[64,384]{1,0:T(8,128)S(1)}, u32[]{:S(2)}, u32[]{:S(2)}) collective-permute-start(f32[64,384]{1,0:T(8,128)S(1)} %bitcast_add_fusion.4.refs_3_), channel_id=1, source_target_pairs={{0,4},{1,5},{2,6},{3,7},{4,0},{5,1},{6,2},{7,3},{8,12},{9,13},{10,... | collective-permute-start | bytes 294920 | tf_op jit(solution)/shard_map/ppermute | solution.py:106
  33.7 18.9 %collective-permute-start.12 = (bf16[384,512]{1,0:T(8,128)(2,1)S(1)}, bf16[384,512]{1,0:T(8,128)(2,1)S(1)}, u32[]{:S(2)}, u32[]{:S(2)}) collective-permute-start(bf16[384,512]{1,0:T(8,128)(2,1)S(1)} %fusion.10.refs_1_), channel_id=1, source_target_pairs={{0,2},{1,3},{2,0},{3,1},{4,6},{5,7},{6,4},{7,5},{8,10},{9,11},{10,... | collective-permute-start | bytes 1179656 | tf_op jit(solution)/shard_map/ppermute | solution.py:106
  44.3 23.9 %collective-permute-start.11 = (bf16[384,512]{1,0:T(8,128)(2,1)S(1)}, bf16[384,512]{1,0:T(8,128)(2,1)S(1)}, u32[]{:S(2)}, u32[]{:S(2)}) collective-permute-start(bf16[384,512]{1,0:T(8,128)(2,1)S(1)} %fusion.6.refs_2_), channel_id=1, source_target_pairs={{0,8},{1,9},{2,10},{3,11},{4,12},{5,13},{6,14},{7,15},{8,0},{9,1},... | collective-permute-start | bytes 1179656 | tf_op jit(solution)/shard_map/ppermute | solution.py:106
  52.3 13.1 %copy-start.1 = (bf16[32,64,512]{2,1,0:T(8,128)(2,1)S(1)}, bf16[32,64,512]{2,1,0:T(8,128)(2,1)}, u32[]{:S(2)}) copy-start(bf16[32,64,512]{2,1,0:T(8,128)(2,1)} %param.11) | copy-start | bytes 6291460
  52.3 13.1 %copy-start.2 = (s32[32]{0:T(128)S(1)}, s32[32]{0:T(128)}, u32[]{:S(2)}) copy-start(s32[32]{0:T(128)} %first_ref.1) | copy-start | bytes 388
  52.3 13.1 %copy-start.3 = (s32[32]{0:T(128)S(1)}, s32[32]{0:T(128)}, u32[]{:S(2)}) copy-start(s32[32]{0:T(128)} %length_ref.1) | copy-start | bytes 388
  52.4 15.9 %collective-permute-start.8 = (bf16[1,384,512]{2,1,0:T(8,128)(2,1)S(1)}, bf16[1,384,512]{2,1,0:T(8,128)(2,1)S(1)}, u32[]{:S(2)}, u32[]{:S(2)}) collective-permute-start(bf16[1,384,512]{2,1,0:T(8,128)(2,1)S(1)} %get-tuple-element.49), channel_id=1, source_target_pairs={{0,1},{1,0},{2,3},{3,2},{4,5},{5,4},{6,7},{7,6},{8,9},{9,8},{10,11... | collective-permute-start | bytes 1179656 | tf_op jit(solution)/shard_map/ppermute | solution.py:106
  52.8 19.0 %collective-permute-start.13 = (bf16[384,512]{1,0:T(8,128)(2,1)S(1)}, bf16[384,512]{1,0:T(8,128)(2,1)S(1)}, u32[]{:S(2)}, u32[]{:S(2)}) collective-permute-start(bf16[384,512]{1,0:T(8,128)(2,1)S(1)} %fusion), channel_id=1, source_target_pairs={{0,4},{1,5},{2,6},{3,7},{4,0},{5,1},{6,2},{7,3},{8,12},{9,13},{10,... | collective-permute-start | bytes 1179656 | tf_op jit(solution)/shard_map/ppermute | solution.py:106
  53.3 18.5 %collective-permute-start.10 = (bf16[384,512]{1,0:T(8,128)(2,1)S(1)}, bf16[384,512]{1,0:T(8,128)(2,1)S(1)}, u32[]{:S(2)}, u32[]{:S(2)}) collective-permute-start(bf16[384,512]{1,0:T(8,128)(2,1)S(1)} %fusion.11), channel_id=1, source_target_pairs={{0,2},{1,3},{2,0},{3,1},{4,6},{5,7},{6,4},{7,5},{8,10},{9,11},{10,... | collective-permute-start | bytes 1179656 | tf_op jit(solution)/shard_map/ppermute | solution.py:106
  54.3 9.7 %collective-permute-start.14 = (bf16[64,384]{1,0:T(8,128)(2,1)S(1)}, bf16[64,384]{1,0:T(8,128)(2,1)S(1)}, u32[]{:S(2)}, u32[]{:S(2)}) collective-permute-start(bf16[64,384]{1,0:T(8,128)(2,1)S(1)} %get-tuple-element.55), channel_id=1, source_target_pairs={{0,8},{1,9},{2,10},{3,11},{4,12},{5,13},{6,14},{7,15},{8,0},{9,1},... | collective-permute-start | bytes 147464 | tf_op jit(solution)/shard_map/ppermute | solution.py:106
  64.0 1.4 %collective-permute-start.15 = (f32[64,384]{1,0:T(8,128)S(1)}, f32[64,384]{1,0:T(8,128)S(1)}, u32[]{:S(2)}, u32[]{:S(2)}) collective-permute-start(f32[64,384]{1,0:T(8,128)S(1)} %convert_add_fusion), channel_id=1, source_target_pairs={{0,1},{1,0},{2,3},{3,2},{4,5},{5,4},{6,7},{7,6},{8,9},{9,8},{10,11... | collective-permute-start | bytes 294920 | tf_op jit(solution)/shard_map/ppermute | solution.py:106

commit v12 on v11

--- a/solution.py
+++ b/solution.py
@@ -10,7 +10,7 @@
 VMEM_LIMIT = 39 * 1024 * 1024
 WINDOW = 128
 TOGETHER = 4
-FLOPS = 2_500_000_000
+FLOPS = 10_000_000_000
 FIRST_FLOPS = 10_000_000_000
 EXPAND_FLOPS = 1_000_000
 

time: 73.3 us -> 73.5 us (level)
  no operation moved by 1% of the time
where the time goes in v12:
time: 73.5 us; the launch traced here: 73.1 us
  Pallas kernels  26.8 us (36%)
  waiting for transfers between devices  22.8 us (31%)
  starting transfers between devices  14.4 us (20%)
  matrix products  4.12 us (6%)
  other arithmetic  3.38 us (5%)
  local copies, waits for them, and re-layouts  1.34 us (2%)
    pallas_call x5, Pallas kernels, product(): pl.pallas_call(functools.partial(product_body, base=base, sent=sent, kept...  24 us
    ppermute x16, waiting for transfers between devices, swap(): lax.ppermute(value, 'tensor', [(place, place ^ bit) for place in range(to...  22.8 us
    ppermute x16, starting transfers between devices, swap(): lax.ppermute(value, 'tensor', [(place, place ^ bit) for place in range(to...  14.4 us
    unnamed x1, matrix products  4.12 us
    pallas_call x1, Pallas kernels, expand(): pl.pallas_call(expand_body, grid_spec=pltpu.PrefetchScalarGridSpec(num_sc...  2.78 us
  transfers between devices with their start and end apart: 16, of which 5 were waited for; matrix products, arithmetic and copies ran while one was open for 8% of the time, Pallas kernels for 33%

profile of v12, /device:TPU:0, one launch (start us, length us, event | category | flops | bytes accessed | tf_op | source)
XLA Modules:
  0.0 73.1 jit_solution(1470711410923728130)
XLA Ops:
  0.0 0.7 broadcast_xor_fusion.table_ref
  0.7 1.3 %copy-done.3 = bf16[384,1664]{1,0:T(8,128)(2,1)S(1)} copy-done((bf16[384,1664]{1,0:T(8,128)(2,1)S(1)}, bf16[384,1664]{1,0:T(8,128)(2,1)}, u32[]{:S(2)}) %copy-start.3) | copy-done | bytes 1277976
  2.0 2.9 %shard_map.82 = (bf16[1,384,512]{2,1,0:T(8,128)(2,1)S(1)}, bf16[2,1664,512]{2,1,0:T(8,128)(2,1)S(1)}) custom-call(s32[16]{0:T(128)S(1)} %broadcast_xor_fusion.table_ref, bf16[384,1664]{1,0:T(8,128)(2,1)S(1)} %copy-done.3, bf16[1664,8192]{1,0:T(8,128)(2,1)} %down_ref.9), custom_call_target="tpu_custom_call" | custom-call | flops 10000000000 | bytes 1024 | tf_op jit(solution)/shard_map/pallas_call | solution.py:83
  5.4 4.4 %shard_map.83 = (bf16[2,384,512]{2,1,0:T(8,128)(2,1)S(1)}, f32[1,384,512]{2,1,0:T(8,128)S(1)}, bf16[2,1664,512]{2,1,0:T(8,128)(2,1)S(1)}) custom-call(s32[16]{0:T(128)S(1)} %broadcast_xor_fusion.table_ref, bf16[384,1664]{1,0:T(8,128)(2,1)S(1)} %copy-done.3, bf16[1664,8192]{1,0:T(8,128)(2,1)} %down_ref.9, ...), custom_call_target="tpu_custom_call", output_to_operand_aliasing={{2}: (3, {})} | custom-call | flops 10000000000 | bytes 1024 | tf_op jit(solution)/shard_map/pallas_call | solution.py:83
  10.1 3.0 %collective-permute-start.3 = (bf16[384,512]{1,0:T(8,128)(2,1)S(1)}, bf16[384,512]{1,0:T(8,128)(2,1)S(1)}, u32[]{:S(2)}, u32[]{:S(2)}) collective-permute-start(bf16[384,512]{1,0:T(8,128)(2,1)S(1)} %fusion.8.refs_1_), channel_id=1, source_target_pairs={{0,2},{1,3},{2,0},{3,1},{4,6},{5,7},{6,4},{7,5},{8,10},{9,11},{10,... | collective-permute-start | bytes 1179656 | tf_op jit(solution)/shard_map/ppermute | solution.py:106
  13.2 5.7 %shard_map.84 = (bf16[2,384,512]{2,1,0:T(8,128)(2,1)S(1)}, f32[2,384,512]{2,1,0:T(8,128)S(1)}, bf16[2,1664,512]{2,1,0:T(8,128)(2,1)S(1)}) custom-call(s32[16]{0:T(128)S(1)} %broadcast_xor_fusion.table_ref, bf16[384,1664]{1,0:T(8,128)(2,1)S(1)} %copy-done.3, bf16[1664,8192]{1,0:T(8,128)(2,1)} %down_ref.9, ...), custom_call_target="tpu_custom_call", output_to_operand_aliasing={{2}: (3, {})} | custom-call | flops 10000000000 | bytes 1024 | tf_op jit(solution)/shard_map/pallas_call | solution.py:83
  19.1 4.1 %fusion.13 = f32[384,2048]{0,1:S(1)} fusion(bf16[384,1664]{1,0:T(8,128)(2,1)S(1)} %copy-done.3, bf16[1664,2048]{0,1:T(8,128)(2,1)S(1)} %bitcast.47), kind=kOutput, calls=%fused_computation.26 | convolution fusion | flops 2617245696 | bytes 11239424
  23.7 0.7 collective-permute-start.2
  24.5 2.1 %collective-permute-start.7 = (bf16[384,512]{1,0:T(8,128)(2,1)S(1)}, bf16[384,512]{1,0:T(8,128)(2,1)S(1)}, u32[]{:S(2)}, u32[]{:S(2)}) collective-permute-start(bf16[384,512]{1,0:T(8,128)(2,1)S(1)} %fusion.7.refs_2_), channel_id=1, source_target_pairs={{0,4},{1,5},{2,6},{3,7},{4,0},{5,1},{6,2},{7,3},{8,12},{9,13},{10,... | collective-permute-start | bytes 1179656 | tf_op jit(solution)/shard_map/ppermute | solution.py:106
  26.6 5.6 %shard_map.85 = (bf16[2,384,512]{2,1,0:T(8,128)(2,1)S(1)}, f32[2,384,512]{2,1,0:T(8,128)S(1)}, bf16[2,1664,512]{2,1,0:T(8,128)(2,1)S(1)}) custom-call(s32[16]{0:T(128)S(1)} %broadcast_xor_fusion.table_ref, bf16[384,1664]{1,0:T(8,128)(2,1)S(1)} %copy-done.3, bf16[1664,8192]{1,0:T(8,128)(2,1)} %down_ref.9, ...), custom_call_target="tpu_custom_call", output_to_operand_aliasing={{2}: (3, {})} | custom-call | flops 10000000000 | bytes 1024 | tf_op jit(solution)/shard_map/pallas_call | solution.py:83
  32.2 1.0 %collective-permute-start.6 = (bf16[384,512]{1,0:T(8,128)(2,1)S(1)}, bf16[384,512]{1,0:T(8,128)(2,1)S(1)}, u32[]{:S(2)}, u32[]{:S(2)}) collective-permute-start(bf16[384,512]{1,0:T(8,128)(2,1)S(1)} %fusion.9.refs_1_), channel_id=1, source_target_pairs={{0,2},{1,3},{2,0},{3,1},{4,6},{5,7},{6,4},{7,5},{8,10},{9,11},{10,... | collective-permute-start | bytes 1179656 | tf_op jit(solution)/shard_map/ppermute | solution.py:106
  33.2 0.6 collective-permute-start.4
  33.9 0.7 collective-permute-start.12
  34.6 1.3 %collective-permute-done.7 = bf16[384,512]{1,0:T(8,128)(2,1)S(1)} collective-permute-done((bf16[384,512]{1,0:T(8,128)(2,1)S(1)}, bf16[384,512]{1,0:T(8,128)(2,1)S(1)}, u32[]{:S(2)}, u32[]{:S(2)}) %collective-permute-start.7) | collective-permute-done | bytes 393248 | tf_op jit(solution)/shard_map/ppermute | solution.py:106
  35.9 8.3 %collective-permute-done.6 = bf16[384,512]{1,0:T(8,128)(2,1)S(1)} collective-permute-done((bf16[384,512]{1,0:T(8,128)(2,1)S(1)}, bf16[384,512]{1,0:T(8,128)(2,1)S(1)}, u32[]{:S(2)}, u32[]{:S(2)}) %collective-permute-start.6) | collective-permute-done | bytes 393248 | tf_op jit(solution)/shard_map/ppermute | solution.py:106
  44.5 2.7 %collective-permute-start.11 = (bf16[384,512]{1,0:T(8,128)(2,1)S(1)}, bf16[384,512]{1,0:T(8,128)(2,1)S(1)}, u32[]{:S(2)}, u32[]{:S(2)}) collective-permute-start(bf16[384,512]{1,0:T(8,128)(2,1)S(1)} %fusion.6.refs_2_), channel_id=1, source_target_pairs={{0,8},{1,9},{2,10},{3,11},{4,12},{5,13},{6,14},{7,15},{8,0},{9,1},... | collective-permute-start | bytes 1179656 | tf_op jit(solution)/shard_map/ppermute | solution.py:106
  47.1 5.4 %shard_map.86 = (bf16[1,384,512]{2,1,0:T(8,128)(2,1)S(1)}, f32[3,384,512]{2,1,0:T(8,128)S(1)}, bf16[2,1664,512]{2,1,0:T(8,128)(2,1)S(1)}) custom-call(s32[16]{0:T(128)S(1)} %broadcast_xor_fusion.table_ref, bf16[384,1664]{1,0:T(8,128)(2,1)S(1)} %copy-done.3, bf16[1664,8192]{1,0:T(8,128)(2,1)} %down_ref.9, ...), custom_call_target="tpu_custom_call", output_to_operand_aliasing={{2}: (3, {})} | custom-call | flops 10000000000 | bytes 1024 | tf_op jit(solution)/shard_map/pallas_call | solution.py:83
  53.5 0.9 %collective-permute-start.10 = (bf16[384,512]{1,0:T(8,128)(2,1)S(1)}, bf16[384,512]{1,0:T(8,128)(2,1)S(1)}, u32[]{:S(2)}, u32[]{:S(2)}) collective-permute-start(bf16[384,512]{1,0:T(8,128)(2,1)S(1)} %fusion.11), channel_id=1, source_target_pairs={{0,2},{1,3},{2,0},{3,1},{4,6},{5,7},{6,4},{7,5},{8,10},{9,11},{10,... | collective-permute-start | bytes 1179656 | tf_op jit(solution)/shard_map/ppermute | solution.py:106
  54.5 1.5 %collective-permute-start.14 = (bf16[64,384]{1,0:T(8,128)(2,1)S(1)}, bf16[64,384]{1,0:T(8,128)(2,1)S(1)}, u32[]{:S(2)}, u32[]{:S(2)}) collective-permute-start(bf16[64,384]{1,0:T(8,128)(2,1)S(1)} %get-tuple-element.55), channel_id=1, source_target_pairs={{0,8},{1,9},{2,10},{3,11},{4,12},{5,13},{6,14},{7,15},{8,0},{9,1},... | collective-permute-start | bytes 147464 | tf_op jit(solution)/shard_map/ppermute | solution.py:106
  56.0 8.2 %collective-permute-done.14 = bf16[64,384]{1,0:T(8,128)(2,1)S(1)} collective-permute-done((bf16[64,384]{1,0:T(8,128)(2,1)S(1)}, bf16[64,384]{1,0:T(8,128)(2,1)S(1)}, u32[]{:S(2)}, u32[]{:S(2)}) %collective-permute-start.14) | collective-permute-done | bytes 49184 | tf_op jit(solution)/shard_map/ppermute | solution.py:106
  64.3 1.3 %collective-permute-done.15 = f32[64,384]{1,0:T(8,128)S(1)} collective-permute-done((f32[64,384]{1,0:T(8,128)S(1)}, f32[64,384]{1,0:T(8,128)S(1)}, u32[]{:S(2)}, u32[]{:S(2)}) %collective-permute-start.15) | collective-permute-done | bytes 98336 | tf_op jit(solution)/shard_map/ppermute | solution.py:106
  65.6 2.8 %shard_map.87 = f32[384,512]{1,0:T(8,128)S(1)} custom-call(s32[32]{0:T(128)S(1)} %copy-done.1, s32[32]{0:T(128)S(1)} %copy-done.2, f32[64,384]{1,0:T(8,128)S(1)} %add.98.packed_ref, bf16[2048,512]{1,0:T(8,128)(2,1)S(1)} %bitcast.41), custom_call_target="tpu_custom_call" | custom-call | flops 1000000 | bytes 1 | tf_op jit(solution)/shard_map/pallas_call | solution.py:162
  68.4 3.6 %collective-permute-done.13 = bf16[384,512]{1,0:T(8,128)(2,1)S(1)} collective-permute-done((bf16[384,512]{1,0:T(8,128)(2,1)S(1)}, bf16[384,512]{1,0:T(8,128)(2,1)S(1)}, u32[]{:S(2)}, u32[]{:S(2)}) %collective-permute-start.13) | collective-permute-done | bytes 393248 | tf_op jit(solution)/shard_map/ppermute | solution.py:106
  72.0 1.1 %fusion.4 = bf16[384,512]{1,0:T(8,128)(2,1)} fusion(f32[384,512]{1,0:T(8,128)S(1)} %shard_map.87, bf16[384,512]{1,0:T(8,128)(2,1)S(1)} %collective-permute-done.13, bf16[384,512]{1,0:T(8,128)(2,1)S(1)} %collective-permute-done.11, bf16[384,512]{1,0:T(8,128)(2,1)S(1)} %collective-permute-done.10, bf16[1,384,512]{2,1,0:T(8,128)(2,1)S(1)} %collective-permute-done.8, ...), kind=kLoop, calls=%fused_computation.7 | loop fusion | flops 1966080 | bytes 3538944 | tf_op jit(solution)/shard_map/convert_element_type | solution.py:252
  (45 shorter events, 3.0 us)
Async XLA Ops:
  0.7 1.3 %copy-start.3 = (bf16[384,1664]{1,0:T(8,128)(2,1)S(1)}, bf16[384,1664]{1,0:T(8,128)(2,1)}, u32[]{:S(2)}) copy-start(bf16[384,1664]{1,0:T(8,128)(2,1)} %hidden_ref.9) | copy-start | bytes 3833860
  4.9 5.1 %collective-permute-start = (bf16[1,384,512]{2,1,0:T(8,128)(2,1)S(1)}, bf16[1,384,512]{2,1,0:T(8,128)(2,1)S(1)}, u32[]{:S(2)}, u32[]{:S(2)}) collective-permute-start(bf16[1,384,512]{2,1,0:T(8,128)(2,1)S(1)} %get-tuple-element.33), channel_id=1, source_target_pairs={{0,1},{1,0},{2,3},{3,2},{4,5},{5,4},{6,7},{7,6},{8,9},{9,8},{10,11... | collective-permute-start | bytes 1179656 | tf_op jit(solution)/shard_map/ppermute | solution.py:106
  5.4 4.6 %copy-start.4 = (s32[384]{0:T(512)S(1)}, s32[384]{0:T(512)}, u32[]{:S(2)}) copy-start(s32[384]{0:T(512)} %param.12) | copy-start | bytes 4612
  9.8 9.1 %collective-permute-start.1 = (bf16[2,384,512]{2,1,0:T(8,128)(2,1)S(1)}, bf16[2,384,512]{2,1,0:T(8,128)(2,1)S(1)}, u32[]{:S(2)}, u32[]{:S(2)}) collective-permute-start(bf16[2,384,512]{2,1,0:T(8,128)(2,1)S(1)} %get-tuple-element.35), channel_id=1, source_target_pairs={{0,1},{1,0},{2,3},{3,2},{4,5},{5,4},{6,7},{7,6},{8,9},{9,8},{10,11... | collective-permute-start | bytes 2359304 | tf_op jit(solution)/shard_map/ppermute | solution.py:106
  10.0 9.1 %slice-start = ((s8[6815744]{0:T(1024)(128)(4,1)}), s8[4194304]{0:T(1024)(128)(4,1)S(1)}, s32[]{:S(2)}) async-start(s8[6815744]{0:T(1024)(128)(4,1)} %bitcast.45), calls=%async_computation | async-start | bytes 8388608
  10.1 14.2 %collective-permute-start.3 = (bf16[384,512]{1,0:T(8,128)(2,1)S(1)}, bf16[384,512]{1,0:T(8,128)(2,1)S(1)}, u32[]{:S(2)}, u32[]{:S(2)}) collective-permute-start(bf16[384,512]{1,0:T(8,128)(2,1)S(1)} %fusion.8.refs_1_), channel_id=1, source_target_pairs={{0,2},{1,3},{2,0},{3,1},{4,6},{5,7},{6,4},{7,5},{8,10},{9,11},{10,... | collective-permute-start | bytes 1179656 | tf_op jit(solution)/shard_map/ppermute | solution.py:106
  13.2 6.0 %slice-start.1 = ((s8[6815744]{0:T(1024)(128)(4,1)}), s8[2621440]{0:T(1024)(128)(4,1)S(1)}, s32[]{:S(2)}) async-start(s8[6815744]{0:T(1024)(128)(4,1)} %bitcast.45), calls=%async_computation.1 | async-start | bytes 5242880
  18.9 14.9 %collective-permute-start.5 = (bf16[2,384,512]{2,1,0:T(8,128)(2,1)S(1)}, bf16[2,384,512]{2,1,0:T(8,128)(2,1)S(1)}, u32[]{:S(2)}, u32[]{:S(2)}) collective-permute-start(bf16[2,384,512]{2,1,0:T(8,128)(2,1)S(1)} %get-tuple-element.44), channel_id=1, source_target_pairs={{0,1},{1,0},{2,3},{3,2},{4,5},{5,4},{6,7},{7,6},{8,9},{9,8},{10,11... | collective-permute-start | bytes 2359304 | tf_op jit(solution)/shard_map/ppermute | solution.py:106
  23.7 9.5 %collective-permute-start.2 = (f32[64,384]{1,0:T(8,128)S(1)}, f32[64,384]{1,0:T(8,128)S(1)}, u32[]{:S(2)}, u32[]{:S(2)}) collective-permute-start(f32[64,384]{1,0:T(8,128)S(1)} %bitcast.42), channel_id=1, source_target_pairs={{0,2},{1,3},{2,0},{3,1},{4,6},{5,7},{6,4},{7,5},{8,10},{9,11},{10,... | collective-permute-start | bytes 294920 | tf_op jit(solution)/shard_map/ppermute | solution.py:106
  24.5 11.4 %collective-permute-start.7 = (bf16[384,512]{1,0:T(8,128)(2,1)S(1)}, bf16[384,512]{1,0:T(8,128)(2,1)S(1)}, u32[]{:S(2)}, u32[]{:S(2)}) collective-permute-start(bf16[384,512]{1,0:T(8,128)(2,1)S(1)} %fusion.7.refs_2_), channel_id=1, source_target_pairs={{0,4},{1,5},{2,6},{3,7},{4,0},{5,1},{6,2},{7,3},{8,12},{9,13},{10,... | collective-permute-start | bytes 1179656 | tf_op jit(solution)/shard_map/ppermute | solution.py:106
  32.2 12.1 %collective-permute-start.6 = (bf16[384,512]{1,0:T(8,128)(2,1)S(1)}, bf16[384,512]{1,0:T(8,128)(2,1)S(1)}, u32[]{:S(2)}, u32[]{:S(2)}) collective-permute-start(bf16[384,512]{1,0:T(8,128)(2,1)S(1)} %fusion.9.refs_1_), channel_id=1, source_target_pairs={{0,2},{1,3},{2,0},{3,1},{4,6},{5,7},{6,4},{7,5},{8,10},{9,11},{10,... | collective-permute-start | bytes 1179656 | tf_op jit(solution)/shard_map/ppermute | solution.py:106
  33.2 19.4 %collective-permute-start.9 = (bf16[2,384,512]{2,1,0:T(8,128)(2,1)S(1)}, bf16[2,384,512]{2,1,0:T(8,128)(2,1)S(1)}, u32[]{:S(2)}, u32[]{:S(2)}) collective-permute-start(bf16[2,384,512]{2,1,0:T(8,128)(2,1)S(1)} %get-tuple-element.50), channel_id=1, source_target_pairs={{0,1},{1,0},{2,3},{3,2},{4,5},{5,4},{6,7},{7,6},{8,9},{9,8},{10,11... | collective-permute-start | bytes 2359304 | tf_op jit(solution)/shard_map/ppermute | solution.py:106
  33.2 19.3 %collective-permute-start.4 = (f32[64,384]{1,0:T(8,128)S(1)}, f32[64,384]{1,0:T(8,128)S(1)}, u32[]{:S(2)}, u32[]{:S(2)}) collective-permute-start(f32[64,384]{1,0:T(8,128)S(1)} %bitcast_add_fusion.4.refs_3_), channel_id=1, source_target_pairs={{0,4},{1,5},{2,6},{3,7},{4,0},{5,1},{6,2},{7,3},{8,12},{9,13},{10,... | collective-permute-start | bytes 294920 | tf_op jit(solution)/shard_map/ppermute | solution.py:106
  33.9 18.9 %collective-permute-start.12 = (bf16[384,512]{1,0:T(8,128)(2,1)S(1)}, bf16[384,512]{1,0:T(8,128)(2,1)S(1)}, u32[]{:S(2)}, u32[]{:S(2)}) collective-permute-start(bf16[384,512]{1,0:T(8,128)(2,1)S(1)} %fusion.10.refs_1_), channel_id=1, source_target_pairs={{0,2},{1,3},{2,0},{3,1},{4,6},{5,7},{6,4},{7,5},{8,10},{9,11},{10,... | collective-permute-start | bytes 1179656 | tf_op jit(solution)/shard_map/ppermute | solution.py:106
  44.5 23.9 %collective-permute-start.11 = (bf16[384,512]{1,0:T(8,128)(2,1)S(1)}, bf16[384,512]{1,0:T(8,128)(2,1)S(1)}, u32[]{:S(2)}, u32[]{:S(2)}) collective-permute-start(bf16[384,512]{1,0:T(8,128)(2,1)S(1)} %fusion.6.refs_2_), channel_id=1, source_target_pairs={{0,8},{1,9},{2,10},{3,11},{4,12},{5,13},{6,14},{7,15},{8,0},{9,1},... | collective-permute-start | bytes 1179656 | tf_op jit(solution)/shard_map/ppermute | solution.py:106
  52.5 13.1 %copy-start = (bf16[32,64,512]{2,1,0:T(8,128)(2,1)S(1)}, bf16[32,64,512]{2,1,0:T(8,128)(2,1)}, u32[]{:S(2)}) copy-start(bf16[32,64,512]{2,1,0:T(8,128)(2,1)} %param.11) | copy-start | bytes 6291460
  52.5 13.1 %copy-start.1 = (s32[32]{0:T(128)S(1)}, s32[32]{0:T(128)}, u32[]{:S(2)}) copy-start(s32[32]{0:T(128)} %first_ref.1) | copy-start | bytes 388
  52.5 13.1 %copy-start.2 = (s32[32]{0:T(128)S(1)}, s32[32]{0:T(128)}, u32[]{:S(2)}) copy-start(s32[32]{0:T(128)} %length_ref.1) | copy-start | bytes 388
  52.6 15.8 %collective-permute-start.8 = (bf16[1,384,512]{2,1,0:T(8,128)(2,1)S(1)}, bf16[1,384,512]{2,1,0:T(8,128)(2,1)S(1)}, u32[]{:S(2)}, u32[]{:S(2)}) collective-permute-start(bf16[1,384,512]{2,1,0:T(8,128)(2,1)S(1)} %get-tuple-element.49), channel_id=1, source_target_pairs={{0,1},{1,0},{2,3},{3,2},{4,5},{5,4},{6,7},{7,6},{8,9},{9,8},{10,11... | collective-permute-start | bytes 1179656 | tf_op jit(solution)/shard_map/ppermute | solution.py:106
  53.0 19.0 %collective-permute-start.13 = (bf16[384,512]{1,0:T(8,128)(2,1)S(1)}, bf16[384,512]{1,0:T(8,128)(2,1)S(1)}, u32[]{:S(2)}, u32[]{:S(2)}) collective-permute-start(bf16[384,512]{1,0:T(8,128)(2,1)S(1)} %fusion), channel_id=1, source_target_pairs={{0,4},{1,5},{2,6},{3,7},{4,0},{5,1},{6,2},{7,3},{8,12},{9,13},{10,... | collective-permute-start | bytes 1179656 | tf_op jit(solution)/shard_map/ppermute | solution.py:106
  53.5 18.5 %collective-permute-start.10 = (bf16[384,512]{1,0:T(8,128)(2,1)S(1)}, bf16[384,512]{1,0:T(8,128)(2,1)S(1)}, u32[]{:S(2)}, u32[]{:S(2)}) collective-permute-start(bf16[384,512]{1,0:T(8,128)(2,1)S(1)} %fusion.11), channel_id=1, source_target_pairs={{0,2},{1,3},{2,0},{3,1},{4,6},{5,7},{6,4},{7,5},{8,10},{9,11},{10,... | collective-permute-start | bytes 1179656 | tf_op jit(solution)/shard_map/ppermute | solution.py:106
  54.5 9.7 %collective-permute-start.14 = (bf16[64,384]{1,0:T(8,128)(2,1)S(1)}, bf16[64,384]{1,0:T(8,128)(2,1)S(1)}, u32[]{:S(2)}, u32[]{:S(2)}) collective-permute-start(bf16[64,384]{1,0:T(8,128)(2,1)S(1)} %get-tuple-element.55), channel_id=1, source_target_pairs={{0,8},{1,9},{2,10},{3,11},{4,12},{5,13},{6,14},{7,15},{8,0},{9,1},... | collective-permute-start | bytes 147464 | tf_op jit(solution)/shard_map/ppermute | solution.py:106
  64.2 1.4 %collective-permute-start.15 = (f32[64,384]{1,0:T(8,128)S(1)}, f32[64,384]{1,0:T(8,128)S(1)}, u32[]{:S(2)}, u32[]{:S(2)}) collective-permute-start(f32[64,384]{1,0:T(8,128)S(1)} %convert_add_fusion), channel_id=1, source_target_pairs={{0,1},{1,0},{2,3},{3,2},{4,5},{5,4},{6,7},{7,6},{8,9},{9,8},{10,11... | collective-permute-start | bytes 294920 | tf_op jit(solution)/shard_map/ppermute | solution.py:106

commit v13 on v12

--- a/solution.py
+++ b/solution.py
@@ -10,8 +10,8 @@
 VMEM_LIMIT = 39 * 1024 * 1024
 WINDOW = 128
 TOGETHER = 4
-FLOPS = 10_000_000_000
-FIRST_FLOPS = 10_000_000_000
+FLOPS = 3_000_000_000
+FIRST_FLOPS = 3_000_000_000
 EXPAND_FLOPS = 1_000_000
 
 
@@ -200,10 +200,10 @@
         value = kept_home[unit] + arrived.astype(jnp.float32) + crossed[unit].astype(jnp.float32)
         for moved in incoming.pop(unit, []):
             value = value + moved.astype(jnp.float32)
-        if not unit:
-            return value
+        return value.astype(jnp.bfloat16) if unit else value
+
+    def send_on(unit, moving):
         bit = unit & -unit
-        moving = value.astype(jnp.bfloat16)
         incoming.setdefault(unit ^ bit, []).append(swap(moving, 4 * bit, total))
         return moving
 
@@ -231,15 +231,15 @@
             kept_home[unit + 1] = results[1]
         if not unit:
             kept_home[0] = results[-1]
+        ready = []
+        if unit < top:
+            moving, arrived = lax.optimization_barrier((settle(unit + 1, arrived[1]), arrived))
+            ready.append(send_on(unit + 1, moving))
         leaving = (results[0] + arrived[0].astype(jnp.float32)).astype(jnp.bfloat16)
         if unit == max(top - 1, 0):
-            late, leaving = lax.optimization_barrier((hidden, leaving))
-        ready = [leaving]
-        if unit < top:
-            leaving, arrived = lax.optimization_barrier((leaving, arrived))
-            ready.append(settle(unit + 1, arrived[1]))
-        if unit == max(top - 1, 0):
+            late, results = lax.optimization_barrier((hidden, results))
             packed = shrink(late, shrink_matrices, row_adapter_index)
+        ready.append(leaving)
         if packed is not None:
             ready.append(packed)
         crossed[unit] = swap(leaving, near, total)

time: 73.5 us -> 69.6 us (0.947)
  waiting for transfers between devices: 22.8 us -> 15.8 us
  starting transfers between devices: 14.4 us -> 17.9 us
    ppermute x16, waiting for transfers between devices: 22.8 us -> 15.8 us  [swap(): lax.ppermute(value, 'tensor', [(place, place ^ bit) for place in range(to...]
    ppermute x16, starting transfers between devices: 14.4 us -> 17.9 us  [swap(): lax.ppermute(value, 'tensor', [(place, place ^ bit) for place in range(to...]
  transfers between devices with their start and end apart: 16 -> 16, of which waited for: 5 -> 5; matrix products, arithmetic and copies ran while one was open for 8% -> 8% of each run, Pallas kernels for 33% -> 34%
where the time goes in v13:
time: 69.6 us; the launch traced here: 69.2 us
  Pallas kernels  26.7 us (38%)
  starting transfers between devices  17.9 us (26%)
  waiting for transfers between devices  15.8 us (23%)
  matrix products  3.92 us (6%)
  other arithmetic  3.3 us (5%)
  local copies, waits for them, and re-layouts  1.34 us (2%)
    pallas_call x5, Pallas kernels, product(): pl.pallas_call(functools.partial(product_body, base=base, sent=sent, kept...  24 us
    ppermute x16, starting transfers between devices, swap(): lax.ppermute(value, 'tensor', [(place, place ^ bit) for place in range(to...  17.9 us
    ppermute x16, waiting for transfers between devices, swap(): lax.ppermute(value, 'tensor', [(place, place ^ bit) for place in range(to...  15.8 us
    unnamed x1, matrix products  3.92 us
    pallas_call x1, Pallas kernels, expand(): pl.pallas_call(expand_body, grid_spec=pltpu.PrefetchScalarGridSpec(num_sc...  2.78 us
  transfers between devices with their start and end apart: 16, of which 5 were waited for; matrix products, arithmetic and copies ran while one was open for 8% of the time, Pallas kernels for 34%

profile of v13, /device:TPU:0, one launch (start us, length us, event | category | flops | bytes accessed | tf_op | source)
XLA Modules:
  0.0 69.2 jit_solution(1931040210718584946)
XLA Ops:
  0.0 0.7 broadcast_xor_fusion.table_ref
  0.7 1.3 %copy-done = bf16[384,1664]{1,0:T(8,128)(2,1)S(1)} copy-done((bf16[384,1664]{1,0:T(8,128)(2,1)S(1)}, bf16[384,1664]{1,0:T(8,128)(2,1)}, u32[]{:S(2)}) %copy-start) | copy-done | bytes 1277976
  2.0 2.9 %shard_map.82 = (bf16[1,384,512]{2,1,0:T(8,128)(2,1)S(1)}, bf16[2,1664,512]{2,1,0:T(8,128)(2,1)S(1)}) custom-call(s32[16]{0:T(128)S(1)} %broadcast_xor_fusion.table_ref, bf16[384,1664]{1,0:T(8,128)(2,1)S(1)} %copy-done, bf16[1664,8192]{1,0:T(8,128)(2,1)} %down_ref.9), custom_call_target="tpu_custom_call" | custom-call | flops 3000000000 | bytes 1024 | tf_op jit(solution)/shard_map/pallas_call | solution.py:83
  5.4 4.4 %shard_map.83 = (bf16[2,384,512]{2,1,0:T(8,128)(2,1)S(1)}, f32[1,384,512]{2,1,0:T(8,128)S(1)}, bf16[2,1664,512]{2,1,0:T(8,128)(2,1)S(1)}) custom-call(s32[16]{0:T(128)S(1)} %broadcast_xor_fusion.table_ref, bf16[384,1664]{1,0:T(8,128)(2,1)S(1)} %copy-done, bf16[1664,8192]{1,0:T(8,128)(2,1)} %down_ref.9, ...), custom_call_target="tpu_custom_call", output_to_operand_aliasing={{2}: (3, {})} | custom-call | flops 3000000000 | bytes 1024 | tf_op jit(solution)/shard_map/pallas_call | solution.py:83
  10.1 3.0 %collective-permute-start.3 = (bf16[384,512]{1,0:T(8,128)(2,1)S(1)}, bf16[384,512]{1,0:T(8,128)(2,1)S(1)}, u32[]{:S(2)}, u32[]{:S(2)}) collective-permute-start(bf16[384,512]{1,0:T(8,128)(2,1)S(1)} %fusion.8.refs_1_), channel_id=1, source_target_pairs={{0,2},{1,3},{2,0},{3,1},{4,6},{5,7},{6,4},{7,5},{8,10},{9,11},{10,... | collective-permute-start | bytes 1179656 | tf_op jit(solution)/shard_map/ppermute | solution.py:106
  13.1 5.7 %shard_map.84 = (bf16[2,384,512]{2,1,0:T(8,128)(2,1)S(1)}, f32[2,384,512]{2,1,0:T(8,128)S(1)}, bf16[2,1664,512]{2,1,0:T(8,128)(2,1)S(1)}) custom-call(s32[16]{0:T(128)S(1)} %broadcast_xor_fusion.table_ref, bf16[384,1664]{1,0:T(8,128)(2,1)S(1)} %copy-done, bf16[1664,8192]{1,0:T(8,128)(2,1)} %down_ref.9, ...), custom_call_target="tpu_custom_call", output_to_operand_aliasing={{2}: (3, {})} | custom-call | flops 3000000000 | bytes 1024 | tf_op jit(solution)/shard_map/pallas_call | solution.py:83
  19.0 3.9 %fusion.13 = f32[384,2048]{0,1:S(1)} fusion(bf16[384,1664]{1,0:T(8,128)(2,1)S(1)} %copy-done, bf16[1664,2048]{0,1:T(8,128)(2,1)S(1)} %bitcast.47), kind=kOutput, calls=%fused_computation.26 | convolution fusion | flops 2617245696 | bytes 11239424
  23.2 1.3 %collective-permute-start.6 = (bf16[384,512]{1,0:T(8,128)(2,1)S(1)}, bf16[384,512]{1,0:T(8,128)(2,1)S(1)}, u32[]{:S(2)}, u32[]{:S(2)}) collective-permute-start(bf16[384,512]{1,0:T(8,128)(2,1)S(1)} %fusion.9.refs_2_), channel_id=1, source_target_pairs={{0,2},{1,3},{2,0},{3,1},{4,6},{5,7},{6,4},{7,5},{8,10},{9,11},{10,... | collective-permute-start | bytes 1179656 | tf_op jit(solution)/shard_map/ppermute | solution.py:106
  24.6 1.6 %collective-permute-start.7 = (bf16[384,512]{1,0:T(8,128)(2,1)S(1)}, bf16[384,512]{1,0:T(8,128)(2,1)S(1)}, u32[]{:S(2)}, u32[]{:S(2)}) collective-permute-start(bf16[384,512]{1,0:T(8,128)(2,1)S(1)} %fusion.7.refs_1_), channel_id=1, source_target_pairs={{0,4},{1,5},{2,6},{3,7},{4,0},{5,1},{6,2},{7,3},{8,12},{9,13},{10,... | collective-permute-start | bytes 1179656 | tf_op jit(solution)/shard_map/ppermute | solution.py:106
  26.5 0.8 %collective-permute-start.1 = (f32[64,384]{1,0:T(8,128)S(1)}, f32[64,384]{1,0:T(8,128)S(1)}, u32[]{:S(2)}, u32[]{:S(2)}) collective-permute-start(f32[64,384]{1,0:T(8,128)S(1)} %bitcast.42), channel_id=1, source_target_pairs={{0,2},{1,3},{2,0},{3,1},{4,6},{5,7},{6,4},{7,5},{8,10},{9,11},{10,... | collective-permute-start | bytes 294920 | tf_op jit(solution)/shard_map/ppermute | solution.py:106
  27.3 5.6 %shard_map.85 = (bf16[2,384,512]{2,1,0:T(8,128)(2,1)S(1)}, f32[2,384,512]{2,1,0:T(8,128)S(1)}, bf16[2,1664,512]{2,1,0:T(8,128)(2,1)S(1)}) custom-call(s32[16]{0:T(128)S(1)} %broadcast_xor_fusion.table_ref, bf16[384,1664]{1,0:T(8,128)(2,1)S(1)} %copy-done, bf16[1664,8192]{1,0:T(8,128)(2,1)} %down_ref.9, ...), custom_call_target="tpu_custom_call", output_to_operand_aliasing={{2}: (3, {})} | custom-call | flops 3000000000 | bytes 1024 | tf_op jit(solution)/shard_map/pallas_call | solution.py:83
  32.9 4.0 %collective-permute-done.1 = f32[64,384]{1,0:T(8,128)S(1)} collective-permute-done((f32[64,384]{1,0:T(8,128)S(1)}, f32[64,384]{1,0:T(8,128)S(1)}, u32[]{:S(2)}, u32[]{:S(2)}) %collective-permute-start.1) | collective-permute-done | bytes 98336 | tf_op jit(solution)/shard_map/ppermute | solution.py:106
  37.3 0.7 collective-permute-start.10
  37.9 1.9 %collective-permute-start.4 = (f32[64,384]{1,0:T(8,128)S(1)}, f32[64,384]{1,0:T(8,128)S(1)}, u32[]{:S(2)}, u32[]{:S(2)}) collective-permute-start(f32[64,384]{1,0:T(8,128)S(1)} %bitcast_add_fusion.4.refs_3_), channel_id=1, source_target_pairs={{0,4},{1,5},{2,6},{3,7},{4,0},{5,1},{6,2},{7,3},{8,12},{9,13},{10,... | collective-permute-start | bytes 294920 | tf_op jit(solution)/shard_map/ppermute | solution.py:106
  39.8 2.6 %collective-permute-start.12 = (bf16[384,512]{1,0:T(8,128)(2,1)S(1)}, bf16[384,512]{1,0:T(8,128)(2,1)S(1)}, u32[]{:S(2)}, u32[]{:S(2)}) collective-permute-start(bf16[384,512]{1,0:T(8,128)(2,1)S(1)} %fusion.6.refs_1_), channel_id=1, source_target_pairs={{0,8},{1,9},{2,10},{3,11},{4,12},{5,13},{6,14},{7,15},{8,0},{9,1},... | collective-permute-start | bytes 1179656 | tf_op jit(solution)/shard_map/ppermute | solution.py:106
  42.4 5.4 %shard_map.86 = (bf16[1,384,512]{2,1,0:T(8,128)(2,1)S(1)}, f32[3,384,512]{2,1,0:T(8,128)S(1)}, bf16[2,1664,512]{2,1,0:T(8,128)(2,1)S(1)}) custom-call(s32[16]{0:T(128)S(1)} %broadcast_xor_fusion.table_ref, bf16[384,1664]{1,0:T(8,128)(2,1)S(1)} %copy-done, bf16[1664,8192]{1,0:T(8,128)(2,1)} %down_ref.9, ...), custom_call_target="tpu_custom_call", output_to_operand_aliasing={{2}: (3, {})} | custom-call | flops 3000000000 | bytes 1024 | tf_op jit(solution)/shard_map/pallas_call | solution.py:83
  47.9 0.9 %collective-permute-done.10 = bf16[384,512]{1,0:T(8,128)(2,1)S(1)} collective-permute-done((bf16[384,512]{1,0:T(8,128)(2,1)S(1)}, bf16[384,512]{1,0:T(8,128)(2,1)S(1)}, u32[]{:S(2)}, u32[]{:S(2)}) %collective-permute-start.10) | collective-permute-done | bytes 393248 | tf_op jit(solution)/shard_map/ppermute | solution.py:106
  49.8 1.8 %collective-permute-start.13 = (bf16[384,512]{1,0:T(8,128)(2,1)S(1)}, bf16[384,512]{1,0:T(8,128)(2,1)S(1)}, u32[]{:S(2)}, u32[]{:S(2)}) collective-permute-start(bf16[384,512]{1,0:T(8,128)(2,1)S(1)} %fusion), channel_id=1, source_target_pairs={{0,4},{1,5},{2,6},{3,7},{4,0},{5,1},{6,2},{7,3},{8,12},{9,13},{10,... | collective-permute-start | bytes 1179656 | tf_op jit(solution)/shard_map/ppermute | solution.py:106
  51.7 2.7 %collective-permute-start.14 = (bf16[64,384]{1,0:T(8,128)(2,1)S(1)}, bf16[64,384]{1,0:T(8,128)(2,1)S(1)}, u32[]{:S(2)}, u32[]{:S(2)}) collective-permute-start(bf16[64,384]{1,0:T(8,128)(2,1)S(1)} %get-tuple-element.53), channel_id=1, source_target_pairs={{0,8},{1,9},{2,10},{3,11},{4,12},{5,13},{6,14},{7,15},{8,0},{9,1},... | collective-permute-start | bytes 147464 | tf_op jit(solution)/shard_map/ppermute | solution.py:106
  54.3 7.1 %collective-permute-done.14 = bf16[64,384]{1,0:T(8,128)(2,1)S(1)} collective-permute-done((bf16[64,384]{1,0:T(8,128)(2,1)S(1)}, bf16[64,384]{1,0:T(8,128)(2,1)S(1)}, u32[]{:S(2)}, u32[]{:S(2)}) %collective-permute-start.14) | collective-permute-done | bytes 49184 | tf_op jit(solution)/shard_map/ppermute | solution.py:106
  61.6 1.3 %collective-permute-done.15 = f32[64,384]{1,0:T(8,128)S(1)} collective-permute-done((f32[64,384]{1,0:T(8,128)S(1)}, f32[64,384]{1,0:T(8,128)S(1)}, u32[]{:S(2)}, u32[]{:S(2)}) %collective-permute-start.15) | collective-permute-done | bytes 98336 | tf_op jit(solution)/shard_map/ppermute | solution.py:106
  62.9 2.8 %shard_map.87 = f32[384,512]{1,0:T(8,128)S(1)} custom-call(s32[32]{0:T(128)S(1)} %copy-done.2, s32[32]{0:T(128)S(1)} %copy-done.3, f32[64,384]{1,0:T(8,128)S(1)} %add.98.packed_ref, bf16[2048,512]{1,0:T(8,128)(2,1)S(1)} %bitcast.41), custom_call_target="tpu_custom_call" | custom-call | flops 1000000 | bytes 1 | tf_op jit(solution)/shard_map/pallas_call | solution.py:162
  65.7 2.4 %collective-permute-done.13 = bf16[384,512]{1,0:T(8,128)(2,1)S(1)} collective-permute-done((bf16[384,512]{1,0:T(8,128)(2,1)S(1)}, bf16[384,512]{1,0:T(8,128)(2,1)S(1)}, u32[]{:S(2)}, u32[]{:S(2)}) %collective-permute-start.13) | collective-permute-done | bytes 393248 | tf_op jit(solution)/shard_map/ppermute | solution.py:106
  68.1 1.1 %fusion.4 = bf16[384,512]{1,0:T(8,128)(2,1)} fusion(f32[384,512]{1,0:T(8,128)S(1)} %shard_map.87, bf16[384,512]{1,0:T(8,128)(2,1)S(1)} %collective-permute-done.13, bf16[384,512]{1,0:T(8,128)(2,1)S(1)} %collective-permute-done.12, bf16[384,512]{1,0:T(8,128)(2,1)S(1)} %collective-permute-done.11, bf16[1,384,512]{2,1,0:T(8,128)(2,1)S(1)} %collective-permute-done.8, ...), kind=kLoop, calls=%fused_computation.7 | loop fusion | flops 1966080 | bytes 3538944 | tf_op jit(solution)/shard_map/convert_element_type | solution.py:252
  (45 shorter events, 3.1 us)
Async XLA Ops:
  0.7 1.3 %copy-start = (bf16[384,1664]{1,0:T(8,128)(2,1)S(1)}, bf16[384,1664]{1,0:T(8,128)(2,1)}, u32[]{:S(2)}) copy-start(bf16[384,1664]{1,0:T(8,128)(2,1)} %hidden_ref.9) | copy-start | bytes 3833860
  4.9 5.1 %collective-permute-start = (bf16[1,384,512]{2,1,0:T(8,128)(2,1)S(1)}, bf16[1,384,512]{2,1,0:T(8,128)(2,1)S(1)}, u32[]{:S(2)}, u32[]{:S(2)}) collective-permute-start(bf16[1,384,512]{2,1,0:T(8,128)(2,1)S(1)} %get-tuple-element.32), channel_id=1, source_target_pairs={{0,1},{1,0},{2,3},{3,2},{4,5},{5,4},{6,7},{7,6},{8,9},{9,8},{10,11... | collective-permute-start | bytes 1179656 | tf_op jit(solution)/shard_map/ppermute | solution.py:106
  5.4 4.6 %copy-start.4 = (s32[384]{0:T(512)S(1)}, s32[384]{0:T(512)}, u32[]{:S(2)}) copy-start(s32[384]{0:T(512)} %param.12) | copy-start | bytes 4612
  9.8 13.1 %collective-permute-start.2 = (bf16[2,384,512]{2,1,0:T(8,128)(2,1)S(1)}, bf16[2,384,512]{2,1,0:T(8,128)(2,1)S(1)}, u32[]{:S(2)}, u32[]{:S(2)}) collective-permute-start(bf16[2,384,512]{2,1,0:T(8,128)(2,1)S(1)} %get-tuple-element.36), channel_id=1, source_target_pairs={{0,1},{1,0},{2,3},{3,2},{4,5},{5,4},{6,7},{7,6},{8,9},{9,8},{10,11... | collective-permute-start | bytes 2359304 | tf_op jit(solution)/shard_map/ppermute | solution.py:106
  10.0 9.0 %slice-start = ((s8[6815744]{0:T(1024)(128)(4,1)}), s8[4194304]{0:T(1024)(128)(4,1)S(1)}, s32[]{:S(2)}) async-start(s8[6815744]{0:T(1024)(128)(4,1)} %bitcast.45), calls=%async_computation | async-start | bytes 8388608
  10.1 12.8 %collective-permute-start.3 = (bf16[384,512]{1,0:T(8,128)(2,1)S(1)}, bf16[384,512]{1,0:T(8,128)(2,1)S(1)}, u32[]{:S(2)}, u32[]{:S(2)}) collective-permute-start(bf16[384,512]{1,0:T(8,128)(2,1)S(1)} %fusion.8.refs_1_), channel_id=1, source_target_pairs={{0,2},{1,3},{2,0},{3,1},{4,6},{5,7},{6,4},{7,5},{8,10},{9,11},{10,... | collective-permute-start | bytes 1179656 | tf_op jit(solution)/shard_map/ppermute | solution.py:106
  13.1 5.8 %slice-start.1 = ((s8[6815744]{0:T(1024)(128)(4,1)}), s8[2621440]{0:T(1024)(128)(4,1)S(1)}, s32[]{:S(2)}) async-start(s8[6815744]{0:T(1024)(128)(4,1)} %bitcast.45), calls=%async_computation.1 | async-start | bytes 5242880
  18.9 18.0 %collective-permute-start.5 = (bf16[2,384,512]{2,1,0:T(8,128)(2,1)S(1)}, bf16[2,384,512]{2,1,0:T(8,128)(2,1)S(1)}, u32[]{:S(2)}, u32[]{:S(2)}) collective-permute-start(bf16[2,384,512]{2,1,0:T(8,128)(2,1)S(1)} %get-tuple-element.43), channel_id=1, source_target_pairs={{0,1},{1,0},{2,3},{3,2},{4,5},{5,4},{6,7},{7,6},{8,9},{9,8},{10,11... | collective-permute-start | bytes 2359304 | tf_op jit(solution)/shard_map/ppermute | solution.py:106
  23.2 13.7 %collective-permute-start.6 = (bf16[384,512]{1,0:T(8,128)(2,1)S(1)}, bf16[384,512]{1,0:T(8,128)(2,1)S(1)}, u32[]{:S(2)}, u32[]{:S(2)}) collective-permute-start(bf16[384,512]{1,0:T(8,128)(2,1)S(1)} %fusion.9.refs_2_), channel_id=1, source_target_pairs={{0,2},{1,3},{2,0},{3,1},{4,6},{5,7},{6,4},{7,5},{8,10},{9,11},{10,... | collective-permute-start | bytes 1179656 | tf_op jit(solution)/shard_map/ppermute | solution.py:106
  24.6 12.3 %collective-permute-start.7 = (bf16[384,512]{1,0:T(8,128)(2,1)S(1)}, bf16[384,512]{1,0:T(8,128)(2,1)S(1)}, u32[]{:S(2)}, u32[]{:S(2)}) collective-permute-start(bf16[384,512]{1,0:T(8,128)(2,1)S(1)} %fusion.7.refs_1_), channel_id=1, source_target_pairs={{0,4},{1,5},{2,6},{3,7},{4,0},{5,1},{6,2},{7,3},{8,12},{9,13},{10,... | collective-permute-start | bytes 1179656 | tf_op jit(solution)/shard_map/ppermute | solution.py:106
  26.5 10.4 %collective-permute-start.1 = (f32[64,384]{1,0:T(8,128)S(1)}, f32[64,384]{1,0:T(8,128)S(1)}, u32[]{:S(2)}, u32[]{:S(2)}) collective-permute-start(f32[64,384]{1,0:T(8,128)S(1)} %bitcast.42), channel_id=1, source_target_pairs={{0,2},{1,3},{2,0},{3,1},{4,6},{5,7},{6,4},{7,5},{8,10},{9,11},{10,... | collective-permute-start | bytes 294920 | tf_op jit(solution)/shard_map/ppermute | solution.py:106
  36.9 12.0 %collective-permute-start.9 = (bf16[2,384,512]{2,1,0:T(8,128)(2,1)S(1)}, bf16[2,384,512]{2,1,0:T(8,128)(2,1)S(1)}, u32[]{:S(2)}, u32[]{:S(2)}) collective-permute-start(bf16[2,384,512]{2,1,0:T(8,128)(2,1)S(1)} %get-tuple-element.49), channel_id=1, source_target_pairs={{0,1},{1,0},{2,3},{3,2},{4,5},{5,4},{6,7},{7,6},{8,9},{9,8},{10,11... | collective-permute-start | bytes 2359304 | tf_op jit(solution)/shard_map/ppermute | solution.py:106
  37.3 11.6 %collective-permute-start.10 = (bf16[384,512]{1,0:T(8,128)(2,1)S(1)}, bf16[384,512]{1,0:T(8,128)(2,1)S(1)}, u32[]{:S(2)}, u32[]{:S(2)}) collective-permute-start(bf16[384,512]{1,0:T(8,128)(2,1)S(1)} %fusion.10.refs_2_), channel_id=1, source_target_pairs={{0,2},{1,3},{2,0},{3,1},{4,6},{5,7},{6,4},{7,5},{8,10},{9,11},{10,... | collective-permute-start | bytes 1179656 | tf_op jit(solution)/shard_map/ppermute | solution.py:106
  37.9 9.9 %collective-permute-start.4 = (f32[64,384]{1,0:T(8,128)S(1)}, f32[64,384]{1,0:T(8,128)S(1)}, u32[]{:S(2)}, u32[]{:S(2)}) collective-permute-start(f32[64,384]{1,0:T(8,128)S(1)} %bitcast_add_fusion.4.refs_3_), channel_id=1, source_target_pairs={{0,4},{1,5},{2,6},{3,7},{4,0},{5,1},{6,2},{7,3},{8,12},{9,13},{10,... | collective-permute-start | bytes 294920 | tf_op jit(solution)/shard_map/ppermute | solution.py:106
  39.8 25.9 %collective-permute-start.12 = (bf16[384,512]{1,0:T(8,128)(2,1)S(1)}, bf16[384,512]{1,0:T(8,128)(2,1)S(1)}, u32[]{:S(2)}, u32[]{:S(2)}) collective-permute-start(bf16[384,512]{1,0:T(8,128)(2,1)S(1)} %fusion.6.refs_1_), channel_id=1, source_target_pairs={{0,8},{1,9},{2,10},{3,11},{4,12},{5,13},{6,14},{7,15},{8,0},{9,1},... | collective-permute-start | bytes 1179656 | tf_op jit(solution)/shard_map/ppermute | solution.py:106
  47.8 15.1 %copy-start.1 = (bf16[32,64,512]{2,1,0:T(8,128)(2,1)S(1)}, bf16[32,64,512]{2,1,0:T(8,128)(2,1)}, u32[]{:S(2)}) copy-start(bf16[32,64,512]{2,1,0:T(8,128)(2,1)} %param.11) | copy-start | bytes 6291460
  47.8 15.1 %copy-start.2 = (s32[32]{0:T(128)S(1)}, s32[32]{0:T(128)}, u32[]{:S(2)}) copy-start(s32[32]{0:T(128)} %first_ref.1) | copy-start | bytes 388
  47.8 15.1 %copy-start.3 = (s32[32]{0:T(128)S(1)}, s32[32]{0:T(128)}, u32[]{:S(2)}) copy-start(s32[32]{0:T(128)} %length_ref.1) | copy-start | bytes 388
  47.9 17.8 %collective-permute-start.8 = (bf16[1,384,512]{2,1,0:T(8,128)(2,1)S(1)}, bf16[1,384,512]{2,1,0:T(8,128)(2,1)S(1)}, u32[]{:S(2)}, u32[]{:S(2)}) collective-permute-start(bf16[1,384,512]{2,1,0:T(8,128)(2,1)S(1)} %get-tuple-element.48), channel_id=1, source_target_pairs={{0,1},{1,0},{2,3},{3,2},{4,5},{5,4},{6,7},{7,6},{8,9},{9,8},{10,11... | collective-permute-start | bytes 1179656 | tf_op jit(solution)/shard_map/ppermute | solution.py:106
  49.2 16.5 %collective-permute-start.11 = (bf16[384,512]{1,0:T(8,128)(2,1)S(1)}, bf16[384,512]{1,0:T(8,128)(2,1)S(1)}, u32[]{:S(2)}, u32[]{:S(2)}) collective-permute-start(bf16[384,512]{1,0:T(8,128)(2,1)S(1)} %fusion.11), channel_id=1, source_target_pairs={{0,2},{1,3},{2,0},{3,1},{4,6},{5,7},{6,4},{7,5},{8,10},{9,11},{10,... | collective-permute-start | bytes 1179656 | tf_op jit(solution)/shard_map/ppermute | solution.py:106
  49.8 18.3 %collective-permute-start.13 = (bf16[384,512]{1,0:T(8,128)(2,1)S(1)}, bf16[384,512]{1,0:T(8,128)(2,1)S(1)}, u32[]{:S(2)}, u32[]{:S(2)}) collective-permute-start(bf16[384,512]{1,0:T(8,128)(2,1)S(1)} %fusion), channel_id=1, source_target_pairs={{0,4},{1,5},{2,6},{3,7},{4,0},{5,1},{6,2},{7,3},{8,12},{9,13},{10,... | collective-permute-start | bytes 1179656 | tf_op jit(solution)/shard_map/ppermute | solution.py:106
  51.7 9.8 %collective-permute-start.14 = (bf16[64,384]{1,0:T(8,128)(2,1)S(1)}, bf16[64,384]{1,0:T(8,128)(2,1)S(1)}, u32[]{:S(2)}, u32[]{:S(2)}) collective-permute-start(bf16[64,384]{1,0:T(8,128)(2,1)S(1)} %get-tuple-element.53), channel_id=1, source_target_pairs={{0,8},{1,9},{2,10},{3,11},{4,12},{5,13},{6,14},{7,15},{8,0},{9,1},... | collective-permute-start | bytes 147464 | tf_op jit(solution)/shard_map/ppermute | solution.py:106
  61.5 1.4 %collective-permute-start.15 = (f32[64,384]{1,0:T(8,128)S(1)}, f32[64,384]{1,0:T(8,128)S(1)}, u32[]{:S(2)}, u32[]{:S(2)}) collective-permute-start(f32[64,384]{1,0:T(8,128)S(1)} %convert_add_fusion), channel_id=1, source_target_pairs={{0,1},{1,0},{2,3},{3,2},{4,5},{5,4},{6,7},{7,6},{8,9},{9,8},{10,11... | collective-permute-start | bytes 294920 | tf_op jit(solution)/shard_map/ppermute | solution.py:106

commit v14 on v13

--- a/solution.py
+++ b/solution.py
@@ -11,7 +11,6 @@
 WINDOW = 128
 TOGETHER = 4
 FLOPS = 3_000_000_000
-FIRST_FLOPS = 3_000_000_000
 EXPAND_FLOPS = 1_000_000
 
 
@@ -137,41 +136,39 @@
 
 
 def expand_body(first_ref, length_ref, packed_ref, table_ref, result_ref, shrunk_ref):
-    group = pl.program_id(0)
-
-    @pl.when(group == 0)
-    def _():
-        shrunk_ref[...] = packed_ref[...].T.astype(jnp.bfloat16)
-        result_ref[...] = jnp.zeros_like(result_ref)
-
-    def body(window, masks):
-        shrunk = shrunk_ref[window, :]
-        spread = [jnp.where(mask, shrunk, jnp.zeros((), jnp.bfloat16)) for mask in masks]
-        part = jnp.dot(
-            jnp.concatenate(spread, axis=1), table_ref[...], preferred_element_type=jnp.float32
-        )
-        result_ref[window, :] = result_ref[window, :] + part
-
-    for_each_window(first_ref, length_ref, group, shrunk_ref.shape[0], body)
+    rows, rank = shrunk_ref.shape
+    span = TOGETHER * rank
+    shrunk_ref[...] = packed_ref[...].T.astype(jnp.bfloat16)
+    result_ref[...] = jnp.zeros_like(result_ref)
+
+    def step(group, carry):
+        def body(window, masks):
+            shrunk = shrunk_ref[window, :]
+            spread = [jnp.where(mask, shrunk, jnp.zeros((), jnp.bfloat16)) for mask in masks]
+            part = jnp.dot(
+                jnp.concatenate(spread, axis=1),
+                table_ref[pl.ds(pl.multiple_of(group * span, span), span), :],
+                preferred_element_type=jnp.float32,
+            )
+            result_ref[window, :] = result_ref[window, :] + part
+
+        for_each_window(first_ref, length_ref, group, rows, body)
+        return carry
+
+    lax.fori_loop(0, table_ref.shape[0] // span, step, 0)
 
 
 def expand(packed, expand_matrices, segment_first_row, segment_length):
     rows = packed.shape[1]
     adapters, rank, width = expand_matrices.shape
     table = expand_matrices.reshape(adapters * rank, width)
+    vmem = pl.BlockSpec(memory_space=pltpu.VMEM)
     return pl.pallas_call(
         expand_body,
-        grid_spec=pltpu.PrefetchScalarGridSpec(
-            num_scalar_prefetch=2,
-            grid=(adapters // TOGETHER,),
-            in_specs=[
-                pl.BlockSpec((rank, rows), lambda group, *_: (0, 0)),
-                pl.BlockSpec((TOGETHER * rank, width), lambda group, *_: (group, 0)),
-            ],
-            out_specs=pl.BlockSpec((rows, width), lambda group, *_: (0, 0)),
-            scratch_shapes=[pltpu.VMEM((rows, rank), jnp.bfloat16)],
-        ),
+        in_specs=[pl.BlockSpec(memory_space=pltpu.SMEM)] * 2 + [vmem] * 2,
+        out_specs=vmem,
         out_shape=jax.ShapeDtypeStruct((rows, width), jnp.float32),
+        scratch_shapes=[pltpu.VMEM((rows, rank), jnp.bfloat16)],
         compiler_params=pltpu.CompilerParams(vmem_limit_bytes=VMEM_LIMIT),
         cost_estimate=pl.CostEstimate(flops=EXPAND_FLOPS, bytes_accessed=1, transcendentals=0),
     )(segment_first_row, segment_length, packed, table)
@@ -194,7 +191,7 @@
 
     kept_home, crossed, incoming = {}, {}, {}
 
-    packed, steps = None, [near, *(4 << at for at in range((units - 1).bit_length())), core]
+    packed, steps = None, [core, *(4 << at for at in range((units - 1).bit_length())), near]
 
     def settle(unit, arrived):
         value = kept_home[unit] + arrived.astype(jnp.float32) + crossed[unit].astype(jnp.float32)
@@ -221,10 +218,10 @@
         sent, kept = 1 + (unit > 0), 1 + (unit < top) + (not unit)
         values, results, buffer = product(
             table, hidden, down_matrix, buffer, base, sent, kept, width, not unit,
-            FIRST_FLOPS if unit == top - 1 else FLOPS, ready,
+            FLOPS, ready,
         )
         base += sent + kept
-        if packed is not None and steps and steps[0] != core:
+        if packed is not None and steps and steps[0] != near:
             moved, results = lax.optimization_barrier((swap(packed, steps.pop(0), total), results))
             packed = packed + moved
         if unit < top:

time: 69.6 us -> 68.4 us (0.983)
  waiting for transfers between devices: 15.8 us -> 13.9 us
    ppermute x16, waiting for transfers between devices: 15.8 us -> 13.9 us  [swap(): lax.ppermute(value, 'tensor', [(place, place ^ bit) for place in range(to...]
  transfers between devices with their start and end apart: 16 -> 16, of which waited for: 5 -> 4; matrix products, arithmetic and copies ran while one was open for 8% -> 8% of each run, Pallas kernels for 34% -> 35%
where the time goes in v14:
time: 68.4 us; the launch traced here: 68 us
  Pallas kernels  26.7 us (39%)
  starting transfers between devices  18.5 us (27%)
  waiting for transfers between devices  13.9 us (20%)
  matrix products  3.92 us (6%)
  other arithmetic  3.3 us (5%)
  local copies, waits for them, and re-layouts  1.34 us (2%)
    pallas_call x5, Pallas kernels, product(): pl.pallas_call(functools.partial(product_body, base=base, sent=sent, kept...  24 us
    ppermute x16, starting transfers between devices, swap(): lax.ppermute(value, 'tensor', [(place, place ^ bit) for place in range(to...  18.5 us
    ppermute x16, waiting for transfers between devices, swap(): lax.ppermute(value, 'tensor', [(place, place ^ bit) for place in range(to...  13.9 us
    unnamed x1, matrix products  3.92 us
    pallas_call x1, Pallas kernels, expand(): pl.pallas_call(expand_body, in_specs=[pl.BlockSpec(memory_space=pltpu.SME...  2.71 us
  transfers between devices with their start and end apart: 16, of which 4 were waited for; matrix products, arithmetic and copies ran while one was open for 8% of the time, Pallas kernels for 35%

profile of v14, /device:TPU:0, one launch (start us, length us, event | category | flops | bytes accessed | tf_op | source)
XLA Modules:
  0.0 68.0 jit_solution(1261229745252417232)
XLA Ops:
  0.0 0.7 broadcast_xor_fusion.table_ref
  0.7 1.3 %copy-done = bf16[384,1664]{1,0:T(8,128)(2,1)S(1)} copy-done((bf16[384,1664]{1,0:T(8,128)(2,1)S(1)}, bf16[384,1664]{1,0:T(8,128)(2,1)}, u32[]{:S(2)}) %copy-start) | copy-done | bytes 1277976
  2.0 2.9 %shard_map.82 = (bf16[1,384,512]{2,1,0:T(8,128)(2,1)S(1)}, bf16[2,1664,512]{2,1,0:T(8,128)(2,1)S(1)}) custom-call(s32[16]{0:T(128)S(1)} %broadcast_xor_fusion.table_ref, bf16[384,1664]{1,0:T(8,128)(2,1)S(1)} %copy-done, bf16[1664,8192]{1,0:T(8,128)(2,1)} %down_ref.9), custom_call_target="tpu_custom_call" | custom-call | flops 3000000000 | bytes 1024 | tf_op jit(solution)/shard_map/pallas_call | solution.py:82
  5.4 4.4 %shard_map.83 = (bf16[2,384,512]{2,1,0:T(8,128)(2,1)S(1)}, f32[1,384,512]{2,1,0:T(8,128)S(1)}, bf16[2,1664,512]{2,1,0:T(8,128)(2,1)S(1)}) custom-call(s32[16]{0:T(128)S(1)} %broadcast_xor_fusion.table_ref, bf16[384,1664]{1,0:T(8,128)(2,1)S(1)} %copy-done, bf16[1664,8192]{1,0:T(8,128)(2,1)} %down_ref.9, ...), custom_call_target="tpu_custom_call", output_to_operand_aliasing={{2}: (3, {})} | custom-call | flops 3000000000 | bytes 1024 | tf_op jit(solution)/shard_map/pallas_call | solution.py:82
  10.1 3.0 %collective-permute-start.3 = (bf16[384,512]{1,0:T(8,128)(2,1)S(1)}, bf16[384,512]{1,0:T(8,128)(2,1)S(1)}, u32[]{:S(2)}, u32[]{:S(2)}) collective-permute-start(bf16[384,512]{1,0:T(8,128)(2,1)S(1)} %fusion.8.refs_1_), channel_id=1, source_target_pairs={{0,2},{1,3},{2,0},{3,1},{4,6},{5,7},{6,4},{7,5},{8,10},{9,11},{10,... | collective-permute-start | bytes 1179656 | tf_op jit(solution)/shard_map/ppermute | solution.py:105
  13.1 5.7 %shard_map.84 = (bf16[2,384,512]{2,1,0:T(8,128)(2,1)S(1)}, f32[2,384,512]{2,1,0:T(8,128)S(1)}, bf16[2,1664,512]{2,1,0:T(8,128)(2,1)S(1)}) custom-call(s32[16]{0:T(128)S(1)} %broadcast_xor_fusion.table_ref, bf16[384,1664]{1,0:T(8,128)(2,1)S(1)} %copy-done, bf16[1664,8192]{1,0:T(8,128)(2,1)} %down_ref.9, ...), custom_call_target="tpu_custom_call", output_to_operand_aliasing={{2}: (3, {})} | custom-call | flops 3000000000 | bytes 1024 | tf_op jit(solution)/shard_map/pallas_call | solution.py:82
  19.0 3.9 %fusion.13 = f32[384,2048]{0,1:S(1)} fusion(bf16[384,1664]{1,0:T(8,128)(2,1)S(1)} %copy-done, bf16[1664,2048]{0,1:T(8,128)(2,1)S(1)} %bitcast.47), kind=kOutput, calls=%fused_computation.26 | convolution fusion | flops 2617245696 | bytes 11239424
  23.2 1.3 %collective-permute-start.6 = (bf16[384,512]{1,0:T(8,128)(2,1)S(1)}, bf16[384,512]{1,0:T(8,128)(2,1)S(1)}, u32[]{:S(2)}, u32[]{:S(2)}) collective-permute-start(bf16[384,512]{1,0:T(8,128)(2,1)S(1)} %fusion.9.refs_2_), channel_id=1, source_target_pairs={{0,2},{1,3},{2,0},{3,1},{4,6},{5,7},{6,4},{7,5},{8,10},{9,11},{10,... | collective-permute-start | bytes 1179656 | tf_op jit(solution)/shard_map/ppermute | solution.py:105
  24.6 1.6 %collective-permute-start.7 = (bf16[384,512]{1,0:T(8,128)(2,1)S(1)}, bf16[384,512]{1,0:T(8,128)(2,1)S(1)}, u32[]{:S(2)}, u32[]{:S(2)}) collective-permute-start(bf16[384,512]{1,0:T(8,128)(2,1)S(1)} %fusion.7.refs_1_), channel_id=1, source_target_pairs={{0,4},{1,5},{2,6},{3,7},{4,0},{5,1},{6,2},{7,3},{8,12},{9,13},{10,... | collective-permute-start | bytes 1179656 | tf_op jit(solution)/shard_map/ppermute | solution.py:105
  26.6 5.6 %shard_map.85 = (bf16[2,384,512]{2,1,0:T(8,128)(2,1)S(1)}, f32[2,384,512]{2,1,0:T(8,128)S(1)}, bf16[2,1664,512]{2,1,0:T(8,128)(2,1)S(1)}) custom-call(s32[16]{0:T(128)S(1)} %broadcast_xor_fusion.table_ref, bf16[384,1664]{1,0:T(8,128)(2,1)S(1)} %copy-done, bf16[1664,8192]{1,0:T(8,128)(2,1)} %down_ref.9, ...), custom_call_target="tpu_custom_call", output_to_operand_aliasing={{2}: (3, {})} | custom-call | flops 3000000000 | bytes 1024 | tf_op jit(solution)/shard_map/pallas_call | solution.py:82
  32.2 0.6 collective-permute-start.9
  32.8 2.0 %collective-permute-done.6 = bf16[384,512]{1,0:T(8,128)(2,1)S(1)} collective-permute-done((bf16[384,512]{1,0:T(8,128)(2,1)S(1)}, bf16[384,512]{1,0:T(8,128)(2,1)S(1)}, u32[]{:S(2)}, u32[]{:S(2)}) %collective-permute-start.6) | collective-permute-done | bytes 393248 | tf_op jit(solution)/shard_map/ppermute | solution.py:105
  35.5 1.4 %collective-permute-start.10 = (bf16[384,512]{1,0:T(8,128)(2,1)S(1)}, bf16[384,512]{1,0:T(8,128)(2,1)S(1)}, u32[]{:S(2)}, u32[]{:S(2)}) collective-permute-start(bf16[384,512]{1,0:T(8,128)(2,1)S(1)} %fusion.10.refs_2_), channel_id=1, source_target_pairs={{0,2},{1,3},{2,0},{3,1},{4,6},{5,7},{6,4},{7,5},{8,10},{9,11},{10,... | collective-permute-start | bytes 1179656 | tf_op jit(solution)/shard_map/ppermute | solution.py:105
  37.0 1.6 %collective-permute-start.4 = (f32[64,384]{1,0:T(8,128)S(1)}, f32[64,384]{1,0:T(8,128)S(1)}, u32[]{:S(2)}, u32[]{:S(2)}) collective-permute-start(f32[64,384]{1,0:T(8,128)S(1)} %bitcast_add_fusion.4.refs_3_), channel_id=1, source_target_pairs={{0,4},{1,5},{2,6},{3,7},{4,0},{5,1},{6,2},{7,3},{8,12},{9,13},{10,... | collective-permute-start | bytes 294920 | tf_op jit(solution)/shard_map/ppermute | solution.py:105
  38.6 2.6 %collective-permute-start.12 = (bf16[384,512]{1,0:T(8,128)(2,1)S(1)}, bf16[384,512]{1,0:T(8,128)(2,1)S(1)}, u32[]{:S(2)}, u32[]{:S(2)}) collective-permute-start(bf16[384,512]{1,0:T(8,128)(2,1)S(1)} %fusion.6.refs_1_), channel_id=1, source_target_pairs={{0,8},{1,9},{2,10},{3,11},{4,12},{5,13},{6,14},{7,15},{8,0},{9,1},... | collective-permute-start | bytes 1179656 | tf_op jit(solution)/shard_map/ppermute | solution.py:105
  41.1 5.4 %shard_map.86 = (bf16[1,384,512]{2,1,0:T(8,128)(2,1)S(1)}, f32[3,384,512]{2,1,0:T(8,128)S(1)}, bf16[2,1664,512]{2,1,0:T(8,128)(2,1)S(1)}) custom-call(s32[16]{0:T(128)S(1)} %broadcast_xor_fusion.table_ref, bf16[384,1664]{1,0:T(8,128)(2,1)S(1)} %copy-done, bf16[1664,8192]{1,0:T(8,128)(2,1)} %down_ref.9, ...), custom_call_target="tpu_custom_call", output_to_operand_aliasing={{2}: (3, {})} | custom-call | flops 3000000000 | bytes 1024 | tf_op jit(solution)/shard_map/pallas_call | solution.py:82
  47.0 1.0 %collective-permute-start.11 = (bf16[384,512]{1,0:T(8,128)(2,1)S(1)}, bf16[384,512]{1,0:T(8,128)(2,1)S(1)}, u32[]{:S(2)}, u32[]{:S(2)}) collective-permute-start(bf16[384,512]{1,0:T(8,128)(2,1)S(1)} %fusion.11), channel_id=1, source_target_pairs={{0,2},{1,3},{2,0},{3,1},{4,6},{5,7},{6,4},{7,5},{8,10},{9,11},{10,... | collective-permute-start | bytes 1179656 | tf_op jit(solution)/shard_map/ppermute | solution.py:105
  48.0 1.3 %collective-permute-start.13 = (bf16[384,512]{1,0:T(8,128)(2,1)S(1)}, bf16[384,512]{1,0:T(8,128)(2,1)S(1)}, u32[]{:S(2)}, u32[]{:S(2)}) collective-permute-start(bf16[384,512]{1,0:T(8,128)(2,1)S(1)} %fusion), channel_id=1, source_target_pairs={{0,4},{1,5},{2,6},{3,7},{4,0},{5,1},{6,2},{7,3},{8,12},{9,13},{10,... | collective-permute-start | bytes 1179656 | tf_op jit(solution)/shard_map/ppermute | solution.py:105
  49.3 2.6 %collective-permute-start.14 = (bf16[64,384]{1,0:T(8,128)(2,1)S(1)}, bf16[64,384]{1,0:T(8,128)(2,1)S(1)}, u32[]{:S(2)}, u32[]{:S(2)}) collective-permute-start(bf16[64,384]{1,0:T(8,128)(2,1)S(1)} %get-tuple-element.53), channel_id=1, source_target_pairs={{0,8},{1,9},{2,10},{3,11},{4,12},{5,13},{6,14},{7,15},{8,0},{9,1},... | collective-permute-start | bytes 147464 | tf_op jit(solution)/shard_map/ppermute | solution.py:105
  51.9 7.5 %collective-permute-done.14 = bf16[64,384]{1,0:T(8,128)(2,1)S(1)} collective-permute-done((bf16[64,384]{1,0:T(8,128)(2,1)S(1)}, bf16[64,384]{1,0:T(8,128)(2,1)S(1)}, u32[]{:S(2)}, u32[]{:S(2)}) %collective-permute-start.14) | collective-permute-done | bytes 49184 | tf_op jit(solution)/shard_map/ppermute | solution.py:105
  59.4 0.7 collective-permute-start.15
  60.1 4.0 %collective-permute-done.15 = f32[64,384]{1,0:T(8,128)S(1)} collective-permute-done((f32[64,384]{1,0:T(8,128)S(1)}, f32[64,384]{1,0:T(8,128)S(1)}, u32[]{:S(2)}, u32[]{:S(2)}) %collective-permute-start.15) | collective-permute-done | bytes 98336 | tf_op jit(solution)/shard_map/ppermute | solution.py:105
  64.1 2.7 %shard_map.87 = f32[384,512]{1,0:T(8,128)S(1)} custom-call(s32[32]{0:T(128)S(1)} %copy-done.2, s32[32]{0:T(128)S(1)} %copy-done.3, f32[64,384]{1,0:T(8,128)S(1)} %add.98.packed_ref, bf16[2048,512]{1,0:T(8,128)(2,1)S(1)} %bitcast.41), custom_call_target="tpu_custom_call" | custom-call | flops 1000000 | bytes 1 | tf_op jit(solution)/shard_map/pallas_call | solution.py:166
  66.9 1.1 %fusion.4 = bf16[384,512]{1,0:T(8,128)(2,1)} fusion(f32[384,512]{1,0:T(8,128)S(1)} %shard_map.87, bf16[384,512]{1,0:T(8,128)(2,1)S(1)} %collective-permute-done.13, bf16[384,512]{1,0:T(8,128)(2,1)S(1)} %collective-permute-done.12, bf16[384,512]{1,0:T(8,128)(2,1)S(1)} %collective-permute-done.11, bf16[1,384,512]{2,1,0:T(8,128)(2,1)S(1)} %collective-permute-done.8, ...), kind=kLoop, calls=%fused_computation.7 | loop fusion | flops 1966080 | bytes 3538944 | tf_op jit(solution)/shard_map/convert_element_type | solution.py:249
  (45 shorter events, 2.9 us)
Async XLA Ops:
  0.7 1.3 %copy-start = (bf16[384,1664]{1,0:T(8,128)(2,1)S(1)}, bf16[384,1664]{1,0:T(8,128)(2,1)}, u32[]{:S(2)}) copy-start(bf16[384,1664]{1,0:T(8,128)(2,1)} %hidden_ref.9) | copy-start | bytes 3833860
  4.9 5.1 %collective-permute-start = (bf16[1,384,512]{2,1,0:T(8,128)(2,1)S(1)}, bf16[1,384,512]{2,1,0:T(8,128)(2,1)S(1)}, u32[]{:S(2)}, u32[]{:S(2)}) collective-permute-start(bf16[1,384,512]{2,1,0:T(8,128)(2,1)S(1)} %get-tuple-element.32), channel_id=1, source_target_pairs={{0,1},{1,0},{2,3},{3,2},{4,5},{5,4},{6,7},{7,6},{8,9},{9,8},{10,11... | collective-permute-start | bytes 1179656 | tf_op jit(solution)/shard_map/ppermute | solution.py:105
  5.4 4.6 %copy-start.4 = (s32[384]{0:T(512)S(1)}, s32[384]{0:T(512)}, u32[]{:S(2)}) copy-start(s32[384]{0:T(512)} %param.12) | copy-start | bytes 4612
  9.8 13.1 %collective-permute-start.2 = (bf16[2,384,512]{2,1,0:T(8,128)(2,1)S(1)}, bf16[2,384,512]{2,1,0:T(8,128)(2,1)S(1)}, u32[]{:S(2)}, u32[]{:S(2)}) collective-permute-start(bf16[2,384,512]{2,1,0:T(8,128)(2,1)S(1)} %get-tuple-element.36), channel_id=1, source_target_pairs={{0,1},{1,0},{2,3},{3,2},{4,5},{5,4},{6,7},{7,6},{8,9},{9,8},{10,11... | collective-permute-start | bytes 2359304 | tf_op jit(solution)/shard_map/ppermute | solution.py:105
  10.0 9.0 %slice-start = ((s8[6815744]{0:T(1024)(128)(4,1)}), s8[4194304]{0:T(1024)(128)(4,1)S(1)}, s32[]{:S(2)}) async-start(s8[6815744]{0:T(1024)(128)(4,1)} %bitcast.45), calls=%async_computation | async-start | bytes 8388608
  10.1 12.8 %collective-permute-start.3 = (bf16[384,512]{1,0:T(8,128)(2,1)S(1)}, bf16[384,512]{1,0:T(8,128)(2,1)S(1)}, u32[]{:S(2)}, u32[]{:S(2)}) collective-permute-start(bf16[384,512]{1,0:T(8,128)(2,1)S(1)} %fusion.8.refs_1_), channel_id=1, source_target_pairs={{0,2},{1,3},{2,0},{3,1},{4,6},{5,7},{6,4},{7,5},{8,10},{9,11},{10,... | collective-permute-start | bytes 1179656 | tf_op jit(solution)/shard_map/ppermute | solution.py:105
  13.1 5.8 %slice-start.1 = ((s8[6815744]{0:T(1024)(128)(4,1)}), s8[2621440]{0:T(1024)(128)(4,1)S(1)}, s32[]{:S(2)}) async-start(s8[6815744]{0:T(1024)(128)(4,1)} %bitcast.45), calls=%async_computation.1 | async-start | bytes 5242880
  18.9 16.3 %collective-permute-start.5 = (bf16[2,384,512]{2,1,0:T(8,128)(2,1)S(1)}, bf16[2,384,512]{2,1,0:T(8,128)(2,1)S(1)}, u32[]{:S(2)}, u32[]{:S(2)}) collective-permute-start(bf16[2,384,512]{2,1,0:T(8,128)(2,1)S(1)} %get-tuple-element.43), channel_id=1, source_target_pairs={{0,1},{1,0},{2,3},{3,2},{4,5},{5,4},{6,7},{7,6},{8,9},{9,8},{10,11... | collective-permute-start | bytes 2359304 | tf_op jit(solution)/shard_map/ppermute | solution.py:105
  23.2 11.6 %collective-permute-start.6 = (bf16[384,512]{1,0:T(8,128)(2,1)S(1)}, bf16[384,512]{1,0:T(8,128)(2,1)S(1)}, u32[]{:S(2)}, u32[]{:S(2)}) collective-permute-start(bf16[384,512]{1,0:T(8,128)(2,1)S(1)} %fusion.9.refs_2_), channel_id=1, source_target_pairs={{0,2},{1,3},{2,0},{3,1},{4,6},{5,7},{6,4},{7,5},{8,10},{9,11},{10,... | collective-permute-start | bytes 1179656 | tf_op jit(solution)/shard_map/ppermute | solution.py:105
  24.6 10.6 %collective-permute-start.7 = (bf16[384,512]{1,0:T(8,128)(2,1)S(1)}, bf16[384,512]{1,0:T(8,128)(2,1)S(1)}, u32[]{:S(2)}, u32[]{:S(2)}) collective-permute-start(bf16[384,512]{1,0:T(8,128)(2,1)S(1)} %fusion.7.refs_1_), channel_id=1, source_target_pairs={{0,4},{1,5},{2,6},{3,7},{4,0},{5,1},{6,2},{7,3},{8,12},{9,13},{10,... | collective-permute-start | bytes 1179656 | tf_op jit(solution)/shard_map/ppermute | solution.py:105
  26.5 5.7 %collective-permute-start.1 = (f32[64,384]{1,0:T(8,128)S(1)}, f32[64,384]{1,0:T(8,128)S(1)}, u32[]{:S(2)}, u32[]{:S(2)}) collective-permute-start(f32[64,384]{1,0:T(8,128)S(1)} %bitcast.42), channel_id=1, source_target_pairs={{0,1},{1,0},{2,3},{3,2},{4,5},{5,4},{6,7},{7,6},{8,9},{9,8},{10,11... | collective-permute-start | bytes 294920 | tf_op jit(solution)/shard_map/ppermute | solution.py:105
  32.2 14.5 %collective-permute-start.9 = (bf16[2,384,512]{2,1,0:T(8,128)(2,1)S(1)}, bf16[2,384,512]{2,1,0:T(8,128)(2,1)S(1)}, u32[]{:S(2)}, u32[]{:S(2)}) collective-permute-start(bf16[2,384,512]{2,1,0:T(8,128)(2,1)S(1)} %get-tuple-element.49), channel_id=1, source_target_pairs={{0,1},{1,0},{2,3},{3,2},{4,5},{5,4},{6,7},{7,6},{8,9},{9,8},{10,11... | collective-permute-start | bytes 2359304 | tf_op jit(solution)/shard_map/ppermute | solution.py:105
  35.5 11.1 %collective-permute-start.10 = (bf16[384,512]{1,0:T(8,128)(2,1)S(1)}, bf16[384,512]{1,0:T(8,128)(2,1)S(1)}, u32[]{:S(2)}, u32[]{:S(2)}) collective-permute-start(bf16[384,512]{1,0:T(8,128)(2,1)S(1)} %fusion.10.refs_2_), channel_id=1, source_target_pairs={{0,2},{1,3},{2,0},{3,1},{4,6},{5,7},{6,4},{7,5},{8,10},{9,11},{10,... | collective-permute-start | bytes 1179656 | tf_op jit(solution)/shard_map/ppermute | solution.py:105
  37.0 9.6 %collective-permute-start.4 = (f32[64,384]{1,0:T(8,128)S(1)}, f32[64,384]{1,0:T(8,128)S(1)}, u32[]{:S(2)}, u32[]{:S(2)}) collective-permute-start(f32[64,384]{1,0:T(8,128)S(1)} %bitcast_add_fusion.4.refs_3_), channel_id=1, source_target_pairs={{0,4},{1,5},{2,6},{3,7},{4,0},{5,1},{6,2},{7,3},{8,12},{9,13},{10,... | collective-permute-start | bytes 294920 | tf_op jit(solution)/shard_map/ppermute | solution.py:105
  38.6 28.3 %collective-permute-start.12 = (bf16[384,512]{1,0:T(8,128)(2,1)S(1)}, bf16[384,512]{1,0:T(8,128)(2,1)S(1)}, u32[]{:S(2)}, u32[]{:S(2)}) collective-permute-start(bf16[384,512]{1,0:T(8,128)(2,1)S(1)} %fusion.6.refs_1_), channel_id=1, source_target_pairs={{0,8},{1,9},{2,10},{3,11},{4,12},{5,13},{6,14},{7,15},{8,0},{9,1},... | collective-permute-start | bytes 1179656 | tf_op jit(solution)/shard_map/ppermute | solution.py:105
  46.5 17.6 %copy-start.1 = (bf16[32,64,512]{2,1,0:T(8,128)(2,1)S(1)}, bf16[32,64,512]{2,1,0:T(8,128)(2,1)}, u32[]{:S(2)}) copy-start(bf16[32,64,512]{2,1,0:T(8,128)(2,1)} %param.11) | copy-start | bytes 6291460
  46.5 17.6 %copy-start.2 = (s32[32]{0:T(128)S(1)}, s32[32]{0:T(128)}, u32[]{:S(2)}) copy-start(s32[32]{0:T(128)} %first_ref.1) | copy-start | bytes 388
  46.5 17.6 %copy-start.3 = (s32[32]{0:T(128)S(1)}, s32[32]{0:T(128)}, u32[]{:S(2)}) copy-start(s32[32]{0:T(128)} %length_ref.1) | copy-start | bytes 388
  46.6 20.3 %collective-permute-start.8 = (bf16[1,384,512]{2,1,0:T(8,128)(2,1)S(1)}, bf16[1,384,512]{2,1,0:T(8,128)(2,1)S(1)}, u32[]{:S(2)}, u32[]{:S(2)}) collective-permute-start(bf16[1,384,512]{2,1,0:T(8,128)(2,1)S(1)} %get-tuple-element.48), channel_id=1, source_target_pairs={{0,1},{1,0},{2,3},{3,2},{4,5},{5,4},{6,7},{7,6},{8,9},{9,8},{10,11... | collective-permute-start | bytes 1179656 | tf_op jit(solution)/shard_map/ppermute | solution.py:105
  47.0 19.9 %collective-permute-start.11 = (bf16[384,512]{1,0:T(8,128)(2,1)S(1)}, bf16[384,512]{1,0:T(8,128)(2,1)S(1)}, u32[]{:S(2)}, u32[]{:S(2)}) collective-permute-start(bf16[384,512]{1,0:T(8,128)(2,1)S(1)} %fusion.11), channel_id=1, source_target_pairs={{0,2},{1,3},{2,0},{3,1},{4,6},{5,7},{6,4},{7,5},{8,10},{9,11},{10,... | collective-permute-start | bytes 1179656 | tf_op jit(solution)/shard_map/ppermute | solution.py:105
  48.0 18.9 %collective-permute-start.13 = (bf16[384,512]{1,0:T(8,128)(2,1)S(1)}, bf16[384,512]{1,0:T(8,128)(2,1)S(1)}, u32[]{:S(2)}, u32[]{:S(2)}) collective-permute-start(bf16[384,512]{1,0:T(8,128)(2,1)S(1)} %fusion), channel_id=1, source_target_pairs={{0,4},{1,5},{2,6},{3,7},{4,0},{5,1},{6,2},{7,3},{8,12},{9,13},{10,... | collective-permute-start | bytes 1179656 | tf_op jit(solution)/shard_map/ppermute | solution.py:105
  49.3 10.1 %collective-permute-start.14 = (bf16[64,384]{1,0:T(8,128)(2,1)S(1)}, bf16[64,384]{1,0:T(8,128)(2,1)S(1)}, u32[]{:S(2)}, u32[]{:S(2)}) collective-permute-start(bf16[64,384]{1,0:T(8,128)(2,1)S(1)} %get-tuple-element.53), channel_id=1, source_target_pairs={{0,8},{1,9},{2,10},{3,11},{4,12},{5,13},{6,14},{7,15},{8,0},{9,1},... | collective-permute-start | bytes 147464 | tf_op jit(solution)/shard_map/ppermute | solution.py:105
  59.4 4.7 %collective-permute-start.15 = (f32[64,384]{1,0:T(8,128)S(1)}, f32[64,384]{1,0:T(8,128)S(1)}, u32[]{:S(2)}, u32[]{:S(2)}) collective-permute-start(f32[64,384]{1,0:T(8,128)S(1)} %convert_add_fusion), channel_id=1, source_target_pairs={{0,2},{1,3},{2,0},{3,1},{4,6},{5,7},{6,4},{7,5},{8,10},{9,11},{10,... | collective-permute-start | bytes 294920 | tf_op jit(solution)/shard_map/ppermute | solution.py:105

commit v15 on v14

--- a/solution.py
+++ b/solution.py
@@ -191,7 +191,10 @@
 
     kept_home, crossed, incoming = {}, {}, {}
 
-    packed, steps = None, [core, *(4 << at for at in range((units - 1).bit_length())), near]
+    packed, steps = None, [core, *(4 << at for at in reversed(range((units - 1).bit_length()))), near]
+
+    def step(value, bit):
+        return swap(value.astype(jnp.bfloat16 if bit > near else jnp.float32), bit, total)
 
     def settle(unit, arrived):
         value = kept_home[unit] + arrived.astype(jnp.float32) + crossed[unit].astype(jnp.float32)
@@ -222,8 +225,8 @@
         )
         base += sent + kept
         if packed is not None and steps and steps[0] != near:
-            moved, results = lax.optimization_barrier((swap(packed, steps.pop(0), total), results))
-            packed = packed + moved
+            moved, results = lax.optimization_barrier((step(packed, steps.pop(0)), results))
+            packed = packed + moved.astype(jnp.float32)
         if unit < top:
             kept_home[unit + 1] = results[1]
         if not unit:
@@ -243,8 +246,7 @@
     kept = [settle(0, swap(values, core, total)[0])]
 
     for bit in steps:
-        kind = jnp.bfloat16 if bit > near else jnp.float32
-        packed = packed + swap(packed.astype(kind), bit, total).astype(jnp.float32)
+        packed = packed + step(packed, bit).astype(jnp.float32)
     adapter_output = expand(packed, expand_matrices, segment_first_row, segment_length)
     return (kept[0] + adapter_output).astype(jnp.bfloat16)
 

time: 68.4 us -> 78.2 us (1.14)
  waiting for transfers between devices: 13.9 us -> 26.1 us
  starting transfers between devices: 18.5 us -> 16.2 us
    ppermute x16, waiting for transfers between devices: 13.9 us -> 26.1 us  [swap(): lax.ppermute(value, 'tensor', [(place, place ^ bit) for place in range(to...]
    ppermute x16, starting transfers between devices: 18.5 us -> 16.2 us  [swap(): lax.ppermute(value, 'tensor', [(place, place ^ bit) for place in range(to...]
  transfers between devices with their start and end apart: 16 -> 16, of which waited for: 4 -> 5; matrix products, arithmetic and copies ran while one was open for 8% -> 7% of each run, Pallas kernels for 35% -> 31%
where the time goes in v15:
time: 78.2 us; the launch traced here: 77.8 us
  Pallas kernels  26.7 us (34%)
  waiting for transfers between devices  26.1 us (33%)
  starting transfers between devices  16.2 us (21%)
  matrix products  3.92 us (5%)
  other arithmetic  3.3 us (4%)
  local copies, waits for them, and re-layouts  1.34 us (2%)
    ppermute x16, waiting for transfers between devices, swap(): lax.ppermute(value, 'tensor', [(place, place ^ bit) for place in range(to...  26.1 us
    pallas_call x5, Pallas kernels, product(): pl.pallas_call(functools.partial(product_body, base=base, sent=sent, kept...  24 us
    ppermute x16, starting transfers between devices, swap(): lax.ppermute(value, 'tensor', [(place, place ^ bit) for place in range(to...  16.2 us
    unnamed x1, matrix products  3.92 us
    pallas_call x1, Pallas kernels, expand(): pl.pallas_call(expand_body, in_specs=[pl.BlockSpec(memory_space=pltpu.SME...  2.71 us
  transfers between devices with their start and end apart: 16, of which 5 were waited for; matrix products, arithmetic and copies ran while one was open for 7% of the time, Pallas kernels for 31%

profile of v15, /device:TPU:0, one launch (start us, length us, event | category | flops | bytes accessed | tf_op | source)
XLA Modules:
  0.0 77.8 jit_solution(4150112764342359296)
XLA Ops:
  0.0 0.7 broadcast_xor_fusion.table_ref
  0.7 1.3 %copy-done = bf16[384,1664]{1,0:T(8,128)(2,1)S(1)} copy-done((bf16[384,1664]{1,0:T(8,128)(2,1)S(1)}, bf16[384,1664]{1,0:T(8,128)(2,1)}, u32[]{:S(2)}) %copy-start) | copy-done | bytes 1277976
  2.0 2.9 %shard_map.82 = (bf16[1,384,512]{2,1,0:T(8,128)(2,1)S(1)}, bf16[2,1664,512]{2,1,0:T(8,128)(2,1)S(1)}) custom-call(s32[16]{0:T(128)S(1)} %broadcast_xor_fusion.table_ref, bf16[384,1664]{1,0:T(8,128)(2,1)S(1)} %copy-done, bf16[1664,8192]{1,0:T(8,128)(2,1)} %down_ref.9), custom_call_target="tpu_custom_call" | custom-call | flops 3000000000 | bytes 1024 | tf_op jit(solution)/shard_map/pallas_call | solution.py:82
  5.4 4.4 %shard_map.83 = (bf16[2,384,512]{2,1,0:T(8,128)(2,1)S(1)}, f32[1,384,512]{2,1,0:T(8,128)S(1)}, bf16[2,1664,512]{2,1,0:T(8,128)(2,1)S(1)}) custom-call(s32[16]{0:T(128)S(1)} %broadcast_xor_fusion.table_ref, bf16[384,1664]{1,0:T(8,128)(2,1)S(1)} %copy-done, bf16[1664,8192]{1,0:T(8,128)(2,1)} %down_ref.9, ...), custom_call_target="tpu_custom_call", output_to_operand_aliasing={{2}: (3, {})} | custom-call | flops 3000000000 | bytes 1024 | tf_op jit(solution)/shard_map/pallas_call | solution.py:82
  10.1 3.0 %collective-permute-start.3 = (bf16[384,512]{1,0:T(8,128)(2,1)S(1)}, bf16[384,512]{1,0:T(8,128)(2,1)S(1)}, u32[]{:S(2)}, u32[]{:S(2)}) collective-permute-start(bf16[384,512]{1,0:T(8,128)(2,1)S(1)} %fusion.8.refs_1_), channel_id=1, source_target_pairs={{0,2},{1,3},{2,0},{3,1},{4,6},{5,7},{6,4},{7,5},{8,10},{9,11},{10,... | collective-permute-start | bytes 1179656 | tf_op jit(solution)/shard_map/ppermute | solution.py:105
  13.1 5.7 %shard_map.84 = (bf16[2,384,512]{2,1,0:T(8,128)(2,1)S(1)}, f32[2,384,512]{2,1,0:T(8,128)S(1)}, bf16[2,1664,512]{2,1,0:T(8,128)(2,1)S(1)}) custom-call(s32[16]{0:T(128)S(1)} %broadcast_xor_fusion.table_ref, bf16[384,1664]{1,0:T(8,128)(2,1)S(1)} %copy-done, bf16[1664,8192]{1,0:T(8,128)(2,1)} %down_ref.9, ...), custom_call_target="tpu_custom_call", output_to_operand_aliasing={{2}: (3, {})} | custom-call | flops 3000000000 | bytes 1024 | tf_op jit(solution)/shard_map/pallas_call | solution.py:82
  19.0 3.9 %fusion.14 = f32[384,2048]{0,1:S(1)} fusion(bf16[384,1664]{1,0:T(8,128)(2,1)S(1)} %copy-done, bf16[1664,2048]{0,1:T(8,128)(2,1)S(1)} %bitcast.48), kind=kOutput, calls=%fused_computation.28 | convolution fusion | flops 2617245696 | bytes 11239424
  23.1 1.6 %collective-permute-start.7 = (bf16[384,512]{1,0:T(8,128)(2,1)S(1)}, bf16[384,512]{1,0:T(8,128)(2,1)S(1)}, u32[]{:S(2)}, u32[]{:S(2)}) collective-permute-start(bf16[384,512]{1,0:T(8,128)(2,1)S(1)} %fusion.7.refs_1_), channel_id=1, source_target_pairs={{0,4},{1,5},{2,6},{3,7},{4,0},{5,1},{6,2},{7,3},{8,12},{9,13},{10,... | collective-permute-start | bytes 1179656 | tf_op jit(solution)/shard_map/ppermute | solution.py:105
  24.8 1.4 %collective-permute-start.6 = (bf16[384,512]{1,0:T(8,128)(2,1)S(1)}, bf16[384,512]{1,0:T(8,128)(2,1)S(1)}, u32[]{:S(2)}, u32[]{:S(2)}) collective-permute-start(bf16[384,512]{1,0:T(8,128)(2,1)S(1)} %fusion.9.refs_2_), channel_id=1, source_target_pairs={{0,2},{1,3},{2,0},{3,1},{4,6},{5,7},{6,4},{7,5},{8,10},{9,11},{10,... | collective-permute-start | bytes 1179656 | tf_op jit(solution)/shard_map/ppermute | solution.py:105
  26.7 5.6 %shard_map.85 = (bf16[2,384,512]{2,1,0:T(8,128)(2,1)S(1)}, f32[2,384,512]{2,1,0:T(8,128)S(1)}, bf16[2,1664,512]{2,1,0:T(8,128)(2,1)S(1)}) custom-call(s32[16]{0:T(128)S(1)} %broadcast_xor_fusion.table_ref, bf16[384,1664]{1,0:T(8,128)(2,1)S(1)} %copy-done, bf16[1664,8192]{1,0:T(8,128)(2,1)} %down_ref.9, ...), custom_call_target="tpu_custom_call", output_to_operand_aliasing={{2}: (3, {})} | custom-call | flops 3000000000 | bytes 1024 | tf_op jit(solution)/shard_map/pallas_call | solution.py:82
  32.3 0.6 collective-permute-start.9
  32.8 1.8 %collective-permute-done.7 = bf16[384,512]{1,0:T(8,128)(2,1)S(1)} collective-permute-done((bf16[384,512]{1,0:T(8,128)(2,1)S(1)}, bf16[384,512]{1,0:T(8,128)(2,1)S(1)}, u32[]{:S(2)}, u32[]{:S(2)}) %collective-permute-start.7) | collective-permute-done | bytes 393248 | tf_op jit(solution)/shard_map/ppermute | solution.py:105
  34.6 1.5 %collective-permute-done.6 = bf16[384,512]{1,0:T(8,128)(2,1)S(1)} collective-permute-done((bf16[384,512]{1,0:T(8,128)(2,1)S(1)}, bf16[384,512]{1,0:T(8,128)(2,1)S(1)}, u32[]{:S(2)}, u32[]{:S(2)}) %collective-permute-start.6) | collective-permute-done | bytes 393248 | tf_op jit(solution)/shard_map/ppermute | solution.py:105
  36.5 1.0 %collective-permute-start.10 = (bf16[384,512]{1,0:T(8,128)(2,1)S(1)}, bf16[384,512]{1,0:T(8,128)(2,1)S(1)}, u32[]{:S(2)}, u32[]{:S(2)}) collective-permute-start(bf16[384,512]{1,0:T(8,128)(2,1)S(1)} %fusion.10.refs_2_), channel_id=1, source_target_pairs={{0,2},{1,3},{2,0},{3,1},{4,6},{5,7},{6,4},{7,5},{8,10},{9,11},{10,... | collective-permute-start | bytes 1179656 | tf_op jit(solution)/shard_map/ppermute | solution.py:105
  37.4 2.7 %collective-permute-start.4 = (bf16[64,384]{1,0:T(8,128)(2,1)S(1)}, bf16[64,384]{1,0:T(8,128)(2,1)S(1)}, u32[]{:S(2)}, u32[]{:S(2)}) collective-permute-start(bf16[64,384]{1,0:T(8,128)(2,1)S(1)} %get-tuple-element.53), channel_id=1, source_target_pairs={{0,8},{1,9},{2,10},{3,11},{4,12},{5,13},{6,14},{7,15},{8,0},{9,1},... | collective-permute-start | bytes 147464 | tf_op jit(solution)/shard_map/ppermute | solution.py:105
  40.4 5.4 %shard_map.86 = (bf16[1,384,512]{2,1,0:T(8,128)(2,1)S(1)}, f32[3,384,512]{2,1,0:T(8,128)S(1)}, bf16[2,1664,512]{2,1,0:T(8,128)(2,1)S(1)}) custom-call(s32[16]{0:T(128)S(1)} %broadcast_xor_fusion.table_ref, bf16[384,1664]{1,0:T(8,128)(2,1)S(1)} %copy-done, bf16[1664,8192]{1,0:T(8,128)(2,1)} %down_ref.9, ...), custom_call_target="tpu_custom_call", output_to_operand_aliasing={{2}: (3, {})} | custom-call | flops 3000000000 | bytes 1024 | tf_op jit(solution)/shard_map/pallas_call | solution.py:82
  45.8 5.9 %collective-permute-done.4 = bf16[64,384]{1,0:T(8,128)(2,1)S(1)} collective-permute-done((bf16[64,384]{1,0:T(8,128)(2,1)S(1)}, bf16[64,384]{1,0:T(8,128)(2,1)S(1)}, u32[]{:S(2)}, u32[]{:S(2)}) %collective-permute-start.4) | collective-permute-done | bytes 49184 | tf_op jit(solution)/shard_map/ppermute | solution.py:105
  52.1 1.4 %collective-permute-start.11 = (bf16[384,512]{1,0:T(8,128)(2,1)S(1)}, bf16[384,512]{1,0:T(8,128)(2,1)S(1)}, u32[]{:S(2)}, u32[]{:S(2)}) collective-permute-start(bf16[384,512]{1,0:T(8,128)(2,1)S(1)} %fusion.11), channel_id=1, source_target_pairs={{0,2},{1,3},{2,0},{3,1},{4,6},{5,7},{6,4},{7,5},{8,10},{9,11},{10,... | collective-permute-start | bytes 1179656 | tf_op jit(solution)/shard_map/ppermute | solution.py:105
  53.5 2.1 %collective-permute-start.14 = (bf16[64,384]{1,0:T(8,128)(2,1)S(1)}, bf16[64,384]{1,0:T(8,128)(2,1)S(1)}, u32[]{:S(2)}, u32[]{:S(2)}) collective-permute-start(bf16[64,384]{1,0:T(8,128)(2,1)S(1)} %fusion.12), channel_id=1, source_target_pairs={{0,4},{1,5},{2,6},{3,7},{4,0},{5,1},{6,2},{7,3},{8,12},{9,13},{10,... | collective-permute-start | bytes 147464 | tf_op jit(solution)/shard_map/ppermute | solution.py:105
  55.6 13.5 %collective-permute-done.14 = bf16[64,384]{1,0:T(8,128)(2,1)S(1)} collective-permute-done((bf16[64,384]{1,0:T(8,128)(2,1)S(1)}, bf16[64,384]{1,0:T(8,128)(2,1)S(1)}, u32[]{:S(2)}, u32[]{:S(2)}) %collective-permute-start.14) | collective-permute-done | bytes 49184 | tf_op jit(solution)/shard_map/ppermute | solution.py:105
  69.1 1.4 %collective-permute-start.15 = (f32[64,384]{1,0:T(8,128)S(1)}, f32[64,384]{1,0:T(8,128)S(1)}, u32[]{:S(2)}, u32[]{:S(2)}) collective-permute-start(f32[64,384]{1,0:T(8,128)S(1)} %convert_add_fusion), channel_id=1, source_target_pairs={{0,2},{1,3},{2,0},{3,1},{4,6},{5,7},{6,4},{7,5},{8,10},{9,11},{10,... | collective-permute-start | bytes 294920 | tf_op jit(solution)/shard_map/ppermute | solution.py:105
  70.5 3.4 %collective-permute-done.15 = f32[64,384]{1,0:T(8,128)S(1)} collective-permute-done((f32[64,384]{1,0:T(8,128)S(1)}, f32[64,384]{1,0:T(8,128)S(1)}, u32[]{:S(2)}, u32[]{:S(2)}) %collective-permute-start.15) | collective-permute-done | bytes 98336 | tf_op jit(solution)/shard_map/ppermute | solution.py:105
  74.0 2.7 %shard_map.87 = f32[384,512]{1,0:T(8,128)S(1)} custom-call(s32[32]{0:T(128)S(1)} %copy-done.2, s32[32]{0:T(128)S(1)} %copy-done.3, f32[64,384]{1,0:T(8,128)S(1)} %add.98.packed_ref, bf16[2048,512]{1,0:T(8,128)(2,1)S(1)} %bitcast.42), custom_call_target="tpu_custom_call" | custom-call | flops 1000000 | bytes 1 | tf_op jit(solution)/shard_map/pallas_call | solution.py:166
  76.7 1.1 %fusion.4 = bf16[384,512]{1,0:T(8,128)(2,1)} fusion(f32[384,512]{1,0:T(8,128)S(1)} %shard_map.87, bf16[384,512]{1,0:T(8,128)(2,1)S(1)} %collective-permute-done.13, bf16[384,512]{1,0:T(8,128)(2,1)S(1)} %collective-permute-done.12, bf16[384,512]{1,0:T(8,128)(2,1)S(1)} %collective-permute-done.11, bf16[1,384,512]{2,1,0:T(8,128)(2,1)S(1)} %collective-permute-done.8, ...), kind=kLoop, calls=%fused_computation.7 | loop fusion | flops 1966080 | bytes 3538944 | tf_op jit(solution)/shard_map/convert_element_type | solution.py:251
  (45 shorter events, 2.8 us)
Async XLA Ops:
  0.7 1.3 %copy-start = (bf16[384,1664]{1,0:T(8,128)(2,1)S(1)}, bf16[384,1664]{1,0:T(8,128)(2,1)}, u32[]{:S(2)}) copy-start(bf16[384,1664]{1,0:T(8,128)(2,1)} %hidden_ref.9) | copy-start | bytes 3833860
  4.9 5.1 %collective-permute-start = (bf16[1,384,512]{2,1,0:T(8,128)(2,1)S(1)}, bf16[1,384,512]{2,1,0:T(8,128)(2,1)S(1)}, u32[]{:S(2)}, u32[]{:S(2)}) collective-permute-start(bf16[1,384,512]{2,1,0:T(8,128)(2,1)S(1)} %get-tuple-element.32), channel_id=1, source_target_pairs={{0,1},{1,0},{2,3},{3,2},{4,5},{5,4},{6,7},{7,6},{8,9},{9,8},{10,11... | collective-permute-start | bytes 1179656 | tf_op jit(solution)/shard_map/ppermute | solution.py:105
  5.4 4.6 %copy-start.4 = (s32[384]{0:T(512)S(1)}, s32[384]{0:T(512)}, u32[]{:S(2)}) copy-start(s32[384]{0:T(512)} %param.12) | copy-start | bytes 4612
  9.8 13.1 %collective-permute-start.2 = (bf16[2,384,512]{2,1,0:T(8,128)(2,1)S(1)}, bf16[2,384,512]{2,1,0:T(8,128)(2,1)S(1)}, u32[]{:S(2)}, u32[]{:S(2)}) collective-permute-start(bf16[2,384,512]{2,1,0:T(8,128)(2,1)S(1)} %get-tuple-element.36), channel_id=1, source_target_pairs={{0,1},{1,0},{2,3},{3,2},{4,5},{5,4},{6,7},{7,6},{8,9},{9,8},{10,11... | collective-permute-start | bytes 2359304 | tf_op jit(solution)/shard_map/ppermute | solution.py:105
  10.0 9.0 %slice-start = ((s8[6815744]{0:T(1024)(128)(4,1)}), s8[4194304]{0:T(1024)(128)(4,1)S(1)}, s32[]{:S(2)}) async-start(s8[6815744]{0:T(1024)(128)(4,1)} %bitcast.46), calls=%async_computation | async-start | bytes 8388608
  10.1 12.8 %collective-permute-start.3 = (bf16[384,512]{1,0:T(8,128)(2,1)S(1)}, bf16[384,512]{1,0:T(8,128)(2,1)S(1)}, u32[]{:S(2)}, u32[]{:S(2)}) collective-permute-start(bf16[384,512]{1,0:T(8,128)(2,1)S(1)} %fusion.8.refs_1_), channel_id=1, source_target_pairs={{0,2},{1,3},{2,0},{3,1},{4,6},{5,7},{6,4},{7,5},{8,10},{9,11},{10,... | collective-permute-start | bytes 1179656 | tf_op jit(solution)/shard_map/ppermute | solution.py:105
  13.1 5.8 %slice-start.1 = ((s8[6815744]{0:T(1024)(128)(4,1)}), s8[2621440]{0:T(1024)(128)(4,1)S(1)}, s32[]{:S(2)}) async-start(s8[6815744]{0:T(1024)(128)(4,1)} %bitcast.46), calls=%async_computation.1 | async-start | bytes 5242880
  18.9 17.2 %collective-permute-start.5 = (bf16[2,384,512]{2,1,0:T(8,128)(2,1)S(1)}, bf16[2,384,512]{2,1,0:T(8,128)(2,1)S(1)}, u32[]{:S(2)}, u32[]{:S(2)}) collective-permute-start(bf16[2,384,512]{2,1,0:T(8,128)(2,1)S(1)} %get-tuple-element.43), channel_id=1, source_target_pairs={{0,1},{1,0},{2,3},{3,2},{4,5},{5,4},{6,7},{7,6},{8,9},{9,8},{10,11... | collective-permute-start | bytes 2359304 | tf_op jit(solution)/shard_map/ppermute | solution.py:105
  23.1 11.6 %collective-permute-start.7 = (bf16[384,512]{1,0:T(8,128)(2,1)S(1)}, bf16[384,512]{1,0:T(8,128)(2,1)S(1)}, u32[]{:S(2)}, u32[]{:S(2)}) collective-permute-start(bf16[384,512]{1,0:T(8,128)(2,1)S(1)} %fusion.7.refs_1_), channel_id=1, source_target_pairs={{0,4},{1,5},{2,6},{3,7},{4,0},{5,1},{6,2},{7,3},{8,12},{9,13},{10,... | collective-permute-start | bytes 1179656 | tf_op jit(solution)/shard_map/ppermute | solution.py:105
  24.8 11.3 %collective-permute-start.6 = (bf16[384,512]{1,0:T(8,128)(2,1)S(1)}, bf16[384,512]{1,0:T(8,128)(2,1)S(1)}, u32[]{:S(2)}, u32[]{:S(2)}) collective-permute-start(bf16[384,512]{1,0:T(8,128)(2,1)S(1)} %fusion.9.refs_2_), channel_id=1, source_target_pairs={{0,2},{1,3},{2,0},{3,1},{4,6},{5,7},{6,4},{7,5},{8,10},{9,11},{10,... | collective-permute-start | bytes 1179656 | tf_op jit(solution)/shard_map/ppermute | solution.py:105
  26.6 5.7 %collective-permute-start.1 = (f32[64,384]{1,0:T(8,128)S(1)}, f32[64,384]{1,0:T(8,128)S(1)}, u32[]{:S(2)}, u32[]{:S(2)}) collective-permute-start(f32[64,384]{1,0:T(8,128)S(1)} %bitcast.43), channel_id=1, source_target_pairs={{0,1},{1,0},{2,3},{3,2},{4,5},{5,4},{6,7},{7,6},{8,9},{9,8},{10,11... | collective-permute-start | bytes 294920 | tf_op jit(solution)/shard_map/ppermute | solution.py:105
  32.3 19.4 %collective-permute-start.9 = (bf16[2,384,512]{2,1,0:T(8,128)(2,1)S(1)}, bf16[2,384,512]{2,1,0:T(8,128)(2,1)S(1)}, u32[]{:S(2)}, u32[]{:S(2)}) collective-permute-start(bf16[2,384,512]{2,1,0:T(8,128)(2,1)S(1)} %get-tuple-element.49), channel_id=1, source_target_pairs={{0,1},{1,0},{2,3},{3,2},{4,5},{5,4},{6,7},{7,6},{8,9},{9,8},{10,11... | collective-permute-start | bytes 2359304 | tf_op jit(solution)/shard_map/ppermute | solution.py:105
  36.5 15.2 %collective-permute-start.10 = (bf16[384,512]{1,0:T(8,128)(2,1)S(1)}, bf16[384,512]{1,0:T(8,128)(2,1)S(1)}, u32[]{:S(2)}, u32[]{:S(2)}) collective-permute-start(bf16[384,512]{1,0:T(8,128)(2,1)S(1)} %fusion.10.refs_2_), channel_id=1, source_target_pairs={{0,2},{1,3},{2,0},{3,1},{4,6},{5,7},{6,4},{7,5},{8,10},{9,11},{10,... | collective-permute-start | bytes 1179656 | tf_op jit(solution)/shard_map/ppermute | solution.py:105
  37.4 14.3 %collective-permute-start.4 = (bf16[64,384]{1,0:T(8,128)(2,1)S(1)}, bf16[64,384]{1,0:T(8,128)(2,1)S(1)}, u32[]{:S(2)}, u32[]{:S(2)}) collective-permute-start(bf16[64,384]{1,0:T(8,128)(2,1)S(1)} %get-tuple-element.53), channel_id=1, source_target_pairs={{0,8},{1,9},{2,10},{3,11},{4,12},{5,13},{6,14},{7,15},{8,0},{9,1},... | collective-permute-start | bytes 147464 | tf_op jit(solution)/shard_map/ppermute | solution.py:105
  40.1 36.6 %collective-permute-start.12 = (bf16[384,512]{1,0:T(8,128)(2,1)S(1)}, bf16[384,512]{1,0:T(8,128)(2,1)S(1)}, u32[]{:S(2)}, u32[]{:S(2)}) collective-permute-start(bf16[384,512]{1,0:T(8,128)(2,1)S(1)} %fusion.6.refs_1_), channel_id=1, source_target_pairs={{0,8},{1,9},{2,10},{3,11},{4,12},{5,13},{6,14},{7,15},{8,0},{9,1},... | collective-permute-start | bytes 1179656 | tf_op jit(solution)/shard_map/ppermute | solution.py:105
  45.8 28.1 %copy-start.1 = (bf16[32,64,512]{2,1,0:T(8,128)(2,1)S(1)}, bf16[32,64,512]{2,1,0:T(8,128)(2,1)}, u32[]{:S(2)}) copy-start(bf16[32,64,512]{2,1,0:T(8,128)(2,1)} %param.11) | copy-start | bytes 6291460
  45.8 28.1 %copy-start.2 = (s32[32]{0:T(128)S(1)}, s32[32]{0:T(128)}, u32[]{:S(2)}) copy-start(s32[32]{0:T(128)} %first_ref.1) | copy-start | bytes 388
  45.8 28.1 %copy-start.3 = (s32[32]{0:T(128)S(1)}, s32[32]{0:T(128)}, u32[]{:S(2)}) copy-start(s32[32]{0:T(128)} %length_ref.1) | copy-start | bytes 388
  51.7 25.0 %collective-permute-start.8 = (bf16[1,384,512]{2,1,0:T(8,128)(2,1)S(1)}, bf16[1,384,512]{2,1,0:T(8,128)(2,1)S(1)}, u32[]{:S(2)}, u32[]{:S(2)}) collective-permute-start(bf16[1,384,512]{2,1,0:T(8,128)(2,1)S(1)} %get-tuple-element.48), channel_id=1, source_target_pairs={{0,1},{1,0},{2,3},{3,2},{4,5},{5,4},{6,7},{7,6},{8,9},{9,8},{10,11... | collective-permute-start | bytes 1179656 | tf_op jit(solution)/shard_map/ppermute | solution.py:105
  51.9 24.8 %collective-permute-start.13 = (bf16[384,512]{1,0:T(8,128)(2,1)S(1)}, bf16[384,512]{1,0:T(8,128)(2,1)S(1)}, u32[]{:S(2)}, u32[]{:S(2)}) collective-permute-start(bf16[384,512]{1,0:T(8,128)(2,1)S(1)} %fusion), channel_id=1, source_target_pairs={{0,4},{1,5},{2,6},{3,7},{4,0},{5,1},{6,2},{7,3},{8,12},{9,13},{10,... | collective-permute-start | bytes 1179656 | tf_op jit(solution)/shard_map/ppermute | solution.py:105
  52.1 24.6 %collective-permute-start.11 = (bf16[384,512]{1,0:T(8,128)(2,1)S(1)}, bf16[384,512]{1,0:T(8,128)(2,1)S(1)}, u32[]{:S(2)}, u32[]{:S(2)}) collective-permute-start(bf16[384,512]{1,0:T(8,128)(2,1)S(1)} %fusion.11), channel_id=1, source_target_pairs={{0,2},{1,3},{2,0},{3,1},{4,6},{5,7},{6,4},{7,5},{8,10},{9,11},{10,... | collective-permute-start | bytes 1179656 | tf_op jit(solution)/shard_map/ppermute | solution.py:105
  53.5 15.6 %collective-permute-start.14 = (bf16[64,384]{1,0:T(8,128)(2,1)S(1)}, bf16[64,384]{1,0:T(8,128)(2,1)S(1)}, u32[]{:S(2)}, u32[]{:S(2)}) collective-permute-start(bf16[64,384]{1,0:T(8,128)(2,1)S(1)} %fusion.12), channel_id=1, source_target_pairs={{0,4},{1,5},{2,6},{3,7},{4,0},{5,1},{6,2},{7,3},{8,12},{9,13},{10,... | collective-permute-start | bytes 147464 | tf_op jit(solution)/shard_map/ppermute | solution.py:105
  69.1 4.8 %collective-permute-start.15 = (f32[64,384]{1,0:T(8,128)S(1)}, f32[64,384]{1,0:T(8,128)S(1)}, u32[]{:S(2)}, u32[]{:S(2)}) collective-permute-start(f32[64,384]{1,0:T(8,128)S(1)} %convert_add_fusion), channel_id=1, source_target_pairs={{0,2},{1,3},{2,0},{3,1},{4,6},{5,7},{6,4},{7,5},{8,10},{9,11},{10,... | collective-permute-start | bytes 294920 | tf_op jit(solution)/shard_map/ppermute | solution.py:105

commit v16 on v14

--- a/solution.py
+++ b/solution.py
@@ -67,7 +67,7 @@
         copy(targets).wait()
 
 
-def product(table, hidden, down_matrix, buffer, base, sent, kept, width, last, flops, earlier):
+def product(table, hidden, down_matrix, buffer, base, sent, kept, width, last, earlier):
     rows, depth = hidden.shape
     first = buffer is None
     vmem = pl.BlockSpec(memory_space=pltpu.VMEM)
@@ -96,13 +96,24 @@
         scratch_shapes=[pltpu.SemaphoreType.DMA((2,))],
         input_output_aliases={} if first else {3: place},
         compiler_params=pltpu.CompilerParams(vmem_limit_bytes=VMEM_LIMIT),
-        cost_estimate=pl.CostEstimate(flops=flops, bytes_accessed=1024, transcendentals=0),
+        cost_estimate=pl.CostEstimate(flops=FLOPS, bytes_accessed=1024, transcendentals=0),
     )(table, hidden, down_matrix, *([] if first else [buffer]), *earlier)
     return results[0] if sent else None, results[place - 1] if kept else None, results[place]
 
 
 def swap(value, bit, total):
     return lax.ppermute(value, "tensor", [(place, place ^ bit) for place in range(total)])
+
+
+def attach(value, packed):
+    below = jnp.pad(packed.astype(jnp.bfloat16), ((0, 0), (0, value.shape[1] - packed.shape[1])))
+    return jnp.concatenate([value, below])
+
+
+def detach(value, packed):
+    height, columns = packed.shape
+    above = value.shape[0] - height
+    return value[:above], value[above:, :columns].astype(jnp.float32)
 
 
 def for_each_window(first_ref, length_ref, group, rows, body):
@@ -191,18 +202,26 @@
 
     kept_home, crossed, incoming = {}, {}, {}
 
-    packed, steps = None, [core, *(4 << at for at in range((units - 1).bit_length())), near]
+    far = [4 << at for at in range((units - 1).bit_length())]
+    packed, steps = None, [*far[:1], near, *far[1:], core]
+
+    def send(value, bit):
+        nonlocal packed
+        if packed is None or steps[:1] != [bit] or packed.shape[1] > value.shape[1]:
+            return value, swap(value, bit, total), None
+        steps.pop(0)
+        own, packed = packed, None
+        leaving = attach(value, own)
+        arrived, shrinks = detach(swap(leaving, bit, total), own)
+        return leaving, arrived, own + shrinks
 
     def settle(unit, arrived):
+        nonlocal packed
         value = kept_home[unit] + arrived.astype(jnp.float32) + crossed[unit].astype(jnp.float32)
-        for moved in incoming.pop(unit, []):
+        for moved, shrinks in incoming.pop(unit, []):
             value = value + moved.astype(jnp.float32)
+            packed = packed if shrinks is None else shrinks
         return value.astype(jnp.bfloat16) if unit else value
-
-    def send_on(unit, moving):
-        bit = unit & -unit
-        incoming.setdefault(unit ^ bit, []).append(swap(moving, 4 * bit, total))
-        return moving
 
     top = units - 1
     order = [top * 4 | near | core]
@@ -211,35 +230,34 @@
         order += [(unit + 1) * 4] * (unit < top) + [0] * (not unit)
     table = jnp.array(order, dtype=jnp.int32) ^ me
 
-    values, _, buffer = product(table, hidden, down_matrix, None, 0, 1, 0, width, False, FLOPS, [])
+    values, _, buffer = product(table, hidden, down_matrix, None, 0, 1, 0, width, False, [])
     base, ready = 1, []
     for unit in reversed(range(units)):
         arrived = swap(values, core, total)
         sent, kept = 1 + (unit > 0), 1 + (unit < top) + (not unit)
         values, results, buffer = product(
             table, hidden, down_matrix, buffer, base, sent, kept, width, not unit,
-            FLOPS, ready,
+            ready,
         )
         base += sent + kept
-        if packed is not None and steps and steps[0] != near:
-            moved, results = lax.optimization_barrier((swap(packed, steps.pop(0), total), results))
-            packed = packed + moved
         if unit < top:
             kept_home[unit + 1] = results[1]
         if not unit:
             kept_home[0] = results[-1]
+        if unit == max(top - 1, 0):
+            late, results = lax.optimization_barrier((hidden, results))
+            packed = shrink(late, shrink_matrices, row_adapter_index)
         ready = []
         if unit < top:
             moving, arrived = lax.optimization_barrier((settle(unit + 1, arrived[1]), arrived))
-            ready.append(send_on(unit + 1, moving))
+            bit = (unit + 1) & -(unit + 1)
+            moving, *came = send(moving, 4 * bit)
+            incoming.setdefault((unit + 1) ^ bit, []).append(came)
+            ready.append(moving)
         leaving = (results[0] + arrived[0].astype(jnp.float32)).astype(jnp.bfloat16)
-        if unit == max(top - 1, 0):
-            late, results = lax.optimization_barrier((hidden, results))
-            packed = shrink(late, shrink_matrices, row_adapter_index)
+        leaving, crossed[unit], shrinks = send(leaving, near)
+        packed = packed if shrinks is None else shrinks
         ready.append(leaving)
-        if packed is not None:
-            ready.append(packed)
-        crossed[unit] = swap(leaving, near, total)
     kept = [settle(0, swap(values, core, total)[0])]
 
     for bit in steps:

time: 68.4 us -> 68.4 us (level)
  starting transfers between devices: 18.5 us -> 15.2 us
  waiting for transfers between devices: 13.9 us -> 17.1 us
    ppermute x16 -> x14, starting transfers between devices: 18.5 us -> 15.2 us  [swap(): lax.ppermute(value, 'tensor', [(place, place ^ bit) for place in range(to...]
    ppermute x16 -> x14, waiting for transfers between devices: 13.9 us -> 17.1 us  [swap(): lax.ppermute(value, 'tensor', [(place, place ^ bit) for place in range(to...]
  transfers between devices with their start and end apart: 16 -> 14, of which waited for: 4 -> 5; matrix products, arithmetic and copies ran while one was open for 8% -> 8% of each run, Pallas kernels for 35% -> 35%
where the time goes in v16:
time: 68.4 us; the launch traced here: 68 us
  Pallas kernels  26.7 us (39%)
  waiting for transfers between devices  17.1 us (25%)
  starting transfers between devices  15.2 us (22%)
  matrix products  3.92 us (6%)
  other arithmetic  3.48 us (5%)
  local copies, waits for them, and re-layouts  1.34 us (2%)
    pallas_call x5, Pallas kernels, product(): pl.pallas_call(functools.partial(product_body, base=base, sent=sent, kept...  24 us
    ppermute x14, waiting for transfers between devices, swap(): lax.ppermute(value, 'tensor', [(place, place ^ bit) for place in range(to...  17.1 us
    ppermute x14, starting transfers between devices, swap(): lax.ppermute(value, 'tensor', [(place, place ^ bit) for place in range(to...  15.2 us
    unnamed x1, matrix products  3.92 us
    pallas_call x1, Pallas kernels, expand(): pl.pallas_call(expand_body, in_specs=[pl.BlockSpec(memory_space=pltpu.SME...  2.71 us
  transfers between devices with their start and end apart: 14, of which 5 were waited for; matrix products, arithmetic and copies ran while one was open for 8% of the time, Pallas kernels for 35%

profile of v16, /device:TPU:0, one launch (start us, length us, event | category | flops | bytes accessed | tf_op | source)
XLA Modules:
  0.0 68.0 jit_solution(15183774329154222600)
XLA Ops:
  0.0 0.7 broadcast_xor_fusion.table_ref
  0.7 1.3 %copy-done = bf16[384,1664]{1,0:T(8,128)(2,1)S(1)} copy-done((bf16[384,1664]{1,0:T(8,128)(2,1)S(1)}, bf16[384,1664]{1,0:T(8,128)(2,1)}, u32[]{:S(2)}) %copy-start) | copy-done | bytes 1277976
  2.0 2.9 %shard_map.82 = (bf16[1,384,512]{2,1,0:T(8,128)(2,1)S(1)}, bf16[2,1664,512]{2,1,0:T(8,128)(2,1)S(1)}) custom-call(s32[16]{0:T(128)S(1)} %broadcast_xor_fusion.table_ref, bf16[384,1664]{1,0:T(8,128)(2,1)S(1)} %copy-done, bf16[1664,8192]{1,0:T(8,128)(2,1)} %down_ref.9), custom_call_target="tpu_custom_call" | custom-call | flops 3000000000 | bytes 1024 | tf_op jit(solution)/shard_map/pallas_call | solution.py:82
  4.9 0.5 collective-permute-start
  5.4 4.4 %shard_map.83 = (bf16[2,384,512]{2,1,0:T(8,128)(2,1)S(1)}, f32[1,384,512]{2,1,0:T(8,128)S(1)}, bf16[2,1664,512]{2,1,0:T(8,128)(2,1)S(1)}) custom-call(s32[16]{0:T(128)S(1)} %broadcast_xor_fusion.table_ref, bf16[384,1664]{1,0:T(8,128)(2,1)S(1)} %copy-done, bf16[1664,8192]{1,0:T(8,128)(2,1)} %down_ref.9, ...), custom_call_target="tpu_custom_call", output_to_operand_aliasing={{2}: (3, {})} | custom-call | flops 3000000000 | bytes 1024 | tf_op jit(solution)/shard_map/pallas_call | solution.py:82
  10.1 3.0 %collective-permute-start.2 = (bf16[384,512]{1,0:T(8,128)(2,1)S(1)}, bf16[384,512]{1,0:T(8,128)(2,1)S(1)}, u32[]{:S(2)}, u32[]{:S(2)}) collective-permute-start(bf16[384,512]{1,0:T(8,128)(2,1)S(1)} %fusion.12.refs_1_), channel_id=1, source_target_pairs={{0,2},{1,3},{2,0},{3,1},{4,6},{5,7},{6,4},{7,5},{8,10},{9,11},{10,... | collective-permute-start | bytes 1179656 | tf_op jit(solution)/shard_map/ppermute | solution.py:105
  13.1 5.7 %shard_map.84 = (bf16[2,384,512]{2,1,0:T(8,128)(2,1)S(1)}, f32[2,384,512]{2,1,0:T(8,128)S(1)}, bf16[2,1664,512]{2,1,0:T(8,128)(2,1)S(1)}) custom-call(s32[16]{0:T(128)S(1)} %broadcast_xor_fusion.table_ref, bf16[384,1664]{1,0:T(8,128)(2,1)S(1)} %copy-done, bf16[1664,8192]{1,0:T(8,128)(2,1)} %down_ref.9, ...), custom_call_target="tpu_custom_call", output_to_operand_aliasing={{2}: (3, {})} | custom-call | flops 3000000000 | bytes 1024 | tf_op jit(solution)/shard_map/pallas_call | solution.py:82
  19.0 3.9 %fusion.18 = f32[384,2048]{0,1:S(1)} fusion(bf16[384,1664]{1,0:T(8,128)(2,1)S(1)} %copy-done, bf16[1664,2048]{0,1:T(8,128)(2,1)S(1)} %bitcast.52), kind=kOutput, calls=%fused_computation.34 | convolution fusion | flops 2617245696 | bytes 11239424
  23.6 1.6 %collective-permute-start.5 = (bf16[448,512]{1,0:T(8,128)(2,1)S(1)}, bf16[448,512]{1,0:T(8,128)(2,1)S(1)}, u32[]{:S(2)}, u32[]{:S(2)}) collective-permute-start(bf16[448,512]{1,0:T(8,128)(2,1)S(1)} %fusion.10.refs_1_), channel_id=1, source_target_pairs={{0,4},{1,5},{2,6},{3,7},{4,0},{5,1},{6,2},{7,3},{8,12},{9,13},{10,... | collective-permute-start | bytes 1376264 | tf_op jit(solution)/shard_map/ppermute | solution.py:105
  25.3 1.1 %collective-permute-start.4 = (bf16[384,512]{1,0:T(8,128)(2,1)S(1)}, bf16[384,512]{1,0:T(8,128)(2,1)S(1)}, u32[]{:S(2)}, u32[]{:S(2)}) collective-permute-start(bf16[384,512]{1,0:T(8,128)(2,1)S(1)} %fusion.13.refs_2_), channel_id=1, source_target_pairs={{0,2},{1,3},{2,0},{3,1},{4,6},{5,7},{6,4},{7,5},{8,10},{9,11},{10,... | collective-permute-start | bytes 1179656 | tf_op jit(solution)/shard_map/ppermute | solution.py:105
  26.4 5.6 %shard_map.85 = (bf16[2,384,512]{2,1,0:T(8,128)(2,1)S(1)}, f32[2,384,512]{2,1,0:T(8,128)S(1)}, bf16[2,1664,512]{2,1,0:T(8,128)(2,1)S(1)}) custom-call(s32[16]{0:T(128)S(1)} %broadcast_xor_fusion.table_ref, bf16[384,1664]{1,0:T(8,128)(2,1)S(1)} %copy-done, bf16[1664,8192]{1,0:T(8,128)(2,1)} %down_ref.9, ...), custom_call_target="tpu_custom_call", output_to_operand_aliasing={{2}: (3, {})} | custom-call | flops 3000000000 | bytes 1024 | tf_op jit(solution)/shard_map/pallas_call | solution.py:82
  32.1 4.5 %collective-permute-done.4 = bf16[384,512]{1,0:T(8,128)(2,1)S(1)} collective-permute-done((bf16[384,512]{1,0:T(8,128)(2,1)S(1)}, bf16[384,512]{1,0:T(8,128)(2,1)S(1)}, u32[]{:S(2)}, u32[]{:S(2)}) %collective-permute-start.4) | collective-permute-done | bytes 393248 | tf_op jit(solution)/shard_map/ppermute | solution.py:105
  37.0 1.0 %collective-permute-start.8 = (bf16[448,512]{1,0:T(8,128)(2,1)S(1)}, bf16[448,512]{1,0:T(8,128)(2,1)S(1)}, u32[]{:S(2)}, u32[]{:S(2)}) collective-permute-start(bf16[448,512]{1,0:T(8,128)(2,1)S(1)} %fusion.11.refs_2_), channel_id=1, source_target_pairs={{0,2},{1,3},{2,0},{3,1},{4,6},{5,7},{6,4},{7,5},{8,10},{9,11},{10,... | collective-permute-start | bytes 1376264 | tf_op jit(solution)/shard_map/ppermute | solution.py:105
  38.0 2.6 %collective-permute-start.10 = (bf16[384,512]{1,0:T(8,128)(2,1)S(1)}, bf16[384,512]{1,0:T(8,128)(2,1)S(1)}, u32[]{:S(2)}, u32[]{:S(2)}) collective-permute-start(bf16[384,512]{1,0:T(8,128)(2,1)S(1)} %fusion.8.refs_1_), channel_id=1, source_target_pairs={{0,8},{1,9},{2,10},{3,11},{4,12},{5,13},{6,14},{7,15},{8,0},{9,1},... | collective-permute-start | bytes 1179656 | tf_op jit(solution)/shard_map/ppermute | solution.py:105
  40.6 5.4 %shard_map.86 = (bf16[1,384,512]{2,1,0:T(8,128)(2,1)S(1)}, f32[3,384,512]{2,1,0:T(8,128)S(1)}, bf16[2,1664,512]{2,1,0:T(8,128)(2,1)S(1)}) custom-call(s32[16]{0:T(128)S(1)} %broadcast_xor_fusion.table_ref, bf16[384,1664]{1,0:T(8,128)(2,1)S(1)} %copy-done, bf16[1664,8192]{1,0:T(8,128)(2,1)} %down_ref.9, ...), custom_call_target="tpu_custom_call", output_to_operand_aliasing={{2}: (3, {})} | custom-call | flops 3000000000 | bytes 1024 | tf_op jit(solution)/shard_map/pallas_call | solution.py:82
  46.1 3.1 %collective-permute-done.8 = bf16[448,512]{1,0:T(8,128)(2,1)S(1)} collective-permute-done((bf16[448,512]{1,0:T(8,128)(2,1)S(1)}, bf16[448,512]{1,0:T(8,128)(2,1)S(1)}, u32[]{:S(2)}, u32[]{:S(2)}) %collective-permute-start.8) | collective-permute-done | bytes 458784 | tf_op jit(solution)/shard_map/ppermute | solution.py:105
  49.5 0.6 collective-permute-start.9
  50.0 1.8 %collective-permute-start.11 = (bf16[384,512]{1,0:T(8,128)(2,1)S(1)}, bf16[384,512]{1,0:T(8,128)(2,1)S(1)}, u32[]{:S(2)}, u32[]{:S(2)}) collective-permute-start(bf16[384,512]{1,0:T(8,128)(2,1)S(1)} %fusion.2), channel_id=1, source_target_pairs={{0,4},{1,5},{2,6},{3,7},{4,0},{5,1},{6,2},{7,3},{8,12},{9,13},{10,... | collective-permute-start | bytes 1179656 | tf_op jit(solution)/shard_map/ppermute | solution.py:105
  51.8 2.7 %collective-permute-start.12 = (bf16[64,384]{1,0:T(8,128)(2,1)S(1)}, bf16[64,384]{1,0:T(8,128)(2,1)S(1)}, u32[]{:S(2)}, u32[]{:S(2)}) collective-permute-start(bf16[64,384]{1,0:T(8,128)(2,1)S(1)} %fusion.16), channel_id=1, source_target_pairs={{0,8},{1,9},{2,10},{3,11},{4,12},{5,13},{6,14},{7,15},{8,0},{9,1},... | collective-permute-start | bytes 147464 | tf_op jit(solution)/shard_map/ppermute | solution.py:105
  54.5 5.2 %collective-permute-done.12 = bf16[64,384]{1,0:T(8,128)(2,1)S(1)} collective-permute-done((bf16[64,384]{1,0:T(8,128)(2,1)S(1)}, bf16[64,384]{1,0:T(8,128)(2,1)S(1)}, u32[]{:S(2)}, u32[]{:S(2)}) %collective-permute-start.12) | collective-permute-done | bytes 49184 | tf_op jit(solution)/shard_map/ppermute | solution.py:105
  59.8 1.3 %collective-permute-done.13 = f32[64,384]{1,0:T(8,128)S(1)} collective-permute-done((f32[64,384]{1,0:T(8,128)S(1)}, f32[64,384]{1,0:T(8,128)S(1)}, u32[]{:S(2)}, u32[]{:S(2)}) %collective-permute-start.13) | collective-permute-done | bytes 98336 | tf_op jit(solution)/shard_map/ppermute | solution.py:105
  61.2 2.7 %shard_map.87 = f32[384,512]{1,0:T(8,128)S(1)} custom-call(s32[32]{0:T(128)S(1)} %copy-done.2, s32[32]{0:T(128)S(1)} %copy-done.3, f32[64,384]{1,0:T(8,128)S(1)} %add.102.packed_ref, bf16[2048,512]{1,0:T(8,128)(2,1)S(1)} %bitcast.48), custom_call_target="tpu_custom_call" | custom-call | flops 1000000 | bytes 1 | tf_op jit(solution)/shard_map/pallas_call | solution.py:177
  63.9 3.0 %collective-permute-done.11 = bf16[384,512]{1,0:T(8,128)(2,1)S(1)} collective-permute-done((bf16[384,512]{1,0:T(8,128)(2,1)S(1)}, bf16[384,512]{1,0:T(8,128)(2,1)S(1)}, u32[]{:S(2)}, u32[]{:S(2)}) %collective-permute-start.11) | collective-permute-done | bytes 393248 | tf_op jit(solution)/shard_map/ppermute | solution.py:105
  66.9 1.1 %fusion.6 = bf16[384,512]{1,0:T(8,128)(2,1)} fusion(f32[384,512]{1,0:T(8,128)S(1)} %shard_map.87, bf16[384,512]{1,0:T(8,128)(2,1)S(1)} %collective-permute-done.11, bf16[384,512]{1,0:T(8,128)(2,1)S(1)} %collective-permute-done.10, bf16[384,512]{1,0:T(8,128)(2,1)S(1)} %collective-permute-done.9, bf16[1,384,512]{2,1,0:T(8,128)(2,1)S(1)} %collective-permute-done.6, ...), kind=kLoop, calls=%fused_computation.10 | loop fusion | flops 1966080 | bytes 3538944 | tf_op jit(solution)/shard_map/convert_element_type | solution.py:267
  (44 shorter events, 2.2 us)
Async XLA Ops:
  0.7 1.3 %copy-start = (bf16[384,1664]{1,0:T(8,128)(2,1)S(1)}, bf16[384,1664]{1,0:T(8,128)(2,1)}, u32[]{:S(2)}) copy-start(bf16[384,1664]{1,0:T(8,128)(2,1)} %hidden_ref.9) | copy-start | bytes 3833860
  4.9 5.1 %collective-permute-start = (bf16[1,384,512]{2,1,0:T(8,128)(2,1)S(1)}, bf16[1,384,512]{2,1,0:T(8,128)(2,1)S(1)}, u32[]{:S(2)}, u32[]{:S(2)}) collective-permute-start(bf16[1,384,512]{2,1,0:T(8,128)(2,1)S(1)} %get-tuple-element.29), channel_id=1, source_target_pairs={{0,1},{1,0},{2,3},{3,2},{4,5},{5,4},{6,7},{7,6},{8,9},{9,8},{10,11... | collective-permute-start | bytes 1179656 | tf_op jit(solution)/shard_map/ppermute | solution.py:105
  5.4 4.6 %copy-start.4 = (s32[384]{0:T(512)S(1)}, s32[384]{0:T(512)}, u32[]{:S(2)}) copy-start(s32[384]{0:T(512)} %param.12) | copy-start | bytes 4612
  9.8 13.5 %collective-permute-start.1 = (bf16[2,384,512]{2,1,0:T(8,128)(2,1)S(1)}, bf16[2,384,512]{2,1,0:T(8,128)(2,1)S(1)}, u32[]{:S(2)}, u32[]{:S(2)}) collective-permute-start(bf16[2,384,512]{2,1,0:T(8,128)(2,1)S(1)} %get-tuple-element.32), channel_id=1, source_target_pairs={{0,1},{1,0},{2,3},{3,2},{4,5},{5,4},{6,7},{7,6},{8,9},{9,8},{10,11... | collective-permute-start | bytes 2359304 | tf_op jit(solution)/shard_map/ppermute | solution.py:105
  10.0 9.0 %slice-start = ((s8[6815744]{0:T(1024)(128)(4,1)}), s8[4194304]{0:T(1024)(128)(4,1)S(1)}, s32[]{:S(2)}) async-start(s8[6815744]{0:T(1024)(128)(4,1)} %bitcast.50), calls=%async_computation | async-start | bytes 8388608
  10.1 13.2 %collective-permute-start.2 = (bf16[384,512]{1,0:T(8,128)(2,1)S(1)}, bf16[384,512]{1,0:T(8,128)(2,1)S(1)}, u32[]{:S(2)}, u32[]{:S(2)}) collective-permute-start(bf16[384,512]{1,0:T(8,128)(2,1)S(1)} %fusion.12.refs_1_), channel_id=1, source_target_pairs={{0,2},{1,3},{2,0},{3,1},{4,6},{5,7},{6,4},{7,5},{8,10},{9,11},{10,... | collective-permute-start | bytes 1179656 | tf_op jit(solution)/shard_map/ppermute | solution.py:105
  13.1 5.8 %slice-start.1 = ((s8[6815744]{0:T(1024)(128)(4,1)}), s8[2621440]{0:T(1024)(128)(4,1)S(1)}, s32[]{:S(2)}) async-start(s8[6815744]{0:T(1024)(128)(4,1)} %bitcast.50), calls=%async_computation.1 | async-start | bytes 5242880
  18.9 17.7 %collective-permute-start.3 = (bf16[2,384,512]{2,1,0:T(8,128)(2,1)S(1)}, bf16[2,384,512]{2,1,0:T(8,128)(2,1)S(1)}, u32[]{:S(2)}, u32[]{:S(2)}) collective-permute-start(bf16[2,384,512]{2,1,0:T(8,128)(2,1)S(1)} %get-tuple-element.39), channel_id=1, source_target_pairs={{0,1},{1,0},{2,3},{3,2},{4,5},{5,4},{6,7},{7,6},{8,9},{9,8},{10,11... | collective-permute-start | bytes 2359304 | tf_op jit(solution)/shard_map/ppermute | solution.py:105
  23.6 13.0 %collective-permute-start.5 = (bf16[448,512]{1,0:T(8,128)(2,1)S(1)}, bf16[448,512]{1,0:T(8,128)(2,1)S(1)}, u32[]{:S(2)}, u32[]{:S(2)}) collective-permute-start(bf16[448,512]{1,0:T(8,128)(2,1)S(1)} %fusion.10.refs_1_), channel_id=1, source_target_pairs={{0,4},{1,5},{2,6},{3,7},{4,0},{5,1},{6,2},{7,3},{8,12},{9,13},{10,... | collective-permute-start | bytes 1376264 | tf_op jit(solution)/shard_map/ppermute | solution.py:105
  25.3 11.3 %collective-permute-start.4 = (bf16[384,512]{1,0:T(8,128)(2,1)S(1)}, bf16[384,512]{1,0:T(8,128)(2,1)S(1)}, u32[]{:S(2)}, u32[]{:S(2)}) collective-permute-start(bf16[384,512]{1,0:T(8,128)(2,1)S(1)} %fusion.13.refs_2_), channel_id=1, source_target_pairs={{0,2},{1,3},{2,0},{3,1},{4,6},{5,7},{6,4},{7,5},{8,10},{9,11},{10,... | collective-permute-start | bytes 1179656 | tf_op jit(solution)/shard_map/ppermute | solution.py:105
  32.0 14.1 %collective-permute-start.7 = (bf16[2,384,512]{2,1,0:T(8,128)(2,1)S(1)}, bf16[2,384,512]{2,1,0:T(8,128)(2,1)S(1)}, u32[]{:S(2)}, u32[]{:S(2)}) collective-permute-start(bf16[2,384,512]{2,1,0:T(8,128)(2,1)S(1)} %get-tuple-element.44), channel_id=1, source_target_pairs={{0,1},{1,0},{2,3},{3,2},{4,5},{5,4},{6,7},{7,6},{8,9},{9,8},{10,11... | collective-permute-start | bytes 2359304 | tf_op jit(solution)/shard_map/ppermute | solution.py:105
  37.0 12.1 %collective-permute-start.8 = (bf16[448,512]{1,0:T(8,128)(2,1)S(1)}, bf16[448,512]{1,0:T(8,128)(2,1)S(1)}, u32[]{:S(2)}, u32[]{:S(2)}) collective-permute-start(bf16[448,512]{1,0:T(8,128)(2,1)S(1)} %fusion.11.refs_2_), channel_id=1, source_target_pairs={{0,2},{1,3},{2,0},{3,1},{4,6},{5,7},{6,4},{7,5},{8,10},{9,11},{10,... | collective-permute-start | bytes 1376264 | tf_op jit(solution)/shard_map/ppermute | solution.py:105
  38.0 25.9 %collective-permute-start.10 = (bf16[384,512]{1,0:T(8,128)(2,1)S(1)}, bf16[384,512]{1,0:T(8,128)(2,1)S(1)}, u32[]{:S(2)}, u32[]{:S(2)}) collective-permute-start(bf16[384,512]{1,0:T(8,128)(2,1)S(1)} %fusion.8.refs_1_), channel_id=1, source_target_pairs={{0,8},{1,9},{2,10},{3,11},{4,12},{5,13},{6,14},{7,15},{8,0},{9,1},... | collective-permute-start | bytes 1179656 | tf_op jit(solution)/shard_map/ppermute | solution.py:105
  46.0 15.2 %copy-start.1 = (bf16[32,64,512]{2,1,0:T(8,128)(2,1)S(1)}, bf16[32,64,512]{2,1,0:T(8,128)(2,1)}, u32[]{:S(2)}) copy-start(bf16[32,64,512]{2,1,0:T(8,128)(2,1)} %param.11) | copy-start | bytes 6291460
  46.0 15.2 %copy-start.2 = (s32[32]{0:T(128)S(1)}, s32[32]{0:T(128)}, u32[]{:S(2)}) copy-start(s32[32]{0:T(128)} %first_ref.1) | copy-start | bytes 388
  46.0 15.2 %copy-start.3 = (s32[32]{0:T(128)S(1)}, s32[32]{0:T(128)}, u32[]{:S(2)}) copy-start(s32[32]{0:T(128)} %length_ref.1) | copy-start | bytes 388
  46.0 17.9 %collective-permute-start.6 = (bf16[1,384,512]{2,1,0:T(8,128)(2,1)S(1)}, bf16[1,384,512]{2,1,0:T(8,128)(2,1)S(1)}, u32[]{:S(2)}, u32[]{:S(2)}) collective-permute-start(bf16[1,384,512]{2,1,0:T(8,128)(2,1)S(1)} %get-tuple-element.43), channel_id=1, source_target_pairs={{0,1},{1,0},{2,3},{3,2},{4,5},{5,4},{6,7},{7,6},{8,9},{9,8},{10,11... | collective-permute-start | bytes 1179656 | tf_op jit(solution)/shard_map/ppermute | solution.py:105
  49.5 14.4 %collective-permute-start.9 = (bf16[384,512]{1,0:T(8,128)(2,1)S(1)}, bf16[384,512]{1,0:T(8,128)(2,1)S(1)}, u32[]{:S(2)}, u32[]{:S(2)}) collective-permute-start(bf16[384,512]{1,0:T(8,128)(2,1)S(1)} %fusion.15), channel_id=1, source_target_pairs={{0,2},{1,3},{2,0},{3,1},{4,6},{5,7},{6,4},{7,5},{8,10},{9,11},{10,... | collective-permute-start | bytes 1179656 | tf_op jit(solution)/shard_map/ppermute | solution.py:105
  50.0 16.9 %collective-permute-start.11 = (bf16[384,512]{1,0:T(8,128)(2,1)S(1)}, bf16[384,512]{1,0:T(8,128)(2,1)S(1)}, u32[]{:S(2)}, u32[]{:S(2)}) collective-permute-start(bf16[384,512]{1,0:T(8,128)(2,1)S(1)} %fusion.2), channel_id=1, source_target_pairs={{0,4},{1,5},{2,6},{3,7},{4,0},{5,1},{6,2},{7,3},{8,12},{9,13},{10,... | collective-permute-start | bytes 1179656 | tf_op jit(solution)/shard_map/ppermute | solution.py:105
  51.8 7.9 %collective-permute-start.12 = (bf16[64,384]{1,0:T(8,128)(2,1)S(1)}, bf16[64,384]{1,0:T(8,128)(2,1)S(1)}, u32[]{:S(2)}, u32[]{:S(2)}) collective-permute-start(bf16[64,384]{1,0:T(8,128)(2,1)S(1)} %fusion.16), channel_id=1, source_target_pairs={{0,8},{1,9},{2,10},{3,11},{4,12},{5,13},{6,14},{7,15},{8,0},{9,1},... | collective-permute-start | bytes 147464 | tf_op jit(solution)/shard_map/ppermute | solution.py:105
  59.7 1.4 %collective-permute-start.13 = (f32[64,384]{1,0:T(8,128)S(1)}, f32[64,384]{1,0:T(8,128)S(1)}, u32[]{:S(2)}, u32[]{:S(2)}) collective-permute-start(f32[64,384]{1,0:T(8,128)S(1)} %convert_add_fusion), channel_id=1, source_target_pairs={{0,1},{1,0},{2,3},{3,2},{4,5},{5,4},{6,7},{7,6},{8,9},{9,8},{10,11... | collective-permute-start | bytes 294920 | tf_op jit(solution)/shard_map/ppermute | solution.py:105

commit v17 on v16

--- a/solution.py
+++ b/solution.py
@@ -10,7 +10,7 @@
 VMEM_LIMIT = 39 * 1024 * 1024
 WINDOW = 128
 TOGETHER = 4
-FLOPS = 3_000_000_000
+FLOPS = 20_000_000_000
 EXPAND_FLOPS = 1_000_000
 
 
@@ -244,17 +244,20 @@
             kept_home[unit + 1] = results[1]
         if not unit:
             kept_home[0] = results[-1]
-        if unit == max(top - 1, 0):
-            late, results = lax.optimization_barrier((hidden, results))
+        early = unit == max(top - 1, 0)
+        ready = []
+        if early:
+            leaving = (results[0] + arrived[0].astype(jnp.float32)).astype(jnp.bfloat16)
+            leaving, arrived, late = lax.optimization_barrier((leaving, arrived, hidden))
             packed = shrink(late, shrink_matrices, row_adapter_index)
-        ready = []
         if unit < top:
             moving, arrived = lax.optimization_barrier((settle(unit + 1, arrived[1]), arrived))
             bit = (unit + 1) & -(unit + 1)
             moving, *came = send(moving, 4 * bit)
             incoming.setdefault((unit + 1) ^ bit, []).append(came)
             ready.append(moving)
-        leaving = (results[0] + arrived[0].astype(jnp.float32)).astype(jnp.bfloat16)
+        if not early:
+            leaving = (results[0] + arrived[0].astype(jnp.float32)).astype(jnp.bfloat16)
         leaving, crossed[unit], shrinks = send(leaving, near)
         packed = packed if shrinks is None else shrinks
         ready.append(leaving)

time: 68.4 us -> 70.4 us (1.029)
  starting transfers between devices: 15.2 us -> 16.8 us
    ppermute x14, starting transfers between devices: 15.2 us -> 16.8 us  [swap(): lax.ppermute(value, 'tensor', [(place, place ^ bit) for place in range(to...]
  transfers between devices with their start and end apart: 14 -> 14, of which waited for: 5 -> 7; matrix products, arithmetic and copies ran while one was open for 8% -> 8% of each run, Pallas kernels for 35% -> 35%
where the time goes in v17:
time: 70.4 us; the launch traced here: 70 us
  Pallas kernels  27.2 us (39%)
  starting transfers between devices  16.8 us (24%)
  waiting for transfers between devices  16.8 us (24%)
  matrix products  4.12 us (6%)
  other arithmetic  3.43 us (5%)
  local copies, waits for them, and re-layouts  1.33 us (2%)
    pallas_call x5, Pallas kernels, product(): pl.pallas_call(functools.partial(product_body, base=base, sent=sent, kept...  24.5 us
    ppermute x14, waiting for transfers between devices, swap(): lax.ppermute(value, 'tensor', [(place, place ^ bit) for place in range(to...  16.8 us
    ppermute x14, starting transfers between devices, swap(): lax.ppermute(value, 'tensor', [(place, place ^ bit) for place in range(to...  16.8 us
    unnamed x1, matrix products  4.12 us
    pallas_call x1, Pallas kernels, expand(): pl.pallas_call(expand_body, in_specs=[pl.BlockSpec(memory_space=pltpu.SME...  2.71 us
  transfers between devices with their start and end apart: 14, of which 7 were waited for; matrix products, arithmetic and copies ran while one was open for 8% of the time, Pallas kernels for 35%

profile of v17, /device:TPU:0, one launch (start us, length us, event | category | flops | bytes accessed | tf_op | source)
XLA Modules:
  0.0 70.0 jit_solution(13430875185275278374)
XLA Ops:
  0.0 0.7 broadcast_xor_fusion.table_ref
  0.7 1.3 %copy-done.3 = bf16[384,1664]{1,0:T(8,128)(2,1)S(1)} copy-done((bf16[384,1664]{1,0:T(8,128)(2,1)S(1)}, bf16[384,1664]{1,0:T(8,128)(2,1)}, u32[]{:S(2)}) %copy-start.3) | copy-done | bytes 1277976
  2.0 2.9 %shard_map.82 = (bf16[1,384,512]{2,1,0:T(8,128)(2,1)S(1)}, bf16[2,1664,512]{2,1,0:T(8,128)(2,1)S(1)}) custom-call(s32[16]{0:T(128)S(1)} %broadcast_xor_fusion.table_ref, bf16[384,1664]{1,0:T(8,128)(2,1)S(1)} %copy-done.3, bf16[1664,8192]{1,0:T(8,128)(2,1)} %down_ref.9), custom_call_target="tpu_custom_call" | custom-call | flops 20000000000 | bytes 1024 | tf_op jit(solution)/shard_map/pallas_call | solution.py:82
  5.4 4.4 %shard_map.83 = (bf16[2,384,512]{2,1,0:T(8,128)(2,1)S(1)}, f32[1,384,512]{2,1,0:T(8,128)S(1)}, bf16[2,1664,512]{2,1,0:T(8,128)(2,1)S(1)}) custom-call(s32[16]{0:T(128)S(1)} %broadcast_xor_fusion.table_ref, bf16[384,1664]{1,0:T(8,128)(2,1)S(1)} %copy-done.3, bf16[1664,8192]{1,0:T(8,128)(2,1)} %down_ref.9, ...), custom_call_target="tpu_custom_call", output_to_operand_aliasing={{2}: (3, {})} | custom-call | flops 20000000000 | bytes 1024 | tf_op jit(solution)/shard_map/pallas_call | solution.py:82
  10.1 3.0 %collective-permute-start.2 = (bf16[384,512]{1,0:T(8,128)(2,1)S(1)}, bf16[384,512]{1,0:T(8,128)(2,1)S(1)}, u32[]{:S(2)}, u32[]{:S(2)}) collective-permute-start(bf16[384,512]{1,0:T(8,128)(2,1)S(1)} %fusion.12.refs_1_), channel_id=1, source_target_pairs={{0,2},{1,3},{2,0},{3,1},{4,6},{5,7},{6,4},{7,5},{8,10},{9,11},{10,... | collective-permute-start | bytes 1179656 | tf_op jit(solution)/shard_map/ppermute | solution.py:105
  13.2 6.2 %shard_map.84 = (bf16[2,384,512]{2,1,0:T(8,128)(2,1)S(1)}, f32[2,384,512]{2,1,0:T(8,128)S(1)}, bf16[2,1664,512]{2,1,0:T(8,128)(2,1)S(1)}) custom-call(s32[16]{0:T(128)S(1)} %broadcast_xor_fusion.table_ref, bf16[384,1664]{1,0:T(8,128)(2,1)S(1)} %copy-done.3, bf16[1664,8192]{1,0:T(8,128)(2,1)} %down_ref.9, ...), custom_call_target="tpu_custom_call", output_to_operand_aliasing={{2}: (3, {})} | custom-call | flops 20000000000 | bytes 1024 | tf_op jit(solution)/shard_map/pallas_call | solution.py:82
  19.6 2.9 %collective-permute-done.2 = bf16[384,512]{1,0:T(8,128)(2,1)S(1)} collective-permute-done((bf16[384,512]{1,0:T(8,128)(2,1)S(1)}, bf16[384,512]{1,0:T(8,128)(2,1)S(1)}, u32[]{:S(2)}, u32[]{:S(2)}) %collective-permute-start.2) | collective-permute-done | bytes 393248 | tf_op jit(solution)/shard_map/ppermute | solution.py:105
  22.6 4.1 %fusion.18 = f32[384,2048]{0,1:S(1)} fusion(bf16[384,1664]{1,0:T(8,128)(2,1)S(1)} %copy-done.3, bf16[1664,2048]{0,1:T(8,128)(2,1)S(1)} %bitcast.52), kind=kOutput, calls=%fused_computation.34 | convolution fusion | flops 2617245696 | bytes 11239424
  27.2 1.9 %collective-permute-start.5 = (bf16[448,512]{1,0:T(8,128)(2,1)S(1)}, bf16[448,512]{1,0:T(8,128)(2,1)S(1)}, u32[]{:S(2)}, u32[]{:S(2)}) collective-permute-start(bf16[448,512]{1,0:T(8,128)(2,1)S(1)} %fusion.10.refs_1_), channel_id=1, source_target_pairs={{0,4},{1,5},{2,6},{3,7},{4,0},{5,1},{6,2},{7,3},{8,12},{9,13},{10,... | collective-permute-start | bytes 1376264 | tf_op jit(solution)/shard_map/ppermute | solution.py:105
  29.1 1.5 %collective-permute-start.4 = (bf16[384,512]{1,0:T(8,128)(2,1)S(1)}, bf16[384,512]{1,0:T(8,128)(2,1)S(1)}, u32[]{:S(2)}, u32[]{:S(2)}) collective-permute-start(bf16[384,512]{1,0:T(8,128)(2,1)S(1)} %fusion.13.refs_2_), channel_id=1, source_target_pairs={{0,2},{1,3},{2,0},{3,1},{4,6},{5,7},{6,4},{7,5},{8,10},{9,11},{10,... | collective-permute-start | bytes 1179656 | tf_op jit(solution)/shard_map/ppermute | solution.py:105
  30.6 5.6 %shard_map.85 = (bf16[2,384,512]{2,1,0:T(8,128)(2,1)S(1)}, f32[2,384,512]{2,1,0:T(8,128)S(1)}, bf16[2,1664,512]{2,1,0:T(8,128)(2,1)S(1)}) custom-call(s32[16]{0:T(128)S(1)} %broadcast_xor_fusion.table_ref, bf16[384,1664]{1,0:T(8,128)(2,1)S(1)} %copy-done.3, bf16[1664,8192]{1,0:T(8,128)(2,1)} %down_ref.9, ...), custom_call_target="tpu_custom_call", output_to_operand_aliasing={{2}: (3, {})} | custom-call | flops 20000000000 | bytes 1024 | tf_op jit(solution)/shard_map/pallas_call | solution.py:82
  36.3 2.7 %collective-permute-done.4 = bf16[384,512]{1,0:T(8,128)(2,1)S(1)} collective-permute-done((bf16[384,512]{1,0:T(8,128)(2,1)S(1)}, bf16[384,512]{1,0:T(8,128)(2,1)S(1)}, u32[]{:S(2)}, u32[]{:S(2)}) %collective-permute-start.4) | collective-permute-done | bytes 393248 | tf_op jit(solution)/shard_map/ppermute | solution.py:105
  39.6 1.5 %collective-permute-start.8 = (bf16[448,512]{1,0:T(8,128)(2,1)S(1)}, bf16[448,512]{1,0:T(8,128)(2,1)S(1)}, u32[]{:S(2)}, u32[]{:S(2)}) collective-permute-start(bf16[448,512]{1,0:T(8,128)(2,1)S(1)} %fusion.11.refs_2_), channel_id=1, source_target_pairs={{0,2},{1,3},{2,0},{3,1},{4,6},{5,7},{6,4},{7,5},{8,10},{9,11},{10,... | collective-permute-start | bytes 1376264 | tf_op jit(solution)/shard_map/ppermute | solution.py:105
  41.1 2.6 %collective-permute-start.10 = (bf16[384,512]{1,0:T(8,128)(2,1)S(1)}, bf16[384,512]{1,0:T(8,128)(2,1)S(1)}, u32[]{:S(2)}, u32[]{:S(2)}) collective-permute-start(bf16[384,512]{1,0:T(8,128)(2,1)S(1)} %fusion.8.refs_1_), channel_id=1, source_target_pairs={{0,8},{1,9},{2,10},{3,11},{4,12},{5,13},{6,14},{7,15},{8,0},{9,1},... | collective-permute-start | bytes 1179656 | tf_op jit(solution)/shard_map/ppermute | solution.py:105
  43.7 5.4 %shard_map.86 = (bf16[1,384,512]{2,1,0:T(8,128)(2,1)S(1)}, f32[3,384,512]{2,1,0:T(8,128)S(1)}, bf16[2,1664,512]{2,1,0:T(8,128)(2,1)S(1)}) custom-call(s32[16]{0:T(128)S(1)} %broadcast_xor_fusion.table_ref, bf16[384,1664]{1,0:T(8,128)(2,1)S(1)} %copy-done.3, bf16[1664,8192]{1,0:T(8,128)(2,1)} %down_ref.9, ...), custom_call_target="tpu_custom_call", output_to_operand_aliasing={{2}: (3, {})} | custom-call | flops 20000000000 | bytes 1024 | tf_op jit(solution)/shard_map/pallas_call | solution.py:82
  49.2 1.5 %collective-permute-done.8 = bf16[448,512]{1,0:T(8,128)(2,1)S(1)} collective-permute-done((bf16[448,512]{1,0:T(8,128)(2,1)S(1)}, bf16[448,512]{1,0:T(8,128)(2,1)S(1)}, u32[]{:S(2)}, u32[]{:S(2)}) %collective-permute-start.8) | collective-permute-done | bytes 458784 | tf_op jit(solution)/shard_map/ppermute | solution.py:105
  51.0 1.2 %collective-permute-start.9 = (bf16[384,512]{1,0:T(8,128)(2,1)S(1)}, bf16[384,512]{1,0:T(8,128)(2,1)S(1)}, u32[]{:S(2)}, u32[]{:S(2)}) collective-permute-start(bf16[384,512]{1,0:T(8,128)(2,1)S(1)} %fusion.15), channel_id=1, source_target_pairs={{0,2},{1,3},{2,0},{3,1},{4,6},{5,7},{6,4},{7,5},{8,10},{9,11},{10,... | collective-permute-start | bytes 1179656 | tf_op jit(solution)/shard_map/ppermute | solution.py:105
  52.2 1.6 %collective-permute-start.11 = (bf16[384,512]{1,0:T(8,128)(2,1)S(1)}, bf16[384,512]{1,0:T(8,128)(2,1)S(1)}, u32[]{:S(2)}, u32[]{:S(2)}) collective-permute-start(bf16[384,512]{1,0:T(8,128)(2,1)S(1)} %fusion.2), channel_id=1, source_target_pairs={{0,4},{1,5},{2,6},{3,7},{4,0},{5,1},{6,2},{7,3},{8,12},{9,13},{10,... | collective-permute-start | bytes 1179656 | tf_op jit(solution)/shard_map/ppermute | solution.py:105
  53.8 2.6 %collective-permute-start.12 = (bf16[64,384]{1,0:T(8,128)(2,1)S(1)}, bf16[64,384]{1,0:T(8,128)(2,1)S(1)}, u32[]{:S(2)}, u32[]{:S(2)}) collective-permute-start(bf16[64,384]{1,0:T(8,128)(2,1)S(1)} %fusion.16), channel_id=1, source_target_pairs={{0,8},{1,9},{2,10},{3,11},{4,12},{5,13},{6,14},{7,15},{8,0},{9,1},... | collective-permute-start | bytes 147464 | tf_op jit(solution)/shard_map/ppermute | solution.py:105
  56.5 5.1 %collective-permute-done.12 = bf16[64,384]{1,0:T(8,128)(2,1)S(1)} collective-permute-done((bf16[64,384]{1,0:T(8,128)(2,1)S(1)}, bf16[64,384]{1,0:T(8,128)(2,1)S(1)}, u32[]{:S(2)}, u32[]{:S(2)}) %collective-permute-start.12) | collective-permute-done | bytes 49184 | tf_op jit(solution)/shard_map/ppermute | solution.py:105
  61.6 1.3 %collective-permute-done.13 = f32[64,384]{1,0:T(8,128)S(1)} collective-permute-done((f32[64,384]{1,0:T(8,128)S(1)}, f32[64,384]{1,0:T(8,128)S(1)}, u32[]{:S(2)}, u32[]{:S(2)}) %collective-permute-start.13) | collective-permute-done | bytes 98336 | tf_op jit(solution)/shard_map/ppermute | solution.py:105
  63.0 2.7 %shard_map.87 = f32[384,512]{1,0:T(8,128)S(1)} custom-call(s32[32]{0:T(128)S(1)} %copy-done.1, s32[32]{0:T(128)S(1)} %copy-done.2, f32[64,384]{1,0:T(8,128)S(1)} %add.102.packed_ref, bf16[2048,512]{1,0:T(8,128)(2,1)S(1)} %bitcast.48), custom_call_target="tpu_custom_call" | custom-call | flops 1000000 | bytes 1 | tf_op jit(solution)/shard_map/pallas_call | solution.py:177
  65.7 3.2 %collective-permute-done.11 = bf16[384,512]{1,0:T(8,128)(2,1)S(1)} collective-permute-done((bf16[384,512]{1,0:T(8,128)(2,1)S(1)}, bf16[384,512]{1,0:T(8,128)(2,1)S(1)}, u32[]{:S(2)}, u32[]{:S(2)}) %collective-permute-start.11) | collective-permute-done | bytes 393248 | tf_op jit(solution)/shard_map/ppermute | solution.py:105
  68.9 1.1 %fusion.6 = bf16[384,512]{1,0:T(8,128)(2,1)} fusion(f32[384,512]{1,0:T(8,128)S(1)} %shard_map.87, bf16[384,512]{1,0:T(8,128)(2,1)S(1)} %collective-permute-done.11, bf16[384,512]{1,0:T(8,128)(2,1)S(1)} %collective-permute-done.10, bf16[384,512]{1,0:T(8,128)(2,1)S(1)} %collective-permute-done.9, bf16[1,384,512]{2,1,0:T(8,128)(2,1)S(1)} %collective-permute-done.6, ...), kind=kLoop, calls=%fused_computation.10 | loop fusion | flops 1966080 | bytes 3538944 | tf_op jit(solution)/shard_map/convert_element_type | solution.py:270
  (44 shorter events, 2.8 us)
Async XLA Ops:
  0.7 1.3 %copy-start.3 = (bf16[384,1664]{1,0:T(8,128)(2,1)S(1)}, bf16[384,1664]{1,0:T(8,128)(2,1)}, u32[]{:S(2)}) copy-start(bf16[384,1664]{1,0:T(8,128)(2,1)} %hidden_ref.9) | copy-start | bytes 3833860
  4.9 5.1 %collective-permute-start = (bf16[1,384,512]{2,1,0:T(8,128)(2,1)S(1)}, bf16[1,384,512]{2,1,0:T(8,128)(2,1)S(1)}, u32[]{:S(2)}, u32[]{:S(2)}) collective-permute-start(bf16[1,384,512]{2,1,0:T(8,128)(2,1)S(1)} %get-tuple-element.29), channel_id=1, source_target_pairs={{0,1},{1,0},{2,3},{3,2},{4,5},{5,4},{6,7},{7,6},{8,9},{9,8},{10,11... | collective-permute-start | bytes 1179656 | tf_op jit(solution)/shard_map/ppermute | solution.py:105
  5.4 4.6 %copy-start.4 = (s32[384]{0:T(512)S(1)}, s32[384]{0:T(512)}, u32[]{:S(2)}) copy-start(s32[384]{0:T(512)} %param.12) | copy-start | bytes 4612
  9.8 9.6 %collective-permute-start.1 = (bf16[2,384,512]{2,1,0:T(8,128)(2,1)S(1)}, bf16[2,384,512]{2,1,0:T(8,128)(2,1)S(1)}, u32[]{:S(2)}, u32[]{:S(2)}) collective-permute-start(bf16[2,384,512]{2,1,0:T(8,128)(2,1)S(1)} %get-tuple-element.32), channel_id=1, source_target_pairs={{0,1},{1,0},{2,3},{3,2},{4,5},{5,4},{6,7},{7,6},{8,9},{9,8},{10,11... | collective-permute-start | bytes 2359304 | tf_op jit(solution)/shard_map/ppermute | solution.py:105
  10.1 12.3 %collective-permute-start.2 = (bf16[384,512]{1,0:T(8,128)(2,1)S(1)}, bf16[384,512]{1,0:T(8,128)(2,1)S(1)}, u32[]{:S(2)}, u32[]{:S(2)}) collective-permute-start(bf16[384,512]{1,0:T(8,128)(2,1)S(1)} %fusion.12.refs_1_), channel_id=1, source_target_pairs={{0,2},{1,3},{2,0},{3,1},{4,6},{5,7},{6,4},{7,5},{8,10},{9,11},{10,... | collective-permute-start | bytes 1179656 | tf_op jit(solution)/shard_map/ppermute | solution.py:105
  13.1 9.5 %slice-start = ((s8[6815744]{0:T(1024)(128)(4,1)}), s8[4194304]{0:T(1024)(128)(4,1)S(1)}, s32[]{:S(2)}) async-start(s8[6815744]{0:T(1024)(128)(4,1)} %bitcast.50), calls=%async_computation | async-start | bytes 8388608
  13.1 9.5 %slice-start.1 = ((s8[6815744]{0:T(1024)(128)(4,1)}), s8[2621440]{0:T(1024)(128)(4,1)S(1)}, s32[]{:S(2)}) async-start(s8[6815744]{0:T(1024)(128)(4,1)} %bitcast.50), calls=%async_computation.1 | async-start | bytes 5242880
  19.4 19.6 %collective-permute-start.3 = (bf16[2,384,512]{2,1,0:T(8,128)(2,1)S(1)}, bf16[2,384,512]{2,1,0:T(8,128)(2,1)S(1)}, u32[]{:S(2)}, u32[]{:S(2)}) collective-permute-start(bf16[2,384,512]{2,1,0:T(8,128)(2,1)S(1)} %get-tuple-element.39), channel_id=1, source_target_pairs={{0,1},{1,0},{2,3},{3,2},{4,5},{5,4},{6,7},{7,6},{8,9},{9,8},{10,11... | collective-permute-start | bytes 2359304 | tf_op jit(solution)/shard_map/ppermute | solution.py:105
  27.2 12.0 %collective-permute-start.5 = (bf16[448,512]{1,0:T(8,128)(2,1)S(1)}, bf16[448,512]{1,0:T(8,128)(2,1)S(1)}, u32[]{:S(2)}, u32[]{:S(2)}) collective-permute-start(bf16[448,512]{1,0:T(8,128)(2,1)S(1)} %fusion.10.refs_1_), channel_id=1, source_target_pairs={{0,4},{1,5},{2,6},{3,7},{4,0},{5,1},{6,2},{7,3},{8,12},{9,13},{10,... | collective-permute-start | bytes 1376264 | tf_op jit(solution)/shard_map/ppermute | solution.py:105
  29.1 9.9 %collective-permute-start.4 = (bf16[384,512]{1,0:T(8,128)(2,1)S(1)}, bf16[384,512]{1,0:T(8,128)(2,1)S(1)}, u32[]{:S(2)}, u32[]{:S(2)}) collective-permute-start(bf16[384,512]{1,0:T(8,128)(2,1)S(1)} %fusion.13.refs_2_), channel_id=1, source_target_pairs={{0,2},{1,3},{2,0},{3,1},{4,6},{5,7},{6,4},{7,5},{8,10},{9,11},{10,... | collective-permute-start | bytes 1179656 | tf_op jit(solution)/shard_map/ppermute | solution.py:105
  36.2 13.0 %collective-permute-start.7 = (bf16[2,384,512]{2,1,0:T(8,128)(2,1)S(1)}, bf16[2,384,512]{2,1,0:T(8,128)(2,1)S(1)}, u32[]{:S(2)}, u32[]{:S(2)}) collective-permute-start(bf16[2,384,512]{2,1,0:T(8,128)(2,1)S(1)} %get-tuple-element.44), channel_id=1, source_target_pairs={{0,1},{1,0},{2,3},{3,2},{4,5},{5,4},{6,7},{7,6},{8,9},{9,8},{10,11... | collective-permute-start | bytes 2359304 | tf_op jit(solution)/shard_map/ppermute | solution.py:105
  39.6 11.1 %collective-permute-start.8 = (bf16[448,512]{1,0:T(8,128)(2,1)S(1)}, bf16[448,512]{1,0:T(8,128)(2,1)S(1)}, u32[]{:S(2)}, u32[]{:S(2)}) collective-permute-start(bf16[448,512]{1,0:T(8,128)(2,1)S(1)} %fusion.11.refs_2_), channel_id=1, source_target_pairs={{0,2},{1,3},{2,0},{3,1},{4,6},{5,7},{6,4},{7,5},{8,10},{9,11},{10,... | collective-permute-start | bytes 1376264 | tf_op jit(solution)/shard_map/ppermute | solution.py:105
  41.1 24.6 %collective-permute-start.10 = (bf16[384,512]{1,0:T(8,128)(2,1)S(1)}, bf16[384,512]{1,0:T(8,128)(2,1)S(1)}, u32[]{:S(2)}, u32[]{:S(2)}) collective-permute-start(bf16[384,512]{1,0:T(8,128)(2,1)S(1)} %fusion.8.refs_1_), channel_id=1, source_target_pairs={{0,8},{1,9},{2,10},{3,11},{4,12},{5,13},{6,14},{7,15},{8,0},{9,1},... | collective-permute-start | bytes 1179656 | tf_op jit(solution)/shard_map/ppermute | solution.py:105
  49.1 13.8 %copy-start = (bf16[32,64,512]{2,1,0:T(8,128)(2,1)S(1)}, bf16[32,64,512]{2,1,0:T(8,128)(2,1)}, u32[]{:S(2)}) copy-start(bf16[32,64,512]{2,1,0:T(8,128)(2,1)} %param.11) | copy-start | bytes 6291460
  49.1 13.8 %copy-start.1 = (s32[32]{0:T(128)S(1)}, s32[32]{0:T(128)}, u32[]{:S(2)}) copy-start(s32[32]{0:T(128)} %first_ref.1) | copy-start | bytes 388
  49.1 13.8 %copy-start.2 = (s32[32]{0:T(128)S(1)}, s32[32]{0:T(128)}, u32[]{:S(2)}) copy-start(s32[32]{0:T(128)} %length_ref.1) | copy-start | bytes 388
  49.1 16.6 %collective-permute-start.6 = (bf16[1,384,512]{2,1,0:T(8,128)(2,1)S(1)}, bf16[1,384,512]{2,1,0:T(8,128)(2,1)S(1)}, u32[]{:S(2)}, u32[]{:S(2)}) collective-permute-start(bf16[1,384,512]{2,1,0:T(8,128)(2,1)S(1)} %get-tuple-element.43), channel_id=1, source_target_pairs={{0,1},{1,0},{2,3},{3,2},{4,5},{5,4},{6,7},{7,6},{8,9},{9,8},{10,11... | collective-permute-start | bytes 1179656 | tf_op jit(solution)/shard_map/ppermute | solution.py:105
  51.0 14.7 %collective-permute-start.9 = (bf16[384,512]{1,0:T(8,128)(2,1)S(1)}, bf16[384,512]{1,0:T(8,128)(2,1)S(1)}, u32[]{:S(2)}, u32[]{:S(2)}) collective-permute-start(bf16[384,512]{1,0:T(8,128)(2,1)S(1)} %fusion.15), channel_id=1, source_target_pairs={{0,2},{1,3},{2,0},{3,1},{4,6},{5,7},{6,4},{7,5},{8,10},{9,11},{10,... | collective-permute-start | bytes 1179656 | tf_op jit(solution)/shard_map/ppermute | solution.py:105
  52.2 16.7 %collective-permute-start.11 = (bf16[384,512]{1,0:T(8,128)(2,1)S(1)}, bf16[384,512]{1,0:T(8,128)(2,1)S(1)}, u32[]{:S(2)}, u32[]{:S(2)}) collective-permute-start(bf16[384,512]{1,0:T(8,128)(2,1)S(1)} %fusion.2), channel_id=1, source_target_pairs={{0,4},{1,5},{2,6},{3,7},{4,0},{5,1},{6,2},{7,3},{8,12},{9,13},{10,... | collective-permute-start | bytes 1179656 | tf_op jit(solution)/shard_map/ppermute | solution.py:105
  53.8 7.7 %collective-permute-start.12 = (bf16[64,384]{1,0:T(8,128)(2,1)S(1)}, bf16[64,384]{1,0:T(8,128)(2,1)S(1)}, u32[]{:S(2)}, u32[]{:S(2)}) collective-permute-start(bf16[64,384]{1,0:T(8,128)(2,1)S(1)} %fusion.16), channel_id=1, source_target_pairs={{0,8},{1,9},{2,10},{3,11},{4,12},{5,13},{6,14},{7,15},{8,0},{9,1},... | collective-permute-start | bytes 147464 | tf_op jit(solution)/shard_map/ppermute | solution.py:105
  61.6 1.4 %collective-permute-start.13 = (f32[64,384]{1,0:T(8,128)S(1)}, f32[64,384]{1,0:T(8,128)S(1)}, u32[]{:S(2)}, u32[]{:S(2)}) collective-permute-start(f32[64,384]{1,0:T(8,128)S(1)} %convert_add_fusion), channel_id=1, source_target_pairs={{0,1},{1,0},{2,3},{3,2},{4,5},{5,4},{6,7},{7,6},{8,9},{9,8},{10,11... | collective-permute-start | bytes 294920 | tf_op jit(solution)/shard_map/ppermute | solution.py:105

commit v18 on v16

--- a/solution.py
+++ b/solution.py
@@ -10,7 +10,7 @@
 VMEM_LIMIT = 39 * 1024 * 1024
 WINDOW = 128
 TOGETHER = 4
-FLOPS = 3_000_000_000
+FLOPS = 10_000_000_000
 EXPAND_FLOPS = 1_000_000
 
 
@@ -248,23 +248,27 @@
             late, results = lax.optimization_barrier((hidden, results))
             packed = shrink(late, shrink_matrices, row_adapter_index)
         ready = []
+        if not unit:
+            leaving = (results[0] + arrived[0].astype(jnp.float32)).astype(jnp.bfloat16)
+            leaving, arrived = lax.optimization_barrier((leaving, arrived))
         if unit < top:
             moving, arrived = lax.optimization_barrier((settle(unit + 1, arrived[1]), arrived))
             bit = (unit + 1) & -(unit + 1)
             moving, *came = send(moving, 4 * bit)
             incoming.setdefault((unit + 1) ^ bit, []).append(came)
             ready.append(moving)
-        leaving = (results[0] + arrived[0].astype(jnp.float32)).astype(jnp.bfloat16)
+        if unit:
+            leaving = (results[0] + arrived[0].astype(jnp.float32)).astype(jnp.bfloat16)
         leaving, crossed[unit], shrinks = send(leaving, near)
         packed = packed if shrinks is None else shrinks
         ready.append(leaving)
-    kept = [settle(0, swap(values, core, total)[0])]
+    arrived = swap(values, core, total)[0]
 
     for bit in steps:
         kind = jnp.bfloat16 if bit > near else jnp.float32
         packed = packed + swap(packed.astype(kind), bit, total).astype(jnp.float32)
     adapter_output = expand(packed, expand_matrices, segment_first_row, segment_length)
-    return (kept[0] + adapter_output).astype(jnp.bfloat16)
+    return (settle(0, arrived) + adapter_output).astype(jnp.bfloat16)
 
 
 def solution(mesh):

time: 68.4 us -> 69.6 us (1.018)
  starting transfers between devices: 15.2 us -> 17.1 us
  waiting for transfers between devices: 17.1 us -> 16.2 us
    ppermute x14, starting transfers between devices: 15.2 us -> 17.1 us  [swap(): lax.ppermute(value, 'tensor', [(place, place ^ bit) for place in range(to...]
    ppermute x14, waiting for transfers between devices: 17.1 us -> 16.2 us  [swap(): lax.ppermute(value, 'tensor', [(place, place ^ bit) for place in range(to...]
  transfers between devices with their start and end apart: 14 -> 14, of which waited for: 5 -> 6; matrix products, arithmetic and copies ran while one was open for 8% -> 8% of each run, Pallas kernels for 35% -> 34%
where the time goes in v18:
time: 69.6 us; the launch traced here: 69.2 us
  Pallas kernels  26.7 us (38%)
  starting transfers between devices  17.1 us (25%)
  waiting for transfers between devices  16.2 us (23%)
  matrix products  4.12 us (6%)
  other arithmetic  3.46 us (5%)
  local copies, waits for them, and re-layouts  1.34 us (2%)
    pallas_call x5, Pallas kernels, product(): pl.pallas_call(functools.partial(product_body, base=base, sent=sent, kept...  24 us
    ppermute x14, starting transfers between devices, swap(): lax.ppermute(value, 'tensor', [(place, place ^ bit) for place in range(to...  17.1 us
    ppermute x14, waiting for transfers between devices, swap(): lax.ppermute(value, 'tensor', [(place, place ^ bit) for place in range(to...  16.2 us
    unnamed x1, matrix products  4.12 us
    pallas_call x1, Pallas kernels, expand(): pl.pallas_call(expand_body, in_specs=[pl.BlockSpec(memory_space=pltpu.SME...  2.71 us
  transfers between devices with their start and end apart: 14, of which 6 were waited for; matrix products, arithmetic and copies ran while one was open for 8% of the time, Pallas kernels for 34%

profile of v18, /device:TPU:0, one launch (start us, length us, event | category | flops | bytes accessed | tf_op | source)
XLA Modules:
  0.0 69.2 jit_solution(13609804363267739631)
XLA Ops:
  0.0 0.7 broadcast_xor_fusion.table_ref
  0.7 1.3 %copy-done.3 = bf16[384,1664]{1,0:T(8,128)(2,1)S(1)} copy-done((bf16[384,1664]{1,0:T(8,128)(2,1)S(1)}, bf16[384,1664]{1,0:T(8,128)(2,1)}, u32[]{:S(2)}) %copy-start.3) | copy-done | bytes 1277976
  2.0 2.9 %shard_map.82 = (bf16[1,384,512]{2,1,0:T(8,128)(2,1)S(1)}, bf16[2,1664,512]{2,1,0:T(8,128)(2,1)S(1)}) custom-call(s32[16]{0:T(128)S(1)} %broadcast_xor_fusion.table_ref, bf16[384,1664]{1,0:T(8,128)(2,1)S(1)} %copy-done.3, bf16[1664,8192]{1,0:T(8,128)(2,1)} %down_ref.9), custom_call_target="tpu_custom_call" | custom-call | flops 10000000000 | bytes 1024 | tf_op jit(solution)/shard_map/pallas_call | solution.py:82
  5.4 4.4 %shard_map.83 = (bf16[2,384,512]{2,1,0:T(8,128)(2,1)S(1)}, f32[1,384,512]{2,1,0:T(8,128)S(1)}, bf16[2,1664,512]{2,1,0:T(8,128)(2,1)S(1)}) custom-call(s32[16]{0:T(128)S(1)} %broadcast_xor_fusion.table_ref, bf16[384,1664]{1,0:T(8,128)(2,1)S(1)} %copy-done.3, bf16[1664,8192]{1,0:T(8,128)(2,1)} %down_ref.9, ...), custom_call_target="tpu_custom_call", output_to_operand_aliasing={{2}: (3, {})} | custom-call | flops 10000000000 | bytes 1024 | tf_op jit(solution)/shard_map/pallas_call | solution.py:82
  10.1 3.0 %collective-permute-start.2 = (bf16[384,512]{1,0:T(8,128)(2,1)S(1)}, bf16[384,512]{1,0:T(8,128)(2,1)S(1)}, u32[]{:S(2)}, u32[]{:S(2)}) collective-permute-start(bf16[384,512]{1,0:T(8,128)(2,1)S(1)} %fusion.12.refs_1_), channel_id=1, source_target_pairs={{0,2},{1,3},{2,0},{3,1},{4,6},{5,7},{6,4},{7,5},{8,10},{9,11},{10,... | collective-permute-start | bytes 1179656 | tf_op jit(solution)/shard_map/ppermute | solution.py:105
  13.2 5.7 %shard_map.84 = (bf16[2,384,512]{2,1,0:T(8,128)(2,1)S(1)}, f32[2,384,512]{2,1,0:T(8,128)S(1)}, bf16[2,1664,512]{2,1,0:T(8,128)(2,1)S(1)}) custom-call(s32[16]{0:T(128)S(1)} %broadcast_xor_fusion.table_ref, bf16[384,1664]{1,0:T(8,128)(2,1)S(1)} %copy-done.3, bf16[1664,8192]{1,0:T(8,128)(2,1)} %down_ref.9, ...), custom_call_target="tpu_custom_call", output_to_operand_aliasing={{2}: (3, {})} | custom-call | flops 10000000000 | bytes 1024 | tf_op jit(solution)/shard_map/pallas_call | solution.py:82
  19.0 4.1 %fusion.18 = f32[384,2048]{0,1:S(1)} fusion(bf16[384,1664]{1,0:T(8,128)(2,1)S(1)} %copy-done.3, bf16[1664,2048]{0,1:T(8,128)(2,1)S(1)} %bitcast.52), kind=kOutput, calls=%fused_computation.34 | convolution fusion | flops 2617245696 | bytes 11239424
  23.9 0.7 %collective-permute-start.4 = (bf16[384,512]{1,0:T(8,128)(2,1)S(1)}, bf16[384,512]{1,0:T(8,128)(2,1)S(1)}, u32[]{:S(2)}, u32[]{:S(2)}) collective-permute-start(bf16[384,512]{1,0:T(8,128)(2,1)S(1)} %fusion.13.refs_2_), channel_id=1, source_target_pairs={{0,2},{1,3},{2,0},{3,1},{4,6},{5,7},{6,4},{7,5},{8,10},{9,11},{10,... | collective-permute-start | bytes 1179656 | tf_op jit(solution)/shard_map/ppermute | solution.py:105
  24.6 2.0 %collective-permute-start.5 = (bf16[448,512]{1,0:T(8,128)(2,1)S(1)}, bf16[448,512]{1,0:T(8,128)(2,1)S(1)}, u32[]{:S(2)}, u32[]{:S(2)}) collective-permute-start(bf16[448,512]{1,0:T(8,128)(2,1)S(1)} %fusion.10.refs_1_), channel_id=1, source_target_pairs={{0,4},{1,5},{2,6},{3,7},{4,0},{5,1},{6,2},{7,3},{8,12},{9,13},{10,... | collective-permute-start | bytes 1376264 | tf_op jit(solution)/shard_map/ppermute | solution.py:105
  26.6 5.6 %shard_map.85 = (bf16[2,384,512]{2,1,0:T(8,128)(2,1)S(1)}, f32[2,384,512]{2,1,0:T(8,128)S(1)}, bf16[2,1664,512]{2,1,0:T(8,128)(2,1)S(1)}) custom-call(s32[16]{0:T(128)S(1)} %broadcast_xor_fusion.table_ref, bf16[384,1664]{1,0:T(8,128)(2,1)S(1)} %copy-done.3, bf16[1664,8192]{1,0:T(8,128)(2,1)} %down_ref.9, ...), custom_call_target="tpu_custom_call", output_to_operand_aliasing={{2}: (3, {})} | custom-call | flops 10000000000 | bytes 1024 | tf_op jit(solution)/shard_map/pallas_call | solution.py:82
  32.3 3.2 %collective-permute-done.4 = bf16[384,512]{1,0:T(8,128)(2,1)S(1)} collective-permute-done((bf16[384,512]{1,0:T(8,128)(2,1)S(1)}, bf16[384,512]{1,0:T(8,128)(2,1)S(1)}, u32[]{:S(2)}, u32[]{:S(2)}) %collective-permute-start.4) | collective-permute-done | bytes 393248 | tf_op jit(solution)/shard_map/ppermute | solution.py:105
  35.4 1.9 %collective-permute-done.5 = bf16[448,512]{1,0:T(8,128)(2,1)S(1)} collective-permute-done((bf16[448,512]{1,0:T(8,128)(2,1)S(1)}, bf16[448,512]{1,0:T(8,128)(2,1)S(1)}, u32[]{:S(2)}, u32[]{:S(2)}) %collective-permute-start.5) | collective-permute-done | bytes 458784 | tf_op jit(solution)/shard_map/ppermute | solution.py:105
  37.8 1.4 %collective-permute-start.10 = (bf16[448,512]{1,0:T(8,128)(2,1)S(1)}, bf16[448,512]{1,0:T(8,128)(2,1)S(1)}, u32[]{:S(2)}, u32[]{:S(2)}) collective-permute-start(bf16[448,512]{1,0:T(8,128)(2,1)S(1)} %fusion.11.refs_2_), channel_id=1, source_target_pairs={{0,2},{1,3},{2,0},{3,1},{4,6},{5,7},{6,4},{7,5},{8,10},{9,11},{10,... | collective-permute-start | bytes 1376264 | tf_op jit(solution)/shard_map/ppermute | solution.py:105
  39.2 2.5 %collective-permute-start.9 = (bf16[384,512]{1,0:T(8,128)(2,1)S(1)}, bf16[384,512]{1,0:T(8,128)(2,1)S(1)}, u32[]{:S(2)}, u32[]{:S(2)}) collective-permute-start(bf16[384,512]{1,0:T(8,128)(2,1)S(1)} %fusion.8.refs_1_), channel_id=1, source_target_pairs={{0,8},{1,9},{2,10},{3,11},{4,12},{5,13},{6,14},{7,15},{8,0},{9,1},... | collective-permute-start | bytes 1179656 | tf_op jit(solution)/shard_map/ppermute | solution.py:105
  41.7 5.4 %shard_map.86 = (bf16[1,384,512]{2,1,0:T(8,128)(2,1)S(1)}, f32[3,384,512]{2,1,0:T(8,128)S(1)}, bf16[2,1664,512]{2,1,0:T(8,128)(2,1)S(1)}) custom-call(s32[16]{0:T(128)S(1)} %broadcast_xor_fusion.table_ref, bf16[384,1664]{1,0:T(8,128)(2,1)S(1)} %copy-done.3, bf16[1664,8192]{1,0:T(8,128)(2,1)} %down_ref.9, ...), custom_call_target="tpu_custom_call", output_to_operand_aliasing={{2}: (3, {})} | custom-call | flops 10000000000 | bytes 1024 | tf_op jit(solution)/shard_map/pallas_call | solution.py:82
  47.4 1.0 %collective-permute-start.8 = (bf16[384,512]{1,0:T(8,128)(2,1)S(1)}, bf16[384,512]{1,0:T(8,128)(2,1)S(1)}, u32[]{:S(2)}, u32[]{:S(2)}) collective-permute-start(bf16[384,512]{1,0:T(8,128)(2,1)S(1)} %fusion.15), channel_id=1, source_target_pairs={{0,2},{1,3},{2,0},{3,1},{4,6},{5,7},{6,4},{7,5},{8,10},{9,11},{10,... | collective-permute-start | bytes 1179656 | tf_op jit(solution)/shard_map/ppermute | solution.py:105
  48.3 1.3 %collective-permute-done.10 = bf16[448,512]{1,0:T(8,128)(2,1)S(1)} collective-permute-done((bf16[448,512]{1,0:T(8,128)(2,1)S(1)}, bf16[448,512]{1,0:T(8,128)(2,1)S(1)}, u32[]{:S(2)}, u32[]{:S(2)}) %collective-permute-start.10) | collective-permute-done | bytes 458784 | tf_op jit(solution)/shard_map/ppermute | solution.py:105
  49.9 1.6 %collective-permute-start.11 = (bf16[384,512]{1,0:T(8,128)(2,1)S(1)}, bf16[384,512]{1,0:T(8,128)(2,1)S(1)}, u32[]{:S(2)}, u32[]{:S(2)}) collective-permute-start(bf16[384,512]{1,0:T(8,128)(2,1)S(1)} %fusion.2), channel_id=1, source_target_pairs={{0,4},{1,5},{2,6},{3,7},{4,0},{5,1},{6,2},{7,3},{8,12},{9,13},{10,... | collective-permute-start | bytes 1179656 | tf_op jit(solution)/shard_map/ppermute | solution.py:105
  51.5 3.9 %collective-permute-start.12 = (bf16[64,384]{1,0:T(8,128)(2,1)S(1)}, bf16[64,384]{1,0:T(8,128)(2,1)S(1)}, u32[]{:S(2)}, u32[]{:S(2)}) collective-permute-start(bf16[64,384]{1,0:T(8,128)(2,1)S(1)} %fusion.16), channel_id=1, source_target_pairs={{0,8},{1,9},{2,10},{3,11},{4,12},{5,13},{6,14},{7,15},{8,0},{9,1},... | collective-permute-start | bytes 147464 | tf_op jit(solution)/shard_map/ppermute | solution.py:105
  55.4 4.8 %collective-permute-done.12 = bf16[64,384]{1,0:T(8,128)(2,1)S(1)} collective-permute-done((bf16[64,384]{1,0:T(8,128)(2,1)S(1)}, bf16[64,384]{1,0:T(8,128)(2,1)S(1)}, u32[]{:S(2)}, u32[]{:S(2)}) %collective-permute-start.12) | collective-permute-done | bytes 49184 | tf_op jit(solution)/shard_map/ppermute | solution.py:105
  60.4 1.3 %collective-permute-done.13 = f32[64,384]{1,0:T(8,128)S(1)} collective-permute-done((f32[64,384]{1,0:T(8,128)S(1)}, f32[64,384]{1,0:T(8,128)S(1)}, u32[]{:S(2)}, u32[]{:S(2)}) %collective-permute-start.13) | collective-permute-done | bytes 98336 | tf_op jit(solution)/shard_map/ppermute | solution.py:105
  61.7 2.7 %shard_map.87 = f32[384,512]{1,0:T(8,128)S(1)} custom-call(s32[32]{0:T(128)S(1)} %copy-done.1, s32[32]{0:T(128)S(1)} %copy-done.2, f32[64,384]{1,0:T(8,128)S(1)} %add.102.packed_ref, bf16[2048,512]{1,0:T(8,128)(2,1)S(1)} %bitcast.48), custom_call_target="tpu_custom_call" | custom-call | flops 1000000 | bytes 1 | tf_op jit(solution)/shard_map/pallas_call | solution.py:177
  64.5 3.6 %collective-permute-done.11 = bf16[384,512]{1,0:T(8,128)(2,1)S(1)} collective-permute-done((bf16[384,512]{1,0:T(8,128)(2,1)S(1)}, bf16[384,512]{1,0:T(8,128)(2,1)S(1)}, u32[]{:S(2)}, u32[]{:S(2)}) %collective-permute-start.11) | collective-permute-done | bytes 393248 | tf_op jit(solution)/shard_map/ppermute | solution.py:105
  68.1 1.1 %fusion.6 = bf16[384,512]{1,0:T(8,128)(2,1)} fusion(f32[384,512]{1,0:T(8,128)S(1)} %shard_map.87, bf16[384,512]{1,0:T(8,128)(2,1)S(1)} %collective-permute-done.11, bf16[384,512]{1,0:T(8,128)(2,1)S(1)} %collective-permute-done.9, bf16[384,512]{1,0:T(8,128)(2,1)S(1)} %collective-permute-done.8, bf16[1,384,512]{2,1,0:T(8,128)(2,1)S(1)} %collective-permute-done.6, ...), kind=kLoop, calls=%fused_computation.10 | loop fusion | flops 1966080 | bytes 3538944 | tf_op jit(solution)/shard_map/convert_element_type | solution.py:271
  (44 shorter events, 2.7 us)
Async XLA Ops:
  0.7 1.3 %copy-start.3 = (bf16[384,1664]{1,0:T(8,128)(2,1)S(1)}, bf16[384,1664]{1,0:T(8,128)(2,1)}, u32[]{:S(2)}) copy-start(bf16[384,1664]{1,0:T(8,128)(2,1)} %hidden_ref.9) | copy-start | bytes 3833860
  4.9 5.1 %collective-permute-start = (bf16[1,384,512]{2,1,0:T(8,128)(2,1)S(1)}, bf16[1,384,512]{2,1,0:T(8,128)(2,1)S(1)}, u32[]{:S(2)}, u32[]{:S(2)}) collective-permute-start(bf16[1,384,512]{2,1,0:T(8,128)(2,1)S(1)} %get-tuple-element.30), channel_id=1, source_target_pairs={{0,1},{1,0},{2,3},{3,2},{4,5},{5,4},{6,7},{7,6},{8,9},{9,8},{10,11... | collective-permute-start | bytes 1179656 | tf_op jit(solution)/shard_map/ppermute | solution.py:105
  5.4 4.6 %copy-start.4 = (s32[384]{0:T(512)S(1)}, s32[384]{0:T(512)}, u32[]{:S(2)}) copy-start(s32[384]{0:T(512)} %param.12) | copy-start | bytes 4612
  9.8 13.7 %collective-permute-start.1 = (bf16[2,384,512]{2,1,0:T(8,128)(2,1)S(1)}, bf16[2,384,512]{2,1,0:T(8,128)(2,1)S(1)}, u32[]{:S(2)}, u32[]{:S(2)}) collective-permute-start(bf16[2,384,512]{2,1,0:T(8,128)(2,1)S(1)} %get-tuple-element.33), channel_id=1, source_target_pairs={{0,1},{1,0},{2,3},{3,2},{4,5},{5,4},{6,7},{7,6},{8,9},{9,8},{10,11... | collective-permute-start | bytes 2359304 | tf_op jit(solution)/shard_map/ppermute | solution.py:105
  10.0 9.0 %slice-start = ((s8[6815744]{0:T(1024)(128)(4,1)}), s8[4194304]{0:T(1024)(128)(4,1)S(1)}, s32[]{:S(2)}) async-start(s8[6815744]{0:T(1024)(128)(4,1)} %bitcast.50), calls=%async_computation | async-start | bytes 8388608
  10.1 13.4 %collective-permute-start.2 = (bf16[384,512]{1,0:T(8,128)(2,1)S(1)}, bf16[384,512]{1,0:T(8,128)(2,1)S(1)}, u32[]{:S(2)}, u32[]{:S(2)}) collective-permute-start(bf16[384,512]{1,0:T(8,128)(2,1)S(1)} %fusion.12.refs_1_), channel_id=1, source_target_pairs={{0,2},{1,3},{2,0},{3,1},{4,6},{5,7},{6,4},{7,5},{8,10},{9,11},{10,... | collective-permute-start | bytes 1179656 | tf_op jit(solution)/shard_map/ppermute | solution.py:105
  13.2 5.8 %slice-start.1 = ((s8[6815744]{0:T(1024)(128)(4,1)}), s8[2621440]{0:T(1024)(128)(4,1)S(1)}, s32[]{:S(2)}) async-start(s8[6815744]{0:T(1024)(128)(4,1)} %bitcast.50), calls=%async_computation.1 | async-start | bytes 5242880
  18.9 16.5 %collective-permute-start.3 = (bf16[2,384,512]{2,1,0:T(8,128)(2,1)S(1)}, bf16[2,384,512]{2,1,0:T(8,128)(2,1)S(1)}, u32[]{:S(2)}, u32[]{:S(2)}) collective-permute-start(bf16[2,384,512]{2,1,0:T(8,128)(2,1)S(1)} %get-tuple-element.40), channel_id=1, source_target_pairs={{0,1},{1,0},{2,3},{3,2},{4,5},{5,4},{6,7},{7,6},{8,9},{9,8},{10,11... | collective-permute-start | bytes 2359304 | tf_op jit(solution)/shard_map/ppermute | solution.py:105
  23.9 11.6 %collective-permute-start.4 = (bf16[384,512]{1,0:T(8,128)(2,1)S(1)}, bf16[384,512]{1,0:T(8,128)(2,1)S(1)}, u32[]{:S(2)}, u32[]{:S(2)}) collective-permute-start(bf16[384,512]{1,0:T(8,128)(2,1)S(1)} %fusion.13.refs_2_), channel_id=1, source_target_pairs={{0,2},{1,3},{2,0},{3,1},{4,6},{5,7},{6,4},{7,5},{8,10},{9,11},{10,... | collective-permute-start | bytes 1179656 | tf_op jit(solution)/shard_map/ppermute | solution.py:105
  24.6 12.7 %collective-permute-start.5 = (bf16[448,512]{1,0:T(8,128)(2,1)S(1)}, bf16[448,512]{1,0:T(8,128)(2,1)S(1)}, u32[]{:S(2)}, u32[]{:S(2)}) collective-permute-start(bf16[448,512]{1,0:T(8,128)(2,1)S(1)} %fusion.10.refs_1_), channel_id=1, source_target_pairs={{0,4},{1,5},{2,6},{3,7},{4,0},{5,1},{6,2},{7,3},{8,12},{9,13},{10,... | collective-permute-start | bytes 1376264 | tf_op jit(solution)/shard_map/ppermute | solution.py:105
  32.2 15.0 %collective-permute-start.7 = (bf16[2,384,512]{2,1,0:T(8,128)(2,1)S(1)}, bf16[2,384,512]{2,1,0:T(8,128)(2,1)S(1)}, u32[]{:S(2)}, u32[]{:S(2)}) collective-permute-start(bf16[2,384,512]{2,1,0:T(8,128)(2,1)S(1)} %get-tuple-element.45), channel_id=1, source_target_pairs={{0,1},{1,0},{2,3},{3,2},{4,5},{5,4},{6,7},{7,6},{8,9},{9,8},{10,11... | collective-permute-start | bytes 2359304 | tf_op jit(solution)/shard_map/ppermute | solution.py:105
  37.8 11.9 %collective-permute-start.10 = (bf16[448,512]{1,0:T(8,128)(2,1)S(1)}, bf16[448,512]{1,0:T(8,128)(2,1)S(1)}, u32[]{:S(2)}, u32[]{:S(2)}) collective-permute-start(bf16[448,512]{1,0:T(8,128)(2,1)S(1)} %fusion.11.refs_2_), channel_id=1, source_target_pairs={{0,2},{1,3},{2,0},{3,1},{4,6},{5,7},{6,4},{7,5},{8,10},{9,11},{10,... | collective-permute-start | bytes 1376264 | tf_op jit(solution)/shard_map/ppermute | solution.py:105
  39.2 25.3 %collective-permute-start.9 = (bf16[384,512]{1,0:T(8,128)(2,1)S(1)}, bf16[384,512]{1,0:T(8,128)(2,1)S(1)}, u32[]{:S(2)}, u32[]{:S(2)}) collective-permute-start(bf16[384,512]{1,0:T(8,128)(2,1)S(1)} %fusion.8.refs_1_), channel_id=1, source_target_pairs={{0,8},{1,9},{2,10},{3,11},{4,12},{5,13},{6,14},{7,15},{8,0},{9,1},... | collective-permute-start | bytes 1179656 | tf_op jit(solution)/shard_map/ppermute | solution.py:105
  47.1 14.6 %copy-start = (bf16[32,64,512]{2,1,0:T(8,128)(2,1)S(1)}, bf16[32,64,512]{2,1,0:T(8,128)(2,1)}, u32[]{:S(2)}) copy-start(bf16[32,64,512]{2,1,0:T(8,128)(2,1)} %param.11) | copy-start | bytes 6291460
  47.1 14.6 %copy-start.1 = (s32[32]{0:T(128)S(1)}, s32[32]{0:T(128)}, u32[]{:S(2)}) copy-start(s32[32]{0:T(128)} %first_ref.1) | copy-start | bytes 388
  47.1 14.6 %copy-start.2 = (s32[32]{0:T(128)S(1)}, s32[32]{0:T(128)}, u32[]{:S(2)}) copy-start(s32[32]{0:T(128)} %length_ref.1) | copy-start | bytes 388
  47.1 17.3 %collective-permute-start.6 = (bf16[1,384,512]{2,1,0:T(8,128)(2,1)S(1)}, bf16[1,384,512]{2,1,0:T(8,128)(2,1)S(1)}, u32[]{:S(2)}, u32[]{:S(2)}) collective-permute-start(bf16[1,384,512]{2,1,0:T(8,128)(2,1)S(1)} %get-tuple-element.44), channel_id=1, source_target_pairs={{0,1},{1,0},{2,3},{3,2},{4,5},{5,4},{6,7},{7,6},{8,9},{9,8},{10,11... | collective-permute-start | bytes 1179656 | tf_op jit(solution)/shard_map/ppermute | solution.py:105
  47.4 17.1 %collective-permute-start.8 = (bf16[384,512]{1,0:T(8,128)(2,1)S(1)}, bf16[384,512]{1,0:T(8,128)(2,1)S(1)}, u32[]{:S(2)}, u32[]{:S(2)}) collective-permute-start(bf16[384,512]{1,0:T(8,128)(2,1)S(1)} %fusion.15), channel_id=1, source_target_pairs={{0,2},{1,3},{2,0},{3,1},{4,6},{5,7},{6,4},{7,5},{8,10},{9,11},{10,... | collective-permute-start | bytes 1179656 | tf_op jit(solution)/shard_map/ppermute | solution.py:105
  49.9 18.2 %collective-permute-start.11 = (bf16[384,512]{1,0:T(8,128)(2,1)S(1)}, bf16[384,512]{1,0:T(8,128)(2,1)S(1)}, u32[]{:S(2)}, u32[]{:S(2)}) collective-permute-start(bf16[384,512]{1,0:T(8,128)(2,1)S(1)} %fusion.2), channel_id=1, source_target_pairs={{0,4},{1,5},{2,6},{3,7},{4,0},{5,1},{6,2},{7,3},{8,12},{9,13},{10,... | collective-permute-start | bytes 1179656 | tf_op jit(solution)/shard_map/ppermute | solution.py:105
  51.5 8.8 %collective-permute-start.12 = (bf16[64,384]{1,0:T(8,128)(2,1)S(1)}, bf16[64,384]{1,0:T(8,128)(2,1)S(1)}, u32[]{:S(2)}, u32[]{:S(2)}) collective-permute-start(bf16[64,384]{1,0:T(8,128)(2,1)S(1)} %fusion.16), channel_id=1, source_target_pairs={{0,8},{1,9},{2,10},{3,11},{4,12},{5,13},{6,14},{7,15},{8,0},{9,1},... | collective-permute-start | bytes 147464 | tf_op jit(solution)/shard_map/ppermute | solution.py:105
  60.3 1.4 %collective-permute-start.13 = (f32[64,384]{1,0:T(8,128)S(1)}, f32[64,384]{1,0:T(8,128)S(1)}, u32[]{:S(2)}, u32[]{:S(2)}) collective-permute-start(f32[64,384]{1,0:T(8,128)S(1)} %convert_add_fusion), channel_id=1, source_target_pairs={{0,1},{1,0},{2,3},{3,2},{4,5},{5,4},{6,7},{7,6},{8,9},{9,8},{10,11... | collective-permute-start | bytes 294920 | tf_op jit(solution)/shard_map/ppermute | solution.py:105

commit v19 on v18

--- a/solution.py
+++ b/solution.py
@@ -10,7 +10,7 @@
 VMEM_LIMIT = 39 * 1024 * 1024
 WINDOW = 128
 TOGETHER = 4
-FLOPS = 10_000_000_000
+FLOPS = 3_000_000_000
 EXPAND_FLOPS = 1_000_000
 
 

time: 69.6 us -> 68.4 us (0.983)
  waiting for transfers between devices: 16.2 us -> 15.4 us
    ppermute x14, waiting for transfers between devices: 16.2 us -> 15.4 us  [swap(): lax.ppermute(value, 'tensor', [(place, place ^ bit) for place in range(to...]
  transfers between devices with their start and end apart: 14 -> 14, of which waited for: 6 -> 5; matrix products, arithmetic and copies ran while one was open for 8% -> 8% of each run, Pallas kernels for 34% -> 35%
where the time goes in v19:
time: 68.4 us; the launch traced here: 68 us
  Pallas kernels  26.7 us (39%)
  starting transfers between devices  17 us (25%)
  waiting for transfers between devices  15.4 us (23%)
  matrix products  3.92 us (6%)
  other arithmetic  3.48 us (5%)
  local copies, waits for them, and re-layouts  1.34 us (2%)
    pallas_call x5, Pallas kernels, product(): pl.pallas_call(functools.partial(product_body, base=base, sent=sent, kept...  24 us
    ppermute x14, starting transfers between devices, swap(): lax.ppermute(value, 'tensor', [(place, place ^ bit) for place in range(to...  17 us
    ppermute x14, waiting for transfers between devices, swap(): lax.ppermute(value, 'tensor', [(place, place ^ bit) for place in range(to...  15.4 us
    unnamed x1, matrix products  3.92 us
    pallas_call x1, Pallas kernels, expand(): pl.pallas_call(expand_body, in_specs=[pl.BlockSpec(memory_space=pltpu.SME...  2.71 us
  transfers between devices with their start and end apart: 14, of which 5 were waited for; matrix products, arithmetic and copies ran while one was open for 8% of the time, Pallas kernels for 35%

profile of v19, /device:TPU:0, one launch (start us, length us, event | category | flops | bytes accessed | tf_op | source)
XLA Modules:
  0.0 68.0 jit_solution(2308401938570556941)
XLA Ops:
  0.0 0.7 broadcast_xor_fusion.table_ref
  0.7 1.3 %copy-done = bf16[384,1664]{1,0:T(8,128)(2,1)S(1)} copy-done((bf16[384,1664]{1,0:T(8,128)(2,1)S(1)}, bf16[384,1664]{1,0:T(8,128)(2,1)}, u32[]{:S(2)}) %copy-start) | copy-done | bytes 1277976
  2.0 2.9 %shard_map.82 = (bf16[1,384,512]{2,1,0:T(8,128)(2,1)S(1)}, bf16[2,1664,512]{2,1,0:T(8,128)(2,1)S(1)}) custom-call(s32[16]{0:T(128)S(1)} %broadcast_xor_fusion.table_ref, bf16[384,1664]{1,0:T(8,128)(2,1)S(1)} %copy-done, bf16[1664,8192]{1,0:T(8,128)(2,1)} %down_ref.9), custom_call_target="tpu_custom_call" | custom-call | flops 3000000000 | bytes 1024 | tf_op jit(solution)/shard_map/pallas_call | solution.py:82
  4.9 0.5 collective-permute-start
  5.4 4.4 %shard_map.83 = (bf16[2,384,512]{2,1,0:T(8,128)(2,1)S(1)}, f32[1,384,512]{2,1,0:T(8,128)S(1)}, bf16[2,1664,512]{2,1,0:T(8,128)(2,1)S(1)}) custom-call(s32[16]{0:T(128)S(1)} %broadcast_xor_fusion.table_ref, bf16[384,1664]{1,0:T(8,128)(2,1)S(1)} %copy-done, bf16[1664,8192]{1,0:T(8,128)(2,1)} %down_ref.9, ...), custom_call_target="tpu_custom_call", output_to_operand_aliasing={{2}: (3, {})} | custom-call | flops 3000000000 | bytes 1024 | tf_op jit(solution)/shard_map/pallas_call | solution.py:82
  10.1 3.0 %collective-permute-start.2 = (bf16[384,512]{1,0:T(8,128)(2,1)S(1)}, bf16[384,512]{1,0:T(8,128)(2,1)S(1)}, u32[]{:S(2)}, u32[]{:S(2)}) collective-permute-start(bf16[384,512]{1,0:T(8,128)(2,1)S(1)} %fusion.12.refs_1_), channel_id=1, source_target_pairs={{0,2},{1,3},{2,0},{3,1},{4,6},{5,7},{6,4},{7,5},{8,10},{9,11},{10,... | collective-permute-start | bytes 1179656 | tf_op jit(solution)/shard_map/ppermute | solution.py:105
  13.1 5.7 %shard_map.84 = (bf16[2,384,512]{2,1,0:T(8,128)(2,1)S(1)}, f32[2,384,512]{2,1,0:T(8,128)S(1)}, bf16[2,1664,512]{2,1,0:T(8,128)(2,1)S(1)}) custom-call(s32[16]{0:T(128)S(1)} %broadcast_xor_fusion.table_ref, bf16[384,1664]{1,0:T(8,128)(2,1)S(1)} %copy-done, bf16[1664,8192]{1,0:T(8,128)(2,1)} %down_ref.9, ...), custom_call_target="tpu_custom_call", output_to_operand_aliasing={{2}: (3, {})} | custom-call | flops 3000000000 | bytes 1024 | tf_op jit(solution)/shard_map/pallas_call | solution.py:82
  19.0 3.9 %fusion.18 = f32[384,2048]{0,1:S(1)} fusion(bf16[384,1664]{1,0:T(8,128)(2,1)S(1)} %copy-done, bf16[1664,2048]{0,1:T(8,128)(2,1)S(1)} %bitcast.52), kind=kOutput, calls=%fused_computation.34 | convolution fusion | flops 2617245696 | bytes 11239424
  23.6 1.6 %collective-permute-start.5 = (bf16[448,512]{1,0:T(8,128)(2,1)S(1)}, bf16[448,512]{1,0:T(8,128)(2,1)S(1)}, u32[]{:S(2)}, u32[]{:S(2)}) collective-permute-start(bf16[448,512]{1,0:T(8,128)(2,1)S(1)} %fusion.10.refs_1_), channel_id=1, source_target_pairs={{0,4},{1,5},{2,6},{3,7},{4,0},{5,1},{6,2},{7,3},{8,12},{9,13},{10,... | collective-permute-start | bytes 1376264 | tf_op jit(solution)/shard_map/ppermute | solution.py:105
  25.3 1.1 %collective-permute-start.4 = (bf16[384,512]{1,0:T(8,128)(2,1)S(1)}, bf16[384,512]{1,0:T(8,128)(2,1)S(1)}, u32[]{:S(2)}, u32[]{:S(2)}) collective-permute-start(bf16[384,512]{1,0:T(8,128)(2,1)S(1)} %fusion.13.refs_2_), channel_id=1, source_target_pairs={{0,2},{1,3},{2,0},{3,1},{4,6},{5,7},{6,4},{7,5},{8,10},{9,11},{10,... | collective-permute-start | bytes 1179656 | tf_op jit(solution)/shard_map/ppermute | solution.py:105
  26.4 5.6 %shard_map.85 = (bf16[2,384,512]{2,1,0:T(8,128)(2,1)S(1)}, f32[2,384,512]{2,1,0:T(8,128)S(1)}, bf16[2,1664,512]{2,1,0:T(8,128)(2,1)S(1)}) custom-call(s32[16]{0:T(128)S(1)} %broadcast_xor_fusion.table_ref, bf16[384,1664]{1,0:T(8,128)(2,1)S(1)} %copy-done, bf16[1664,8192]{1,0:T(8,128)(2,1)} %down_ref.9, ...), custom_call_target="tpu_custom_call", output_to_operand_aliasing={{2}: (3, {})} | custom-call | flops 3000000000 | bytes 1024 | tf_op jit(solution)/shard_map/pallas_call | solution.py:82
  32.1 4.5 %collective-permute-done.4 = bf16[384,512]{1,0:T(8,128)(2,1)S(1)} collective-permute-done((bf16[384,512]{1,0:T(8,128)(2,1)S(1)}, bf16[384,512]{1,0:T(8,128)(2,1)S(1)}, u32[]{:S(2)}, u32[]{:S(2)}) %collective-permute-start.4) | collective-permute-done | bytes 393248 | tf_op jit(solution)/shard_map/ppermute | solution.py:105
  37.0 1.0 %collective-permute-start.10 = (bf16[448,512]{1,0:T(8,128)(2,1)S(1)}, bf16[448,512]{1,0:T(8,128)(2,1)S(1)}, u32[]{:S(2)}, u32[]{:S(2)}) collective-permute-start(bf16[448,512]{1,0:T(8,128)(2,1)S(1)} %fusion.11.refs_2_), channel_id=1, source_target_pairs={{0,2},{1,3},{2,0},{3,1},{4,6},{5,7},{6,4},{7,5},{8,10},{9,11},{10,... | collective-permute-start | bytes 1376264 | tf_op jit(solution)/shard_map/ppermute | solution.py:105
  38.0 2.6 %collective-permute-start.9 = (bf16[384,512]{1,0:T(8,128)(2,1)S(1)}, bf16[384,512]{1,0:T(8,128)(2,1)S(1)}, u32[]{:S(2)}, u32[]{:S(2)}) collective-permute-start(bf16[384,512]{1,0:T(8,128)(2,1)S(1)} %fusion.8.refs_1_), channel_id=1, source_target_pairs={{0,8},{1,9},{2,10},{3,11},{4,12},{5,13},{6,14},{7,15},{8,0},{9,1},... | collective-permute-start | bytes 1179656 | tf_op jit(solution)/shard_map/ppermute | solution.py:105
  40.6 5.4 %shard_map.86 = (bf16[1,384,512]{2,1,0:T(8,128)(2,1)S(1)}, f32[3,384,512]{2,1,0:T(8,128)S(1)}, bf16[2,1664,512]{2,1,0:T(8,128)(2,1)S(1)}) custom-call(s32[16]{0:T(128)S(1)} %broadcast_xor_fusion.table_ref, bf16[384,1664]{1,0:T(8,128)(2,1)S(1)} %copy-done, bf16[1664,8192]{1,0:T(8,128)(2,1)} %down_ref.9, ...), custom_call_target="tpu_custom_call", output_to_operand_aliasing={{2}: (3, {})} | custom-call | flops 3000000000 | bytes 1024 | tf_op jit(solution)/shard_map/pallas_call | solution.py:82
  46.2 1.2 %collective-permute-start.8 = (bf16[384,512]{1,0:T(8,128)(2,1)S(1)}, bf16[384,512]{1,0:T(8,128)(2,1)S(1)}, u32[]{:S(2)}, u32[]{:S(2)}) collective-permute-start(bf16[384,512]{1,0:T(8,128)(2,1)S(1)} %fusion.15), channel_id=1, source_target_pairs={{0,2},{1,3},{2,0},{3,1},{4,6},{5,7},{6,4},{7,5},{8,10},{9,11},{10,... | collective-permute-start | bytes 1179656 | tf_op jit(solution)/shard_map/ppermute | solution.py:105
  47.4 1.7 %collective-permute-done.10 = bf16[448,512]{1,0:T(8,128)(2,1)S(1)} collective-permute-done((bf16[448,512]{1,0:T(8,128)(2,1)S(1)}, bf16[448,512]{1,0:T(8,128)(2,1)S(1)}, u32[]{:S(2)}, u32[]{:S(2)}) %collective-permute-start.10) | collective-permute-done | bytes 458784 | tf_op jit(solution)/shard_map/ppermute | solution.py:105
  49.3 1.6 %collective-permute-start.11 = (bf16[384,512]{1,0:T(8,128)(2,1)S(1)}, bf16[384,512]{1,0:T(8,128)(2,1)S(1)}, u32[]{:S(2)}, u32[]{:S(2)}) collective-permute-start(bf16[384,512]{1,0:T(8,128)(2,1)S(1)} %fusion.2), channel_id=1, source_target_pairs={{0,4},{1,5},{2,6},{3,7},{4,0},{5,1},{6,2},{7,3},{8,12},{9,13},{10,... | collective-permute-start | bytes 1179656 | tf_op jit(solution)/shard_map/ppermute | solution.py:105
  51.0 4.0 %collective-permute-start.12 = (bf16[64,384]{1,0:T(8,128)(2,1)S(1)}, bf16[64,384]{1,0:T(8,128)(2,1)S(1)}, u32[]{:S(2)}, u32[]{:S(2)}) collective-permute-start(bf16[64,384]{1,0:T(8,128)(2,1)S(1)} %fusion.16), channel_id=1, source_target_pairs={{0,8},{1,9},{2,10},{3,11},{4,12},{5,13},{6,14},{7,15},{8,0},{9,1},... | collective-permute-start | bytes 147464 | tf_op jit(solution)/shard_map/ppermute | solution.py:105
  54.9 4.4 %collective-permute-done.12 = bf16[64,384]{1,0:T(8,128)(2,1)S(1)} collective-permute-done((bf16[64,384]{1,0:T(8,128)(2,1)S(1)}, bf16[64,384]{1,0:T(8,128)(2,1)S(1)}, u32[]{:S(2)}, u32[]{:S(2)}) %collective-permute-start.12) | collective-permute-done | bytes 49184 | tf_op jit(solution)/shard_map/ppermute | solution.py:105
  59.4 1.3 %collective-permute-done.13 = f32[64,384]{1,0:T(8,128)S(1)} collective-permute-done((f32[64,384]{1,0:T(8,128)S(1)}, f32[64,384]{1,0:T(8,128)S(1)}, u32[]{:S(2)}, u32[]{:S(2)}) %collective-permute-start.13) | collective-permute-done | bytes 98336 | tf_op jit(solution)/shard_map/ppermute | solution.py:105
  60.8 2.7 %shard_map.87 = f32[384,512]{1,0:T(8,128)S(1)} custom-call(s32[32]{0:T(128)S(1)} %copy-done.2, s32[32]{0:T(128)S(1)} %copy-done.3, f32[64,384]{1,0:T(8,128)S(1)} %add.102.packed_ref, bf16[2048,512]{1,0:T(8,128)(2,1)S(1)} %bitcast.48), custom_call_target="tpu_custom_call" | custom-call | flops 1000000 | bytes 1 | tf_op jit(solution)/shard_map/pallas_call | solution.py:177
  63.5 3.4 %collective-permute-done.11 = bf16[384,512]{1,0:T(8,128)(2,1)S(1)} collective-permute-done((bf16[384,512]{1,0:T(8,128)(2,1)S(1)}, bf16[384,512]{1,0:T(8,128)(2,1)S(1)}, u32[]{:S(2)}, u32[]{:S(2)}) %collective-permute-start.11) | collective-permute-done | bytes 393248 | tf_op jit(solution)/shard_map/ppermute | solution.py:105
  66.9 1.1 %fusion.6 = bf16[384,512]{1,0:T(8,128)(2,1)} fusion(f32[384,512]{1,0:T(8,128)S(1)} %shard_map.87, bf16[384,512]{1,0:T(8,128)(2,1)S(1)} %collective-permute-done.11, bf16[384,512]{1,0:T(8,128)(2,1)S(1)} %collective-permute-done.9, bf16[384,512]{1,0:T(8,128)(2,1)S(1)} %collective-permute-done.8, bf16[1,384,512]{2,1,0:T(8,128)(2,1)S(1)} %collective-permute-done.6, ...), kind=kLoop, calls=%fused_computation.10 | loop fusion | flops 1966080 | bytes 3538944 | tf_op jit(solution)/shard_map/convert_element_type | solution.py:271
  (44 shorter events, 2.2 us)
Async XLA Ops:
  0.7 1.3 %copy-start = (bf16[384,1664]{1,0:T(8,128)(2,1)S(1)}, bf16[384,1664]{1,0:T(8,128)(2,1)}, u32[]{:S(2)}) copy-start(bf16[384,1664]{1,0:T(8,128)(2,1)} %hidden_ref.9) | copy-start | bytes 3833860
  4.9 5.1 %collective-permute-start = (bf16[1,384,512]{2,1,0:T(8,128)(2,1)S(1)}, bf16[1,384,512]{2,1,0:T(8,128)(2,1)S(1)}, u32[]{:S(2)}, u32[]{:S(2)}) collective-permute-start(bf16[1,384,512]{2,1,0:T(8,128)(2,1)S(1)} %get-tuple-element.30), channel_id=1, source_target_pairs={{0,1},{1,0},{2,3},{3,2},{4,5},{5,4},{6,7},{7,6},{8,9},{9,8},{10,11... | collective-permute-start | bytes 1179656 | tf_op jit(solution)/shard_map/ppermute | solution.py:105
  5.4 4.6 %copy-start.4 = (s32[384]{0:T(512)S(1)}, s32[384]{0:T(512)}, u32[]{:S(2)}) copy-start(s32[384]{0:T(512)} %param.12) | copy-start | bytes 4612
  9.8 13.5 %collective-permute-start.1 = (bf16[2,384,512]{2,1,0:T(8,128)(2,1)S(1)}, bf16[2,384,512]{2,1,0:T(8,128)(2,1)S(1)}, u32[]{:S(2)}, u32[]{:S(2)}) collective-permute-start(bf16[2,384,512]{2,1,0:T(8,128)(2,1)S(1)} %get-tuple-element.33), channel_id=1, source_target_pairs={{0,1},{1,0},{2,3},{3,2},{4,5},{5,4},{6,7},{7,6},{8,9},{9,8},{10,11... | collective-permute-start | bytes 2359304 | tf_op jit(solution)/shard_map/ppermute | solution.py:105
  10.0 9.0 %slice-start = ((s8[6815744]{0:T(1024)(128)(4,1)}), s8[4194304]{0:T(1024)(128)(4,1)S(1)}, s32[]{:S(2)}) async-start(s8[6815744]{0:T(1024)(128)(4,1)} %bitcast.50), calls=%async_computation | async-start | bytes 8388608
  10.1 13.2 %collective-permute-start.2 = (bf16[384,512]{1,0:T(8,128)(2,1)S(1)}, bf16[384,512]{1,0:T(8,128)(2,1)S(1)}, u32[]{:S(2)}, u32[]{:S(2)}) collective-permute-start(bf16[384,512]{1,0:T(8,128)(2,1)S(1)} %fusion.12.refs_1_), channel_id=1, source_target_pairs={{0,2},{1,3},{2,0},{3,1},{4,6},{5,7},{6,4},{7,5},{8,10},{9,11},{10,... | collective-permute-start | bytes 1179656 | tf_op jit(solution)/shard_map/ppermute | solution.py:105
  13.1 5.8 %slice-start.1 = ((s8[6815744]{0:T(1024)(128)(4,1)}), s8[2621440]{0:T(1024)(128)(4,1)S(1)}, s32[]{:S(2)}) async-start(s8[6815744]{0:T(1024)(128)(4,1)} %bitcast.50), calls=%async_computation.1 | async-start | bytes 5242880
  18.9 17.7 %collective-permute-start.3 = (bf16[2,384,512]{2,1,0:T(8,128)(2,1)S(1)}, bf16[2,384,512]{2,1,0:T(8,128)(2,1)S(1)}, u32[]{:S(2)}, u32[]{:S(2)}) collective-permute-start(bf16[2,384,512]{2,1,0:T(8,128)(2,1)S(1)} %get-tuple-element.40), channel_id=1, source_target_pairs={{0,1},{1,0},{2,3},{3,2},{4,5},{5,4},{6,7},{7,6},{8,9},{9,8},{10,11... | collective-permute-start | bytes 2359304 | tf_op jit(solution)/shard_map/ppermute | solution.py:105
  23.6 13.0 %collective-permute-start.5 = (bf16[448,512]{1,0:T(8,128)(2,1)S(1)}, bf16[448,512]{1,0:T(8,128)(2,1)S(1)}, u32[]{:S(2)}, u32[]{:S(2)}) collective-permute-start(bf16[448,512]{1,0:T(8,128)(2,1)S(1)} %fusion.10.refs_1_), channel_id=1, source_target_pairs={{0,4},{1,5},{2,6},{3,7},{4,0},{5,1},{6,2},{7,3},{8,12},{9,13},{10,... | collective-permute-start | bytes 1376264 | tf_op jit(solution)/shard_map/ppermute | solution.py:105
  25.3 11.3 %collective-permute-start.4 = (bf16[384,512]{1,0:T(8,128)(2,1)S(1)}, bf16[384,512]{1,0:T(8,128)(2,1)S(1)}, u32[]{:S(2)}, u32[]{:S(2)}) collective-permute-start(bf16[384,512]{1,0:T(8,128)(2,1)S(1)} %fusion.13.refs_2_), channel_id=1, source_target_pairs={{0,2},{1,3},{2,0},{3,1},{4,6},{5,7},{6,4},{7,5},{8,10},{9,11},{10,... | collective-permute-start | bytes 1179656 | tf_op jit(solution)/shard_map/ppermute | solution.py:105
  32.0 14.1 %collective-permute-start.7 = (bf16[2,384,512]{2,1,0:T(8,128)(2,1)S(1)}, bf16[2,384,512]{2,1,0:T(8,128)(2,1)S(1)}, u32[]{:S(2)}, u32[]{:S(2)}) collective-permute-start(bf16[2,384,512]{2,1,0:T(8,128)(2,1)S(1)} %get-tuple-element.45), channel_id=1, source_target_pairs={{0,1},{1,0},{2,3},{3,2},{4,5},{5,4},{6,7},{7,6},{8,9},{9,8},{10,11... | collective-permute-start | bytes 2359304 | tf_op jit(solution)/shard_map/ppermute | solution.py:105
  37.0 12.1 %collective-permute-start.10 = (bf16[448,512]{1,0:T(8,128)(2,1)S(1)}, bf16[448,512]{1,0:T(8,128)(2,1)S(1)}, u32[]{:S(2)}, u32[]{:S(2)}) collective-permute-start(bf16[448,512]{1,0:T(8,128)(2,1)S(1)} %fusion.11.refs_2_), channel_id=1, source_target_pairs={{0,2},{1,3},{2,0},{3,1},{4,6},{5,7},{6,4},{7,5},{8,10},{9,11},{10,... | collective-permute-start | bytes 1376264 | tf_op jit(solution)/shard_map/ppermute | solution.py:105
  38.0 25.5 %collective-permute-start.9 = (bf16[384,512]{1,0:T(8,128)(2,1)S(1)}, bf16[384,512]{1,0:T(8,128)(2,1)S(1)}, u32[]{:S(2)}, u32[]{:S(2)}) collective-permute-start(bf16[384,512]{1,0:T(8,128)(2,1)S(1)} %fusion.8.refs_1_), channel_id=1, source_target_pairs={{0,8},{1,9},{2,10},{3,11},{4,12},{5,13},{6,14},{7,15},{8,0},{9,1},... | collective-permute-start | bytes 1179656 | tf_op jit(solution)/shard_map/ppermute | solution.py:105
  46.0 14.8 %copy-start.1 = (bf16[32,64,512]{2,1,0:T(8,128)(2,1)S(1)}, bf16[32,64,512]{2,1,0:T(8,128)(2,1)}, u32[]{:S(2)}) copy-start(bf16[32,64,512]{2,1,0:T(8,128)(2,1)} %param.11) | copy-start | bytes 6291460
  46.0 14.8 %copy-start.2 = (s32[32]{0:T(128)S(1)}, s32[32]{0:T(128)}, u32[]{:S(2)}) copy-start(s32[32]{0:T(128)} %first_ref.1) | copy-start | bytes 388
  46.0 14.8 %copy-start.3 = (s32[32]{0:T(128)S(1)}, s32[32]{0:T(128)}, u32[]{:S(2)}) copy-start(s32[32]{0:T(128)} %length_ref.1) | copy-start | bytes 388
  46.0 17.5 %collective-permute-start.6 = (bf16[1,384,512]{2,1,0:T(8,128)(2,1)S(1)}, bf16[1,384,512]{2,1,0:T(8,128)(2,1)S(1)}, u32[]{:S(2)}, u32[]{:S(2)}) collective-permute-start(bf16[1,384,512]{2,1,0:T(8,128)(2,1)S(1)} %get-tuple-element.44), channel_id=1, source_target_pairs={{0,1},{1,0},{2,3},{3,2},{4,5},{5,4},{6,7},{7,6},{8,9},{9,8},{10,11... | collective-permute-start | bytes 1179656 | tf_op jit(solution)/shard_map/ppermute | solution.py:105
  46.2 17.3 %collective-permute-start.8 = (bf16[384,512]{1,0:T(8,128)(2,1)S(1)}, bf16[384,512]{1,0:T(8,128)(2,1)S(1)}, u32[]{:S(2)}, u32[]{:S(2)}) collective-permute-start(bf16[384,512]{1,0:T(8,128)(2,1)S(1)} %fusion.15), channel_id=1, source_target_pairs={{0,2},{1,3},{2,0},{3,1},{4,6},{5,7},{6,4},{7,5},{8,10},{9,11},{10,... | collective-permute-start | bytes 1179656 | tf_op jit(solution)/shard_map/ppermute | solution.py:105
  49.3 17.6 %collective-permute-start.11 = (bf16[384,512]{1,0:T(8,128)(2,1)S(1)}, bf16[384,512]{1,0:T(8,128)(2,1)S(1)}, u32[]{:S(2)}, u32[]{:S(2)}) collective-permute-start(bf16[384,512]{1,0:T(8,128)(2,1)S(1)} %fusion.2), channel_id=1, source_target_pairs={{0,4},{1,5},{2,6},{3,7},{4,0},{5,1},{6,2},{7,3},{8,12},{9,13},{10,... | collective-permute-start | bytes 1179656 | tf_op jit(solution)/shard_map/ppermute | solution.py:105
  51.0 8.4 %collective-permute-start.12 = (bf16[64,384]{1,0:T(8,128)(2,1)S(1)}, bf16[64,384]{1,0:T(8,128)(2,1)S(1)}, u32[]{:S(2)}, u32[]{:S(2)}) collective-permute-start(bf16[64,384]{1,0:T(8,128)(2,1)S(1)} %fusion.16), channel_id=1, source_target_pairs={{0,8},{1,9},{2,10},{3,11},{4,12},{5,13},{6,14},{7,15},{8,0},{9,1},... | collective-permute-start | bytes 147464 | tf_op jit(solution)/shard_map/ppermute | solution.py:105
  59.4 1.4 %collective-permute-start.13 = (f32[64,384]{1,0:T(8,128)S(1)}, f32[64,384]{1,0:T(8,128)S(1)}, u32[]{:S(2)}, u32[]{:S(2)}) collective-permute-start(f32[64,384]{1,0:T(8,128)S(1)} %convert_add_fusion), channel_id=1, source_target_pairs={{0,1},{1,0},{2,3},{3,2},{4,5},{5,4},{6,7},{7,6},{8,9},{9,8},{10,11... | collective-permute-start | bytes 294920 | tf_op jit(solution)/shard_map/ppermute | solution.py:105

commit v20 on v16

--- a/solution.py
+++ b/solution.py
@@ -203,7 +203,7 @@
     kept_home, crossed, incoming = {}, {}, {}
 
     far = [4 << at for at in range((units - 1).bit_length())]
-    packed, steps = None, [*far[:1], near, *far[1:], core]
+    packed, steps = None, [*far[:1], core, *far[1:], near]
 
     def send(value, bit):
         nonlocal packed
@@ -240,6 +240,10 @@
             ready,
         )
         base += sent + kept
+        if packed is not None and steps[:1] == [core]:
+            steps.pop(0)
+            moved, results = lax.optimization_barrier((swap(packed, core, total), results))
+            packed = packed + moved
         if unit < top:
             kept_home[unit + 1] = results[1]
         if not unit:

time: 68.4 us -> 70.2 us (1.026)
  starting transfers between devices: 15.2 us -> 16.7 us
    ppermute x14 -> x15, starting transfers between devices: 15.2 us -> 16.7 us  [swap(): lax.ppermute(value, 'tensor', [(place, place ^ bit) for place in range(to...]
    ppermute x14 -> x15, waiting for transfers between devices: 17.1 us -> 17.4 us  [swap(): lax.ppermute(value, 'tensor', [(place, place ^ bit) for place in range(to...]
  transfers between devices with their start and end apart: 14 -> 15, of which waited for: 5 -> 4; matrix products, arithmetic and copies ran while one was open for 8% -> 8% of each run, Pallas kernels for 35% -> 34%
where the time goes in v20:
time: 70.2 us; the launch traced here: 69.8 us
  Pallas kernels  26.7 us (38%)
  waiting for transfers between devices  17.4 us (25%)
  starting transfers between devices  16.7 us (24%)
  matrix products  3.92 us (6%)
  other arithmetic  3.47 us (5%)
  local copies, waits for them, and re-layouts  1.34 us (2%)
    pallas_call x5, Pallas kernels, product(): pl.pallas_call(functools.partial(product_body, base=base, sent=sent, kept...  24 us
    ppermute x15, waiting for transfers between devices, swap(): lax.ppermute(value, 'tensor', [(place, place ^ bit) for place in range(to...  17.4 us
    ppermute x15, starting transfers between devices, swap(): lax.ppermute(value, 'tensor', [(place, place ^ bit) for place in range(to...  16.7 us
    unnamed x1, matrix products  3.92 us
    pallas_call x1, Pallas kernels, expand(): pl.pallas_call(expand_body, in_specs=[pl.BlockSpec(memory_space=pltpu.SME...  2.71 us
  transfers between devices with their start and end apart: 15, of which 4 were waited for; matrix products, arithmetic and copies ran while one was open for 8% of the time, Pallas kernels for 34%

profile of v20, /device:TPU:0, one launch (start us, length us, event | category | flops | bytes accessed | tf_op | source)
XLA Modules:
  0.0 69.8 jit_solution(7553004434463639278)
XLA Ops:
  0.0 0.7 broadcast_xor_fusion.table_ref
  0.7 1.3 %copy-done = bf16[384,1664]{1,0:T(8,128)(2,1)S(1)} copy-done((bf16[384,1664]{1,0:T(8,128)(2,1)S(1)}, bf16[384,1664]{1,0:T(8,128)(2,1)}, u32[]{:S(2)}) %copy-start) | copy-done | bytes 1277976
  2.0 2.9 %shard_map.82 = (bf16[1,384,512]{2,1,0:T(8,128)(2,1)S(1)}, bf16[2,1664,512]{2,1,0:T(8,128)(2,1)S(1)}) custom-call(s32[16]{0:T(128)S(1)} %broadcast_xor_fusion.table_ref, bf16[384,1664]{1,0:T(8,128)(2,1)S(1)} %copy-done, bf16[1664,8192]{1,0:T(8,128)(2,1)} %down_ref.9), custom_call_target="tpu_custom_call" | custom-call | flops 3000000000 | bytes 1024 | tf_op jit(solution)/shard_map/pallas_call | solution.py:82
  4.9 0.5 collective-permute-start
  5.4 4.4 %shard_map.83 = (bf16[2,384,512]{2,1,0:T(8,128)(2,1)S(1)}, f32[1,384,512]{2,1,0:T(8,128)S(1)}, bf16[2,1664,512]{2,1,0:T(8,128)(2,1)S(1)}) custom-call(s32[16]{0:T(128)S(1)} %broadcast_xor_fusion.table_ref, bf16[384,1664]{1,0:T(8,128)(2,1)S(1)} %copy-done, bf16[1664,8192]{1,0:T(8,128)(2,1)} %down_ref.9, ...), custom_call_target="tpu_custom_call", output_to_operand_aliasing={{2}: (3, {})} | custom-call | flops 3000000000 | bytes 1024 | tf_op jit(solution)/shard_map/pallas_call | solution.py:82
  10.1 3.0 %collective-permute-start.2 = (bf16[384,512]{1,0:T(8,128)(2,1)S(1)}, bf16[384,512]{1,0:T(8,128)(2,1)S(1)}, u32[]{:S(2)}, u32[]{:S(2)}) collective-permute-start(bf16[384,512]{1,0:T(8,128)(2,1)S(1)} %fusion.10.refs_1_), channel_id=1, source_target_pairs={{0,2},{1,3},{2,0},{3,1},{4,6},{5,7},{6,4},{7,5},{8,10},{9,11},{10,... | collective-permute-start | bytes 1179656 | tf_op jit(solution)/shard_map/ppermute | solution.py:105
  13.1 5.7 %shard_map.84 = (bf16[2,384,512]{2,1,0:T(8,128)(2,1)S(1)}, f32[2,384,512]{2,1,0:T(8,128)S(1)}, bf16[2,1664,512]{2,1,0:T(8,128)(2,1)S(1)}) custom-call(s32[16]{0:T(128)S(1)} %broadcast_xor_fusion.table_ref, bf16[384,1664]{1,0:T(8,128)(2,1)S(1)} %copy-done, bf16[1664,8192]{1,0:T(8,128)(2,1)} %down_ref.9, ...), custom_call_target="tpu_custom_call", output_to_operand_aliasing={{2}: (3, {})} | custom-call | flops 3000000000 | bytes 1024 | tf_op jit(solution)/shard_map/pallas_call | solution.py:82
  19.0 3.9 %fusion.15 = f32[384,2048]{0,1:S(1)} fusion(bf16[384,1664]{1,0:T(8,128)(2,1)S(1)} %copy-done, bf16[1664,2048]{0,1:T(8,128)(2,1)S(1)} %bitcast.46), kind=kOutput, calls=%fused_computation.30 | convolution fusion | flops 2617245696 | bytes 11239424
  23.6 1.6 %collective-permute-start.3 = (bf16[448,512]{1,0:T(8,128)(2,1)S(1)}, bf16[448,512]{1,0:T(8,128)(2,1)S(1)}, u32[]{:S(2)}, u32[]{:S(2)}) collective-permute-start(bf16[448,512]{1,0:T(8,128)(2,1)S(1)} %fusion.9.refs_1_), channel_id=1, source_target_pairs={{0,4},{1,5},{2,6},{3,7},{4,0},{5,1},{6,2},{7,3},{8,12},{9,13},{10,... | collective-permute-start | bytes 1376264 | tf_op jit(solution)/shard_map/ppermute | solution.py:105
  25.3 1.1 %collective-permute-start.6 = (bf16[384,512]{1,0:T(8,128)(2,1)S(1)}, bf16[384,512]{1,0:T(8,128)(2,1)S(1)}, u32[]{:S(2)}, u32[]{:S(2)}) collective-permute-start(bf16[384,512]{1,0:T(8,128)(2,1)S(1)} %fusion.11.refs_2_), channel_id=1, source_target_pairs={{0,2},{1,3},{2,0},{3,1},{4,6},{5,7},{6,4},{7,5},{8,10},{9,11},{10,... | collective-permute-start | bytes 1179656 | tf_op jit(solution)/shard_map/ppermute | solution.py:105
  26.4 5.6 %shard_map.85 = (bf16[2,384,512]{2,1,0:T(8,128)(2,1)S(1)}, f32[2,384,512]{2,1,0:T(8,128)S(1)}, bf16[2,1664,512]{2,1,0:T(8,128)(2,1)S(1)}) custom-call(s32[16]{0:T(128)S(1)} %broadcast_xor_fusion.table_ref, bf16[384,1664]{1,0:T(8,128)(2,1)S(1)} %copy-done, bf16[1664,8192]{1,0:T(8,128)(2,1)} %down_ref.9, ...), custom_call_target="tpu_custom_call", output_to_operand_aliasing={{2}: (3, {})} | custom-call | flops 3000000000 | bytes 1024 | tf_op jit(solution)/shard_map/pallas_call | solution.py:82
  32.1 4.5 %collective-permute-done.6 = bf16[384,512]{1,0:T(8,128)(2,1)S(1)} collective-permute-done((bf16[384,512]{1,0:T(8,128)(2,1)S(1)}, bf16[384,512]{1,0:T(8,128)(2,1)S(1)}, u32[]{:S(2)}, u32[]{:S(2)}) %collective-permute-start.6) | collective-permute-done | bytes 393248 | tf_op jit(solution)/shard_map/ppermute | solution.py:105
  37.0 1.0 %collective-permute-start.9 = (bf16[384,512]{1,0:T(8,128)(2,1)S(1)}, bf16[384,512]{1,0:T(8,128)(2,1)S(1)}, u32[]{:S(2)}, u32[]{:S(2)}) collective-permute-start(bf16[384,512]{1,0:T(8,128)(2,1)S(1)} %fusion.12.refs_2_), channel_id=1, source_target_pairs={{0,2},{1,3},{2,0},{3,1},{4,6},{5,7},{6,4},{7,5},{8,10},{9,11},{10,... | collective-permute-start | bytes 1179656 | tf_op jit(solution)/shard_map/ppermute | solution.py:105
  38.1 2.7 %collective-permute-start.11 = (bf16[384,512]{1,0:T(8,128)(2,1)S(1)}, bf16[384,512]{1,0:T(8,128)(2,1)S(1)}, u32[]{:S(2)}, u32[]{:S(2)}) collective-permute-start(bf16[384,512]{1,0:T(8,128)(2,1)S(1)} %fusion.7.refs_1_), channel_id=1, source_target_pairs={{0,8},{1,9},{2,10},{3,11},{4,12},{5,13},{6,14},{7,15},{8,0},{9,1},... | collective-permute-start | bytes 1179656 | tf_op jit(solution)/shard_map/ppermute | solution.py:105
  40.7 5.4 %shard_map.86 = (bf16[1,384,512]{2,1,0:T(8,128)(2,1)S(1)}, f32[3,384,512]{2,1,0:T(8,128)S(1)}, bf16[2,1664,512]{2,1,0:T(8,128)(2,1)S(1)}) custom-call(s32[16]{0:T(128)S(1)} %broadcast_xor_fusion.table_ref, bf16[384,1664]{1,0:T(8,128)(2,1)S(1)} %copy-done, bf16[1664,8192]{1,0:T(8,128)(2,1)} %down_ref.9, ...), custom_call_target="tpu_custom_call", output_to_operand_aliasing={{2}: (3, {})} | custom-call | flops 3000000000 | bytes 1024 | tf_op jit(solution)/shard_map/pallas_call | solution.py:82
  46.4 1.4 %collective-permute-done.9 = bf16[384,512]{1,0:T(8,128)(2,1)S(1)} collective-permute-done((bf16[384,512]{1,0:T(8,128)(2,1)S(1)}, bf16[384,512]{1,0:T(8,128)(2,1)S(1)}, u32[]{:S(2)}, u32[]{:S(2)}) %collective-permute-start.9) | collective-permute-done | bytes 393248 | tf_op jit(solution)/shard_map/ppermute | solution.py:105
  47.9 1.6 %collective-permute-start.12 = (bf16[384,512]{1,0:T(8,128)(2,1)S(1)}, bf16[384,512]{1,0:T(8,128)(2,1)S(1)}, u32[]{:S(2)}, u32[]{:S(2)}) collective-permute-start(bf16[384,512]{1,0:T(8,128)(2,1)S(1)} %fusion.1), channel_id=1, source_target_pairs={{0,4},{1,5},{2,6},{3,7},{4,0},{5,1},{6,2},{7,3},{8,12},{9,13},{10,... | collective-permute-start | bytes 1179656 | tf_op jit(solution)/shard_map/ppermute | solution.py:105
  49.7 0.8 %collective-permute-start.10 = (bf16[384,512]{1,0:T(8,128)(2,1)S(1)}, bf16[384,512]{1,0:T(8,128)(2,1)S(1)}, u32[]{:S(2)}, u32[]{:S(2)}) collective-permute-start(bf16[384,512]{1,0:T(8,128)(2,1)S(1)} %fusion.13), channel_id=1, source_target_pairs={{0,2},{1,3},{2,0},{3,1},{4,6},{5,7},{6,4},{7,5},{8,10},{9,11},{10,... | collective-permute-start | bytes 1179656 | tf_op jit(solution)/shard_map/ppermute | solution.py:105
  50.5 2.7 %collective-permute-start.13 = (bf16[64,384]{1,0:T(8,128)(2,1)S(1)}, bf16[64,384]{1,0:T(8,128)(2,1)S(1)}, u32[]{:S(2)}, u32[]{:S(2)}) collective-permute-start(bf16[64,384]{1,0:T(8,128)(2,1)S(1)} %get-tuple-element.51), channel_id=1, source_target_pairs={{0,8},{1,9},{2,10},{3,11},{4,12},{5,13},{6,14},{7,15},{8,0},{9,1},... | collective-permute-start | bytes 147464 | tf_op jit(solution)/shard_map/ppermute | solution.py:105
  53.1 8.0 %collective-permute-done.13 = bf16[64,384]{1,0:T(8,128)(2,1)S(1)} collective-permute-done((bf16[64,384]{1,0:T(8,128)(2,1)S(1)}, bf16[64,384]{1,0:T(8,128)(2,1)S(1)}, u32[]{:S(2)}, u32[]{:S(2)}) %collective-permute-start.13) | collective-permute-done | bytes 49184 | tf_op jit(solution)/shard_map/ppermute | solution.py:105
  61.2 1.2 %collective-permute-start.14 = (f32[64,384]{1,0:T(8,128)S(1)}, f32[64,384]{1,0:T(8,128)S(1)}, u32[]{:S(2)}, u32[]{:S(2)}) collective-permute-start(f32[64,384]{1,0:T(8,128)S(1)} %convert_add_fusion), channel_id=1, source_target_pairs={{0,2},{1,3},{2,0},{3,1},{4,6},{5,7},{6,4},{7,5},{8,10},{9,11},{10,... | collective-permute-start | bytes 294920 | tf_op jit(solution)/shard_map/ppermute | solution.py:105
  62.4 3.5 %collective-permute-done.14 = f32[64,384]{1,0:T(8,128)S(1)} collective-permute-done((f32[64,384]{1,0:T(8,128)S(1)}, f32[64,384]{1,0:T(8,128)S(1)}, u32[]{:S(2)}, u32[]{:S(2)}) %collective-permute-start.14) | collective-permute-done | bytes 98336 | tf_op jit(solution)/shard_map/ppermute | solution.py:105
  65.9 2.7 %shard_map.87 = f32[384,512]{1,0:T(8,128)S(1)} custom-call(s32[32]{0:T(128)S(1)} %copy-done.2, s32[32]{0:T(128)S(1)} %copy-done.3, f32[64,384]{1,0:T(8,128)S(1)} %add.100.packed_ref, bf16[2048,512]{1,0:T(8,128)(2,1)S(1)} %bitcast.42), custom_call_target="tpu_custom_call" | custom-call | flops 1000000 | bytes 1 | tf_op jit(solution)/shard_map/pallas_call | solution.py:177
  68.7 1.1 %fusion.5 = bf16[384,512]{1,0:T(8,128)(2,1)} fusion(f32[384,512]{1,0:T(8,128)S(1)} %shard_map.87, bf16[384,512]{1,0:T(8,128)(2,1)S(1)} %collective-permute-done.12, bf16[384,512]{1,0:T(8,128)(2,1)S(1)} %collective-permute-done.11, bf16[384,512]{1,0:T(8,128)(2,1)S(1)} %collective-permute-done.10, bf16[1,384,512]{2,1,0:T(8,128)(2,1)S(1)} %collective-permute-done.7, ...), kind=kLoop, calls=%fused_computation.9 | loop fusion | flops 1966080 | bytes 3538944 | tf_op jit(solution)/shard_map/convert_element_type | solution.py:271
  (45 shorter events, 2.3 us)
Async XLA Ops:
  0.7 1.3 %copy-start = (bf16[384,1664]{1,0:T(8,128)(2,1)S(1)}, bf16[384,1664]{1,0:T(8,128)(2,1)}, u32[]{:S(2)}) copy-start(bf16[384,1664]{1,0:T(8,128)(2,1)} %hidden_ref.9) | copy-start | bytes 3833860
  4.9 5.1 %collective-permute-start = (bf16[1,384,512]{2,1,0:T(8,128)(2,1)S(1)}, bf16[1,384,512]{2,1,0:T(8,128)(2,1)S(1)}, u32[]{:S(2)}, u32[]{:S(2)}) collective-permute-start(bf16[1,384,512]{2,1,0:T(8,128)(2,1)S(1)} %get-tuple-element.31), channel_id=1, source_target_pairs={{0,1},{1,0},{2,3},{3,2},{4,5},{5,4},{6,7},{7,6},{8,9},{9,8},{10,11... | collective-permute-start | bytes 1179656 | tf_op jit(solution)/shard_map/ppermute | solution.py:105
  5.4 4.6 %copy-start.4 = (s32[384]{0:T(512)S(1)}, s32[384]{0:T(512)}, u32[]{:S(2)}) copy-start(s32[384]{0:T(512)} %param.12) | copy-start | bytes 4612
  9.8 13.5 %collective-permute-start.1 = (bf16[2,384,512]{2,1,0:T(8,128)(2,1)S(1)}, bf16[2,384,512]{2,1,0:T(8,128)(2,1)S(1)}, u32[]{:S(2)}, u32[]{:S(2)}) collective-permute-start(bf16[2,384,512]{2,1,0:T(8,128)(2,1)S(1)} %get-tuple-element.34), channel_id=1, source_target_pairs={{0,1},{1,0},{2,3},{3,2},{4,5},{5,4},{6,7},{7,6},{8,9},{9,8},{10,11... | collective-permute-start | bytes 2359304 | tf_op jit(solution)/shard_map/ppermute | solution.py:105
  10.0 9.0 %slice-start = ((s8[6815744]{0:T(1024)(128)(4,1)}), s8[4194304]{0:T(1024)(128)(4,1)S(1)}, s32[]{:S(2)}) async-start(s8[6815744]{0:T(1024)(128)(4,1)} %bitcast.44), calls=%async_computation | async-start | bytes 8388608
  10.1 13.2 %collective-permute-start.2 = (bf16[384,512]{1,0:T(8,128)(2,1)S(1)}, bf16[384,512]{1,0:T(8,128)(2,1)S(1)}, u32[]{:S(2)}, u32[]{:S(2)}) collective-permute-start(bf16[384,512]{1,0:T(8,128)(2,1)S(1)} %fusion.10.refs_1_), channel_id=1, source_target_pairs={{0,2},{1,3},{2,0},{3,1},{4,6},{5,7},{6,4},{7,5},{8,10},{9,11},{10,... | collective-permute-start | bytes 1179656 | tf_op jit(solution)/shard_map/ppermute | solution.py:105
  13.1 5.8 %slice-start.1 = ((s8[6815744]{0:T(1024)(128)(4,1)}), s8[2621440]{0:T(1024)(128)(4,1)S(1)}, s32[]{:S(2)}) async-start(s8[6815744]{0:T(1024)(128)(4,1)} %bitcast.44), calls=%async_computation.1 | async-start | bytes 5242880
  18.9 17.8 %collective-permute-start.5 = (bf16[2,384,512]{2,1,0:T(8,128)(2,1)S(1)}, bf16[2,384,512]{2,1,0:T(8,128)(2,1)S(1)}, u32[]{:S(2)}, u32[]{:S(2)}) collective-permute-start(bf16[2,384,512]{2,1,0:T(8,128)(2,1)S(1)} %get-tuple-element.41), channel_id=1, source_target_pairs={{0,1},{1,0},{2,3},{3,2},{4,5},{5,4},{6,7},{7,6},{8,9},{9,8},{10,11... | collective-permute-start | bytes 2359304 | tf_op jit(solution)/shard_map/ppermute | solution.py:105
  23.6 13.0 %collective-permute-start.3 = (bf16[448,512]{1,0:T(8,128)(2,1)S(1)}, bf16[448,512]{1,0:T(8,128)(2,1)S(1)}, u32[]{:S(2)}, u32[]{:S(2)}) collective-permute-start(bf16[448,512]{1,0:T(8,128)(2,1)S(1)} %fusion.9.refs_1_), channel_id=1, source_target_pairs={{0,4},{1,5},{2,6},{3,7},{4,0},{5,1},{6,2},{7,3},{8,12},{9,13},{10,... | collective-permute-start | bytes 1376264 | tf_op jit(solution)/shard_map/ppermute | solution.py:105
  25.3 11.3 %collective-permute-start.6 = (bf16[384,512]{1,0:T(8,128)(2,1)S(1)}, bf16[384,512]{1,0:T(8,128)(2,1)S(1)}, u32[]{:S(2)}, u32[]{:S(2)}) collective-permute-start(bf16[384,512]{1,0:T(8,128)(2,1)S(1)} %fusion.11.refs_2_), channel_id=1, source_target_pairs={{0,2},{1,3},{2,0},{3,1},{4,6},{5,7},{6,4},{7,5},{8,10},{9,11},{10,... | collective-permute-start | bytes 1179656 | tf_op jit(solution)/shard_map/ppermute | solution.py:105
  32.0 14.3 %collective-permute-start.8 = (bf16[2,384,512]{2,1,0:T(8,128)(2,1)S(1)}, bf16[2,384,512]{2,1,0:T(8,128)(2,1)S(1)}, u32[]{:S(2)}, u32[]{:S(2)}) collective-permute-start(bf16[2,384,512]{2,1,0:T(8,128)(2,1)S(1)} %get-tuple-element.47), channel_id=1, source_target_pairs={{0,1},{1,0},{2,3},{3,2},{4,5},{5,4},{6,7},{7,6},{8,9},{9,8},{10,11... | collective-permute-start | bytes 2359304 | tf_op jit(solution)/shard_map/ppermute | solution.py:105
  37.0 10.7 %collective-permute-start.9 = (bf16[384,512]{1,0:T(8,128)(2,1)S(1)}, bf16[384,512]{1,0:T(8,128)(2,1)S(1)}, u32[]{:S(2)}, u32[]{:S(2)}) collective-permute-start(bf16[384,512]{1,0:T(8,128)(2,1)S(1)} %fusion.12.refs_2_), channel_id=1, source_target_pairs={{0,2},{1,3},{2,0},{3,1},{4,6},{5,7},{6,4},{7,5},{8,10},{9,11},{10,... | collective-permute-start | bytes 1179656 | tf_op jit(solution)/shard_map/ppermute | solution.py:105
  38.0 8.4 %collective-permute-start.4 = (f32[64,384]{1,0:T(8,128)S(1)}, f32[64,384]{1,0:T(8,128)S(1)}, u32[]{:S(2)}, u32[]{:S(2)}) collective-permute-start(f32[64,384]{1,0:T(8,128)S(1)} %bitcast_add_fusion.4), channel_id=1, source_target_pairs={{0,1},{1,0},{2,3},{3,2},{4,5},{5,4},{6,7},{7,6},{8,9},{9,8},{10,11... | collective-permute-start | bytes 294920 | tf_op jit(solution)/shard_map/ppermute | solution.py:105
  38.1 30.6 %collective-permute-start.11 = (bf16[384,512]{1,0:T(8,128)(2,1)S(1)}, bf16[384,512]{1,0:T(8,128)(2,1)S(1)}, u32[]{:S(2)}, u32[]{:S(2)}) collective-permute-start(bf16[384,512]{1,0:T(8,128)(2,1)S(1)} %fusion.7.refs_1_), channel_id=1, source_target_pairs={{0,8},{1,9},{2,10},{3,11},{4,12},{5,13},{6,14},{7,15},{8,0},{9,1},... | collective-permute-start | bytes 1179656 | tf_op jit(solution)/shard_map/ppermute | solution.py:105
  46.1 19.8 %copy-start.1 = (bf16[32,64,512]{2,1,0:T(8,128)(2,1)S(1)}, bf16[32,64,512]{2,1,0:T(8,128)(2,1)}, u32[]{:S(2)}) copy-start(bf16[32,64,512]{2,1,0:T(8,128)(2,1)} %param.11) | copy-start | bytes 6291460
  46.1 19.8 %copy-start.2 = (s32[32]{0:T(128)S(1)}, s32[32]{0:T(128)}, u32[]{:S(2)}) copy-start(s32[32]{0:T(128)} %first_ref.1) | copy-start | bytes 388
  46.1 19.8 %copy-start.3 = (s32[32]{0:T(128)S(1)}, s32[32]{0:T(128)}, u32[]{:S(2)}) copy-start(s32[32]{0:T(128)} %length_ref.1) | copy-start | bytes 388
  46.1 22.5 %collective-permute-start.7 = (bf16[1,384,512]{2,1,0:T(8,128)(2,1)S(1)}, bf16[1,384,512]{2,1,0:T(8,128)(2,1)S(1)}, u32[]{:S(2)}, u32[]{:S(2)}) collective-permute-start(bf16[1,384,512]{2,1,0:T(8,128)(2,1)S(1)} %get-tuple-element.46), channel_id=1, source_target_pairs={{0,1},{1,0},{2,3},{3,2},{4,5},{5,4},{6,7},{7,6},{8,9},{9,8},{10,11... | collective-permute-start | bytes 1179656 | tf_op jit(solution)/shard_map/ppermute | solution.py:105
  47.9 20.7 %collective-permute-start.12 = (bf16[384,512]{1,0:T(8,128)(2,1)S(1)}, bf16[384,512]{1,0:T(8,128)(2,1)S(1)}, u32[]{:S(2)}, u32[]{:S(2)}) collective-permute-start(bf16[384,512]{1,0:T(8,128)(2,1)S(1)} %fusion.1), channel_id=1, source_target_pairs={{0,4},{1,5},{2,6},{3,7},{4,0},{5,1},{6,2},{7,3},{8,12},{9,13},{10,... | collective-permute-start | bytes 1179656 | tf_op jit(solution)/shard_map/ppermute | solution.py:105
  49.7 19.0 %collective-permute-start.10 = (bf16[384,512]{1,0:T(8,128)(2,1)S(1)}, bf16[384,512]{1,0:T(8,128)(2,1)S(1)}, u32[]{:S(2)}, u32[]{:S(2)}) collective-permute-start(bf16[384,512]{1,0:T(8,128)(2,1)S(1)} %fusion.13), channel_id=1, source_target_pairs={{0,2},{1,3},{2,0},{3,1},{4,6},{5,7},{6,4},{7,5},{8,10},{9,11},{10,... | collective-permute-start | bytes 1179656 | tf_op jit(solution)/shard_map/ppermute | solution.py:105
  50.5 10.7 %collective-permute-start.13 = (bf16[64,384]{1,0:T(8,128)(2,1)S(1)}, bf16[64,384]{1,0:T(8,128)(2,1)S(1)}, u32[]{:S(2)}, u32[]{:S(2)}) collective-permute-start(bf16[64,384]{1,0:T(8,128)(2,1)S(1)} %get-tuple-element.51), channel_id=1, source_target_pairs={{0,8},{1,9},{2,10},{3,11},{4,12},{5,13},{6,14},{7,15},{8,0},{9,1},... | collective-permute-start | bytes 147464 | tf_op jit(solution)/shard_map/ppermute | solution.py:105
  61.2 4.7 %collective-permute-start.14 = (f32[64,384]{1,0:T(8,128)S(1)}, f32[64,384]{1,0:T(8,128)S(1)}, u32[]{:S(2)}, u32[]{:S(2)}) collective-permute-start(f32[64,384]{1,0:T(8,128)S(1)} %convert_add_fusion), channel_id=1, source_target_pairs={{0,2},{1,3},{2,0},{3,1},{4,6},{5,7},{6,4},{7,5},{8,10},{9,11},{10,... | collective-permute-start | bytes 294920 | tf_op jit(solution)/shard_map/ppermute | solution.py:105
